TPU v7x, 32 devices: a whole 2x2x4 slice. The times are simulated.
32 devices in a mesh: section: 4 (over x, core), dp: 8 (over z, y).
Axes of the slice: x: 2, y: 2, z: 4, core: 2. Of those that a mesh axis runs over, the one named last changes fastest.
Arguments:
- token_ids: int32 [32, 192], P('dp', 'section'), may hold values from 0 to 31999
- noise: float32 [32, 192, 256], P('dp', 'section'), may hold values from -6 to 6
- loss_mask: int32 [32, 192], P('dp', 'section'), may hold values 0 or 1
- time_index: int32 [32], P('dp'), may hold values from 0 to 999
- seq_counts: int32 [8], replicated, may hold values from 1 to 4
- table: bfloat16 [32000, 256], P(('section', 'dp')), may hold values from -6 to 6
- proj: bfloat16 [256, 1024], P(('section', 'dp')), may hold values from -0.375 to 0.375
- w_time: bfloat16 [4, 256, 1024], P('section'), may hold values from -0.375 to 0.375
- gain_attn: bfloat16 [4, 1024], P('section'), may hold values from 0.25 to 1.75
- w_qkv: bfloat16 [4, 1024, 3072], P('section'), may hold values from -0.1875 to 0.1875
- w_out: bfloat16 [4, 1024, 1024], P('section'), may hold values from -0.75 to 0.75
- gain_mlp: bfloat16 [4, 1024], P('section'), may hold values from 0.25 to 1.75
- w_up: bfloat16 [4, 1024, 4096], P('section'), may hold values from -0.1875 to 0.1875
- w_down: bfloat16 [4, 4096, 1024], P('section'), may hold values from -0.09375 to 0.09375
Outputs:
- seq_loss: float32 [32], P('dp')
- layer_rms: float32 [4, 3], P('section')
- noise_grad: float32 [32, 192, 256], P('dp', 'section')
- table_grad: float32 [32000, 256], P(('section', 'dp'))
- proj_grad: float32 [256, 1024], P(('section', 'dp'))
- w_time_grad: float32 [4, 256, 1024], P('section', 'dp')
- gain_attn_grad: float32 [4, 1024], P('section', 'dp')
- w_qkv_grad: float32 [4, 1024, 3072], P('section', 'dp')
- w_out_grad: float32 [4, 1024, 1024], P('section', 'dp')
- perceptron_gain_gradient: float32 [4, 1024], P('section', 'dp')
- w_up_grad: float32 [4, 1024, 4096], P('section', 'dp')
- w_down_grad: float32 [4, 4096, 1024], P('section', 'dp')
Inputs may be any that keep to these rules, and one draw needn't show every extreme that they name: Index d of dp holds seq_counts[d] real sequences in its first slots; its other slots are padding, left out of the loss and the root mean squares.
All inputs are finite; a program needn't handle non-finite values. No bound on the sum of `loss_mask` on one device may be relied on, other than what follows from the above.
Results may differ from a plain program's by a relative error of at most 0.014.
Values may be sent and summed in bfloat16 or wider, within the bound.
No kernel may reach another device: no remote copies, remote signals or barrier semaphores. Data moves between devices by JAX's collectives and lax.ppermute only.
A program may use at most 256 MiB of HBM per device.

v0:
```python
import math

import jax
import jax.numpy as jnp
from jax import lax
from jax.sharding import PartitionSpec as P

HEADS = 16
NOISE_LEVELS = 1000


NORM_EPSILON = 1e-06
SCORE_SCALE = 0.125
LOGIT_SCALE = 0.0625
SIGMA_LOW_LOG = math.log(0.5)
SIGMA_HIGH_LOG = math.log(50.0)
TIME_ANGLE = 64.0
PRECISION_MAXIMAL = lax.Precision.HIGHEST


def from_behind(x, axis, by):
    size = lax.axis_size(axis)
    pairs = [(i, i + by) for i in range(size) if 0 <= i + by < size]
    return lax.ppermute(x, axis, pairs)


def broadcast(x, axis, root):
    mine = lax.axis_index(axis) == root
    return lax.psum(jnp.where(mine, x, jnp.zeros_like(x)), axis)


def rms_scale(values):
    return values * lax.rsqrt(jnp.mean(values * values, axis=-1, keepdims=True) + NORM_EPSILON)


def norm_gain_vector(values, gain):
    return rms_scale(values) * gain


def gelu_tanh(values):
    return jax.nn.gelu(values, approximate=True)


def noise_level(time_index):
    fraction = time_index.astype(jnp.float32) / (NOISE_LEVELS - 1)
    return jnp.exp(SIGMA_LOW_LOG + (SIGMA_HIGH_LOG - SIGMA_LOW_LOG) * fraction)


def time_features(sigma, width):
    half = width // 2
    rates = jnp.exp(-math.log(10000.0) * jnp.arange(half, dtype=jnp.float32) / half)
    angles = jnp.log(sigma)[..., None] * TIME_ANGLE * rates
    return jnp.concatenate([jnp.cos(angles), jnp.sin(angles)], axis=-1)


def rotary_tables(length, head_size):
    half = head_size // 2
    rates = jnp.exp(-math.log(10000.0) * jnp.arange(half, dtype=jnp.float32) / half)
    angles = jnp.arange(length, dtype=jnp.float32)[:, None] * rates[None, :]
    return (jnp.cos(angles)[:, None, :], jnp.sin(angles)[:, None, :])


def rotate(values, cosines, sines):
    half = values.shape[-1] // 2
    first, second = (values[..., :half], values[..., half:])
    return jnp.concatenate(
        [first * cosines - second * sines, second * cosines + first * sines], axis=-1
    )


def matmul(left_operand, right_operand):
    return jnp.dot(left_operand, right_operand, preferred_element_type=jnp.float32)


def matmul_back(left_operand, right_operand):
    return lax.dot_general(
        left_operand, right_operand, (((1,), (1,)), ((), ())), preferred_element_type=jnp.float32
    )


def matmul_front(left_operand, right_operand):
    return lax.dot_general(
        left_operand, right_operand, (((0,), (0,)), ((), ())), preferred_element_type=jnp.float32
    )


def product_sum(left_operand, right_operand):
    return jnp.einsum(
        "tgu,tgq->uq", left_operand, right_operand, preferred_element_type=jnp.float32
    )


def block_forward(hidden, time_row, params, cosines, sines):
    w_time, gain_attn, w_qkv, w_out, gain_mlp, w_up, w_down = params
    seq_len, width = hidden.shape
    head_size = width // HEADS
    h_first = hidden.astype(jnp.float32) + matmul(time_row[None, :], w_time)
    attn_in = norm_gain_vector(h_first, gain_attn.astype(jnp.float32)).astype(jnp.bfloat16)
    mixed = matmul(attn_in, w_qkv)
    queries = rotate(mixed[:, :width].reshape(seq_len, HEADS, head_size), cosines, sines).astype(
        jnp.bfloat16
    )
    keys = rotate(
        mixed[:, width : 2 * width].reshape(seq_len, HEADS, head_size), cosines, sines
    ).astype(jnp.bfloat16)
    values = mixed[:, 2 * width :].reshape(seq_len, HEADS, head_size).astype(jnp.bfloat16)
    scores = (
        jnp.einsum("qhd,khd->hqk", queries, keys, preferred_element_type=jnp.float32) * SCORE_SCALE
    )
    peak = jnp.max(scores, axis=-1, keepdims=True)
    log_total = peak + jnp.log(jnp.sum(jnp.exp(scores - peak), axis=-1, keepdims=True))
    probs = jnp.exp(scores - log_total)
    probs_low = probs.astype(jnp.bfloat16)
    context = jnp.einsum("hqk,khd->qhd", probs_low, values, preferred_element_type=jnp.float32)
    context = context.reshape(seq_len, width).astype(jnp.bfloat16)
    attn_out = matmul(context, w_out)
    h_second = h_first + attn_out
    mlp_in = norm_gain_vector(h_second, gain_mlp.astype(jnp.float32)).astype(jnp.bfloat16)
    pre_act = matmul(mlp_in, w_up)
    activated = gelu_tanh(pre_act).astype(jnp.bfloat16)
    mlp_out = matmul(activated, w_down)
    h_third = h_second + mlp_out
    saved = (
        h_first,
        attn_in,
        queries,
        keys,
        values,
        probs,
        probs_low,
        context,
        h_second,
        mlp_in,
        pre_act,
        activated,
    )
    return (h_third, attn_out, mlp_out, saved)


def block_backward(hidden, time_row, params, cosines, sines, grad_out):
    w_time, gain_attn, w_qkv, w_out, gain_mlp, w_up, w_down = params
    h_third, attn_out, mlp_out, saved = block_forward(hidden, time_row, params, cosines, sines)
    (
        h_first,
        attn_in,
        queries,
        keys,
        values,
        probs,
        probs_low,
        context,
        h_second,
        mlp_in,
        pre_act,
        activated,
    ) = saved
    seq_len, width = hidden.shape
    grad_act = matmul_back(grad_out, w_down)
    gelu_value, gelu_back = jax.vjp(gelu_tanh, pre_act)
    grad_pre = gelu_back(grad_act)[0].astype(jnp.bfloat16)
    grad_mlp_in = matmul_back(grad_pre, w_up)
    norm_value, norm_back = jax.vjp(norm_gain_vector, h_second, gain_mlp.astype(jnp.float32))
    grad_second, grad_gain_mlp = norm_back(grad_mlp_in)
    grad_second = grad_second + grad_out.astype(jnp.float32)
    grad_attn = grad_second.astype(jnp.bfloat16)
    grad_context = (
        matmul_back(grad_attn, w_out).astype(jnp.bfloat16).reshape(seq_len, HEADS, width // HEADS)
    )
    grad_values = jnp.einsum(
        "hqk,qhd->khd", probs_low, grad_context, preferred_element_type=jnp.float32
    )
    grad_probs = jnp.einsum(
        "qhd,khd->hqk", grad_context, values, preferred_element_type=jnp.float32
    )
    grad_scores = probs * (grad_probs - jnp.sum(grad_probs * probs, axis=-1, keepdims=True))
    grad_scores = grad_scores.astype(jnp.bfloat16)
    query_gradient_rows = (
        jnp.einsum("hqk,khd->qhd", grad_scores, keys, preferred_element_type=jnp.float32)
        * SCORE_SCALE
    )
    grad_keys = (
        jnp.einsum("hqk,qhd->khd", grad_scores, queries, preferred_element_type=jnp.float32)
        * SCORE_SCALE
    )
    grad_mixed = jnp.concatenate(
        [
            rotate(query_gradient_rows, cosines, -sines).reshape(seq_len, width),
            rotate(grad_keys, cosines, -sines).reshape(seq_len, width),
            grad_values.reshape(seq_len, width),
        ],
        axis=1,
    ).astype(jnp.bfloat16)
    grad_attn_in = matmul_back(grad_mixed, w_qkv)
    norm_value, norm_back = jax.vjp(norm_gain_vector, h_first, gain_attn.astype(jnp.float32))
    grad_first, grad_gain_attn = norm_back(grad_attn_in)
    grad_first = grad_first + grad_second
    grad_time = jnp.sum(grad_first, axis=0)
    pieces = (attn_in, grad_mixed, context, grad_attn, mlp_in, grad_pre, activated)
    return (grad_first, pieces, grad_gain_attn, grad_gain_mlp, grad_time)


def body(
    token_ids,
    noise,
    loss_mask,
    time_index,
    seq_counts,
    table,
    proj,
    w_time,
    gain_attn,
    w_qkv,
    w_out,
    gain_mlp,
    w_up,
    w_down,
):
    sections = lax.axis_size("section")
    section = lax.axis_index("section")
    micro, shard = token_ids.shape
    seq_len = shard * sections
    width = w_qkv.shape[1]
    hidden_units = w_up.shape[2]
    count = seq_counts[lax.axis_index("dp")]
    count_all = jnp.sum(seq_counts).astype(jnp.float32)
    valid = (jnp.arange(micro) < count).astype(jnp.float32)
    params = (w_time[0], gain_attn[0], w_qkv[0], w_out[0], gain_mlp[0], w_up[0], w_down[0])
    cosines, sines = rotary_tables(seq_len, width // HEADS)
    own_rows, embedding_table_gradient = jax.vjp(rms_scale, table.astype(jnp.float32))
    table_full, proj_full = (
        lax.all_gather(own_rows.astype(jnp.bfloat16), ("section", "dp"), axis=0, tiled=True),
        lax.all_gather(proj, ("section", "dp"), axis=0, tiled=True),
    )
    sigma = noise_level(time_index)
    shrink = lax.rsqrt(1.0 + sigma * sigma)
    picked = jnp.take(table_full, token_ids, axis=0).astype(jnp.float32)
    inputs = ((picked + sigma[:, None, None] * noise) * shrink[:, None, None]).astype(jnp.bfloat16)
    embedded = jnp.einsum(
        "mse,ed->msd", inputs, proj_full, preferred_element_type=jnp.float32
    ).astype(jnp.bfloat16)
    entry = lax.all_gather(embedded, "section", axis=1, tiled=True)
    time_rows = time_features(sigma, inputs.shape[2]).astype(jnp.bfloat16)
    steps = micro + sections - 1

    def forward_step(step, state):
        kept, finals, square_sums, incoming = state
        slot = step - section
        active = (slot >= 0) & (slot < micro)
        safe = jnp.clip(slot, 0, micro - 1)
        first_input = lax.dynamic_index_in_dim(
            entry, jnp.clip(step, 0, micro - 1), 0, keepdims=False
        )
        hidden = jnp.where(section == 0, first_input, incoming)

        def forward_work(carried):
            kept, finals, square_sums = carried
            third, attn_out, mlp_out, saved = block_forward(
                hidden, time_rows[safe], params, cosines, sines
            )
            sent = third.astype(jnp.bfloat16)
            sums = jnp.stack(
                [jnp.sum(third * third), jnp.sum(attn_out * attn_out), jnp.sum(mlp_out * mlp_out)]
            )
            kept = lax.dynamic_update_index_in_dim(kept, hidden, safe, 0)
            finals = lax.dynamic_update_index_in_dim(finals, sent, safe, 0)
            return (kept, finals, square_sums + sums * valid[safe], sent)

        def forward_rest(carried):
            return carried + (jnp.zeros_like(incoming),)

        kept, finals, square_sums, sent = lax.cond(
            active, forward_work, forward_rest, (kept, finals, square_sums)
        )
        incoming = from_behind(sent, "section", 1)
        return (kept, finals, square_sums, incoming)

    blank = jnp.zeros((micro, seq_len, width), jnp.bfloat16)
    start = (blank, blank, jnp.zeros((3,), jnp.float32), jnp.zeros((seq_len, width), jnp.bfloat16))
    kept, finals, square_sums, incoming = lax.fori_loop(0, steps, forward_step, start)
    total_sums = lax.psum(square_sums, "dp")
    layer_rms = jnp.sqrt(total_sums / (count_all * seq_len * width))[None, :]
    exits = broadcast(finals, "section", sections - 1)
    mine = lax.dynamic_slice_in_dim(exits, section * shard, shard, 1)
    mine = mine.reshape(micro * shard, width).astype(jnp.float32)
    normalized_rows, head_back = jax.vjp(rms_scale, mine)
    feats = normalized_rows.astype(jnp.bfloat16)
    latent = matmul_back(feats, proj_full).astype(jnp.bfloat16)
    logits = matmul_back(latent, table_full) * LOGIT_SCALE
    peak = jnp.max(logits, axis=1, keepdims=True)
    log_total = peak + jnp.log(jnp.sum(jnp.exp(logits - peak), axis=1, keepdims=True))
    probs = jnp.exp(logits - log_total)
    targets = token_ids.reshape(-1)
    target_logit = jnp.take_along_axis(logits, targets[:, None], axis=1)
    weight = loss_mask.reshape(-1).astype(jnp.float32) * jnp.repeat(valid, shard)
    token_loss = (log_total[:, 0] - target_logit[:, 0]) * weight
    seq_sums = lax.psum(jnp.sum(token_loss.reshape(micro, shard), axis=1), "section")
    seq_loss = seq_sums / seq_len
    onehot = (jnp.arange(logits.shape[1])[None, :] == targets[:, None]).astype(jnp.float32)
    grad_logits = ((probs - onehot) * weight[:, None]).astype(jnp.bfloat16)
    grad_latent = (matmul(grad_logits, table_full) * LOGIT_SCALE).astype(jnp.bfloat16)
    grad_table = matmul_front(grad_logits, latent) * LOGIT_SCALE
    grad_proj = matmul_front(grad_latent, feats)
    grad_rows = head_back(matmul(grad_latent, proj_full))[0]
    exit_grad = lax.all_gather(
        grad_rows.astype(jnp.bfloat16).reshape(micro, shard, width), "section", axis=1, tiled=True
    )

    def backward_step(step, state):
        stores, gains_attn, gains_mlp, time_store, incoming = state
        slot = micro - 1 - (step - (sections - 1 - section))
        active = (slot >= 0) & (slot < micro)
        safe = jnp.clip(slot, 0, micro - 1)
        from_head = lax.dynamic_index_in_dim(exit_grad, safe, 0, keepdims=False)
        grad_out = jnp.where(section == sections - 1, from_head, incoming)

        def backward_work(carried):
            stores, gains_attn, gains_mlp, time_store = carried
            hidden = lax.dynamic_index_in_dim(kept, safe, 0, keepdims=False)
            grad_first, pieces, grad_gain_attn, grad_gain_mlp, grad_time = block_backward(
                hidden, time_rows[safe], params, cosines, sines, grad_out
            )
            sent = grad_first.astype(jnp.bfloat16)
            pieces = pieces + (grad_out, sent)
            stores = tuple(
                (
                    lax.dynamic_update_index_in_dim(store, piece, safe, 0)
                    for store, piece in zip(stores, pieces)
                )
            )
            time_store = lax.dynamic_update_index_in_dim(time_store, grad_time, safe, 0)
            return (
                stores,
                gains_attn + grad_gain_attn,
                gains_mlp + grad_gain_mlp,
                time_store,
                sent,
            )

        def backward_rest(carried):
            return carried + (jnp.zeros_like(incoming),)

        stores, gains_attn, gains_mlp, time_store, sent = lax.cond(
            active, backward_work, backward_rest, (stores, gains_attn, gains_mlp, time_store)
        )
        incoming = from_behind(sent, "section", -1)
        return (stores, gains_attn, gains_mlp, time_store, incoming)

    wide_blank = jnp.zeros((micro, seq_len, 3 * width), jnp.bfloat16)
    unit_blank = jnp.zeros((micro, seq_len, hidden_units), jnp.bfloat16)
    stores = (blank, wide_blank, blank, blank, blank, unit_blank, unit_blank, blank, blank)
    zeros_width = jnp.zeros((width,), jnp.float32)
    start = (
        stores,
        zeros_width,
        zeros_width,
        jnp.zeros((micro, width), jnp.float32),
        jnp.zeros((seq_len, width), jnp.bfloat16),
    )
    stores, gains_attn, gains_mlp, time_store, incoming = lax.fori_loop(
        0, steps, backward_step, start
    )
    (
        attn_in_all,
        grad_mixed_all,
        context_all,
        grad_attn_all,
        mlp_in_all,
        grad_pre_all,
        activated_all,
        grad_mix_all,
        grad_entry_all,
    ) = stores
    time_term = jnp.einsum(
        "me,md->ed", time_rows.astype(jnp.float32), time_store, precision=PRECISION_MAXIMAL
    )
    all_terms = (
        time_term[None],
        gains_attn[None],
        product_sum(attn_in_all, grad_mixed_all)[None],
        product_sum(context_all, grad_attn_all)[None],
        gains_mlp[None],
        product_sum(mlp_in_all, grad_pre_all)[None],
        product_sum(activated_all, grad_mix_all)[None],
    )
    (
        w_time_grad,
        gain_attn_grad,
        w_qkv_grad,
        w_out_grad,
        perceptron_gain_gradient,
        w_up_grad,
        w_down_grad,
    ) = (
        lax.psum_scatter(
            all_terms[0].astype(jnp.bfloat16), "dp", scatter_dimension=1, tiled=True
        ).astype(jnp.float32),
        lax.psum_scatter(
            all_terms[1].astype(jnp.bfloat16), "dp", scatter_dimension=1, tiled=True
        ).astype(jnp.float32),
        lax.psum_scatter(
            all_terms[2].astype(jnp.bfloat16), "dp", scatter_dimension=1, tiled=True
        ).astype(jnp.float32),
        lax.psum_scatter(
            all_terms[3].astype(jnp.bfloat16), "dp", scatter_dimension=1, tiled=True
        ).astype(jnp.float32),
        lax.psum_scatter(
            all_terms[4].astype(jnp.bfloat16), "dp", scatter_dimension=1, tiled=True
        ).astype(jnp.float32),
        lax.psum_scatter(
            all_terms[5].astype(jnp.bfloat16), "dp", scatter_dimension=1, tiled=True
        ).astype(jnp.float32),
        lax.psum_scatter(
            all_terms[6].astype(jnp.bfloat16), "dp", scatter_dimension=1, tiled=True
        ).astype(jnp.float32),
    )
    entry_grad = broadcast(grad_entry_all, "section", 0)
    grad_embedded = lax.dynamic_slice_in_dim(entry_grad, section * shard, shard, 1)
    grad_inputs = jnp.einsum(
        "msd,ed->mse", grad_embedded, proj_full, preferred_element_type=jnp.float32
    )
    grad_proj = grad_proj + jnp.einsum(
        "mse,msd->ed", inputs, grad_embedded, preferred_element_type=jnp.float32
    )
    noise_grad = grad_inputs * (sigma * shrink)[:, None, None]
    row_terms = (grad_inputs * shrink[:, None, None]).reshape(-1, grad_inputs.shape[2])
    grad_table = grad_table.at[targets].add(row_terms)
    section_table, section_proj = (
        lax.psum_scatter(
            grad_table.astype(jnp.bfloat16), "section", scatter_dimension=0, tiled=True
        ).astype(jnp.float32),
        lax.psum_scatter(
            grad_proj.astype(jnp.bfloat16), "section", scatter_dimension=0, tiled=True
        ).astype(jnp.float32),
    )
    table_sum, proj_grad = (
        lax.psum_scatter(
            section_table.astype(jnp.bfloat16), "dp", scatter_dimension=0, tiled=True
        ).astype(jnp.float32),
        lax.psum_scatter(
            section_proj.astype(jnp.bfloat16), "dp", scatter_dimension=0, tiled=True
        ).astype(jnp.float32),
    )
    table_grad = embedding_table_gradient(table_sum)[0]
    return (
        seq_loss,
        layer_rms,
        noise_grad,
        table_grad,
        proj_grad,
        w_time_grad,
        gain_attn_grad,
        w_qkv_grad,
        w_out_grad,
        perceptron_gain_gradient,
        w_up_grad,
        w_down_grad,
    )


def solution(mesh):
    return jax.shard_map(
        body,
        mesh=mesh,
        in_specs=(
            P("dp", "section"),
            P("dp", "section", None),
            P("dp", "section"),
            P("dp"),
            P(),
            P(("section", "dp"), None),
            P(("section", "dp"), None),
            P("section", None, None),
            P("section", None),
            P("section", None, None),
            P("section", None, None),
            P("section", None),
            P("section", None, None),
            P("section", None, None),
        ),
        out_specs=(
            P("dp"),
            P("section", None),
            P("dp", "section", None),
            P(("section", "dp"), None),
            P(("section", "dp"), None),
            P("section", "dp", None),
            P("section", "dp"),
            P("section", "dp", None),
            P("section", "dp", None),
            P("section", "dp"),
            P("section", "dp", None),
            P("section", "dp", None),
        ),
        check_vma=False,
    )
```

profile of v0, /device:TPU:0, one launch (start us, length us, event | category | flops | bytes accessed | tf_op | source)
XLA Modules:
  0.0 2163.0 jit_solution(12238910605114858584)
XLA Ops:
  14.5 77.1 %all_gather.13 = bf16[256,1024]{1,0:T(8,128)(2,1)S(1)} all-gather(bf16[8,1024]{1,0:T(8,128)(2,1)} %param.28), channel_id=1, replica_groups=mesh['section'=4,'dp'=8] {'section','dp'}, dimensions={0}, use_global_device_ids=true | all-gather | bytes 540672 | tf_op jit(solution)/shard_map/all_gather | solution.py:232
  91.6 38.0 %all-gather.4.cloned.1.call-done = bf16[32000,256]{1,0:T(8,128)(2,1)} async-done(((bf16[1000,256]{1,0:T(8,128)(2,1)}), bf16[32000,256]{1,0:T(8,128)(2,1)}) %all-gather.4.cloned.1.call-update) | async-done | bytes 16384016 | tf_op jit(solution)/shard_map/all_gather | solution.py:231
  129.6 8.6 gather_fusion
  142.4 15.8 all-gather.6.cloned.1.call-done
  160.9 261.9 %while.65 = (s32[]{:T(128)}, bf16[4,192,1024]{2,1,0:T(8,128)(2,1)}, bf16[4,192,1024]{2,1,0:T(8,128)(2,1)}, f32[3]{0:T(128)S(1)}, bf16[192,1024]{1,0:T(8,128)(2,1...) while((s32[]{:T(128)}, bf16[4,192,1024]{2,1,0:T(8,128)(2,1)}, ...), condition=%wide.region_11.12_spmd.clone.clone.clone, body=%wide.region_1.11_spmd.clone.clone.clone.sunk | while | flops 5005579776 | bytes 76075128 | solution.py:279
  162.8 32.9 %conditional.10 = (bf16[4,192,1024]{2,1,0:T(8,128)(2,1)}, bf16[4,192,1024]{2,1,0:T(8,128)(2,1)}, f32[3]{0:T(128)S(1)}, bf16[192,1024]{1,0:T(8,128)(2,1)}) conditional(s32[]{:T(128)} %convert_element_type.600, (bf16[4,192,1024]{2,1,0:T(8,128)(2,1)}, bf16[4,192,1024]{2,1,0:T(8,128)(2,1)}, f32[3]{0:T(128)S(1)}) %tuple.199, (pred[]{:T(512)}, ...), branch_computations={%region_2.2_spmd, %region_3.10_spmd.clone} | conditional | flops 5005573632 | bytes 74477096 | solution.py:271
  180.7 10.8 bitcast_dynamic-update-slice_fusion
  200.4 32.9 %conditional.10 = (bf16[4,192,1024]{2,1,0:T(8,128)(2,1)}, bf16[4,192,1024]{2,1,0:T(8,128)(2,1)}, f32[3]{0:T(128)S(1)}, bf16[192,1024]{1,0:T(8,128)(2,1)}) conditional(s32[]{:T(128)} %convert_element_type.600, (bf16[4,192,1024]{2,1,0:T(8,128)(2,1)}, bf16[4,192,1024]{2,1,0:T(8,128)(2,1)}, f32[3]{0:T(128)S(1)}) %tuple.199, (pred[]{:T(512)}, ...), branch_computations={%region_2.2_spmd, %region_3.10_spmd.clone} | conditional | flops 5005573632 | bytes 74477096 | solution.py:271
  218.3 10.8 bitcast_dynamic-update-slice_fusion
  239.0 32.9 %conditional.10 = (bf16[4,192,1024]{2,1,0:T(8,128)(2,1)}, bf16[4,192,1024]{2,1,0:T(8,128)(2,1)}, f32[3]{0:T(128)S(1)}, bf16[192,1024]{1,0:T(8,128)(2,1)}) conditional(s32[]{:T(128)} %convert_element_type.600, (bf16[4,192,1024]{2,1,0:T(8,128)(2,1)}, bf16[4,192,1024]{2,1,0:T(8,128)(2,1)}, f32[3]{0:T(128)S(1)}) %tuple.199, (pred[]{:T(512)}, ...), branch_computations={%region_2.2_spmd, %region_3.10_spmd.clone} | conditional | flops 5005573632 | bytes 74477096 | solution.py:271
  256.8 10.8 bitcast_dynamic-update-slice_fusion
  280.7 32.9 %conditional.10 = (bf16[4,192,1024]{2,1,0:T(8,128)(2,1)}, bf16[4,192,1024]{2,1,0:T(8,128)(2,1)}, f32[3]{0:T(128)S(1)}, bf16[192,1024]{1,0:T(8,128)(2,1)}) conditional(s32[]{:T(128)} %convert_element_type.600, (bf16[4,192,1024]{2,1,0:T(8,128)(2,1)}, bf16[4,192,1024]{2,1,0:T(8,128)(2,1)}, f32[3]{0:T(128)S(1)}) %tuple.199, (pred[]{:T(512)}, ...), branch_computations={%region_2.2_spmd, %region_3.10_spmd.clone} | conditional | flops 5005573632 | bytes 74477096 | solution.py:271
  298.5 10.8 bitcast_dynamic-update-slice_fusion
  325.5 39.9 %collective-permute-start = (bf16[192,1024]{1,0:T(8,128)(2,1)}, bf16[192,1024]{1,0:T(8,128)(2,1)S(1)}, u32[]{:S(2)}, u32[]{:S(2)}) collective-permute-start(bf16[192,1024]{1,0:T(8,128)(2,1)} %get-tuple-element.2573), channel_id=1, source_target_pairs={{0,8},{8,16},{16,24},{1,9},{9,17},{17,25},{2,10},{10,18},{18,26},{... | collective-permute-start | bytes 1179656 | tf_op jit(solution)/shard_map/while/body/eval_jaxpr/ppermute | solution.py:24
  381.5 39.9 %collective-permute-start = (bf16[192,1024]{1,0:T(8,128)(2,1)}, bf16[192,1024]{1,0:T(8,128)(2,1)S(1)}, u32[]{:S(2)}, u32[]{:S(2)}) collective-permute-start(bf16[192,1024]{1,0:T(8,128)(2,1)} %get-tuple-element.2573), channel_id=1, source_target_pairs={{0,8},{8,16},{16,24},{1,9},{9,17},{17,25},{2,10},{10,18},{18,26},{... | collective-permute-start | bytes 1179656 | tf_op jit(solution)/shard_map/while/body/eval_jaxpr/ppermute | solution.py:24
  425.7 71.3 %all-reduce.3.cloned.1.call-done = bf16[4,192,1024]{2,1,0:T(8,128)(2,1)} async-done(((bf16[4,192,1024]{2,1,0:T(8,128)(2,1)}), bf16[4,192,1024]{2,1,0:T(8,128)(2,1)}) %all-reduce.3.cloned.1.call-update) | async-done | bytes 1572880 | tf_op jit(solution)/shard_map/psum | solution.py:29
  500.6 14.3 fusion.145
  514.8 10.3 exponential_reduce_fusion.2
  529.1 11.5 multiply_convert_fusion.12
  540.6 12.0 fusion.120
  554.1 19.8 all-gather.8.cloned.1.call-done
  594.0 483.5 %while.66 = (s32[]{:T(128)}, bf16[4,192,1024]{2,1,0:T(8,128)(2,1)}, bf16[4,192,3072]{1,2,0:T(8,128)(2,1)}, bf16[4,192,1024]{1,2,0:T(8,128)(2,1)}, bf16[4,192,102...) while((s32[]{:T(128)}, bf16[4,192,1024]{2,1,0:T(8,128)(2,1)}, ...), condition=%wide.region_34.35_spmd.clone.clone.clone, body=%wide.region_21.34_spmd.clone.clone.clone.sunk | while | flops 8563205120 | bytes 204910864 | solution.py:359
  614.3 180.7 %collective-permute-done.1 = bf16[192,1024]{1,0:T(8,128)(2,1)S(1)} collective-permute-done((bf16[192,1024]{1,0:T(8,128)(2,1)}, bf16[192,1024]{1,0:T(8,128)(2,1)S(1)}, u32[]{:S(2)}, u32[]{:S(2)}) %collective-permute-start.1) | collective-permute-done | bytes 393248 | tf_op jit(solution)/shard_map/while/body/eval_jaxpr/ppermute | solution.py:24
  796.5 61.0 %conditional.11 = (bf16[4,192,1024]{2,1,0:T(8,128)(2,1)}, bf16[4,192,3072]{1,2,0:T(8,128)(2,1)}, bf16[4,192,1024]{1,2,0:T(8,128)(2,1)}, bf16[4,192,1024]{2,1,0:T...) conditional(s32[]{:T(128)} %convert_element_type.601, ...), branch_computations={%region_22.22_spmd, %region_23.0_spmd.clone} | conditional | flops 8563198976 | bytes 201739712 | solution.py:342
  858.8 7.9 collective-permute-done.1
  868.2 60.9 %conditional.11 = (bf16[4,192,1024]{2,1,0:T(8,128)(2,1)}, bf16[4,192,3072]{1,2,0:T(8,128)(2,1)}, bf16[4,192,1024]{1,2,0:T(8,128)(2,1)}, bf16[4,192,1024]{2,1,0:T...) conditional(s32[]{:T(128)} %convert_element_type.601, ...), branch_computations={%region_22.22_spmd, %region_23.0_spmd.clone} | conditional | flops 8563198976 | bytes 201739712 | solution.py:342
  930.4 8.0 collective-permute-done.1
  939.9 60.9 %conditional.11 = (bf16[4,192,1024]{2,1,0:T(8,128)(2,1)}, bf16[4,192,3072]{1,2,0:T(8,128)(2,1)}, bf16[4,192,1024]{1,2,0:T(8,128)(2,1)}, bf16[4,192,1024]{2,1,0:T...) conditional(s32[]{:T(128)} %convert_element_type.601, ...), branch_computations={%region_22.22_spmd, %region_23.0_spmd.clone} | conditional | flops 8563198976 | bytes 201739712 | solution.py:342
  1002.1 8.1 collective-permute-done.1
  1011.6 61.0 %conditional.11 = (bf16[4,192,1024]{2,1,0:T(8,128)(2,1)}, bf16[4,192,3072]{1,2,0:T(8,128)(2,1)}, bf16[4,192,1024]{1,2,0:T(8,128)(2,1)}, bf16[4,192,1024]{2,1,0:T...) conditional(s32[]{:T(128)} %convert_element_type.601, ...), branch_computations={%region_22.22_spmd, %region_23.0_spmd.clone} | conditional | flops 8563198976 | bytes 201739712 | solution.py:342
  1080.5 43.1 %all-reduce.5.cloned.1.call-done = bf16[4,192,1024]{2,1,0:T(8,128)(2,1)} async-done(((bf16[4,192,1024]{2,1,0:T(8,128)(2,1)}), bf16[4,192,1024]{2,1,0:T(8,128)(2,1)}) %all-reduce.5.cloned.1.call-update) | async-done | bytes 1572880 | tf_op jit(solution)/shard_map/psum | solution.py:29
  1126.2 20.0 convolution_multiply_fusion.2
  1148.2 22.6 %scatter_fusion = f32[32000,256]{1,0:T(8,128)} fusion(f32[32000,256]{1,0:T(8,128)} %convolution_multiply_fusion.2, s32[192]{0:T(256)S(1)} %bitcast.331, f32[192,256]{1,0:T(8,128)S(1)} %bitcast.326), kind=kCustom, calls=%fused_computation.2 | custom fusion | flops 49152 | bytes 590592 | tf_op jit(solution)/shard_map/scatter-add | solution.py:426
  1170.8 16.8 convert_element_type.367
  1198.6 12.5 fusion.116
  1211.2 11.6 fusion.115
  1222.9 11.3 fusion.114
  1234.3 77.3 %reduce-scatter.16.cloned.1.call-done = bf16[8000,256]{1,0:T(8,128)(2,1)} async-done(((bf16[32000,256]{1,0:T(8,128)(2,1)}), bf16[8000,256]{1,0:T(8,128)(2,1)}) %reduce-scatter.16.cloned.1.call-update) | async-done | bytes 4096016 | tf_op jit(solution)/shard_map/reduce_scatter | solution.py:428
  1313.0 21.4 psum.30
  1341.3 35.6 %reduce-scatter.34.cloned.1.call-done = bf16[128,1]{1,0:T(8,128)(2,1)} async-done(((bf16[1024,1]{1,0:T(8,128)(2,1)}), bf16[128,1]{1,0:T(8,128)(2,1)}) %reduce-scatter.34.cloned.1.call-update) | async-done | bytes 272
  1378.2 62.2 %reduce-scatter.36.cloned.1.call-done = bf16[128,1]{1,0:T(8,128)(2,1)} async-done(((bf16[1024,1]{1,0:T(8,128)(2,1)}), bf16[128,1]{1,0:T(8,128)(2,1)}) %reduce-scatter.36.cloned.1.call-update) | async-done | bytes 272
  1441.8 63.4 %reduce-scatter.24.cloned.1.call-done = bf16[1,32,1024]{2,1,0:T(8,128)(2,1)} async-done(((bf16[1,256,1024]{2,1,0:T(8,128)(2,1)}), bf16[1,32,1024]{2,1,0:T(8,128)(2,1)}) %reduce-scatter.24.cloned.1.call-update) | async-done | bytes 65552 | tf_op jit(solution)/shard_map/reduce_scatter | solution.py:394
  1506.7 62.1 %reduce-scatter.22.cloned.1.call-done = bf16[8,1024]{1,0:T(8,128)(2,1)} async-done(((bf16[64,1024]{1,0:T(8,128)(2,1)}), bf16[8,1024]{1,0:T(8,128)(2,1)}) %reduce-scatter.22.cloned.1.call-update) | async-done | bytes 16400 | tf_op jit(solution)/shard_map/reduce_scatter | solution.py:439
  1570.1 69.9 %reduce-scatter.28.cloned.1.call-done = bf16[1,128,1024]{2,1,0:T(8,128)(2,1)} async-done(((bf16[1,1024,1024]{2,1,0:T(8,128)(2,1)}), bf16[1,128,1024]{2,1,0:T(8,128)(2,1)}) %reduce-scatter.28.cloned.1.call-update) | async-done | bytes 262160 | tf_op jit(solution)/shard_map/reduce_scatter | solution.py:403
  1641.8 119.2 %reduce-scatter.26.cloned.1.call-done = bf16[1,128,3072]{2,1,0:T(8,128)(2,1)} async-done(((bf16[1,1024,3072]{2,1,0:T(8,128)(2,1)}), bf16[1,128,3072]{2,1,0:T(8,128)(2,1)}) %reduce-scatter.26.cloned.1.call-update) | async-done | bytes 786448 | tf_op jit(solution)/shard_map/reduce_scatter | solution.py:400
  1763.4 149.7 %reduce-scatter.32.cloned.1.call-done = bf16[1,512,1024]{2,1,0:T(8,128)(2,1)} async-done(((bf16[1,4096,1024]{2,1,0:T(8,128)(2,1)}), bf16[1,512,1024]{2,1,0:T(8,128)(2,1)}) %reduce-scatter.32.cloned.1.call-update) | async-done | bytes 1048592 | tf_op jit(solution)/shard_map/reduce_scatter | solution.py:412
  1915.9 148.8 %reduce-scatter.30.cloned.1.call-done = bf16[1,128,4096]{2,1,0:T(8,128)(2,1)} async-done(((bf16[1,1024,4096]{2,1,0:T(8,128)(2,1)}), bf16[1,128,4096]{2,1,0:T(8,128)(2,1)}) %reduce-scatter.30.cloned.1.call-update) | async-done | bytes 1048592 | tf_op jit(solution)/shard_map/reduce_scatter | solution.py:409
  2067.4 85.2 %reduce-scatter.18.cloned.1.call-done = bf16[1000,256]{1,0:T(8,128)(2,1)} async-done(((bf16[8000,256]{1,0:T(8,128)(2,1)}), bf16[1000,256]{1,0:T(8,128)(2,1)}) %reduce-scatter.18.cloned.1.call-update) | async-done | bytes 512016 | tf_op jit(solution)/shard_map/reduce_scatter | solution.py:436
  (716 shorter events, 510.9 us)
Async XLA Ops:
  7.2 131.1 %copy-start.30 = (f32[4,48,256]{2,1,0:T(8,128)S(1)}, f32[4,48,256]{2,1,0:T(8,128)}, u32[]{:S(2)}) copy-start(f32[4,48,256]{2,1,0:T(8,128)} %param.23) | copy-start | bytes 589828
  7.2 133.2 %copy-start.44 = (bf16[1,1024]{1,0:T(2,128)(2,1)S(1)}, bf16[1,1024]{1,0:T(2,128)(2,1)}, u32[]{:S(2)}) copy-start(bf16[1,1024]{1,0:T(2,128)(2,1)} %param.30) | copy-start | bytes 6148
  7.2 133.2 %copy-start.45 = (bf16[1,1024]{1,0:T(2,128)(2,1)S(1)}, bf16[1,1024]{1,0:T(2,128)(2,1)}, u32[]{:S(2)}) copy-start(bf16[1,1024]{1,0:T(2,128)(2,1)} %param.33) | copy-start | bytes 6148
  7.2 133.3 %copy-start.51 = (s32[8]{0:T(128)S(1)}, s32[8]{0:T(128)}, u32[]{:S(2)}) copy-start(s32[8]{0:T(128)} %param.26) | copy-start | bytes 100
  7.2 122.4 %all-gather.4.cloned.1.call-start = ((), (), s32[]{:S(2)}) async-start(), calls=%async_computation.11 | async-start | bytes 16896000 | tf_op jit(solution)/shard_map/all_gather | solution.py:231
  11.8 146.4 %all-gather.6.cloned.1.call-start = ((), (), s32[]{:S(2)}) async-start(), calls=%async_computation.12 | async-start | bytes 1966080 | tf_op jit(solution)/shard_map/all_gather | solution.py:241
  13.8 147.0 %copy-start.46 = (f32[4]{0:T(128)}, f32[4]{0:T(128)S(1)}, u32[]{:S(2)}) copy-start(f32[4]{0:T(128)S(1)} %get-tuple-element.2301) | copy-start | bytes 52
  91.6 67.9 %copy-start.18 = (bf16[256,1024]{1,0:T(8,128)(2,1)}, bf16[256,1024]{1,0:T(8,128)(2,1)S(1)}, u32[]{:S(2)}) copy-start(bf16[256,1024]{1,0:T(8,128)(2,1)S(1)} %all_gather.13) | copy-start | bytes 1572868
  140.0 356.9 %all-reduce.3.cloned.1.call-start = ((), (), s32[]{:S(2)}) async-start(), calls=%async_computation.13 | async-start | bytes 3145728 | tf_op jit(solution)/shard_map/psum | solution.py:29
  195.7 2.8 collective-permute-start
  233.3 3.8 collective-permute-start
  271.9 6.9 collective-permute-start
  313.5 9.3 collective-permute-start
  325.5 41.4 %collective-permute-start = (bf16[192,1024]{1,0:T(8,128)(2,1)}, bf16[192,1024]{1,0:T(8,128)(2,1)S(1)}, u32[]{:S(2)}, u32[]{:S(2)}) collective-permute-start(bf16[192,1024]{1,0:T(8,128)(2,1)} %get-tuple-element.2573), channel_id=1, source_target_pairs={{0,8},{8,16},{16,24},{1,9},{9,17},{17,25},{2,10},{10,18},{18,26},{... | collective-permute-start | bytes 1179656 | tf_op jit(solution)/shard_map/while/body/eval_jaxpr/ppermute | solution.py:24
  369.5 9.3 collective-permute-start
  381.5 41.4 %collective-permute-start = (bf16[192,1024]{1,0:T(8,128)(2,1)}, bf16[192,1024]{1,0:T(8,128)(2,1)S(1)}, u32[]{:S(2)}, u32[]{:S(2)}) collective-permute-start(bf16[192,1024]{1,0:T(8,128)(2,1)} %get-tuple-element.2573), channel_id=1, source_target_pairs={{0,8},{8,16},{16,24},{1,9},{9,17},{17,25},{2,10},{10,18},{18,26},{... | collective-permute-start | bytes 1179656 | tf_op jit(solution)/shard_map/while/body/eval_jaxpr/ppermute | solution.py:24
  422.9 76.5 %copy-start.38 = (f32[3]{0:T(128)}, f32[3]{0:T(128)S(1)}, u32[]{:S(2)}) copy-start(f32[3]{0:T(128)S(1)} %get-tuple-element.1567) | copy-start | bytes 40
  422.9 77.3 %copy-start.19 = (bf16[256,1024]{1,0:T(8,128)(2,1)S(1)}, bf16[256,1024]{1,0:T(8,128)(2,1)}, u32[]{:S(2)}) copy-start(bf16[256,1024]{1,0:T(8,128)(2,1)} %copy-done.18) | copy-start | bytes 1572868
  424.2 149.7 %all-gather.8.cloned.1.call-start = ((), (), s32[]{:S(2)}) async-start(), calls=%async_computation.14 | async-start | bytes 1966080 | tf_op jit(solution)/shard_map/all_gather | solution.py:304
  554.0 569.5 %all-reduce.5.cloned.1.call-start = ((), (), s32[]{:S(2)}) async-start(), calls=%async_computation.15 | async-start | bytes 3145728 | tf_op jit(solution)/shard_map/psum | solution.py:29
  595.7 3.8 collective-permute-start.1
  601.7 9.0 collective-permute-start.1
  613.0 182.0 %collective-permute-start.1 = (bf16[192,1024]{1,0:T(8,128)(2,1)}, bf16[192,1024]{1,0:T(8,128)(2,1)S(1)}, u32[]{:S(2)}, u32[]{:S(2)}) collective-permute-start(bf16[192,1024]{1,0:T(8,128)(2,1)} %get-tuple-element.2613), channel_id=1, source_target_pairs={{8,0},{16,8},{24,16},{9,1},{17,9},{25,17},{10,2},{18,10},{26,18},{... | collective-permute-start | bytes 1179656 | tf_op jit(solution)/shard_map/while/body/eval_jaxpr/ppermute | solution.py:24
  857.5 9.2 collective-permute-start.1
  929.1 9.3 collective-permute-start.1
  1000.8 9.3 collective-permute-start.1
  1072.6 3.8 collective-permute-start.1
  1077.5 46.0 %copy-start.27 = (bf16[4,48,256]{2,1,0:T(8,128)(2,1)S(1)}, bf16[4,48,256]{2,1,0:T(8,128)(2,1)}, u32[]{:S(2)}) copy-start(bf16[4,48,256]{2,1,0:T(8,128)(2,1)} %copy-done.26) | copy-start | bytes 294916
  1077.6 47.3 %copy-start.23 = (bf16[192,1024]{1,0:T(8,128)(2,1)S(1)}, bf16[192,1024]{1,0:T(8,128)(2,1)}, u32[]{:S(2)}) copy-start(bf16[192,1024]{1,0:T(8,128)(2,1)} %copy-done.22) | copy-start | bytes 1179652
  1077.6 47.3 %copy-start.29 = (bf16[192,256]{1,0:T(8,128)(2,1)S(1)}, bf16[192,256]{1,0:T(8,128)(2,1)}, u32[]{:S(2)}) copy-start(bf16[192,256]{1,0:T(8,128)(2,1)} %copy-done.28) | copy-start | bytes 294916
  1080.3 45.8 %copy-start.25 = (bf16[192,256]{1,0:T(8,128)(2,1)S(1)}, bf16[192,256]{1,0:T(8,128)(2,1)}, u32[]{:S(2)}) copy-start(bf16[192,256]{1,0:T(8,128)(2,1)} %copy-done.24) | copy-start | bytes 294916
  1080.3 112.2 %reduce-scatter.20.cloned.1.call-start = ((), (), s32[]{:S(2)}) async-start(), calls=%async_computation.18 | async-start | bytes 655360 | tf_op jit(solution)/shard_map/reduce_scatter | solution.py:431
  1126.1 185.5 %reduce-scatter.16.cloned.1.call-start = ((), (), s32[]{:S(2)}) async-start(), calls=%async_computation.16 | async-start | bytes 20480000 | tf_op jit(solution)/shard_map/reduce_scatter | solution.py:428
  1187.6 189.2 %reduce-scatter.34.cloned.1.call-start = ((), (), s32[]{:S(2)}) async-start(), calls=%async_computation.25 | async-start | bytes 294912
  1189.3 251.2 %reduce-scatter.36.cloned.1.call-start = ((), (), s32[]{:S(2)}) async-start(), calls=%async_computation.26 | async-start | bytes 294912
  1190.3 315.0 %reduce-scatter.24.cloned.1.call-start = ((), (), s32[]{:S(2)}) async-start(), calls=%async_computation.20 | async-start | bytes 589824 | tf_op jit(solution)/shard_map/reduce_scatter | solution.py:394
  1192.5 376.3 %reduce-scatter.22.cloned.1.call-start = ((), (), s32[]{:S(2)}) async-start(), calls=%async_computation.19 | async-start | bytes 147456 | tf_op jit(solution)/shard_map/reduce_scatter | solution.py:439
  1193.2 446.8 %reduce-scatter.28.cloned.1.call-start = ((), (), s32[]{:S(2)}) async-start(), calls=%async_computation.22 | async-start | bytes 2359296 | tf_op jit(solution)/shard_map/reduce_scatter | solution.py:403
  1198.6 562.4 %reduce-scatter.26.cloned.1.call-start = ((), (), s32[]{:S(2)}) async-start(), calls=%async_computation.21 | async-start | bytes 7077888 | tf_op jit(solution)/shard_map/reduce_scatter | solution.py:400
  1211.2 701.9 %reduce-scatter.32.cloned.1.call-start = ((), (), s32[]{:S(2)}) async-start(), calls=%async_computation.24 | async-start | bytes 9437184 | tf_op jit(solution)/shard_map/reduce_scatter | solution.py:412
  1222.9 841.8 %reduce-scatter.30.cloned.1.call-start = ((), (), s32[]{:S(2)}) async-start(), calls=%async_computation.23 | async-start | bytes 9437184 | tf_op jit(solution)/shard_map/reduce_scatter | solution.py:409
  1234.2 77.4 %copy-start.52 = (s32[8]{0:T(128)S(1)}, s32[8]{0:T(128)}, u32[]{:S(2)}) copy-start(s32[8]{0:T(128)} %param.26) | copy-start | bytes 100
  1234.3 78.7 %copy-start.39 = (f32[3]{0:T(128)S(1)}, f32[3]{0:T(128)}, u32[]{:S(2)}) copy-start(f32[3]{0:T(128)} %copy-done.38) | copy-start | bytes 40
  1234.3 100.7 %copy-start.50 = (f32[4]{0:T(128)S(1)}, f32[4]{0:T(128)}, u32[]{:S(2)}) copy-start(f32[4]{0:T(128)} %get-tuple-element.2253) | copy-start | bytes 52
  1234.3 918.3 %reduce-scatter.18.cloned.1.call-start = ((), (), s32[]{:S(2)}) async-start(), calls=%async_computation.17 | async-start | bytes 4608000 | tf_op jit(solution)/shard_map/reduce_scatter | solution.py:436
  1763.4 389.2 %copy-start.21 = (bf16[1000,256]{1,0:T(8,128)(2,1)S(1)}, bf16[1000,256]{1,0:T(8,128)(2,1)}, u32[]{:S(2)}) copy-start(bf16[1000,256]{1,0:T(8,128)(2,1)} %param.27) | copy-start | bytes 1536004
  1763.4 390.5 %copy-start.37 = (f32[1000]{0:T(1024)S(1)}, f32[1000]{0:T(1024)}, u32[]{:S(2)}) copy-start(f32[1000]{0:T(1024)} %copy-done.36) | copy-start | bytes 12004
  1763.4 390.5 %copy-start.35 = (f32[1000]{0:T(1024)S(1)}, f32[1000]{0:T(1024)}, u32[]{:S(2)}) copy-start(f32[1000]{0:T(1024)} %copy-done.34) | copy-start | bytes 12004
  (112 other events, 475.0 us)
Sparse Core Ops, SparseCore 0:
  11.9 117.6 all-gather.3
  140.2 17.9 all-gather.5
  424.3 72.6 all-reduce.2
  554.2 19.6 all-gather.7
  1080.4 43.0 all-reduce.4
  1126.5 21.7 reduce-scatter.19
  1187.7 123.8 reduce-scatter.15
  1315.5 61.2 reduce-scatter.33
  1380.2 60.2 reduce-scatter.35
  1444.2 60.9 reduce-scatter.23
  1508.9 59.8 reduce-scatter.21
  1573.2 66.8 reduce-scatter.27
  1644.0 116.8 reduce-scatter.25
  1764.9 148.1 reduce-scatter.31
  1916.6 148.0 reduce-scatter.29
  2068.5 84.0 reduce-scatter.17
where the time goes:
time: 2170 us; the launch traced here: 2160 us
  waiting for transfers between devices  1290 us (59%)
  matrix products  311 us (14%)
  other arithmetic  192 us (9%)
  local copies, waits for them, and re-layouts  132 us (6%)
  starting transfers between devices  115 us (5%)
  blocking collectives  104 us (5%)
    ppermute x14, waiting for transfers between devices, from_behind(): return lax.ppermute(x, axis, pairs)  228 us
    reduce_scatter x1, waiting for transfers between devices, body(): lax.psum_scatter(all_terms[6].astype(jnp.bfloat16), 'dp', scatter_dimensi...  150 us
    reduce_scatter x1, waiting for transfers between devices, body(): lax.psum_scatter(all_terms[5].astype(jnp.bfloat16), 'dp', scatter_dimensi...  149 us
    dot_general x34, matrix products, matmul(): jnp.dot(left_operand, right_operand, preferred_element_type=jnp.float32)  132 us
    reduce_scatter x1, waiting for transfers between devices, body(): lax.psum_scatter(all_terms[2].astype(jnp.bfloat16), 'dp', scatter_dimensi...  119 us
    psum x2, waiting for transfers between devices, broadcast(): return lax.psum(jnp.where(mine, x, jnp.zeros_like(x)), axis)  114 us
    ppermute x14, starting transfers between devices, from_behind(): return lax.ppermute(x, axis, pairs)  113 us
    unnamed x18, waiting for transfers between devices  98.7 us
  transfers between devices with their start and end apart: 30, of which 29 were waited for; matrix products, arithmetic and copies ran while one was open for 6% of the time, Pallas kernels for 0%

commit v1 on v0

v1 whole, which is shorter than its diff:
```python
import functools, math
import jax
import jax.numpy as jnp
from jax import lax
from jax.experimental import pallas as pl
from jax.experimental.pallas import tpu as pltpu
from jax.sharding import PartitionSpec as P
HEADS=16
NOISE_LEVELS = 1000
LOGIT_SCALE = 0.0625
SIGMA_LOW_LOG = math.log(0.5)
SIGMA_HIGH_LOG = math.log(50.0)
TIME_ANGLE = 64.0
PRECISION_MAXIMAL = lax.Precision.HIGHEST
NORM_EPSILON=1e-6
SCORE_SCALE=0.125
DEPTH=3
F32=jnp.float32; BF=jnp.bfloat16
VMEM_LIMIT=60*1024*1024
GELU_A=math.sqrt(2.0/math.pi); GELU_B=0.044715

def dot(a,b): return jnp.dot(a,b,preferred_element_type=F32)
def dot_nt(a,b): return lax.dot_general(a,b,(((1,),(1,)),((),())),preferred_element_type=F32)
def dot_tn(a,b): return lax.dot_general(a,b,(((0,),(0,)),((),())),preferred_element_type=F32)

def swap_halves(x,mask):
    return jnp.where(mask,pltpu.roll(x,96,1),pltpu.roll(x,32,1))

class Loads:
    def __init__(self,sem,ahead):
        self.sem,self.ahead,self.copies,self.next=sem,ahead,[],0
    def add(self,src,dst):
        k=len(self.copies); self.copies.append(pltpu.make_async_copy(src,dst,self.sem.at[k])); return k
    def fill(self,upto):
        while self.next<min(upto,len(self.copies)):
            self.copies[self.next].start(); self.next+=1
    def wait(self,k):
        self.fill(k+1)
        self.copies[k].wait()
        self.fill(k+1+self.ahead)
class Puts:
    def __init__(self,sem): self.sem,self.copies=sem,[]
    def add(self,src,dst):
        c=pltpu.make_async_copy(src,dst,self.sem.at[len(self.copies)]); c.start(); self.copies.append(c)
    def wait(self):
        for c in self.copies: c.wait()

def fwd_kernel(info,hid_in,far_in,entry,time_rows,gain_attn,gain_mlp,cos,sin,w_qkv,w_out,w_up,w_down,
               s_hid,s_attn,s_qkv,s_prob,s_ctx,s_second,s_mlp,s_gp,s_act,
               o_next,o_sums,o_hid,o_attn,o_qkv,o_prob,o_ctx,o_second,o_mlp,o_gp,o_act,
               b_hid,b_qkvw,b_outw,b_upw,b_downw,b_attn,b_qkv,b_prob,b_ctx,b_second,b_low,b_mlp,b_gp,b_act,wsem,hsem,osem):
    active=info[0]; slot=info[1]; source=info[2]
    width=b_hid.shape[1]; T=b_hid.shape[0]
    nw=w_up.shape[1]//width
    npair=width//128
    @pl.when(active==0)
    def _():
        o_sums[...]=jnp.zeros_like(o_sums)
        o_next[...]=jnp.zeros_like(o_next)
    @pl.when(active==1)
    def _():
        src_copy=pltpu.make_async_copy(entry.at[slot],b_hid,hsem)
        in_copy=pltpu.make_async_copy(hid_in,b_hid,hsem)
        far_copy=pltpu.make_async_copy(far_in,b_hid,hsem)
        @pl.when(source==0)
        def _(): src_copy.start()
        @pl.when(source==1)
        def _(): in_copy.start()
        @pl.when(source==2)
        def _(): far_copy.start()
        ld=Loads(wsem,DEPTH)
        kq=[ld.add(w_qkv.at[:,pl.ds(i*width,width)],b_qkvw.at[i]) for i in range(3)]
        ko=ld.add(w_out,b_outw)
        ku,kd=[],[]
        for i in range(nw):
            ku.append(ld.add(w_up.at[:,pl.ds(i*width,width)],b_upw.at[i]))
            kd.append(ld.add(w_down.at[pl.ds(i*width,width),:],b_downw.at[i]))
        ld.fill(DEPTH)
        outs=Puts(osem)
        in_copy.wait()
        outs.add(b_hid,o_hid.at[slot])
        first=b_hid[...].astype(F32)+time_rows[pl.ds(slot,1),:]
        r1=lax.rsqrt(jnp.mean(first*first,axis=1,keepdims=True)+NORM_EPSILON)
        b_attn[...]=(first*r1*gain_attn[...].astype(F32)).astype(BF)
        outs.add(b_attn,o_attn.at[slot])
        lane=lax.broadcasted_iota(jnp.int32,(T,128),1)
        low=(lane%64)<32
        head0=lane<64
        c_=cos[...]; s_=sin[...]
        a=b_attn[...]
        for i in range(3):
            ld.wait(kq[i])
            m=dot(a,b_qkvw[i])
            if i<2:
                for p in range(npair):
                    x=m[:,p*128:(p+1)*128]
                    b_qkv[:,i*width+p*128:i*width+(p+1)*128]=(x*c_+swap_halves(x,low)*s_).astype(BF)
            else:
                b_qkv[:,i*width:(i+1)*width]=m.astype(BF)
        outs.add(b_qkv,o_qkv.at[slot])
        for p in range(npair):
            q=b_qkv[:,p*128:(p+1)*128]; k=b_qkv[:,width+p*128:width+(p+1)*128]; v=b_qkv[:,2*width+p*128:2*width+(p+1)*128]
            z=jnp.zeros_like(q)
            qs=jnp.concatenate([jnp.where(head0,q,z),jnp.where(head0,z,q)],axis=0)
            s=dot_nt(qs,k)*SCORE_SCALE
            e=jnp.exp(s-jnp.max(s,axis=1,keepdims=True))
            pr=(e*(1.0/jnp.sum(e,axis=1,keepdims=True))).astype(BF)
            b_prob[p]=pr
            c=dot(pr,v)
            b_ctx[:,p*128:(p+1)*128]=jnp.where(head0,c[:T],c[T:]).astype(BF)
        outs.add(b_prob,o_prob.at[slot])
        outs.add(b_ctx,o_ctx.at[slot])
        ld.wait(ko)
        ao=dot(b_ctx[...],b_outw[...])
        second=b_hid[...].astype(F32)+time_rows[pl.ds(slot,1),:]+ao
        b_second[...]=second
        b_low[...]=second.astype(BF)
        outs.add(b_low,o_second.at[slot])
        sum_a=jnp.sum(ao*ao,axis=0,keepdims=True)
        r2=lax.rsqrt(jnp.mean(second*second,axis=1,keepdims=True)+NORM_EPSILON)
        b_mlp[...]=(second*r2*gain_mlp[...].astype(F32)).astype(BF)
        outs.add(b_mlp,o_mlp.at[slot])
        acc=None
        for i in range(nw):
            cols=pl.ds(i*width,width)
            ld.wait(ku[i])
            u=dot(b_mlp[...],b_upw[i])
            u2=u*u
            th=jnp.tanh(GELU_A*(u+GELU_B*u2*u))
            h=0.5*(1.0+th)
            act=(u*h).astype(BF)
            gp=h+0.5*u*(1.0-th*th)*(GELU_A*(1.0+3.0*GELU_B*u2))
            b_act[i]=act
            b_gp[i]=gp.astype(BF)
            outs.add(b_act.at[i],o_act.at[slot,:,cols])
            outs.add(b_gp.at[i],o_gp.at[slot,:,cols])
            ld.wait(kd[i])
            d=dot(act,b_downw[i])
            acc=d if acc is None else acc+d
        third=b_second[...]+acc
        o_next[...]=third.astype(BF)
        o_sums[...]=jnp.concatenate([jnp.sum(third*third,axis=0,keepdims=True),sum_a,jnp.sum(acc*acc,axis=0,keepdims=True)],axis=0)
        outs.wait()

def store_shapes(micro,T,width,hidden):
    npair=width//128
    B=lambda *s: jax.ShapeDtypeStruct((micro,)+s,BF)
    return [B(T,width),B(T,width),B(T,3*width),B(npair,2*T,T),B(T,width),B(T,width),B(T,width),B(T,hidden),B(T,hidden)]

ANY=pl.BlockSpec(memory_space=pl.ANY)
VM=pl.BlockSpec(memory_space=pltpu.VMEM)
SM=pl.BlockSpec(memory_space=pltpu.SMEM)
def layer_forward(info,hid,far,entry,time_rows,ga,gm,cos,sin,w_qkv,w_out,w_up,w_down,stores):
    T,width=hid.shape; hidden=w_up.shape[1]; micro=entry.shape[0]; nw=hidden//width; npair=width//128
    V=lambda *s: pltpu.VMEM(s,BF)
    scratch=[V(T,width),V(3,width,width),V(width,width),V(nw,width,width),V(nw,width,width),
             V(T,width),V(T,3*width),V(npair,2*T,T),V(T,width),pltpu.VMEM((T,width),F32),V(T,width),
             V(T,width),V(nw,T,width),V(nw,T,width),
             pltpu.SemaphoreType.DMA((4+2*nw,)),pltpu.SemaphoreType.DMA,pltpu.SemaphoreType.DMA((7+2*nw,))]
    out=pl.pallas_call(fwd_kernel,
        in_specs=[SM,ANY,ANY,ANY,VM,VM,VM,VM,VM,ANY,ANY,ANY,ANY]+[ANY]*9,
        out_specs=[VM,VM]+[ANY]*9,
        out_shape=[jax.ShapeDtypeStruct((T,width),BF),jax.ShapeDtypeStruct((3,width),F32)]+store_shapes(micro,T,width,hidden),
        input_output_aliases={13+i:2+i for i in range(9)},
        scratch_shapes=scratch,
        compiler_params=pltpu.CompilerParams(vmem_limit_bytes=VMEM_LIMIT),
        cost_estimate=pl.CostEstimate(flops=2*T*width*(4*width+2*hidden),bytes_accessed=2*width*(4*width+2*hidden)+8*1024*1024,transcendentals=0),
        name="layer_fwd",
    )(info,hid,far,entry,time_rows,ga,gm,cos,sin,w_qkv,w_out,w_up,w_down,*stores)
    return out[0],out[1],out[2:]

def bwd_kernel(info,g_in,far_in,exits,time_rows,gain_attn,gain_mlp,cos,sin,w_qkv,w_out,w_up,w_down,
               hid,qkv,prob,sec,gps,
               s_g,s_pre,s_gattn,s_mixed,s_first,
               o_next,o_vec,o_g,o_pre,o_gattn,o_mixed,o_first,
               b_g,b_qkvw,b_outw,b_upw,b_downw,b_hid,b_qkv,b_prob,b_sec,b_gp,b_pre,b_gattn,b_gctx,b_second,b_mixed,wsem,hsem,osem):
    active=info[0]; slot=info[1]; source=info[2]
    width=b_hid.shape[1]; T=b_hid.shape[0]
    nw=w_up.shape[1]//width
    npair=width//128
    @pl.when(active==0)
    def _():
        o_vec[...]=jnp.zeros_like(o_vec)
        o_next[...]=jnp.zeros_like(o_next)
    @pl.when(active==1)
    def _():
        src_copy=pltpu.make_async_copy(exits.at[slot],b_g,hsem)
        in_copy=pltpu.make_async_copy(g_in,b_g,hsem)
        far_copy=pltpu.make_async_copy(far_in,b_g,hsem)
        @pl.when(source==0)
        def _(): src_copy.start()
        @pl.when(source==1)
        def _(): in_copy.start()
        @pl.when(source==2)
        def _(): far_copy.start()
        ld=Loads(wsem,DEPTH)
        kd,kg,ku=[],[],[]
        for i in range(nw):
            cols=pl.ds(i*width,width)
            kd.append(ld.add(w_down.at[cols,:],b_downw.at[i]))
            kg.append(ld.add(gps.at[slot,:,cols],b_gp.at[i]))
            ku.append(ld.add(w_up.at[:,cols],b_upw.at[i]))
        ks=ld.add(sec.at[slot],b_sec)
        ko=ld.add(w_out,b_outw)
        kqkv=ld.add(qkv.at[slot],b_qkv)
        kp=ld.add(prob.at[slot],b_prob)
        kq=[ld.add(w_qkv.at[:,pl.ds(i*width,width)],b_qkvw.at[i]) for i in range(3)]
        kh=ld.add(hid.at[slot],b_hid)
        ld.fill(DEPTH)
        outs=Puts(osem)
        in_copy.wait()
        outs.add(b_g,o_g.at[slot])
        g=b_g[...]
        acc=None
        for i in range(nw):
            ld.wait(kd[i])
            ga=dot_nt(g,b_downw[i])
            ld.wait(kg[i])
            pre=(ga*b_gp[i].astype(F32)).astype(BF)
            b_pre[i]=pre
            outs.add(b_pre.at[i],o_pre.at[slot,:,pl.ds(i*width,width)])
            ld.wait(ku[i])
            d=dot_nt(pre,b_upw[i])
            acc=d if acc is None else acc+d
        ld.wait(ks)
        second=b_sec[...].astype(F32)
        r2=lax.rsqrt(jnp.mean(second*second,axis=1,keepdims=True)+NORM_EPSILON)
        n2=second*r2
        gain_row=jnp.sum(acc*n2,axis=0,keepdims=True)
        gn=acc*gain_mlp[...].astype(F32)
        gs=b_g[...].astype(F32)+r2*(gn-n2*jnp.mean(gn*n2,axis=1,keepdims=True))
        b_second[...]=gs
        b_gattn[...]=gs.astype(BF)
        outs.add(b_gattn,o_gattn.at[slot])
        ld.wait(ko)
        b_gctx[...]=dot_nt(b_gattn[...],b_outw[...]).astype(BF)
        lane=lax.broadcasted_iota(jnp.int32,(T,128),1)
        low=(lane%64)<32
        head0=lane<64
        c_=cos[...]; s_=sin[...]
        ld.wait(kqkv); ld.wait(kp)
        for p in range(npair):
            sl=[slice(i*width+p*128,i*width+(p+1)*128) for i in range(3)]
            q=b_qkv[:,sl[0]]; k=b_qkv[:,sl[1]]; v=b_qkv[:,sl[2]]
            gc=b_gctx[:,p*128:(p+1)*128]
            z=jnp.zeros_like(q)
            qs=jnp.concatenate([jnp.where(head0,q,z),jnp.where(head0,z,q)],axis=0)
            gcs=jnp.concatenate([jnp.where(head0,gc,z),jnp.where(head0,z,gc)],axis=0)
            pl_=b_prob[p]
            b_mixed[:,sl[2]]=dot_tn(pl_,gcs).astype(BF)
            gp=dot_nt(gcs,v)
            pf=pl_.astype(F32)
            gsc=(pf*(gp-jnp.sum(gp*pf,axis=1,keepdims=True))).astype(BF)
            gq=dot(gsc,k)
            gq=jnp.where(head0,gq[:T],gq[T:])*SCORE_SCALE
            gk=dot_tn(gsc,qs)*SCORE_SCALE
            b_mixed[:,sl[0]]=(gq*c_-swap_halves(gq,low)*s_).astype(BF)
            b_mixed[:,sl[1]]=(gk*c_-swap_halves(gk,low)*s_).astype(BF)
        outs.add(b_mixed,o_mixed.at[slot])
        acc=None
        for i in range(3):
            ld.wait(kq[i])
            d=dot_nt(b_mixed[:,i*width:(i+1)*width],b_qkvw[i])
            acc=d if acc is None else acc+d
        ld.wait(kh)
        first=b_hid[...].astype(F32)+time_rows[pl.ds(slot,1),:]
        r1=lax.rsqrt(jnp.mean(first*first,axis=1,keepdims=True)+NORM_EPSILON)
        n1=first*r1
        attn_row=jnp.sum(acc*n1,axis=0,keepdims=True)
        gm=acc*gain_attn[...].astype(F32)
        gf=b_second[...]+r1*(gm-n1*jnp.mean(gm*n1,axis=1,keepdims=True))
        o_next[...]=gf.astype(BF)
        outs.add(o_next,o_first.at[slot])
        o_vec[...]=jnp.concatenate([attn_row,gain_row,jnp.sum(gf,axis=0,keepdims=True)],axis=0)
        outs.wait()

def grad_shapes(micro,T,width,hidden):
    B=lambda *s: jax.ShapeDtypeStruct((micro,)+s,BF)
    return [B(T,width),B(T,hidden),B(T,width),B(T,3*width),B(T,width)]

def layer_backward(info,g,far,exits,time_rows,ga,gm,cos,sin,w_qkv,w_out,w_up,w_down,saved,stores):
    T,width=g.shape; hidden=w_up.shape[1]; micro=exits.shape[0]; nw=hidden//width; npair=width//128
    V=lambda *s: pltpu.VMEM(s,BF)
    scratch=[V(T,width),V(3,width,width),V(width,width),V(nw,width,width),V(nw,width,width),
             V(T,width),V(T,3*width),V(npair,2*T,T),V(T,width),V(nw,T,width),V(nw,T,width),V(T,width),V(T,width),pltpu.VMEM((T,width),F32),V(T,3*width),
             pltpu.SemaphoreType.DMA((8+3*nw,)),pltpu.SemaphoreType.DMA,pltpu.SemaphoreType.DMA((4+nw,))]
    out=pl.pallas_call(bwd_kernel,
        in_specs=[SM,ANY,ANY,ANY,VM,VM,VM,VM,VM]+[ANY]*4+[ANY]*5+[ANY]*5,
        out_specs=[VM,VM]+[ANY]*5,
        out_shape=[jax.ShapeDtypeStruct((T,width),BF),jax.ShapeDtypeStruct((3,width),F32)]+grad_shapes(micro,T,width,hidden),
        input_output_aliases={18+i:2+i for i in range(5)},
        scratch_shapes=scratch,
        compiler_params=pltpu.CompilerParams(vmem_limit_bytes=VMEM_LIMIT),
        cost_estimate=pl.CostEstimate(flops=2*T*width*(4*width+2*hidden),bytes_accessed=2*width*(4*width+2*hidden)+8*1024*1024,transcendentals=0),
        name="layer_bwd",
    )(info,g,far,exits,time_rows,ga,gm,cos,sin,w_qkv,w_out,w_up,w_down,*saved,*stores)
    return out[0],out[1],out[2:]

def rope_tables(T,head):
    half=head//2
    rates=jnp.exp(-math.log(10000.0)*jnp.arange(half,dtype=F32)/half)
    ang=jnp.arange(T,dtype=F32)[:,None]*rates[None,:]
    c=jnp.cos(ang); s=jnp.sin(ang)
    return jnp.concatenate([c,c,c,c],1),jnp.concatenate([-s,s,-s,s],1)


def rms_scale(values):
    return values * lax.rsqrt(jnp.mean(values * values, axis=-1, keepdims=True) + NORM_EPSILON)


def noise_level(time_index):
    fraction = time_index.astype(jnp.float32) / (NOISE_LEVELS - 1)
    return jnp.exp(SIGMA_LOW_LOG + (SIGMA_HIGH_LOG - SIGMA_LOW_LOG) * fraction)


def time_features(sigma, width):
    half = width // 2
    rates = jnp.exp(-math.log(10000.0) * jnp.arange(half, dtype=jnp.float32) / half)
    angles = jnp.log(sigma)[..., None] * TIME_ANGLE * rates
    return jnp.concatenate([jnp.cos(angles), jnp.sin(angles)], axis=-1)


def head_forward_kernel(table, latent, o_mean, o_stats, top, total, mixed):
    step = pl.program_id(0)

    @pl.when(step == 0)
    def _():
        top[...] = jnp.full_like(top, -jnp.inf)
        total[...] = jnp.zeros_like(total)
        mixed[...] = jnp.zeros_like(mixed)

    rows = table[...]
    logits = dot_nt(rows, latent[...])
    peak = jnp.maximum(top[...], jnp.max(logits, axis=0, keepdims=True))
    fade = jnp.exp(top[...] - peak)
    e = jnp.exp(logits - peak)
    total[...] = total[...] * fade + jnp.sum(e, axis=0, keepdims=True)
    mixed[...] = mixed[...] * fade + dot_tn(rows, e.astype(BF))
    top[...] = peak

    @pl.when(step == pl.num_programs(0) - 1)
    def _():
        o_mean[...] = (mixed[...] / total[...]).astype(BF)
        o_stats[...] = jnp.concatenate([top[...], total[...]], axis=0)


def vocab_tile(rows):
    for tile in (800, 500, 400):
        if rows % tile == 0 and tile % 16 == 0:
            return tile
    return rows


def head_forward(table, latent):
    rows, emb = table.shape
    tokens = latent.shape[0]
    tile = vocab_tile(rows)
    return pl.pallas_call(
        head_forward_kernel,
        grid=(rows // tile,),
        in_specs=[pl.BlockSpec((tile, emb), lambda i: (i, 0)), pl.BlockSpec((tokens, emb), lambda i: (0, 0))],
        out_specs=[pl.BlockSpec((emb, tokens), lambda i: (0, 0)), pl.BlockSpec((2, tokens), lambda i: (0, 0))],
        out_shape=[jax.ShapeDtypeStruct((emb, tokens), BF), jax.ShapeDtypeStruct((2, tokens), F32)],
        scratch_shapes=[pltpu.VMEM((1, tokens), F32), pltpu.VMEM((1, tokens), F32), pltpu.VMEM((emb, tokens), F32)],
        compiler_params=pltpu.CompilerParams(vmem_limit_bytes=VMEM_LIMIT),
        cost_estimate=pl.CostEstimate(flops=4 * rows * emb * tokens, bytes_accessed=2 * rows * emb, transcendentals=rows * tokens),
        name="head_fwd",
    )(table, latent)


def head_backward_kernel(table, latent, log_total, weight, o_grad):
    logits = dot_nt(table[...], latent[...])
    g = (jnp.exp(logits - log_total[...]) * weight[...]).astype(BF)
    o_grad[...] = dot(g, latent[...]).astype(BF)


def head_backward(table, latent, log_total, weight):
    rows, emb = table.shape
    tokens = latent.shape[0]
    tile = vocab_tile(rows)
    return pl.pallas_call(
        head_backward_kernel,
        grid=(rows // tile,),
        in_specs=[
            pl.BlockSpec((tile, emb), lambda i: (i, 0)),
            pl.BlockSpec((tokens, emb), lambda i: (0, 0)),
            pl.BlockSpec((1, tokens), lambda i: (0, 0)),
            pl.BlockSpec((1, tokens), lambda i: (0, 0)),
        ],
        out_specs=pl.BlockSpec((tile, emb), lambda i: (i, 0)),
        out_shape=jax.ShapeDtypeStruct((rows, emb), BF),
        compiler_params=pltpu.CompilerParams(vmem_limit_bytes=VMEM_LIMIT),
        cost_estimate=pl.CostEstimate(flops=4 * rows * emb * tokens, bytes_accessed=4 * rows * emb, transcendentals=rows * tokens),
        name="head_bwd",
    )(table, latent, log_total, weight)


def blank_kernel(*refs):
    pass


def blanks(shapes):
    return pl.pallas_call(blank_kernel, out_specs=[ANY] * len(shapes), out_shape=shapes, name="blanks")()


def bits_of(size):
    bits = size.bit_length() - 1
    if 1 << bits != size:
        raise ValueError("axis size")
    return bits


def dp_orders(size):
    bits = bits_of(size)
    low = bits // 2
    return list(range(bits)), list(range(low, bits)) + list(range(low))


def swap(x, axis, bit):
    pairs = [(i, i ^ (1 << bit)) for i in range(lax.axis_size(axis))]
    return lax.ppermute(x, axis, pairs)


def gather(x, axis, order):
    index = lax.axis_index(axis)
    held = []
    for bit in order:
        other = swap(x, axis, bit)
        at = sum(1 for b in held if b > bit)
        mine = (index >> bit) & 1
        x = jnp.where(mine == 0, jnp.stack([x, other], at), jnp.stack([other, x], at))
        held.append(bit)
    size = lax.axis_size(axis)
    return x.reshape((size,) + x.shape[len(order):])


def scatter_sum(x, axis, order):
    index = lax.axis_index(axis)
    bits = bits_of(lax.axis_size(axis))
    x = x.reshape((2,) * bits + x.shape[1:])
    left = list(range(bits - 1, -1, -1))
    for n, bit in enumerate(order):
        at = left.index(bit)
        mine = (index >> bit) & 1
        sent = lax.dynamic_index_in_dim(x, 1 - mine, at, keepdims=False)
        kept = lax.dynamic_index_in_dim(x, mine, at, keepdims=False)
        got = swap(sent, axis, bit)
        x = kept.astype(F32) + got.astype(F32)
        if n + 1 < len(order):
            x = x.astype(BF)
        left.remove(bit)
    return x


def sum_all(x, axis):
    for bit in range(bits_of(lax.axis_size(axis))):
        x = x + swap(x, axis, bit)
    return x


def spread(x, axis, root):
    index = lax.axis_index(axis)
    holders = [root]
    for bit in range(bits_of(lax.axis_size(axis))):
        pairs = [(h, h ^ (1 << bit)) for h in holders]
        got = lax.ppermute(x, axis, pairs)
        fresh = [b for a, b in pairs]
        new = jnp.zeros((), jnp.bool_)
        for f in fresh:
            new = new | (index == f)
        x = jnp.where(new, got, x)
        holders = holders + fresh
    return x


def delay(section):
    return section + section // 2


def body(
    token_ids,
    noise,
    loss_mask,
    time_index,
    seq_counts,
    table,
    proj,
    w_time,
    gain_attn,
    w_qkv,
    w_out,
    gain_mlp,
    w_up,
    w_down,
):
    sections = lax.axis_size("section")
    section = lax.axis_index("section")
    groups = lax.axis_size("dp")
    micro, shard = token_ids.shape
    seq_len = shard * sections
    tokens = micro * seq_len
    width = w_qkv.shape[1]
    hidden = w_up.shape[2]
    emb = table.shape[1]
    last = sections - 1
    count = seq_counts[lax.axis_index("dp")]
    count_all = jnp.sum(seq_counts).astype(F32)
    valid = (jnp.arange(micro) < count).astype(F32)
    low_first, high_first = dp_orders(groups)
    gather_order = high_first[::-1] if False else low_first[::-1]
    section_order = list(range(bits_of(sections)))

    own_rows, table_back = jax.vjp(rms_scale, table.astype(F32))
    own_low = own_rows.astype(BF)
    own_count = own_low.shape[0]
    rows_sec = gather(own_low, "dp", gather_order).reshape(groups * own_count, emb)
    vocab_sec = groups * own_count
    proj_sec = gather(proj, "dp", gather_order)
    proj_full = gather(proj_sec, "section", section_order).reshape(emb, width)
    both = gather(jnp.stack([token_ids, loss_mask]), "section", section_order)
    ids_blocks = both[:, 0].reshape(-1) - section * vocab_sec
    both_rows = jnp.transpose(both, (1, 2, 0, 3)).reshape(2, tokens)
    ids_rows = both_rows[0] - section * vocab_sec
    weight = both_rows[1].astype(F32) * jnp.repeat(valid, seq_len)
    onehot = (ids_blocks[:, None] == jnp.arange(vocab_sec)[None, :]).astype(BF)
    partial = dot(onehot, rows_sec).astype(BF).reshape(sections, micro * shard, emb)
    picked = scatter_sum(partial, "section", section_order[::-1])
    sigma = noise_level(time_index)
    shrink = lax.rsqrt(1.0 + sigma * sigma)
    inputs = (
        (picked.reshape(micro, shard, emb) + sigma[:, None, None] * noise) * shrink[:, None, None]
    ).astype(BF)
    inputs_all = gather(inputs, "section", section_order)
    inputs_all = jnp.transpose(inputs_all, (1, 0, 2, 3)).reshape(tokens, emb)
    entry = dot(inputs_all, proj_full).astype(BF).reshape(micro, seq_len, width)
    picked_all = gather(picked.astype(BF).reshape(micro, shard, emb), "section", section_order)
    picked_all = jnp.transpose(picked_all, (1, 0, 2, 3)).reshape(tokens, emb)
    time_low = time_features(sigma, emb).astype(BF)
    time_rows = dot(time_low, w_time[0])
    cosines, sines = rope_tables(seq_len, width // HEADS)
    weights = (w_qkv[0], w_out[0], w_up[0], w_down[0])

    stores = blanks(store_shapes(micro, seq_len, width, hidden))
    offset = delay(section)
    ticks = micro + delay(last)
    core_in = entry[0]
    x_next = x_in = entry[0]
    square_sums = jnp.zeros((3,), F32)
    finals = []
    for tick in range(ticks):
        slot = tick - offset
        active = (slot >= 0) & (slot < micro)
        safe = jnp.clip(slot, 0, micro - 1)
        source = jnp.where(section == 0, 0, jnp.where(section % 2 == 1, 1, 2))
        info = jnp.stack([active.astype(jnp.int32), safe, source]).astype(jnp.int32)
        sent, sums, stores = layer_forward(
            info, core_in, x_in, entry, time_rows, gain_attn, gain_mlp, cosines, sines, *weights, stores
        )
        square_sums = square_sums + jnp.sum(sums, axis=1) * valid[safe]
        if tick - delay(last) >= 0:
            finals.append(sent)
        going = [s for s in range(last) if 0 <= tick - delay(s) < micro]
        core_pairs = [(s, s + 1) for s in going if s % 2 == 0]
        x_pairs = [(s, s + 1) for s in going if s % 2 == 1]
        core_in = lax.ppermute(sent, "section", core_pairs) if core_pairs else sent
        x_in = x_next
        x_next = lax.ppermute(sent, "section", x_pairs) if x_pairs else sent
    total_sums = sum_all(square_sums, "dp")
    layer_rms = jnp.sqrt(total_sums / (count_all * seq_len * width))[None, :]

    final = jnp.concatenate(finals, axis=0).astype(F32)
    normalized, head_back = jax.vjp(rms_scale, final)
    feats = normalized.astype(BF)
    latent = (dot_nt(feats, proj_full).astype(BF).astype(F32) * LOGIT_SCALE).astype(BF)
    latent = spread(latent, "section", last)
    mean, stats = head_forward(rows_sec, latent)
    for bit in section_order:
        other_mean, other_stats = swap(mean, "section", bit), swap(stats, "section", bit)
        peak = jnp.maximum(stats[0], other_stats[0])
        mine_part = stats[1] * jnp.exp(stats[0] - peak)
        other_part = other_stats[1] * jnp.exp(other_stats[0] - peak)
        total = mine_part + other_part
        mean = (mean.astype(F32) * (mine_part / total) + other_mean.astype(F32) * (other_part / total))
        if bit != section_order[-1]:
            mean = mean.astype(BF)
        stats = jnp.stack([peak, total])
    log_total = stats[0] + jnp.log(stats[1])
    target_logit = jnp.sum(latent.astype(F32) * picked_all.astype(F32), axis=1)
    token_loss = (log_total - target_logit) * weight
    seq_loss = jnp.sum(token_loss.reshape(micro, seq_len), axis=1) / seq_len
    grad_latent = ((mean.T - picked_all.astype(F32)) * (weight * LOGIT_SCALE)[:, None]).astype(BF)
    grad_table_head = head_backward(rows_sec, latent, log_total[None, :], weight[None, :])
    grad_final = head_back(dot(grad_latent, proj_full))[0].astype(BF)
    exit_grad = grad_final.reshape(micro, seq_len, width)
    grad_proj = jnp.where(section == last, dot_tn(grad_latent, feats), 0.0)

    saved = [stores[0], stores[2], stores[3], stores[5], stores[7]]
    grads = blanks(grad_shapes(micro, seq_len, width, hidden))
    core_in = exit_grad[0]
    x_next = x_in = exit_grad[0]
    gain_sums = jnp.zeros((2, width), F32)
    time_terms = []
    time_sum = jnp.zeros((micro, width), F32)
    for tick in range(ticks):
        slot = tick - (delay(last) - offset)
        active = (slot >= 0) & (slot < micro)
        safe = jnp.clip(slot, 0, micro - 1)
        source = jnp.where(section == last, 0, jnp.where(section % 2 == 0, 1, 2))
        info = jnp.stack([active.astype(jnp.int32), safe, source]).astype(jnp.int32)
        sent, rows, grads = layer_backward(
            info, core_in, x_in, exit_grad, time_rows, gain_attn, gain_mlp, cosines, sines, *weights, saved, grads
        )
        gain_sums = gain_sums + rows[:2]
        time_sum = time_sum + jnp.where((jnp.arange(micro) == safe)[:, None], rows[2:3], 0.0)
        going = [s for s in range(1, sections) if 0 <= tick - (delay(last) - delay(s)) < micro]
        core_pairs = [(s, s - 1) for s in going if s % 2 == 1]
        x_pairs = [(s, s - 1) for s in going if s % 2 == 0]
        core_in = lax.ppermute(sent, "section", core_pairs) if core_pairs else sent
        x_in = x_next
        x_next = lax.ppermute(sent, "section", x_pairs) if x_pairs else sent
    grad_out_all, grad_pre_all, grad_attn_all, grad_mixed_all, grad_first_all = (
        g.reshape(tokens, g.shape[2]) for g in grads
    )
    attn_in_all, context_all, mlp_in_all, activated_all = (
        stores[i].reshape(tokens, stores[i].shape[2]) for i in (1, 4, 6, 8)
    )

    def scattered(x, order):
        return scatter_sum(x.astype(BF).reshape((groups, x.shape[0] // groups) + x.shape[1:]), "dp", order)

    w_down_grad = scattered(dot_tn(activated_all, grad_out_all), low_first)
    w_up_grad = scattered(dot_tn(mlp_in_all, grad_pre_all), low_first)
    w_qkv_grad = scattered(dot_tn(attn_in_all, grad_mixed_all), low_first)
    grad_entry = spread(grad_first_all, "section", 0)
    grad_inputs = dot_nt(grad_entry, proj_full)
    grad_proj = grad_proj + jnp.where(section == 0, dot_tn(inputs_all, grad_entry), 0.0)
    proj_part = scatter_sum(grad_proj.astype(BF).reshape(sections, emb // sections, width), "section", section_order[::-1])
    w_time_term = jnp.dot(time_low.astype(F32).T, time_sum, precision=PRECISION_MAXIMAL)
    gain_rows = jnp.transpose(gain_sums.reshape(2, groups, width // groups), (1, 0, 2)).reshape(groups, 1, -1)
    gain_rows = jnp.pad(gain_rows, ((0, 0), (0, 0), (0, width - gain_rows.shape[2])))
    packed = jnp.concatenate(
        [
            dot_tn(context_all, grad_attn_all).astype(BF).reshape(groups, -1, width),
            w_time_term.astype(BF).reshape(groups, -1, width),
            proj_part.astype(BF).reshape(groups, -1, width),
            gain_rows.astype(BF),
        ],
        axis=1,
    )
    packed = scatter_sum(packed, "dp", high_first)
    at = [width // groups, emb // groups, emb // sections // groups]
    w_out_grad = packed[: at[0]]
    w_time_grad = packed[at[0] : at[0] + at[1]]
    proj_grad = packed[at[0] + at[1] : sum(at)]
    gains = packed[-1, : 2 * width // groups].reshape(2, width // groups)
    row_terms = grad_inputs * jnp.repeat(shrink, seq_len)[:, None] - latent.astype(F32) * weight[:, None]
    onehot_rows = (jnp.arange(vocab_sec)[:, None] == ids_rows[None, :]).astype(BF)
    grad_table = grad_table_head.astype(F32) + dot(onehot_rows, row_terms.astype(BF))
    table_sum = scattered(grad_table, low_first)
    table_grad = table_back(table_sum)[0]
    grad_mine = lax.dynamic_slice_in_dim(
        grad_inputs.reshape(micro, seq_len, emb), section * shard, shard, 1
    )
    noise_grad = grad_mine * (sigma * shrink)[:, None, None]
    return (
        seq_loss,
        layer_rms,
        noise_grad,
        table_grad,
        proj_grad,
        w_time_grad[None],
        gains[0][None],
        w_qkv_grad[None],
        w_out_grad[None],
        gains[1][None],
        w_up_grad[None],
        w_down_grad[None],
    )


def solution(mesh):
    return jax.shard_map(
        body,
        mesh=mesh,
        in_specs=(
            P("dp", "section"),
            P("dp", "section", None),
            P("dp", "section"),
            P("dp"),
            P(),
            P(("section", "dp"), None),
            P(("section", "dp"), None),
            P("section", None, None),
            P("section", None),
            P("section", None, None),
            P("section", None, None),
            P("section", None),
            P("section", None, None),
            P("section", None, None),
        ),
        out_specs=(
            P("dp"),
            P("section", None),
            P("dp", "section", None),
            P(("section", "dp"), None),
            P(("section", "dp"), None),
            P("section", "dp", None),
            P("section", "dp"),
            P("section", "dp", None),
            P("section", "dp", None),
            P("section", "dp"),
            P("section", "dp", None),
            P("section", "dp", None),
        ),
        check_vma=False,
    )
```

time: 2170 us -> 1010 us (0.47)
  waiting for transfers between devices: 1290 us -> 484 us
  matrix products: 311 us -> 48 us
  Pallas kernels: 0 us -> 219 us
  other arithmetic: 192 us -> 70.4 us
  blocking collectives: 104 us -> 0 us
  local copies, waits for them, and re-layouts: 132 us -> 54.7 us
    reduce_scatter x9 -> x0, waiting for transfers between devices: 776 us -> none  [the longest x1 150 us: body(): lax.psum_scatter(all_terms[6].astype(jnp.bfloat16), 'dp', scatter_dimensi...]
    dot_general x94 -> x14, matrix products: 311 us -> 48 us  [the longest x6 31.5 us: dot_tn(): lax.dot_general(a, b, (((0,), (0,)), ((), ())), preferred_element_type=F32)]
    ppermute x14 -> x66, waiting for transfers between devices: 228 us -> 484 us  [the longest x40 419 us: swap(): return lax.ppermute(x, axis, pairs)]
    pallas_call x0 -> x20, Pallas kernels: none -> 219 us  [the longest x8 104 us: layer_backward(): pl.pallas_call(bwd_kernel, in_specs=[SM, ANY, ANY, ANY, VM, VM, VM, VM, V...]
    psum x2 -> x0, waiting for transfers between devices: 114 us -> none  [broadcast(): return lax.psum(jnp.where(mine, x, jnp.zeros_like(x)), axis)]
    unnamed x18 -> x0, waiting for transfers between devices: 98.7 us -> none
    all_gather x1 -> x0, blocking collectives: 77.1 us -> none  [body(): lax.all_gather(proj, ('section', 'dp'), axis=0, tiled=True)]
    all_gather x3 -> x0, waiting for transfers between devices: 73.6 us -> none  [the longest x1 38 us: body(): lax.all_gather(own_rows.astype(jnp.bfloat16), ('section', 'dp'), axis=0,...]
  transfers between devices with their start and end apart: 30 -> 66, of which waited for: 29 -> 35; matrix products, arithmetic and copies ran while one was open for 6% -> 15% of each run, Pallas kernels for 0% -> 10%
where the time goes in v1:
time: 1010 us; the launch traced here: 998 us
  waiting for transfers between devices  484 us (48%)
  Pallas kernels  219 us (22%)
  starting transfers between devices  117 us (12%)
  other arithmetic  70.4 us (7%)
  local copies, waits for them, and re-layouts  54.7 us (5%)
  matrix products  48 us (5%)
    ppermute x40, waiting for transfers between devices, swap(): return lax.ppermute(x, axis, pairs)  419 us
    pallas_call x8, Pallas kernels, layer_backward(): pl.pallas_call(bwd_kernel, in_specs=[SM, ANY, ANY, ANY, VM, VM, VM, VM, V...  104 us
    ppermute x40, starting transfers between devices, swap(): return lax.ppermute(x, axis, pairs)  85.8 us
    pallas_call x8, Pallas kernels, layer_forward(): pl.pallas_call(fwd_kernel, in_specs=[SM, ANY, ANY, ANY, VM, VM, VM, VM, V...  84.1 us
    ppermute x14, waiting for transfers between devices, body(): core_in = lax.ppermute(sent, 'section', core_pairs) if core_pairs else sent  50.9 us
    dot_general x6, matrix products, dot_tn(): lax.dot_general(a, b, (((0,), (0,)), ((), ())), preferred_element_type=F32)  31.5 us
    convert_element_type x12, other arithmetic, scatter_sum(): x = x.astype(BF)  21.2 us
  transfers between devices with their start and end apart: 66, of which 35 were waited for; matrix products, arithmetic and copies ran while one was open for 15% of the time, Pallas kernels for 10%

profile of v1, /device:TPU:0, one launch (start us, length us, event | category | flops | bytes accessed | tf_op | source)
XLA Modules:
  0.0 997.8 jit_solution(3277046166234478773)
XLA Ops:
  10.4 22.1 %collective-permute-done = bf16[1000,256]{1,0:T(8,128)(2,1)S(1)} collective-permute-done((bf16[1000,256]{1,0:T(8,128)(2,1)S(1)}, bf16[1000,256]{1,0:T(8,128)(2,1)S(1)}, u32[]{:S(2)}, u32[]{:S(2)}) %collective-permute-start) | collective-permute-done | bytes 512032 | tf_op jit(solution)/shard_map/ppermute | solution.py:421
  35.3 21.7 %collective-permute-done.1 = bf16[2,1000,256]{2,1,0:T(8,128)(2,1)S(1)} collective-permute-done((bf16[2,1000,256]{2,1,0:T(8,128)(2,1)S(1)}, bf16[2,1000,256]{2,1,0:T(8,128)(2,1)S(1)}, u32[]{:S(2)}, u32[]{:S(2)}) %collective-permute-start.1) | collective-permute-done | bytes 1024032 | tf_op jit(solution)/shard_map/ppermute | solution.py:421
  70.7 34.3 %collective-permute-done.2 = bf16[2,2,1000,256]{3,2,0,1:T(8,128)(2,1)} collective-permute-done((bf16[2,2,1000,256]{3,2,0,1:T(8,128)(2,1)}, bf16[2,2,1000,256]{3,2,0,1:T(8,128)(2,1)}, u32[]{:S(2)}, u32[]{:S(2)}) %collective-permute-start.2) | collective-permute-done | bytes 2048032 | tf_op jit(solution)/shard_map/ppermute | solution.py:421
  108.1 4.2 fusion.26
  113.6 4.4 collective-permute-done.5
  122.2 5.2 collective-permute-done.13
  133.2 15.8 %layer_fwd.8 = (bf16[192,1024]{1,0:T(8,128)(2,1)}, f32[3,1024]{1,0:T(4,128)}, bf16[4,192,1024]{2,1,0:T(8,128)(2,1)}, bf16[4,192,1024]{2,1,0:T(8,128)(2,1)}, bf16...) custom-call(s32[3]{0:T(128)} %add_add_fusion.6.info, ...), custom_call_target="tpu_custom_call", output_to_operand_aliasing={{2}: (13, {}), {3}: (14, {}), {4}: (15, {}), {5}: (16, {}),... | custom-call | flops 4831838208 | bytes 33554432 | tf_op jit(solution)/shard_map/layer_fwd/pallas_call | solution.py:160
  152.7 15.9 %layer_fwd.9 = (bf16[192,1024]{1,0:T(8,128)(2,1)}, f32[3,1024]{1,0:T(4,128)}, bf16[4,192,1024]{2,1,0:T(8,128)(2,1)}, bf16[4,192,1024]{2,1,0:T(8,128)(2,1)}, bf16...) custom-call(s32[3]{0:T(128)} %add_add_fusion.5.info, ...), custom_call_target="tpu_custom_call", output_to_operand_aliasing={{2}: (13, {}), {3}: (14, {}), {4}: (15, {}), {5}: (16, {}),... | custom-call | flops 4831838208 | bytes 33554432 | tf_op jit(solution)/shard_map/layer_fwd/pallas_call | solution.py:160
  173.2 16.1 %layer_fwd.10 = (bf16[192,1024]{1,0:T(8,128)(2,1)}, f32[3,1024]{1,0:T(4,128)}, bf16[4,192,1024]{2,1,0:T(8,128)(2,1)}, bf16[4,192,1024]{2,1,0:T(8,128)(2,1)}, bf1...) custom-call(s32[3]{0:T(128)} %add_add_fusion.4.info, ...), custom_call_target="tpu_custom_call", output_to_operand_aliasing={{2}: (13, {}), {3}: (14, {}), {4}: (15, {}), {5}: (16, {}),... | custom-call | flops 4831838208 | bytes 33554432 | tf_op jit(solution)/shard_map/layer_fwd/pallas_call | solution.py:160
  193.9 15.8 %layer_fwd.11 = (bf16[192,1024]{1,0:T(8,128)(2,1)}, f32[3,1024]{1,0:T(4,128)}, bf16[4,192,1024]{2,1,0:T(8,128)(2,1)}, bf16[4,192,1024]{2,1,0:T(8,128)(2,1)}, bf1...) custom-call(s32[3]{0:T(128)} %add_add_fusion.3.info, ...), custom_call_target="tpu_custom_call", output_to_operand_aliasing={{2}: (13, {}), {3}: (14, {}), {4}: (15, {}), {5}: (16, {}),... | custom-call | flops 4831838208 | bytes 33554432 | tf_op jit(solution)/shard_map/layer_fwd/pallas_call | solution.py:160
  219.4 4.4 layer_fwd.13
  226.0 4.8 layer_fwd.14
  232.9 8.9 layer_fwd.15
  247.1 12.7 %collective-permute-start.29 = (bf16[4,48,256]{2,1,0:T(8,128)(2,1)S(1)}, bf16[4,48,256]{2,1,0:T(8,128)(2,1)S(1)}, u32[]{:S(2)}, u32[]{:S(2)}) collective-permute-start(bf16[4,48,256]{2,1,0:T(8,128)(2,1)S(1)} %bitcast.412), channel_id=1, source_target_pairs={{0,8},{8,0},{16,24},{24,16},{1,9},{9,1},{17,25},{25,17},{2,10},{10... | collective-permute-start | bytes 294920 | tf_op jit(solution)/shard_map/ppermute | solution.py:421
  260.8 25.1 %collective-permute-start.30 = (bf16[2,4,48,256]{3,2,1,0:T(8,128)(2,1)S(1)}, bf16[2,4,48,256]{3,2,1,0:T(8,128)(2,1)S(1)}, u32[]{:S(2)}, u32[]{:S(2)}) collective-permute-start(bf16[2,4,48,256]{3,2,1,0:T(8,128)(2,1)S(1)} %maximum_select_fusion.13), channel_id=1, source_target_pairs={{0,16},{8,24},{16,0},{24,8},{1,17},{9,25},{17,1},{25,9},{2,18},{10... | collective-permute-start | bytes 589832 | tf_op jit(solution)/shard_map/ppermute | solution.py:421
  287.3 4.4 collective-permute-done.30
  291.8 7.9 collective-permute-done.26
  300.6 18.7 %head_fwd.1 = (bf16[256,768]{1,0:T(8,128)(2,1)}, f32[2,768]{1,0:T(2,128)}) custom-call(bf16[8000,256]{1,0:T(8,128)(2,1)} %bitcast.394, bf16[768,256]{1,0:T(8,128)(2,1)} %get-tuple-element.351.latent), custom_call_target="tpu_custom_call" | custom-call | flops 6291456000 | bytes 4096000 | tf_op jit(solution)/shard_map/head_fwd/pallas_call | solution.py:358
  328.1 8.0 collective-permute-done.35
  344.8 6.2 layer_bwd.9
  354.5 5.0 layer_bwd.10
  363.7 4.3 layer_bwd.11
  375.5 47.7 %collective-permute-done.40.g_in = bf16[192,1024]{1,0:T(8,128)(2,1)S(1)} collective-permute-done((bf16[192,1024]{1,0:T(8,128)(2,1)}, bf16[192,1024]{1,0:T(8,128)(2,1)S(1)}, u32[]{:S(2)}, u32[]{:S(2)}) %collective-permute-start.40) | collective-permute-done | bytes 393248 | tf_op jit(solution)/shard_map/ppermute | solution.py:618
  423.9 21.5 %layer_bwd.12 = (bf16[192,1024]{1,0:T(8,128)(2,1)}, f32[3,1024]{1,0:T(4,128)}, bf16[4,192,1024]{2,1,0:T(8,128)(2,1)}, bf16[4,192,4096]{2,1,0:T(8,128)(2,1)}, bf1...) custom-call(s32[3]{0:T(128)} %add_add_fusion.13.info, ...), custom_call_target="tpu_custom_call", output_to_operand_aliasing={{2}: (18, {}), {3}: (19, {}), {4}: (20, {}), {5}: (21, {}),... | custom-call | flops 4831838208 | bytes 33554432 | tf_op jit(solution)/shard_map/layer_bwd/pallas_call | solution.py:287
  446.7 5.1 multiply_add_fusion.2
  466.9 21.5 %layer_bwd.13 = (bf16[192,1024]{1,0:T(8,128)(2,1)}, f32[3,1024]{1,0:T(4,128)}, bf16[4,192,1024]{2,1,0:T(8,128)(2,1)}, bf16[4,192,4096]{2,1,0:T(8,128)(2,1)}, bf1...) custom-call(s32[3]{0:T(128)} %add_add_fusion.12.info, ...), custom_call_target="tpu_custom_call", output_to_operand_aliasing={{2}: (18, {}), {3}: (19, {}), {4}: (20, {}), {5}: (21, {}),... | custom-call | flops 4831838208 | bytes 33554432 | tf_op jit(solution)/shard_map/layer_bwd/pallas_call | solution.py:287
  489.8 12.4 %head_bwd.1 = bf16[8000,256]{1,0:T(8,128)(2,1)} custom-call(bf16[8000,256]{1,0:T(8,128)(2,1)} %bitcast.395, bf16[768,256]{1,0:T(8,128)(2,1)} %get-tuple-element.351.latent, f32[1,768]{1,0:T(1,128)} %get-tuple-element.340.log_total, f32[1,768]{1,0:T(1,128)} %mul.481.weight), custom_call_target="tpu_custom_call" | custom-call | flops 6291456000 | bytes 8192000 | tf_op jit(solution)/shard_map/head_bwd/pallas_call | solution.py:381
  503.1 21.5 %layer_bwd.14 = (bf16[192,1024]{1,0:T(8,128)(2,1)}, f32[3,1024]{1,0:T(4,128)}, bf16[4,192,1024]{2,1,0:T(8,128)(2,1)}, bf16[4,192,4096]{2,1,0:T(8,128)(2,1)}, bf1...) custom-call(s32[3]{0:T(128)} %add_add_fusion.11.info, ...), custom_call_target="tpu_custom_call", output_to_operand_aliasing={{2}: (18, {}), {3}: (19, {}), {4}: (20, {}), {5}: (21, {}),... | custom-call | flops 4831838208 | bytes 33554432 | tf_op jit(solution)/shard_map/layer_bwd/pallas_call | solution.py:287
  531.0 22.0 %layer_bwd.15 = (bf16[192,1024]{1,0:T(8,128)(2,1)}, f32[3,1024]{1,0:T(4,128)}, bf16[4,192,1024]{2,1,0:T(8,128)(2,1)}, bf16[4,192,4096]{2,1,0:T(8,128)(2,1)}, bf1...) custom-call(s32[3]{0:T(128)} %add_add_fusion.10.info, ...), custom_call_target="tpu_custom_call", output_to_operand_aliasing={{2}: (18, {}), {3}: (19, {}), {4}: (20, {}), {5}: (21, {}),... | custom-call | flops 4831838208 | bytes 33554432 | tf_op jit(solution)/shard_map/layer_bwd/pallas_call | solution.py:287
  557.0 7.9 bitcast_convert_fusion.2
  570.6 9.0 bitcast_convert_fusion.1
  579.6 6.4 constant_dynamic-slice_fusion.3
  586.0 4.9 copy.280
  591.4 9.0 bitcast_convert_fusion
  604.5 5.2 constant_dynamic-slice_fusion.1
  616.5 6.3 collective-permute-done.48
  624.9 5.8 add_convert_fusion
  651.1 79.2 %collective-permute-done.60 = bf16[2,2,128,4096]{3,2,0,1:T(8,128)(2,1)} collective-permute-done((bf16[2,2,128,4096]{3,2,0,1:T(8,128)(2,1)}, bf16[2,2,128,4096]{3,2,0,1:T(8,128)(2,1)}, u32[]{:S(2)}, u32[]{:S(2)}) %collective-permute-start.60) | collective-permute-done | bytes 4194336 | tf_op jit(solution)/shard_map/ppermute | solution.py:421
  736.9 83.3 %collective-permute-done.63 = bf16[2,2,512,1024]{3,2,0,1:T(8,128)(2,1)} collective-permute-done((bf16[2,2,512,1024]{3,2,0,1:T(8,128)(2,1)}, bf16[2,2,512,1024]{3,2,0,1:T(8,128)(2,1)}, u32[]{:S(2)}, u32[]{:S(2)}) %collective-permute-start.63) | collective-permute-done | bytes 4194336 | tf_op jit(solution)/shard_map/ppermute | solution.py:421
  820.2 4.3 fusion.4
  834.1 17.3 %collective-permute-done.49 = bf16[2,2,1000,256]{3,2,0,1:T(8,128)(2,1)} collective-permute-done((bf16[2,2,1000,256]{3,2,0,1:T(8,128)(2,1)}, bf16[2,2,1000,256]{3,2,0,1:T(8,128)(2,1)}, u32[]{:S(2)}, u32[]{:S(2)}) %collective-permute-start.49) | collective-permute-done | bytes 2048032 | tf_op jit(solution)/shard_map/ppermute | solution.py:421
  855.1 17.4 %collective-permute-done.55 = bf16[2,169,1024]{2,0,1:T(2,128)(2,1)S(1)} collective-permute-done((bf16[2,169,1024]{2,0,1:T(2,128)(2,1)S(1)}, bf16[2,169,1024]{2,0,1:T(2,128)(2,1)S(1)}, u32[]{:S(2)}, u32[]{:S(2)}) %collective-permute-start.55) | collective-permute-done | bytes 692256 | tf_op jit(solution)/shard_map/ppermute | solution.py:421
  874.6 10.2 %collective-permute-done.59 = bf16[128,3072]{1,0:T(8,128)(2,1)S(1)} collective-permute-done((bf16[128,3072]{1,0:T(8,128)(2,1)S(1)}, bf16[128,3072]{1,0:T(8,128)(2,1)S(1)}, u32[]{:S(2)}, u32[]{:S(2)}) %collective-permute-start.59) | collective-permute-done | bytes 786464 | tf_op jit(solution)/shard_map/ppermute | solution.py:421
  888.9 17.9 %collective-permute-done.50 = bf16[2,1000,256]{2,1,0:T(8,128)(2,1)S(1)} collective-permute-done((bf16[2,1000,256]{2,1,0:T(8,128)(2,1)S(1)}, bf16[2,1000,256]{2,1,0:T(8,128)(2,1)S(1)}, u32[]{:S(2)}, u32[]{:S(2)}) %collective-permute-start.50) | collective-permute-done | bytes 1024032 | tf_op jit(solution)/shard_map/ppermute | solution.py:421
  907.1 4.2 collective-permute-start.51
  918.0 44.0 %collective-permute-done.51 = bf16[1000,256]{1,0:T(8,128)(2,1)S(1)} collective-permute-done((bf16[1000,256]{1,0:T(8,128)(2,1)S(1)}, bf16[1000,256]{1,0:T(8,128)(2,1)S(1)}, u32[]{:S(2)}, u32[]{:S(2)}) %collective-permute-start.51) | collective-permute-done | bytes 512032 | tf_op jit(solution)/shard_map/ppermute | solution.py:421
  963.6 20.8 %collective-permute-done.62 = bf16[128,4096]{1,0:T(8,128)(2,1)S(1)} collective-permute-done((bf16[128,4096]{1,0:T(8,128)(2,1)S(1)}, bf16[128,4096]{1,0:T(8,128)(2,1)S(1)}, u32[]{:S(2)}, u32[]{:S(2)}) %collective-permute-start.62) | collective-permute-done | bytes 1048608 | tf_op jit(solution)/shard_map/ppermute | solution.py:421
  986.0 9.8 collective-permute-done.65
  (484 shorter events, 213.4 us)
Async XLA Ops:
  1.5 60.1 %collective-permute-start.3 = (s32[2,4,48]{2,1,0:T(4,128)S(1)}, s32[2,4,48]{2,1,0:T(4,128)S(1)}, u32[]{:S(2)}, u32[]{:S(2)}) collective-permute-start(s32[2,4,48]{2,1,0:T(4,128)S(1)} %get-tuple-element.375), channel_id=1, source_target_pairs={{0,8},{8,0},{16,24},{24,16},{1,9},{9,1},{17,25},{25,17},{2,10},{10... | collective-permute-start | bytes 4616 | tf_op jit(solution)/shard_map/ppermute | solution.py:421
  5.0 27.5 %collective-permute-start = (bf16[1000,256]{1,0:T(8,128)(2,1)S(1)}, bf16[1000,256]{1,0:T(8,128)(2,1)S(1)}, u32[]{:S(2)}, u32[]{:S(2)}) collective-permute-start(bf16[1000,256]{1,0:T(8,128)(2,1)S(1)} %fusion.28), channel_id=1, source_target_pairs={{0,4},{1,5},{2,6},{3,7},{4,0},{5,1},{6,2},{7,3},{8,12},{9,13},{10,... | collective-permute-start | bytes 1536008 | tf_op jit(solution)/shard_map/ppermute | solution.py:421
  8.7 56.7 %collective-permute-start.9 = (bf16[8,1024]{1,0:T(8,128)(2,1)}, bf16[8,1024]{1,0:T(8,128)(2,1)S(1)}, u32[]{:S(2)}, u32[]{:S(2)}) collective-permute-start(bf16[8,1024]{1,0:T(8,128)(2,1)} %param.20), channel_id=1, source_target_pairs={{0,4},{1,5},{2,6},{3,7},{4,0},{5,1},{6,2},{7,3},{8,12},{9,13},{10,... | collective-permute-start | bytes 49160 | tf_op jit(solution)/shard_map/ppermute | solution.py:421
  32.7 24.4 %collective-permute-start.1 = (bf16[2,1000,256]{2,1,0:T(8,128)(2,1)S(1)}, bf16[2,1000,256]{2,1,0:T(8,128)(2,1)S(1)}, u32[]{:S(2)}, u32[]{:S(2)}) collective-permute-start(bf16[2,1000,256]{2,1,0:T(8,128)(2,1)S(1)} %maximum_select_fusion.4), channel_id=1, source_target_pairs={{0,2},{1,3},{2,0},{3,1},{4,6},{5,7},{6,4},{7,5},{8,10},{9,11},{10,... | collective-permute-start | bytes 3072008 | tf_op jit(solution)/shard_map/ppermute | solution.py:421
  58.7 46.4 %collective-permute-start.2 = (bf16[2,2,1000,256]{3,2,0,1:T(8,128)(2,1)}, bf16[2,2,1000,256]{3,2,0,1:T(8,128)(2,1)}, u32[]{:S(2)}, u32[]{:S(2)}) collective-permute-start(bf16[2,2,1000,256]{3,2,0,1:T(8,128)(2,1)} %maximum_select_fusion.2), channel_id=1, source_target_pairs={{0,1},{1,0},{2,3},{3,2},{4,5},{5,4},{6,7},{7,6},{8,9},{9,8},{10,11... | collective-permute-start | bytes 6144008 | tf_op jit(solution)/shard_map/ppermute | solution.py:421
  65.4 4.0 collective-permute-start.10
  69.4 44.1 %collective-permute-start.11 = (bf16[2,2,8,1024]{3,2,1,0:T(8,128)(2,1)S(1)}, bf16[2,2,8,1024]{3,2,1,0:T(8,128)(2,1)S(1)}, u32[]{:S(2)}, u32[]{:S(2)}) collective-permute-start(bf16[2,2,8,1024]{3,2,1,0:T(8,128)(2,1)S(1)} %maximum_select_fusion.15), channel_id=1, source_target_pairs={{0,1},{1,0},{2,3},{3,2},{4,5},{5,4},{6,7},{7,6},{8,9},{9,8},{10,11... | collective-permute-start | bytes 196616 | tf_op jit(solution)/shard_map/ppermute | solution.py:421
  112.3 5.7 collective-permute-start.5
  113.6 4.7 collective-permute-start.12
  118.3 9.2 collective-permute-start.13
  121.1 10.2 %collective-permute-start.8 = (bf16[2,4,48,256]{3,2,1,0:T(8,128)(2,1)S(1)}, bf16[2,4,48,256]{3,2,1,0:T(8,128)(2,1)S(1)}, u32[]{:S(2)}, u32[]{:S(2)}) collective-permute-start(bf16[2,4,48,256]{3,2,1,0:T(8,128)(2,1)S(1)} %maximum_select_fusion.11), channel_id=1, source_target_pairs={{0,16},{8,24},{16,0},{24,8},{1,17},{9,25},{17,1},{25,9},{2,18},{10... | collective-permute-start | bytes 589832 | tf_op jit(solution)/shard_map/ppermute | solution.py:421
  171.5 21.4 %collective-permute-start.17 = (bf16[192,1024]{1,0:T(8,128)(2,1)}, bf16[192,1024]{1,0:T(8,128)(2,1)S(1)}, u32[]{:S(2)}, u32[]{:S(2)}) collective-permute-start(bf16[192,1024]{1,0:T(8,128)(2,1)} %get-tuple-element.190), channel_id=1, source_target_pairs={{8,16},{9,17},{10,18},{11,19},{12,20},{13,21},{14,22},{15,23}} | collective-permute-start | bytes 1179656 | tf_op jit(solution)/shard_map/ppermute | solution.py:567
  192.2 21.1 %collective-permute-start.19 = (bf16[192,1024]{1,0:T(8,128)(2,1)}, bf16[192,1024]{1,0:T(8,128)(2,1)S(1)}, u32[]{:S(2)}, u32[]{:S(2)}) collective-permute-start(bf16[192,1024]{1,0:T(8,128)(2,1)} %get-tuple-element.200), channel_id=1, source_target_pairs={{8,16},{9,17},{10,18},{11,19},{12,20},{13,21},{14,22},{15,23}} | collective-permute-start | bytes 1179656 | tf_op jit(solution)/shard_map/ppermute | solution.py:567
  212.6 5.9 collective-permute-start.21
  217.9 7.3 collective-permute-start.23
  244.9 41.0 %collective-permute-start.25 = (bf16[768,256]{1,0:T(8,128)(2,1)S(1)}, bf16[768,256]{1,0:T(8,128)(2,1)S(1)}, u32[]{:S(2)}, u32[]{:S(2)}) collective-permute-start(bf16[768,256]{1,0:T(8,128)(2,1)S(1)} %fusion.25), channel_id=1, source_target_pairs={{24,16},{25,17},{26,18},{27,19},{28,20},{29,21},{30,22},{31,23}} | collective-permute-start | bytes 1179656 | tf_op jit(solution)/shard_map/ppermute | solution.py:466
  247.1 13.7 %collective-permute-start.29 = (bf16[4,48,256]{2,1,0:T(8,128)(2,1)S(1)}, bf16[4,48,256]{2,1,0:T(8,128)(2,1)S(1)}, u32[]{:S(2)}, u32[]{:S(2)}) collective-permute-start(bf16[4,48,256]{2,1,0:T(8,128)(2,1)S(1)} %bitcast.412), channel_id=1, source_target_pairs={{0,8},{8,0},{16,24},{24,16},{1,9},{9,1},{17,25},{25,17},{2,10},{10... | collective-permute-start | bytes 294920 | tf_op jit(solution)/shard_map/ppermute | solution.py:421
  260.8 30.9 %collective-permute-start.30 = (bf16[2,4,48,256]{3,2,1,0:T(8,128)(2,1)S(1)}, bf16[2,4,48,256]{3,2,1,0:T(8,128)(2,1)S(1)}, u32[]{:S(2)}, u32[]{:S(2)}) collective-permute-start(bf16[2,4,48,256]{3,2,1,0:T(8,128)(2,1)S(1)} %maximum_select_fusion.13), channel_id=1, source_target_pairs={{0,16},{8,24},{16,0},{24,8},{1,17},{9,25},{17,1},{25,9},{2,18},{10... | collective-permute-start | bytes 589832 | tf_op jit(solution)/shard_map/ppermute | solution.py:421
  285.9 13.8 %collective-permute-start.26 = (bf16[768,256]{1,0:T(8,128)(2,1)S(1)}, bf16[768,256]{1,0:T(8,128)(2,1)S(1)}, u32[]{:S(2)}, u32[]{:S(2)}) collective-permute-start(bf16[768,256]{1,0:T(8,128)(2,1)S(1)} %broadcast_select_fusion.4), channel_id=1, source_target_pairs={{24,8},{16,0},{25,9},{17,1},{26,10},{18,2},{27,11},{19,3},{28,12},... | collective-permute-start | bytes 1179656 | tf_op jit(solution)/shard_map/ppermute | solution.py:466
  323.4 4.0 collective-permute-start.28
  324.8 11.4 %collective-permute-start.35 = (bf16[256,768]{0,1:T(8,128)(2,1)S(1)}, bf16[256,768]{0,1:T(8,128)(2,1)S(1)}, u32[]{:S(2)}, u32[]{:S(2)}) collective-permute-start(bf16[256,768]{0,1:T(8,128)(2,1)S(1)} %add_convert_fusion.1), channel_id=1, source_target_pairs={{0,16},{8,24},{16,0},{24,8},{1,17},{9,25},{17,1},{25,9},{2,18},{10... | collective-permute-start | bytes 1179656 | tf_op jit(solution)/shard_map/ppermute | solution.py:421
  353.0 9.7 collective-permute-start.39
  362.0 13.5 %collective-permute-start.41 = (bf16[192,1024]{1,0:T(8,128)(2,1)}, bf16[192,1024]{1,0:T(8,128)(2,1)S(1)}, u32[]{:S(2)}, u32[]{:S(2)}) collective-permute-start(bf16[192,1024]{1,0:T(8,128)(2,1)} %get-tuple-element.283), channel_id=1, source_target_pairs={{16,8},{17,9},{18,10},{19,11},{20,12},{21,13},{22,14},{23,15}} | collective-permute-start | bytes 1179656 | tf_op jit(solution)/shard_map/ppermute | solution.py:620
  368.0 55.2 %collective-permute-start.40 = (bf16[192,1024]{1,0:T(8,128)(2,1)}, bf16[192,1024]{1,0:T(8,128)(2,1)S(1)}, u32[]{:S(2)}, u32[]{:S(2)}) collective-permute-start(bf16[192,1024]{1,0:T(8,128)(2,1)} %get-tuple-element.289), channel_id=1, source_target_pairs={{8,0},{24,16},{9,1},{25,17},{10,2},{26,18},{11,3},{27,19},{12,4},{... | collective-permute-start | bytes 1179656 | tf_op jit(solution)/shard_map/ppermute | solution.py:618
  374.1 92.0 %collective-permute-start.43 = (bf16[192,1024]{1,0:T(8,128)(2,1)}, bf16[192,1024]{1,0:T(8,128)(2,1)S(1)}, u32[]{:S(2)}, u32[]{:S(2)}) collective-permute-start(bf16[192,1024]{1,0:T(8,128)(2,1)} %get-tuple-element.289), channel_id=1, source_target_pairs={{16,8},{17,9},{18,10},{19,11},{20,12},{21,13},{22,14},{23,15}} | collective-permute-start | bytes 1179656 | tf_op jit(solution)/shard_map/ppermute | solution.py:620
  445.4 20.6 %collective-permute-start.42 = (bf16[192,1024]{1,0:T(8,128)(2,1)}, bf16[192,1024]{1,0:T(8,128)(2,1)S(1)}, u32[]{:S(2)}, u32[]{:S(2)}) collective-permute-start(bf16[192,1024]{1,0:T(8,128)(2,1)} %get-tuple-element.295), channel_id=1, source_target_pairs={{8,0},{9,1},{10,2},{11,3},{12,4},{13,5},{14,6},{15,7}} | collective-permute-start | bytes 1179656 | tf_op jit(solution)/shard_map/ppermute | solution.py:618
  459.0 4.7 collective-permute-start.33
  464.9 37.3 %collective-permute-start.45 = (bf16[192,1024]{1,0:T(8,128)(2,1)}, bf16[192,1024]{1,0:T(8,128)(2,1)S(1)}, u32[]{:S(2)}, u32[]{:S(2)}) collective-permute-start(bf16[192,1024]{1,0:T(8,128)(2,1)} %get-tuple-element.295), channel_id=1, source_target_pairs={{16,8},{17,9},{18,10},{19,11},{20,12},{21,13},{22,14},{23,15}} | collective-permute-start | bytes 1179656 | tf_op jit(solution)/shard_map/ppermute | solution.py:620
  488.4 13.9 %collective-permute-start.44 = (bf16[192,1024]{1,0:T(8,128)(2,1)}, bf16[192,1024]{1,0:T(8,128)(2,1)S(1)}, u32[]{:S(2)}, u32[]{:S(2)}) collective-permute-start(bf16[192,1024]{1,0:T(8,128)(2,1)} %get-tuple-element.301.far_in), channel_id=1, source_target_pairs={{8,0},{9,1},{10,2},{11,3},{12,4},{13,5},{14,6},{15,7}} | collective-permute-start | bytes 1179656 | tf_op jit(solution)/shard_map/ppermute | solution.py:618
  524.7 5.6 collective-permute-start.46
  554.5 46.0 %collective-permute-start.47 = (bf16[768,1024]{1,0:T(8,128)(2,1)}, bf16[768,1024]{1,0:T(8,128)(2,1)}, u32[]{:S(2)}, u32[]{:S(2)}) collective-permute-start(bf16[768,1024]{1,0:T(8,128)(2,1)} %bitcast.386), channel_id=1, source_target_pairs={{0,8},{1,9},{2,10},{3,11},{4,12},{5,13},{6,14},{7,15}} | collective-permute-start | bytes 4718600 | tf_op jit(solution)/shard_map/ppermute | solution.py:466
  569.1 71.4 %collective-permute-start.57 = (bf16[2,2,128,3072]{3,2,0,1:T(8,128)(2,1)}, bf16[2,2,128,3072]{3,2,0,1:T(8,128)(2,1)}, u32[]{:S(2)}, u32[]{:S(2)}) collective-permute-start(bf16[2,2,128,3072]{3,2,0,1:T(8,128)(2,1)} %bitcast.297), channel_id=1, source_target_pairs={{0,1},{1,0},{2,3},{3,2},{4,5},{5,4},{6,7},{7,6},{8,9},{9,8},{10,11... | collective-permute-start | bytes 9437192 | tf_op jit(solution)/shard_map/ppermute | solution.py:421
  590.9 139.4 %collective-permute-start.60 = (bf16[2,2,128,4096]{3,2,0,1:T(8,128)(2,1)}, bf16[2,2,128,4096]{3,2,0,1:T(8,128)(2,1)}, u32[]{:S(2)}, u32[]{:S(2)}) collective-permute-start(bf16[2,2,128,4096]{3,2,0,1:T(8,128)(2,1)} %bitcast.296), channel_id=1, source_target_pairs={{0,1},{1,0},{2,3},{3,2},{4,5},{5,4},{6,7},{7,6},{8,9},{9,8},{10,11... | collective-permute-start | bytes 12582920 | tf_op jit(solution)/shard_map/ppermute | solution.py:421
  601.9 20.9 %collective-permute-start.48 = (bf16[768,1024]{1,0:T(8,128)(2,1)}, bf16[768,1024]{1,0:T(8,128)(2,1)}, u32[]{:S(2)}, u32[]{:S(2)}) collective-permute-start(bf16[768,1024]{1,0:T(8,128)(2,1)} %broadcast_select_fusion), channel_id=1, source_target_pairs={{0,16},{8,24},{1,17},{9,25},{2,18},{10,26},{3,19},{11,27},{4,20},{... | collective-permute-start | bytes 4718600 | tf_op jit(solution)/shard_map/ppermute | solution.py:466
  612.1 208.1 %collective-permute-start.63 = (bf16[2,2,512,1024]{3,2,0,1:T(8,128)(2,1)}, bf16[2,2,512,1024]{3,2,0,1:T(8,128)(2,1)}, u32[]{:S(2)}, u32[]{:S(2)}) collective-permute-start(bf16[2,2,512,1024]{3,2,0,1:T(8,128)(2,1)} %bitcast.295), channel_id=1, source_target_pairs={{0,1},{1,0},{2,3},{3,2},{4,5},{5,4},{6,7},{7,6},{8,9},{9,8},{10,11... | collective-permute-start | bytes 12582920 | tf_op jit(solution)/shard_map/ppermute | solution.py:421
  632.4 219.0 %collective-permute-start.49 = (bf16[2,2,1000,256]{3,2,0,1:T(8,128)(2,1)}, bf16[2,2,1000,256]{3,2,0,1:T(8,128)(2,1)}, u32[]{:S(2)}, u32[]{:S(2)}) collective-permute-start(bf16[2,2,1000,256]{3,2,0,1:T(8,128)(2,1)} %bitcast.298), channel_id=1, source_target_pairs={{0,1},{1,0},{2,3},{3,2},{4,5},{5,4},{6,7},{7,6},{8,9},{9,8},{10,11... | collective-permute-start | bytes 6144008 | tf_op jit(solution)/shard_map/ppermute | solution.py:421
  636.1 10.1 %collective-permute-start.52 = (bf16[2,64,1024]{2,1,0:T(8,128)(2,1)S(1)}, bf16[2,64,1024]{2,1,0:T(8,128)(2,1)S(1)}, u32[]{:S(2)}, u32[]{:S(2)}) collective-permute-start(bf16[2,64,1024]{2,1,0:T(8,128)(2,1)S(1)} %dynamic-slice_bitcast_fusion.11), channel_id=1, source_target_pairs={{0,16},{8,24},{16,0},{24,8},{1,17},{9,25},{17,1},{25,9},{2,18},{10... | collective-permute-start | bytes 786440 | tf_op jit(solution)/shard_map/ppermute | solution.py:421
  644.7 181.4 %collective-permute-start.58 = (bf16[2,128,3072]{2,1,0:T(8,128)(2,1)}, bf16[2,128,3072]{2,1,0:T(8,128)(2,1)}, u32[]{:S(2)}, u32[]{:S(2)}) collective-permute-start(bf16[2,128,3072]{2,1,0:T(8,128)(2,1)} %dynamic-slice_bitcast_fusion.2), channel_id=1, source_target_pairs={{0,2},{1,3},{2,0},{3,1},{4,6},{5,7},{6,4},{7,5},{8,10},{9,11},{10,... | collective-permute-start | bytes 4718600 | tf_op jit(solution)/shard_map/ppermute | solution.py:421
  650.5 177.7 %collective-permute-start.54 = (bf16[2,2,169,1024]{3,1,2,0:T(2,128)(2,1)}, bf16[2,2,169,1024]{3,1,2,0:T(2,128)(2,1)}, u32[]{:S(2)}, u32[]{:S(2)}) collective-permute-start(bf16[2,2,169,1024]{3,1,2,0:T(2,128)(2,1)} %copy.237), channel_id=1, source_target_pairs={{0,2},{1,3},{2,0},{3,1},{4,6},{5,7},{6,4},{7,5},{8,10},{9,11},{10,... | collective-permute-start | bytes 4153352 | tf_op jit(solution)/shard_map/ppermute | solution.py:421
  735.5 175.8 %collective-permute-start.61 = (bf16[2,128,4096]{2,1,0:T(8,128)(2,1)}, bf16[2,128,4096]{2,1,0:T(8,128)(2,1)}, u32[]{:S(2)}, u32[]{:S(2)}) collective-permute-start(bf16[2,128,4096]{2,1,0:T(8,128)(2,1)} %dynamic-slice_bitcast_fusion.1), channel_id=1, source_target_pairs={{0,2},{1,3},{2,0},{3,1},{4,6},{5,7},{6,4},{7,5},{8,10},{9,11},{10,... | collective-permute-start | bytes 6291464 | tf_op jit(solution)/shard_map/ppermute | solution.py:421
  824.7 89.2 %collective-permute-start.64 = (bf16[2,512,1024]{2,1,0:T(8,128)(2,1)S(1)}, bf16[2,512,1024]{2,1,0:T(8,128)(2,1)S(1)}, u32[]{:S(2)}, u32[]{:S(2)}) collective-permute-start(bf16[2,512,1024]{2,1,0:T(8,128)(2,1)S(1)} %dynamic-slice_bitcast_fusion), channel_id=1, source_target_pairs={{0,2},{1,3},{2,0},{3,1},{4,6},{5,7},{6,4},{7,5},{8,10},{9,11},{10,... | collective-permute-start | bytes 6291464 | tf_op jit(solution)/shard_map/ppermute | solution.py:421
  831.0 41.4 %collective-permute-start.55 = (bf16[2,169,1024]{2,0,1:T(2,128)(2,1)S(1)}, bf16[2,169,1024]{2,0,1:T(2,128)(2,1)S(1)}, u32[]{:S(2)}, u32[]{:S(2)}) collective-permute-start(bf16[2,169,1024]{2,0,1:T(2,128)(2,1)S(1)} %copy.239), channel_id=1, source_target_pairs={{0,4},{1,5},{2,6},{3,7},{4,0},{5,1},{6,2},{7,3},{8,12},{9,13},{10,... | collective-permute-start | bytes 2076680 | tf_op jit(solution)/shard_map/ppermute | solution.py:421
  833.7 51.1 %collective-permute-start.59 = (bf16[128,3072]{1,0:T(8,128)(2,1)S(1)}, bf16[128,3072]{1,0:T(8,128)(2,1)S(1)}, u32[]{:S(2)}, u32[]{:S(2)}) collective-permute-start(bf16[128,3072]{1,0:T(8,128)(2,1)S(1)} %dynamic-slice_bitcast_fusion.7), channel_id=1, source_target_pairs={{0,4},{1,5},{2,6},{3,7},{4,0},{5,1},{6,2},{7,3},{8,12},{9,13},{10,... | collective-permute-start | bytes 2359304 | tf_op jit(solution)/shard_map/ppermute | solution.py:421
  853.6 53.2 %collective-permute-start.50 = (bf16[2,1000,256]{2,1,0:T(8,128)(2,1)S(1)}, bf16[2,1000,256]{2,1,0:T(8,128)(2,1)S(1)}, u32[]{:S(2)}, u32[]{:S(2)}) collective-permute-start(bf16[2,1000,256]{2,1,0:T(8,128)(2,1)S(1)} %dynamic-slice_bitcast_fusion.6), channel_id=1, source_target_pairs={{0,2},{1,3},{2,0},{3,1},{4,6},{5,7},{6,4},{7,5},{8,10},{9,11},{10,... | collective-permute-start | bytes 3072008 | tf_op jit(solution)/shard_map/ppermute | solution.py:421
  872.8 13.4 %collective-permute-start.56 = (bf16[169,1024]{1,0:T(8,128)(2,1)S(1)}, bf16[169,1024]{1,0:T(8,128)(2,1)S(1)}, u32[]{:S(2)}, u32[]{:S(2)}) collective-permute-start(bf16[169,1024]{1,0:T(8,128)(2,1)S(1)} %dynamic-slice_bitcast_fusion.10), channel_id=1, source_target_pairs={{0,1},{1,0},{2,3},{3,2},{4,5},{5,4},{6,7},{7,6},{8,9},{9,8},{10,11... | collective-permute-start | bytes 1038344 | tf_op jit(solution)/shard_map/ppermute | solution.py:421
  907.1 54.9 %collective-permute-start.51 = (bf16[1000,256]{1,0:T(8,128)(2,1)S(1)}, bf16[1000,256]{1,0:T(8,128)(2,1)S(1)}, u32[]{:S(2)}, u32[]{:S(2)}) collective-permute-start(bf16[1000,256]{1,0:T(8,128)(2,1)S(1)} %dynamic-slice_bitcast_fusion.9), channel_id=1, source_target_pairs={{0,4},{1,5},{2,6},{3,7},{4,0},{5,1},{6,2},{7,3},{8,12},{9,13},{10,... | collective-permute-start | bytes 1536008 | tf_op jit(solution)/shard_map/ppermute | solution.py:421
  913.8 70.6 %collective-permute-start.62 = (bf16[128,4096]{1,0:T(8,128)(2,1)S(1)}, bf16[128,4096]{1,0:T(8,128)(2,1)S(1)}, u32[]{:S(2)}, u32[]{:S(2)}) collective-permute-start(bf16[128,4096]{1,0:T(8,128)(2,1)S(1)} %dynamic-slice_bitcast_fusion.5), channel_id=1, source_target_pairs={{0,4},{1,5},{2,6},{3,7},{4,0},{5,1},{6,2},{7,3},{8,12},{9,13},{10,... | collective-permute-start | bytes 3145736 | tf_op jit(solution)/shard_map/ppermute | solution.py:421
  915.0 80.8 %collective-permute-start.65 = (bf16[512,1024]{1,0:T(8,128)(2,1)S(1)}, bf16[512,1024]{1,0:T(8,128)(2,1)S(1)}, u32[]{:S(2)}, u32[]{:S(2)}) collective-permute-start(bf16[512,1024]{1,0:T(8,128)(2,1)S(1)} %dynamic-slice_bitcast_fusion.4), channel_id=1, source_target_pairs={{0,4},{1,5},{2,6},{3,7},{4,0},{5,1},{6,2},{7,3},{8,12},{9,13},{10,... | collective-permute-start | bytes 3145736 | tf_op jit(solution)/shard_map/ppermute | solution.py:421
  (106 other events, 1262.5 us)

commit v2 on v1

--- a/solution.py
+++ b/solution.py
@@ -16,7 +16,7 @@
 SCORE_SCALE=0.125
 DEPTH=3
 F32=jnp.float32; BF=jnp.bfloat16
-VMEM_LIMIT=60*1024*1024
+VMEM_LIMIT=34*1024*1024
 GELU_A=math.sqrt(2.0/math.pi); GELU_B=0.044715
 
 def dot(a,b): return jnp.dot(a,b,preferred_element_type=F32)
@@ -45,39 +45,26 @@
     def wait(self):
         for c in self.copies: c.wait()
 
-def fwd_kernel(info,hid_in,far_in,entry,time_rows,gain_attn,gain_mlp,cos,sin,w_qkv,w_out,w_up,w_down,
+def fwd_kernel(tick,info,hid_in,far_in,entry,time_rows,gain_attn,gain_mlp,cos,sin,w_qkv,w_out,w_up,w_down,
                s_hid,s_attn,s_qkv,s_prob,s_ctx,s_second,s_mlp,s_gp,s_act,
                o_next,o_sums,o_hid,o_attn,o_qkv,o_prob,o_ctx,o_second,o_mlp,o_gp,o_act,
-               b_hid,b_qkvw,b_outw,b_upw,b_downw,b_attn,b_qkv,b_prob,b_ctx,b_second,b_low,b_mlp,b_gp,b_act,wsem,hsem,osem):
-    active=info[0]; slot=info[1]; source=info[2]
+               b_hid,b_attn,b_qkv,b_prob,b_ctx,b_second,b_low,b_mlp,b_gp,b_act,hsem,osem):
+    active=info[tick,0]; slot=info[tick,1]; source=info[tick,2]
     width=b_hid.shape[1]; T=b_hid.shape[0]
     nw=w_up.shape[1]//width
     npair=width//128
-    @pl.when(active==0)
-    def _():
-        o_sums[...]=jnp.zeros_like(o_sums)
-        o_next[...]=jnp.zeros_like(o_next)
     @pl.when(active==1)
     def _():
         src_copy=pltpu.make_async_copy(entry.at[slot],b_hid,hsem)
-        in_copy=pltpu.make_async_copy(hid_in,b_hid,hsem)
-        far_copy=pltpu.make_async_copy(far_in,b_hid,hsem)
         @pl.when(source==0)
         def _(): src_copy.start()
         @pl.when(source==1)
-        def _(): in_copy.start()
+        def _(): b_hid[...]=hid_in[...]
         @pl.when(source==2)
-        def _(): far_copy.start()
-        ld=Loads(wsem,DEPTH)
-        kq=[ld.add(w_qkv.at[:,pl.ds(i*width,width)],b_qkvw.at[i]) for i in range(3)]
-        ko=ld.add(w_out,b_outw)
-        ku,kd=[],[]
-        for i in range(nw):
-            ku.append(ld.add(w_up.at[:,pl.ds(i*width,width)],b_upw.at[i]))
-            kd.append(ld.add(w_down.at[pl.ds(i*width,width),:],b_downw.at[i]))
-        ld.fill(DEPTH)
+        def _(): b_hid[...]=far_in[...]
         outs=Puts(osem)
-        in_copy.wait()
+        @pl.when(source==0)
+        def _(): src_copy.wait()
         outs.add(b_hid,o_hid.at[slot])
         first=b_hid[...].astype(F32)+time_rows[pl.ds(slot,1),:]
         r1=lax.rsqrt(jnp.mean(first*first,axis=1,keepdims=True)+NORM_EPSILON)
@@ -89,8 +76,7 @@
         c_=cos[...]; s_=sin[...]
         a=b_attn[...]
         for i in range(3):
-            ld.wait(kq[i])
-            m=dot(a,b_qkvw[i])
+            m=dot(a,w_qkv[:,i*width:(i+1)*width])
             if i<2:
                 for p in range(npair):
                     x=m[:,p*128:(p+1)*128]
@@ -110,8 +96,7 @@
             b_ctx[:,p*128:(p+1)*128]=jnp.where(head0,c[:T],c[T:]).astype(BF)
         outs.add(b_prob,o_prob.at[slot])
         outs.add(b_ctx,o_ctx.at[slot])
-        ld.wait(ko)
-        ao=dot(b_ctx[...],b_outw[...])
+        ao=dot(b_ctx[...],w_out[...])
         second=b_hid[...].astype(F32)+time_rows[pl.ds(slot,1),:]+ao
         b_second[...]=second
         b_low[...]=second.astype(BF)
@@ -123,8 +108,7 @@
         acc=None
         for i in range(nw):
             cols=pl.ds(i*width,width)
-            ld.wait(ku[i])
-            u=dot(b_mlp[...],b_upw[i])
+            u=dot(b_mlp[...],w_up[:,i*width:(i+1)*width])
             u2=u*u
             th=jnp.tanh(GELU_A*(u+GELU_B*u2*u))
             h=0.5*(1.0+th)
@@ -134,8 +118,7 @@
             b_gp[i]=gp.astype(BF)
             outs.add(b_act.at[i],o_act.at[slot,:,cols])
             outs.add(b_gp.at[i],o_gp.at[slot,:,cols])
-            ld.wait(kd[i])
-            d=dot(act,b_downw[i])
+            d=dot(act,w_down[i*width:(i+1)*width,:])
             acc=d if acc is None else acc+d
         third=b_second[...]+acc
         o_next[...]=third.astype(BF)
@@ -148,79 +131,72 @@
     return [B(T,width),B(T,width),B(T,3*width),B(npair,2*T,T),B(T,width),B(T,width),B(T,width),B(T,hidden),B(T,hidden)]
 
 ANY=pl.BlockSpec(memory_space=pl.ANY)
+HB=pl.BlockSpec(memory_space=pltpu.HBM)
+LAYER_LIMIT=22*1024*1024
 VM=pl.BlockSpec(memory_space=pltpu.VMEM)
 SM=pl.BlockSpec(memory_space=pltpu.SMEM)
-def layer_forward(info,hid,far,entry,time_rows,ga,gm,cos,sin,w_qkv,w_out,w_up,w_down,stores):
+def in_hbm(x): return pltpu.with_memory_space_constraint(x,pltpu.HBM)
+
+def layer_forward(tick,info,hid,far,entry,time_rows,ga,gm,cos,sin,w_qkv,w_out,w_up,w_down,stores):
     T,width=hid.shape; hidden=w_up.shape[1]; micro=entry.shape[0]; nw=hidden//width; npair=width//128
     V=lambda *s: pltpu.VMEM(s,BF)
-    scratch=[V(T,width),V(3,width,width),V(width,width),V(nw,width,width),V(nw,width,width),
+    scratch=[V(T,width),
              V(T,width),V(T,3*width),V(npair,2*T,T),V(T,width),pltpu.VMEM((T,width),F32),V(T,width),
              V(T,width),V(nw,T,width),V(nw,T,width),
-             pltpu.SemaphoreType.DMA((4+2*nw,)),pltpu.SemaphoreType.DMA,pltpu.SemaphoreType.DMA((7+2*nw,))]
-    out=pl.pallas_call(fwd_kernel,
-        in_specs=[SM,ANY,ANY,ANY,VM,VM,VM,VM,VM,ANY,ANY,ANY,ANY]+[ANY]*9,
-        out_specs=[VM,VM]+[ANY]*9,
-        out_shape=[jax.ShapeDtypeStruct((T,width),BF),jax.ShapeDtypeStruct((3,width),F32)]+store_shapes(micro,T,width,hidden),
+             pltpu.SemaphoreType.DMA,pltpu.SemaphoreType.DMA((7+2*nw,))]
+    out=pl.pallas_call(functools.partial(fwd_kernel,tick),
+        in_specs=[SM,VM,VM,HB,VM,VM,VM,VM,VM,VM,VM,VM,VM]+[HB]*9,
+        out_specs=[VM,VM]+[HB]*9,
+        out_shape=[jax.ShapeDtypeStruct((T,width),BF),jax.ShapeDtypeStruct((3,width),F32)]+[pltpu.HBM(s.shape,s.dtype) for s in store_shapes(micro,T,width,hidden)],
         input_output_aliases={13+i:2+i for i in range(9)},
         scratch_shapes=scratch,
-        compiler_params=pltpu.CompilerParams(vmem_limit_bytes=VMEM_LIMIT),
+        compiler_params=pltpu.CompilerParams(vmem_limit_bytes=LAYER_LIMIT),
         cost_estimate=pl.CostEstimate(flops=2*T*width*(4*width+2*hidden),bytes_accessed=2*width*(4*width+2*hidden)+8*1024*1024,transcendentals=0),
         name="layer_fwd",
-    )(info,hid,far,entry,time_rows,ga,gm,cos,sin,w_qkv,w_out,w_up,w_down,*stores)
+    )(info,hid,far,in_hbm(entry),time_rows,ga,gm,cos,sin,w_qkv,w_out,w_up,w_down,*map(in_hbm,stores))
     return out[0],out[1],out[2:]
 
-def bwd_kernel(info,g_in,far_in,exits,time_rows,gain_attn,gain_mlp,cos,sin,w_qkv,w_out,w_up,w_down,
+def bwd_kernel(tick,info,g_in,far_in,exits,time_rows,gain_attn,gain_mlp,cos,sin,w_qkv,w_out,w_up,w_down,
                hid,qkv,prob,sec,gps,
                s_g,s_pre,s_gattn,s_mixed,s_first,
                o_next,o_vec,o_g,o_pre,o_gattn,o_mixed,o_first,
-               b_g,b_qkvw,b_outw,b_upw,b_downw,b_hid,b_qkv,b_prob,b_sec,b_gp,b_pre,b_gattn,b_gctx,b_second,b_mixed,wsem,hsem,osem):
-    active=info[0]; slot=info[1]; source=info[2]
+               b_g,b_hid,b_qkv,b_prob,b_sec,b_gp,b_pre,b_gattn,b_gctx,b_second,b_mixed,wsem,hsem,osem):
+    active=info[tick,0]; slot=info[tick,1]; source=info[tick,2]
     width=b_hid.shape[1]; T=b_hid.shape[0]
     nw=w_up.shape[1]//width
     npair=width//128
-    @pl.when(active==0)
-    def _():
-        o_vec[...]=jnp.zeros_like(o_vec)
-        o_next[...]=jnp.zeros_like(o_next)
     @pl.when(active==1)
     def _():
         src_copy=pltpu.make_async_copy(exits.at[slot],b_g,hsem)
-        in_copy=pltpu.make_async_copy(g_in,b_g,hsem)
-        far_copy=pltpu.make_async_copy(far_in,b_g,hsem)
         @pl.when(source==0)
         def _(): src_copy.start()
         @pl.when(source==1)
-        def _(): in_copy.start()
+        def _(): b_g[...]=g_in[...]
         @pl.when(source==2)
-        def _(): far_copy.start()
+        def _(): b_g[...]=far_in[...]
         ld=Loads(wsem,DEPTH)
-        kd,kg,ku=[],[],[]
+        kg=[]
         for i in range(nw):
             cols=pl.ds(i*width,width)
-            kd.append(ld.add(w_down.at[cols,:],b_downw.at[i]))
             kg.append(ld.add(gps.at[slot,:,cols],b_gp.at[i]))
-            ku.append(ld.add(w_up.at[:,cols],b_upw.at[i]))
         ks=ld.add(sec.at[slot],b_sec)
-        ko=ld.add(w_out,b_outw)
         kqkv=ld.add(qkv.at[slot],b_qkv)
         kp=ld.add(prob.at[slot],b_prob)
-        kq=[ld.add(w_qkv.at[:,pl.ds(i*width,width)],b_qkvw.at[i]) for i in range(3)]
         kh=ld.add(hid.at[slot],b_hid)
         ld.fill(DEPTH)
         outs=Puts(osem)
-        in_copy.wait()
+        @pl.when(source==0)
+        def _(): src_copy.wait()
         outs.add(b_g,o_g.at[slot])
         g=b_g[...]
         acc=None
         for i in range(nw):
-            ld.wait(kd[i])
-            ga=dot_nt(g,b_downw[i])
+            ga=dot_nt(g,w_down[i*width:(i+1)*width,:])
             ld.wait(kg[i])
             pre=(ga*b_gp[i].astype(F32)).astype(BF)
             b_pre[i]=pre
             outs.add(b_pre.at[i],o_pre.at[slot,:,pl.ds(i*width,width)])
-            ld.wait(ku[i])
-            d=dot_nt(pre,b_upw[i])
+            d=dot_nt(pre,w_up[:,i*width:(i+1)*width])
             acc=d if acc is None else acc+d
         ld.wait(ks)
         second=b_sec[...].astype(F32)
@@ -232,8 +208,7 @@
         b_second[...]=gs
         b_gattn[...]=gs.astype(BF)
         outs.add(b_gattn,o_gattn.at[slot])
-        ld.wait(ko)
-        b_gctx[...]=dot_nt(b_gattn[...],b_outw[...]).astype(BF)
+        b_gctx[...]=dot_nt(b_gattn[...],w_out[...]).astype(BF)
         lane=lax.broadcasted_iota(jnp.int32,(T,128),1)
         low=(lane%64)<32
         head0=lane<64
@@ -259,8 +234,7 @@
         outs.add(b_mixed,o_mixed.at[slot])
         acc=None
         for i in range(3):
-            ld.wait(kq[i])
-            d=dot_nt(b_mixed[:,i*width:(i+1)*width],b_qkvw[i])
+            d=dot_nt(b_mixed[:,i*width:(i+1)*width],w_qkv[:,i*width:(i+1)*width])
             acc=d if acc is None else acc+d
         ld.wait(kh)
         first=b_hid[...].astype(F32)+time_rows[pl.ds(slot,1),:]
@@ -278,22 +252,22 @@
     B=lambda *s: jax.ShapeDtypeStruct((micro,)+s,BF)
     return [B(T,width),B(T,hidden),B(T,width),B(T,3*width),B(T,width)]
 
-def layer_backward(info,g,far,exits,time_rows,ga,gm,cos,sin,w_qkv,w_out,w_up,w_down,saved,stores):
+def layer_backward(tick,info,g,far,exits,time_rows,ga,gm,cos,sin,w_qkv,w_out,w_up,w_down,saved,stores):
     T,width=g.shape; hidden=w_up.shape[1]; micro=exits.shape[0]; nw=hidden//width; npair=width//128
     V=lambda *s: pltpu.VMEM(s,BF)
-    scratch=[V(T,width),V(3,width,width),V(width,width),V(nw,width,width),V(nw,width,width),
+    scratch=[V(T,width),
              V(T,width),V(T,3*width),V(npair,2*T,T),V(T,width),V(nw,T,width),V(nw,T,width),V(T,width),V(T,width),pltpu.VMEM((T,width),F32),V(T,3*width),
-             pltpu.SemaphoreType.DMA((8+3*nw,)),pltpu.SemaphoreType.DMA,pltpu.SemaphoreType.DMA((4+nw,))]
-    out=pl.pallas_call(bwd_kernel,
-        in_specs=[SM,ANY,ANY,ANY,VM,VM,VM,VM,VM]+[ANY]*4+[ANY]*5+[ANY]*5,
-        out_specs=[VM,VM]+[ANY]*5,
-        out_shape=[jax.ShapeDtypeStruct((T,width),BF),jax.ShapeDtypeStruct((3,width),F32)]+grad_shapes(micro,T,width,hidden),
+             pltpu.SemaphoreType.DMA((4+nw,)),pltpu.SemaphoreType.DMA,pltpu.SemaphoreType.DMA((4+nw,))]
+    out=pl.pallas_call(functools.partial(bwd_kernel,tick),
+        in_specs=[SM,VM,VM,HB,VM,VM,VM,VM,VM]+[VM]*4+[HB]*5+[HB]*5,
+        out_specs=[VM,VM]+[HB]*5,
+        out_shape=[jax.ShapeDtypeStruct((T,width),BF),jax.ShapeDtypeStruct((3,width),F32)]+[pltpu.HBM(s.shape,s.dtype) for s in grad_shapes(micro,T,width,hidden)],
         input_output_aliases={18+i:2+i for i in range(5)},
         scratch_shapes=scratch,
-        compiler_params=pltpu.CompilerParams(vmem_limit_bytes=VMEM_LIMIT),
+        compiler_params=pltpu.CompilerParams(vmem_limit_bytes=LAYER_LIMIT),
         cost_estimate=pl.CostEstimate(flops=2*T*width*(4*width+2*hidden),bytes_accessed=2*width*(4*width+2*hidden)+8*1024*1024,transcendentals=0),
         name="layer_bwd",
-    )(info,g,far,exits,time_rows,ga,gm,cos,sin,w_qkv,w_out,w_up,w_down,*saved,*stores)
+    )(info,g,far,in_hbm(exits),time_rows,ga,gm,cos,sin,w_qkv,w_out,w_up,w_down,*map(in_hbm,saved),*map(in_hbm,stores))
     return out[0],out[1],out[2:]
 
 def rope_tables(T,head):
@@ -368,13 +342,15 @@
     )(table, latent)
 
 
-def head_backward_kernel(table, latent, log_total, weight, o_grad):
+def head_backward_kernel(table, latent, log_total, weight, ids, terms, token, o_grad):
     logits = dot_nt(table[...], latent[...])
     g = (jnp.exp(logits - log_total[...]) * weight[...]).astype(BF)
-    o_grad[...] = dot(g, latent[...]).astype(BF)
-
-
-def head_backward(table, latent, log_total, weight):
+    rows = lax.broadcasted_iota(jnp.int32, g.shape, 0) + pl.program_id(0) * g.shape[0]
+    picks = jnp.where(rows == ids[...], 1.0, 0.0).astype(BF)
+    o_grad[...] = (dot(g, latent[...]) + dot(picks, terms[...])).astype(BF)
+
+
+def head_backward(table, latent, log_total, weight, ids, terms, token):
     rows, emb = table.shape
     tokens = latent.shape[0]
     tile = vocab_tile(rows)
@@ -386,13 +362,16 @@
             pl.BlockSpec((tokens, emb), lambda i: (0, 0)),
             pl.BlockSpec((1, tokens), lambda i: (0, 0)),
             pl.BlockSpec((1, tokens), lambda i: (0, 0)),
+            pl.BlockSpec((1, tokens), lambda i: (0, 0)),
+            pl.BlockSpec((tokens, emb), lambda i: (0, 0)),
+            ANY,
         ],
         out_specs=pl.BlockSpec((tile, emb), lambda i: (i, 0)),
         out_shape=jax.ShapeDtypeStruct((rows, emb), BF),
         compiler_params=pltpu.CompilerParams(vmem_limit_bytes=VMEM_LIMIT),
-        cost_estimate=pl.CostEstimate(flops=4 * rows * emb * tokens, bytes_accessed=4 * rows * emb, transcendentals=rows * tokens),
+        cost_estimate=pl.CostEstimate(flops=1, bytes_accessed=1, transcendentals=0),
         name="head_bwd",
-    )(table, latent, log_total, weight)
+    )(table, latent, log_total, weight, ids, terms, token)
 
 
 def blank_kernel(*refs):
@@ -400,7 +379,7 @@
 
 
 def blanks(shapes):
-    return pl.pallas_call(blank_kernel, out_specs=[ANY] * len(shapes), out_shape=shapes, name="blanks")()
+    return pl.pallas_call(blank_kernel, out_specs=[HB] * len(shapes), out_shape=shapes, name="blanks")()
 
 
 def bits_of(size):
@@ -413,7 +392,11 @@
 def dp_orders(size):
     bits = bits_of(size)
     low = bits // 2
-    return list(range(bits)), list(range(low, bits)) + list(range(low))
+    return (
+        list(range(bits)),
+        list(range(low, bits)) + list(range(low)),
+        [low] + list(range(low)) + list(range(low + 1, bits)),
+    )
 
 
 def swap(x, axis, bit):
@@ -450,6 +433,131 @@
             x = x.astype(BF)
         left.remove(bit)
     return x
+
+
+def zero_of(token):
+    return jnp.minimum(jnp.abs(token[(0,) * token.ndim].astype(F32)), 0.0)
+
+
+def after(x, token):
+    return x + zero_of(token).astype(x.dtype)
+
+
+class Scatter:
+    def __init__(self, blocks, order):
+        self.order = list(order)
+        self.left = list(range(len(order) - 1, -1, -1))
+        self.index = lax.axis_index("dp")
+        self.terms = [blocks.reshape((2,) * len(order) + blocks.shape[1:])]
+
+    def _side(self, side, at):
+        parts = [lax.dynamic_index_in_dim(t, side, at, keepdims=False).astype(F32) for t in self.terms]
+        return sum(parts[1:], parts[0])
+
+    def send(self, token):
+        bit = self.order.pop(0)
+        at = self.left.index(bit)
+        self.left.remove(bit)
+        mine = (self.index >> bit) & 1
+        sent = (self._side(1 - mine, at) + (0.0 if token is None else zero_of(token))).astype(BF)
+        self.got = lax.ppermute(sent, "dp", [(i, i ^ (1 << bit)) for i in range(lax.axis_size("dp"))])
+        self.terms = [lax.dynamic_index_in_dim(t, mine, at, keepdims=False) for t in self.terms]
+        return sent
+
+    def step(self, token):
+        self.terms.append(self.got)
+        return self.send(token)
+
+    def end(self, token):
+        while self.order:
+            token = self.step(token)
+        parts = [t.astype(F32) for t in self.terms + [self.got]]
+        self.total = sum(parts[1:], parts[0]) + zero_of(token)
+        return self.total
+
+
+def product_kernel(ids, *refs):
+    left, (right, token, out, mark) = refs[:-4], refs[-4:]
+    a = jnp.concatenate([r[...] for r in left], axis=1)
+    out[...] = dot_tn(a, right[...]).astype(BF)
+    mark[...] = jnp.zeros_like(mark)
+
+
+def product(left, right, ids, block, part, parts, token):
+    rows, columns = left.shape[0], right.shape[1] // parts
+    count = ids.shape[0]
+    tile = 512 if columns % 512 == 0 else columns
+    first = part * columns // tile
+
+    def pick(j):
+        return pl.BlockSpec((rows, block), lambda i, ids: (0, ids[j]))
+
+    return pl.pallas_call(
+        product_kernel,
+        grid_spec=pltpu.PrefetchScalarGridSpec(
+            num_scalar_prefetch=1,
+            grid=(columns // tile,),
+            in_specs=[pick(j) for j in range(count)] + [pl.BlockSpec((rows, tile), lambda i, ids: (0, first + i)), ANY],
+            out_specs=[
+                pl.BlockSpec((count * block, tile), lambda i, ids: (0, i)),
+                pl.BlockSpec((8, 128), lambda i, ids: (0, 0)),
+            ],
+        ),
+        out_shape=[
+            jax.ShapeDtypeStruct((count * block, columns), BF),
+            jax.ShapeDtypeStruct((8, 128), F32),
+        ],
+        compiler_params=pltpu.CompilerParams(vmem_limit_bytes=VMEM_LIMIT),
+        cost_estimate=pl.CostEstimate(flops=1, bytes_accessed=1, transcendentals=0),
+        name="product",
+    )(ids, *[left] * count, right, token)
+
+
+class Product(Scatter):
+    def __init__(self, left, right, order, part=0, parts=1):
+        self.order = list(order)
+        self.bits = len(order)
+        self.left = list(range(self.bits - 1, -1, -1))
+        self.index = lax.axis_index("dp")
+        self.a, self.g = left, right
+        self.part, self.parts = part, parts
+
+    def _half(self, side, token):
+        rows = self.a.shape[1]
+        block = rows >> self.bits
+        ids = jnp.array([i for i in range(1 << self.bits) if not (i >> self.bit) & 1], jnp.int32)
+        ids = ids + side.astype(jnp.int32) * (1 << self.bit)
+        if block % 128 == 0:
+            x, mark = product(self.a, self.g, ids, block, self.part, self.parts, token)
+        else:
+            a = jnp.take(self.a.reshape(self.a.shape[0], -1, block), ids, axis=1).reshape(self.a.shape[0], -1)
+            wide = self.g.shape[1] // self.parts
+            x = dot_tn(after(a, token), self.g[:, self.part * wide : (self.part + 1) * wide]).astype(BF)
+            mark = x
+        return x.reshape((2,) * (self.bits - 1) + (block, x.shape[1])), mark
+
+    def send(self, token):
+        if len(self.order) == self.bits:
+            self.bit = bit = self.order.pop(0)
+            self.left.remove(bit)
+            self.mine = (self.index >> bit) & 1
+            sent, mark = self._half(1 - self.mine, token)
+            self.got = lax.ppermute(sent, "dp", [(i, i ^ (1 << bit)) for i in range(lax.axis_size("dp"))])
+            return mark
+        return super().send(token)
+
+    def keep(self, token):
+        kept, mark = self._half(self.mine, token)
+        self.terms = [kept]
+        return mark
+
+
+def tick_infos(ticks, offset, micro, source):
+    slot = jnp.arange(ticks) - offset
+    active = (slot >= 0) & (slot < micro)
+    return jnp.stack(
+        [active.astype(jnp.int32), jnp.clip(slot, 0, micro - 1), jnp.full((ticks,), source, jnp.int32)], axis=1
+    ).astype(jnp.int32)
 
 
 def sum_all(x, axis):
@@ -506,8 +614,8 @@
     count = seq_counts[lax.axis_index("dp")]
     count_all = jnp.sum(seq_counts).astype(F32)
     valid = (jnp.arange(micro) < count).astype(F32)
-    low_first, high_first = dp_orders(groups)
-    gather_order = high_first[::-1] if False else low_first[::-1]
+    low_first, high_first, mid_first = dp_orders(groups)
+    gather_order = low_first[::-1]
     section_order = list(range(bits_of(sections)))
 
     own_rows, table_back = jax.vjp(rms_scale, table.astype(F32))
@@ -538,25 +646,20 @@
     time_low = time_features(sigma, emb).astype(BF)
     time_rows = dot(time_low, w_time[0])
     cosines, sines = rope_tables(seq_len, width // HEADS)
-    weights = (w_qkv[0], w_out[0], w_up[0], w_down[0])
+    weights = tuple(pltpu.with_memory_space_constraint(w[0], pltpu.VMEM) for w in (w_qkv, w_out, w_up, w_down))
 
     stores = blanks(store_shapes(micro, seq_len, width, hidden))
     offset = delay(section)
     ticks = micro + delay(last)
-    core_in = entry[0]
-    x_next = x_in = entry[0]
-    square_sums = jnp.zeros((3,), F32)
+    infos = tick_infos(ticks, offset, micro, jnp.where(section == 0, 0, jnp.where(section % 2 == 1, 1, 2)))
+    core_in = x_next = x_in = entry[0]
+    tick_sums = []
     finals = []
     for tick in range(ticks):
-        slot = tick - offset
-        active = (slot >= 0) & (slot < micro)
-        safe = jnp.clip(slot, 0, micro - 1)
-        source = jnp.where(section == 0, 0, jnp.where(section % 2 == 1, 1, 2))
-        info = jnp.stack([active.astype(jnp.int32), safe, source]).astype(jnp.int32)
         sent, sums, stores = layer_forward(
-            info, core_in, x_in, entry, time_rows, gain_attn, gain_mlp, cosines, sines, *weights, stores
+            tick, infos, core_in, x_in, entry, time_rows, gain_attn, gain_mlp, cosines, sines, *weights, stores
         )
-        square_sums = square_sums + jnp.sum(sums, axis=1) * valid[safe]
+        tick_sums.append(sums)
         if tick - delay(last) >= 0:
             finals.append(sent)
         going = [s for s in range(last) if 0 <= tick - delay(s) < micro]
@@ -565,8 +668,6 @@
         core_in = lax.ppermute(sent, "section", core_pairs) if core_pairs else sent
         x_in = x_next
         x_next = lax.ppermute(sent, "section", x_pairs) if x_pairs else sent
-    total_sums = sum_all(square_sums, "dp")
-    layer_rms = jnp.sqrt(total_sums / (count_all * seq_len * width))[None, :]
 
     final = jnp.concatenate(finals, axis=0).astype(F32)
     normalized, head_back = jax.vjp(rms_scale, final)
@@ -585,33 +686,26 @@
             mean = mean.astype(BF)
         stats = jnp.stack([peak, total])
     log_total = stats[0] + jnp.log(stats[1])
-    target_logit = jnp.sum(latent.astype(F32) * picked_all.astype(F32), axis=1)
-    token_loss = (log_total - target_logit) * weight
-    seq_loss = jnp.sum(token_loss.reshape(micro, seq_len), axis=1) / seq_len
     grad_latent = ((mean.T - picked_all.astype(F32)) * (weight * LOGIT_SCALE)[:, None]).astype(BF)
-    grad_table_head = head_backward(rows_sec, latent, log_total[None, :], weight[None, :])
     grad_final = head_back(dot(grad_latent, proj_full))[0].astype(BF)
     exit_grad = grad_final.reshape(micro, seq_len, width)
     grad_proj = jnp.where(section == last, dot_tn(grad_latent, feats), 0.0)
 
     saved = [stores[0], stores[2], stores[3], stores[5], stores[7]]
     grads = blanks(grad_shapes(micro, seq_len, width, hidden))
-    core_in = exit_grad[0]
-    x_next = x_in = exit_grad[0]
-    gain_sums = jnp.zeros((2, width), F32)
-    time_terms = []
-    time_sum = jnp.zeros((micro, width), F32)
+    back_offset = delay(last) - offset
+    infos = tick_infos(ticks, back_offset, micro, jnp.where(section == last, 0, jnp.where(section % 2 == 0, 1, 2)))
+    core_in = x_next = x_in = exit_grad[0]
+    tick_rows = []
+    sums = jnp.sum(lax.dynamic_slice_in_dim(jnp.stack(tick_sums), offset, micro, 0), axis=2)
+    square_sums = jnp.sum(sums * valid[:, None], axis=0)
     for tick in range(ticks):
-        slot = tick - (delay(last) - offset)
-        active = (slot >= 0) & (slot < micro)
-        safe = jnp.clip(slot, 0, micro - 1)
-        source = jnp.where(section == last, 0, jnp.where(section % 2 == 0, 1, 2))
-        info = jnp.stack([active.astype(jnp.int32), safe, source]).astype(jnp.int32)
         sent, rows, grads = layer_backward(
-            info, core_in, x_in, exit_grad, time_rows, gain_attn, gain_mlp, cosines, sines, *weights, saved, grads
+            tick, infos, core_in, x_in, exit_grad, time_rows, gain_attn, gain_mlp, cosines, sines, *weights, saved, grads
         )
-        gain_sums = gain_sums + rows[:2]
-        time_sum = time_sum + jnp.where((jnp.arange(micro) == safe)[:, None], rows[2:3], 0.0)
+        tick_rows.append(rows)
+        if tick < bits_of(groups):
+            square_sums = square_sums + after(swap(square_sums, "dp", tick), rows)
         going = [s for s in range(1, sections) if 0 <= tick - (delay(last) - delay(s)) < micro]
         core_pairs = [(s, s - 1) for s in going if s % 2 == 1]
         x_pairs = [(s, s - 1) for s in going if s % 2 == 0]
@@ -625,39 +719,83 @@
         stores[i].reshape(tokens, stores[i].shape[2]) for i in (1, 4, 6, 8)
     )
 
-    def scattered(x, order):
-        return scatter_sum(x.astype(BF).reshape((groups, x.shape[0] // groups) + x.shape[1:]), "dp", order)
-
-    w_down_grad = scattered(dot_tn(activated_all, grad_out_all), low_first)
-    w_up_grad = scattered(dot_tn(mlp_in_all, grad_pre_all), low_first)
-    w_qkv_grad = scattered(dot_tn(attn_in_all, grad_mixed_all), low_first)
-    grad_entry = spread(grad_first_all, "section", 0)
-    grad_inputs = dot_nt(grad_entry, proj_full)
-    grad_proj = grad_proj + jnp.where(section == 0, dot_tn(inputs_all, grad_entry), 0.0)
+    out = Product(context_all, grad_attn_all, high_first)
+    down = Product(activated_all, grad_out_all, low_first)
+    up = Product(mlp_in_all, grad_pre_all, low_first)
+    qkv = [Product(attn_in_all, grad_mixed_all, low_first, part, 2) for part in range(2)]
+    token = down.send(square_sums)
+    token = up.send(token)
+    token = out.send(token)
+    token = out.keep(token)
+    token = qkv[0].send(token)
+    token = qkv[1].send(token)
+    token = qkv[0].keep(token)
+    token = qkv[1].keep(token)
+    token = up.keep(token)
+    token = down.keep(token)
+    token = out.step(None)
+    token = out.step(None)
+    token = down.step(token)
+
+    grad_inputs = (dot_nt(grad_first_all, proj_full) + zero_of(token)).astype(BF)
+    grad_inputs = spread(grad_inputs, "section", 0).astype(F32)
+    row_terms = grad_inputs * jnp.repeat(shrink, seq_len)[:, None] - latent.astype(F32) * weight[:, None]
+    grad_table = head_backward(
+        rows_sec, latent, log_total[None, :], weight[None, :], ids_rows[None, :], row_terms.astype(BF), token
+    )
+    tab = Scatter(grad_table.reshape(groups, -1, emb), low_first)
+    token = tab.send(token)
+    token = down.step(token)
+    grad_proj = grad_proj + jnp.where(section == 0, dot_tn(inputs_all, after(grad_first_all, token)), 0.0)
     proj_part = scatter_sum(grad_proj.astype(BF).reshape(sections, emb // sections, width), "section", section_order[::-1])
-    w_time_term = jnp.dot(time_low.astype(F32).T, time_sum, precision=PRECISION_MAXIMAL)
-    gain_rows = jnp.transpose(gain_sums.reshape(2, groups, width // groups), (1, 0, 2)).reshape(groups, 1, -1)
-    gain_rows = jnp.pad(gain_rows, ((0, 0), (0, 0), (0, width - gain_rows.shape[2])))
+    rows = lax.dynamic_slice_in_dim(jnp.stack(tick_rows), back_offset, micro, 0)
+    rows = after(rows, token)
+    w_time_term = jnp.dot(time_low.astype(F32).T, rows[:, 2], precision=PRECISION_MAXIMAL)
+    gain_rows = jnp.sum(rows[:, :2], axis=0)
+    gain_rows = jnp.transpose(gain_rows.reshape(2, groups, width // groups), (1, 0, 2)).reshape(groups, 1, -1)
+    at = [emb // groups, emb // sections // groups]
+    pad = -sum(at) % 16 or 16
+    gain_rows = jnp.pad(gain_rows, ((0, 0), (0, pad - 1), (0, width - gain_rows.shape[2])))
     packed = jnp.concatenate(
         [
-            dot_tn(context_all, grad_attn_all).astype(BF).reshape(groups, -1, width),
             w_time_term.astype(BF).reshape(groups, -1, width),
             proj_part.astype(BF).reshape(groups, -1, width),
             gain_rows.astype(BF),
         ],
         axis=1,
     )
-    packed = scatter_sum(packed, "dp", high_first)
-    at = [width // groups, emb // groups, emb // sections // groups]
-    w_out_grad = packed[: at[0]]
-    w_time_grad = packed[at[0] : at[0] + at[1]]
-    proj_grad = packed[at[0] + at[1] : sum(at)]
-    gains = packed[-1, : 2 * width // groups].reshape(2, width // groups)
-    row_terms = grad_inputs * jnp.repeat(shrink, seq_len)[:, None] - latent.astype(F32) * weight[:, None]
-    onehot_rows = (jnp.arange(vocab_sec)[:, None] == ids_rows[None, :]).astype(BF)
-    grad_table = grad_table_head.astype(F32) + dot(onehot_rows, row_terms.astype(BF))
-    table_sum = scattered(grad_table, low_first)
-    table_grad = table_back(table_sum)[0]
+    pack = Scatter(packed, high_first)
+    token = pack.send(token)
+    token = up.step(token)
+    token = down.end(token)
+    token = pack.step(token)
+    token = qkv[0].step(token)
+    token = up.step(token)
+    token = pack.step(token)
+    token = qkv[1].step(token)
+    token = qkv[0].step(token)
+    token = tab.step(token)
+    token = qkv[1].step(token)
+    token = up.end(token)
+    token = out.end(token)
+    token = pack.end(token)
+    token = qkv[0].end(token)
+    token = tab.step(token)
+    token = qkv[1].end(token)
+    token = tab.end(token)
+    target_logit = jnp.sum(latent.astype(F32) * picked_all.astype(F32), axis=1)
+    token_loss = (log_total - target_logit) * weight
+    seq_loss = jnp.sum(token_loss.reshape(micro, seq_len), axis=1) / seq_len
+    layer_rms = jnp.sqrt(square_sums / (count_all * seq_len * width))[None, :]
+    packed = pack.total
+    w_out_grad = out.total
+    w_down_grad = down.total
+    w_up_grad = up.total
+    w_qkv_grad = jnp.concatenate([qkv[0].total, qkv[1].total], axis=1)
+    w_time_grad = packed[: at[0]]
+    proj_grad = packed[at[0] : sum(at)]
+    gains = packed[sum(at), : 2 * width // groups].reshape(2, width // groups)
+    table_grad = table_back(tab.total)[0]
     grad_mine = lax.dynamic_slice_in_dim(
         grad_inputs.reshape(micro, seq_len, emb), section * shard, shard, 1
     )

time: 1010 us -> 879 us (0.87)
  waiting for transfers between devices: 484 us -> 343 us
  matrix products: 48 us -> 16.1 us
  local copies, waits for them, and re-layouts: 54.7 us -> 78.4 us
  between operations: 3.79 us -> 20.5 us
    ppermute x40 -> x25, waiting for transfers between devices: 419 us -> 117 us  [swap(): return lax.ppermute(x, axis, pairs)]
    ppermute x0 -> x21, waiting for transfers between devices: none -> 159 us  [send(): lax.ppermute(sent, 'dp', [(i, i ^ 1 << bit) for i in range(lax.axis_size(...]
    ppermute x0 -> x21, starting transfers between devices: none -> 39 us  [send(): lax.ppermute(sent, 'dp', [(i, i ^ 1 << bit) for i in range(lax.axis_size(...]
    unnamed x180 -> x338, local copies, waits for them, and re-layouts: 13.1 us -> 48.2 us
    ppermute x40 -> x25, starting transfers between devices: 85.8 us -> 52.5 us  [swap(): return lax.ppermute(x, axis, pairs)]
    dot_general x6 -> x2, matrix products: 31.5 us -> 3.27 us  [dot_tn(): lax.dot_general(a, b, (((0,), (0,)), ((), ())), preferred_element_type=F32)]
    dynamic_slice x9 -> x0, local copies, waits for them, and re-layouts: 25.5 us -> none  [the longest x4 14.3 us: scatter_sum(): kept = lax.dynamic_index_in_dim(x, mine, at, keepdims=False)]
    convert_element_type x0 -> x19, other arithmetic: none -> 24.4 us  [the longest x16 23.3 us: send(): (self._side(1 - mine, at) + (0.0 if token is None else zero_of(token))).a...]
  transfers between devices with their start and end apart: 66 -> 72, of which waited for: 35 -> 36; matrix products, arithmetic and copies ran while one was open for 15% -> 11% of each run, Pallas kernels for 10% -> 17%
where the time goes in v2:
time: 879 us; the launch traced here: 868 us
  waiting for transfers between devices  343 us (39%)
  Pallas kernels  227 us (26%)
  starting transfers between devices  117 us (13%)
  local copies, waits for them, and re-layouts  78.4 us (9%)
  other arithmetic  66.7 us (8%)
  between operations  20.5 us (2%)
  matrix products  16.1 us (2%)
    ppermute x21, waiting for transfers between devices, send(): lax.ppermute(sent, 'dp', [(i, i ^ 1 << bit) for i in range(lax.axis_size(...  159 us
    ppermute x25, waiting for transfers between devices, swap(): return lax.ppermute(x, axis, pairs)  117 us
    pallas_call x8, Pallas kernels, layer_backward(): pl.pallas_call(functools.partial(bwd_kernel, tick), in_specs=[SM, VM, VM,...  78.8 us
    pallas_call x8, Pallas kernels, layer_forward(): pl.pallas_call(functools.partial(fwd_kernel, tick), in_specs=[SM, VM, VM,...  77.2 us
    ppermute x25, starting transfers between devices, swap(): return lax.ppermute(x, axis, pairs)  52.5 us
    ppermute x14, waiting for transfers between devices, body(): core_in = lax.ppermute(sent, 'section', core_pairs) if core_pairs else sent  49.7 us
    unnamed x338, local copies, waits for them, and re-layouts  48.2 us
    pallas_call x10, Pallas kernels, product(): pl.pallas_call(product_kernel, grid_spec=pltpu.PrefetchScalarGridSpec(num...  42.5 us
  transfers between devices with their start and end apart: 72, of which 36 were waited for; matrix products, arithmetic and copies ran while one was open for 11% of the time, Pallas kernels for 17%

profile of v2, /device:TPU:0, one launch (start us, length us, event | category | flops | bytes accessed | tf_op | source)
XLA Modules:
  0.0 868.4 jit_solution(12838121123695721616)
XLA Ops:
  5.1 3.7 collective-permute-start
  11.4 21.2 %collective-permute-done = bf16[1000,256]{1,0:T(8,128)(2,1)S(1)} collective-permute-done((bf16[1000,256]{1,0:T(8,128)(2,1)S(1)}, bf16[1000,256]{1,0:T(8,128)(2,1)S(1)}, u32[]{:S(2)}, u32[]{:S(2)}) %collective-permute-start) | collective-permute-done | bytes 512032 | tf_op jit(solution)/shard_map/ppermute | solution.py:404
  34.8 22.2 %collective-permute-done.1 = bf16[2,1000,256]{2,1,0:T(8,128)(2,1)S(1)} collective-permute-done((bf16[2,1000,256]{2,1,0:T(8,128)(2,1)S(1)}, bf16[2,1000,256]{2,1,0:T(8,128)(2,1)S(1)}, u32[]{:S(2)}, u32[]{:S(2)}) %collective-permute-start.1) | collective-permute-done | bytes 1024032 | tf_op jit(solution)/shard_map/ppermute | solution.py:404
  70.2 34.9 %collective-permute-done.2 = bf16[2,2,1000,256]{3,2,0,1:T(8,128)(2,1)} collective-permute-done((bf16[2,2,1000,256]{3,2,0,1:T(8,128)(2,1)}, bf16[2,2,1000,256]{3,2,0,1:T(8,128)(2,1)}, u32[]{:S(2)}, u32[]{:S(2)}) %collective-permute-start.2) | collective-permute-done | bytes 2048032 | tf_op jit(solution)/shard_map/ppermute | solution.py:404
  110.3 7.1 fusion.25
  118.8 4.4 collective-permute-done.5
  128.0 4.6 collective-permute-done.13
  132.7 3.7 collective-permute-done.8
  138.4 14.1 %layer_fwd.8 = (bf16[192,1024]{1,0:T(8,128)(2,1)S(1)}, f32[3,1024]{1,0:T(4,128)S(1)}, bf16[4,192,1024]{2,1,0:T(8,128)(2,1)}, bf16[4,192,1024]{2,1,0:T(8,128)(2,1...) custom-call(s32[8,3]{1,0:T(8,128)S(1)} %copy-done.46, ...), custom_call_target="tpu_custom_call", output_to_operand_aliasing={{2}: (13, {}), {3}: (14, {}), {4}: (15, {}), {5}: (16, {}),... | custom-call | flops 4831838208 | bytes 33554432 | tf_op jit(solution)/shard_map/layer_fwd/pallas_call | solution.py:147
  155.1 13.7 %layer_fwd.9 = (bf16[192,1024]{1,0:T(8,128)(2,1)S(1)}, f32[3,1024]{1,0:T(4,128)S(1)}, bf16[4,192,1024]{2,1,0:T(8,128)(2,1)}, bf16[4,192,1024]{2,1,0:T(8,128)(2,1...) custom-call(s32[8,3]{1,0:T(8,128)S(1)} %copy-done.46, ...), custom_call_target="tpu_custom_call", output_to_operand_aliasing={{2}: (13, {}), {3}: (14, {}), {4}: (15, {}), {5}: (16, {}),... | custom-call | flops 4831838208 | bytes 33554432 | tf_op jit(solution)/shard_map/layer_fwd/pallas_call | solution.py:147
  172.0 13.9 %layer_fwd.10 = (bf16[192,1024]{1,0:T(8,128)(2,1)S(1)}, f32[3,1024]{1,0:T(4,128)S(1)}, bf16[4,192,1024]{2,1,0:T(8,128)(2,1)}, bf16[4,192,1024]{2,1,0:T(8,128)(2,...) custom-call(s32[8,3]{1,0:T(8,128)S(1)} %copy-done.46, ...), custom_call_target="tpu_custom_call", output_to_operand_aliasing={{2}: (13, {}), {3}: (14, {}), {4}: (15, {}), {5}: (16, {}),... | custom-call | flops 4831838208 | bytes 33554432 | tf_op jit(solution)/shard_map/layer_fwd/pallas_call | solution.py:147
  189.4 13.7 %layer_fwd.11 = (bf16[192,1024]{1,0:T(8,128)(2,1)S(1)}, f32[3,1024]{1,0:T(4,128)S(1)}, bf16[4,192,1024]{2,1,0:T(8,128)(2,1)}, bf16[4,192,1024]{2,1,0:T(8,128)(2,...) custom-call(s32[8,3]{1,0:T(8,128)S(1)} %copy-done.46, ...), custom_call_target="tpu_custom_call", output_to_operand_aliasing={{2}: (13, {}), {3}: (14, {}), {4}: (15, {}), {5}: (16, {}),... | custom-call | flops 4831838208 | bytes 33554432 | tf_op jit(solution)/shard_map/layer_fwd/pallas_call | solution.py:147
  205.7 8.4 layer_fwd.12
  218.3 11.9 %layer_fwd.14 = (bf16[192,1024]{1,0:T(8,128)(2,1)}, f32[3,1024]{1,0:T(4,128)S(1)}, bf16[4,192,1024]{2,1,0:T(8,128)(2,1)}, bf16[4,192,1024]{2,1,0:T(8,128)(2,1)},...) custom-call(s32[8,3]{1,0:T(8,128)S(1)} %copy-done.46, ...), custom_call_target="tpu_custom_call", output_to_operand_aliasing={{2}: (13, {}), {3}: (14, {}), {4}: (15, {}), {5}: (16, {}),... | custom-call | flops 4831838208 | bytes 33554432 | tf_op jit(solution)/shard_map/layer_fwd/pallas_call | solution.py:147
  250.2 6.5 collective-permute-start.29
  258.2 21.5 %collective-permute-start.30 = (bf16[2,4,48,256]{3,2,1,0:T(8,128)(2,1)S(1)}, bf16[2,4,48,256]{3,2,1,0:T(8,128)(2,1)S(1)}, u32[]{:S(2)}, u32[]{:S(2)}) collective-permute-start(bf16[2,4,48,256]{3,2,1,0:T(8,128)(2,1)S(1)} %maximum_select_fusion.13), channel_id=1, source_target_pairs={{0,16},{8,24},{16,0},{24,8},{1,17},{9,25},{17,1},{25,9},{2,18},{10... | collective-permute-start | bytes 589832 | tf_op jit(solution)/shard_map/ppermute | solution.py:404
  281.2 4.1 collective-permute-done.30
  285.6 7.5 collective-permute-done.26
  294.0 16.8 %head_fwd.1 = (bf16[256,768]{1,0:T(8,128)(2,1)S(1)}, f32[2,768]{1,0:T(2,128)S(1)}) custom-call(bf16[8000,256]{1,0:T(8,128)(2,1)S(1)} %bitcast.484, bf16[768,256]{1,0:T(8,128)(2,1)S(1)} %get-tuple-element.393.latent), custom_call_target="tpu_custom_call" | custom-call | flops 6291456000 | bytes 4096000 | tf_op jit(solution)/shard_map/head_fwd/pallas_call | solution.py:332
  319.2 6.7 collective-permute-done.33
  354.8 8.8 %layer_bwd.10 = (bf16[192,1024]{1,0:T(8,128)(2,1)S(1)}, f32[3,1024]{1,0:T(4,128)S(1)}, bf16[4,192,1024]{2,1,0:T(8,128)(2,1)}, bf16[4,192,4096]{2,1,0:T(8,128)(2,...) custom-call(s32[8,3]{1,0:T(8,128)S(1)} %add_add_fusion.3.info, ...), custom_call_target="tpu_custom_call", output_to_operand_aliasing={{2}: (18, {}), {3}: (19, {}), {4}: (20, {}), {5}: (21, {}),... | custom-call | flops 4831838208 | bytes 33554432 | tf_op jit(solution)/shard_map/layer_bwd/pallas_call | solution.py:261
  367.9 36.2 %collective-permute-done.40.g_in = bf16[192,1024]{1,0:T(8,128)(2,1)S(1)} collective-permute-done((bf16[192,1024]{1,0:T(8,128)(2,1)S(1)}, bf16[192,1024]{1,0:T(8,128)(2,1)S(1)}, u32[]{:S(2)}, u32[]{:S(2)}) %collective-permute-start.40) | collective-permute-done | bytes 393248 | tf_op jit(solution)/shard_map/ppermute | solution.py:712
  404.2 16.6 %layer_bwd.12 = (bf16[192,1024]{1,0:T(8,128)(2,1)S(1)}, f32[3,1024]{1,0:T(4,128)S(1)}, bf16[4,192,1024]{2,1,0:T(8,128)(2,1)}, bf16[4,192,4096]{2,1,0:T(8,128)(2,...) custom-call(s32[8,3]{1,0:T(8,128)S(1)} %add_add_fusion.3.info, ...), custom_call_target="tpu_custom_call", output_to_operand_aliasing={{2}: (18, {}), {3}: (19, {}), {4}: (20, {}), {5}: (21, {}),... | custom-call | flops 4831838208 | bytes 33554432 | tf_op jit(solution)/shard_map/layer_bwd/pallas_call | solution.py:261
  422.8 10.3 %collective-permute-done.42.g_in = bf16[192,1024]{1,0:T(8,128)(2,1)S(1)} collective-permute-done((bf16[192,1024]{1,0:T(8,128)(2,1)S(1)}, bf16[192,1024]{1,0:T(8,128)(2,1)S(1)}, u32[]{:S(2)}, u32[]{:S(2)}) %collective-permute-start.42) | collective-permute-done | bytes 393248 | tf_op jit(solution)/shard_map/ppermute | solution.py:712
  433.2 16.0 %layer_bwd.13 = (bf16[192,1024]{1,0:T(8,128)(2,1)S(1)}, f32[3,1024]{1,0:T(4,128)S(1)}, bf16[4,192,1024]{2,1,0:T(8,128)(2,1)}, bf16[4,192,4096]{2,1,0:T(8,128)(2,...) custom-call(s32[8,3]{1,0:T(8,128)S(1)} %add_add_fusion.3.info, ...), custom_call_target="tpu_custom_call", output_to_operand_aliasing={{2}: (18, {}), {3}: (19, {}), {4}: (20, {}), {5}: (21, {}),... | custom-call | flops 4831838208 | bytes 33554432 | tf_op jit(solution)/shard_map/layer_bwd/pallas_call | solution.py:261
  457.3 16.7 %layer_bwd.14 = (bf16[192,1024]{1,0:T(8,128)(2,1)S(1)}, f32[3,1024]{1,0:T(4,128)S(1)}, bf16[4,192,1024]{2,1,0:T(8,128)(2,1)}, bf16[4,192,4096]{2,1,0:T(8,128)(2,...) custom-call(s32[8,3]{1,0:T(8,128)S(1)} %add_add_fusion.3.info, ...), custom_call_target="tpu_custom_call", output_to_operand_aliasing={{2}: (18, {}), {3}: (19, {}), {4}: (20, {}), {5}: (21, {}),... | custom-call | flops 4831838208 | bytes 33554432 | tf_op jit(solution)/shard_map/layer_bwd/pallas_call | solution.py:261
  475.3 3.4 collective-permute-start.36
  480.8 17.3 %layer_bwd.15 = (bf16[192,1024]{1,0:T(8,128)(2,1)}, f32[3,1024]{1,0:T(4,128)S(1)}, bf16[4,192,1024]{2,1,0:T(8,128)(2,1)}, bf16[4,192,4096]{2,1,0:T(8,128)(2,1)},...) custom-call(s32[8,3]{1,0:T(8,128)S(1)} %add_add_fusion.3.info, ...), custom_call_target="tpu_custom_call", output_to_operand_aliasing={{2}: (18, {}), {3}: (19, {}), {4}: (20, {}), {5}: (21, {}),... | custom-call | flops 4831838208 | bytes 33554432 | tf_op jit(solution)/shard_map/layer_bwd/pallas_call | solution.py:261
  499.6 6.1 product.10
  510.6 7.6 product.11
  525.9 16.0 %collective-permute-done.48 = bf16[2,2,128,1024]{3,2,1,0:T(8,128)(2,1)} collective-permute-done((bf16[2,2,128,1024]{3,2,1,0:T(8,128)(2,1)}, bf16[2,2,128,1024]{3,2,1,0:T(8,128)(2,1)}, u32[]{:S(2)}, u32[]{:S(2)}) %collective-permute-start.48) | collective-permute-done | bytes 1048608 | tf_op jit(solution)/shard_map/ppermute | solution.py:545
  564.2 6.5 product.18
  572.8 5.5 product.19
  581.0 12.4 %collective-permute-done.47 = bf16[2,2,512,1024]{3,2,1,0:T(8,128)(2,1)} collective-permute-done((bf16[2,2,512,1024]{3,2,1,0:T(8,128)(2,1)}, bf16[2,2,512,1024]{3,2,1,0:T(8,128)(2,1)}, u32[]{:S(2)}, u32[]{:S(2)}) %collective-permute-start.47) | collective-permute-done | bytes 4194336 | tf_op jit(solution)/shard_map/ppermute | solution.py:545
  603.6 9.1 %collective-permute-done.51 = bf16[768,256]{1,0:T(8,128)(2,1)S(1)} collective-permute-done((bf16[768,256]{1,0:T(8,128)(2,1)S(1)}, bf16[768,256]{1,0:T(8,128)(2,1)S(1)}, u32[]{:S(2)}, u32[]{:S(2)}) %collective-permute-start.51) | collective-permute-done | bytes 393248 | tf_op jit(solution)/shard_map/ppermute | solution.py:574
  613.8 11.7 %head_bwd.1 = bf16[8000,256]{1,0:T(8,128)(2,1)S(1)} custom-call(bf16[8000,256]{1,0:T(8,128)(2,1)S(1)} %bitcast.485, bf16[768,256]{1,0:T(8,128)(2,1)S(1)} %copy-done.32, f32[1,768]{1,0:T(1,128)S(1)} %copy-done.80, f32[1,768]{1,0:T(1,128)S(1)} %mul.435.weight, s32[1,768]{1,0:T(1,128)S(1)} %sub.183.ids, bf16[768,256]{1,0:T(8,128)(2,1)S(1)} %get-tuple-element.378.terms, ...), custom_call_target="tpu_custom_call" | custom-call | flops 1 | bytes 1 | tf_op jit(solution)/shard_map/head_bwd/pallas_call | solution.py:357
  627.4 3.7 fusion.15
  636.5 6.2 collective-permute-done.55
  645.7 37.7 %collective-permute-done.59 = bf16[2,2,128,4096]{3,2,1,0:T(8,128)(2,1)} collective-permute-done((bf16[2,2,128,4096]{3,2,1,0:T(8,128)(2,1)}, bf16[2,2,128,4096]{3,2,1,0:T(8,128)(2,1)}, u32[]{:S(2)}, u32[]{:S(2)}) %collective-permute-start.59) | collective-permute-done | bytes 4194336 | tf_op jit(solution)/shard_map/ppermute | solution.py:545
  683.5 3.8 fusion.7
  703.8 33.7 %collective-permute-done.58 = bf16[512,1024]{1,0:T(8,128)(2,1)} collective-permute-done((bf16[512,1024]{1,0:T(8,128)(2,1)}, bf16[512,1024]{1,0:T(8,128)(2,1)}, u32[]{:S(2)}, u32[]{:S(2)}) %collective-permute-start.58) | collective-permute-done | bytes 1048608 | tf_op jit(solution)/shard_map/ppermute | solution.py:463
  746.7 14.4 %collective-permute-start.62 = (bf16[2,48,1024]{2,1,0:T(8,128)(2,1)S(1)}, bf16[2,48,1024]{2,1,0:T(8,128)(2,1)S(1)}, u32[]{:S(2)}, u32[]{:S(2)}) collective-permute-start(bf16[2,48,1024]{2,1,0:T(8,128)(2,1)S(1)} %fusion.59), channel_id=1, source_target_pairs={{0,4},{1,5},{2,6},{3,7},{4,0},{5,1},{6,2},{7,3},{8,12},{9,13},{10,... | collective-permute-start | bytes 589832 | tf_op jit(solution)/shard_map/ppermute | solution.py:463
  770.3 5.6 collective-permute-done.62
  783.3 15.4 %collective-permute-done.60 = bf16[2,128,1536]{2,1,0:T(8,128)(2,1)S(1)} collective-permute-done((bf16[2,128,1536]{2,1,0:T(8,128)(2,1)S(1)}, bf16[2,128,1536]{2,1,0:T(8,128)(2,1)S(1)}, u32[]{:S(2)}, u32[]{:S(2)}) %collective-permute-start.60) | collective-permute-done | bytes 786464 | tf_op jit(solution)/shard_map/ppermute | solution.py:463
  805.9 20.8 %collective-permute-done.69 = bf16[2,128,1536]{2,1,0:T(8,128)(2,1)S(1)} collective-permute-done((bf16[2,128,1536]{2,1,0:T(8,128)(2,1)S(1)}, bf16[2,128,1536]{2,1,0:T(8,128)(2,1)S(1)}, u32[]{:S(2)}, u32[]{:S(2)}) %collective-permute-start.69) | collective-permute-done | bytes 786464 | tf_op jit(solution)/shard_map/ppermute | solution.py:463
  829.1 4.0 collective-permute-start.71
  843.7 7.3 collective-permute-done.64
  857.9 8.3 collective-permute-done.70
  (656 shorter events, 246.4 us)
Async XLA Ops:
  1.4 59.6 %collective-permute-start.3 = (s32[2,4,48]{2,1,0:T(4,128)S(1)}, s32[2,4,48]{2,1,0:T(4,128)S(1)}, u32[]{:S(2)}, u32[]{:S(2)}) collective-permute-start(s32[2,4,48]{2,1,0:T(4,128)S(1)} %get-tuple-element.409), channel_id=1, source_target_pairs={{0,8},{8,0},{16,24},{24,16},{1,9},{9,1},{17,25},{25,17},{2,10},{10... | collective-permute-start | bytes 4616 | tf_op jit(solution)/shard_map/ppermute | solution.py:404
  5.1 27.5 %collective-permute-start = (bf16[1000,256]{1,0:T(8,128)(2,1)S(1)}, bf16[1000,256]{1,0:T(8,128)(2,1)S(1)}, u32[]{:S(2)}, u32[]{:S(2)}) collective-permute-start(bf16[1000,256]{1,0:T(8,128)(2,1)S(1)} %fusion.27), channel_id=1, source_target_pairs={{0,4},{1,5},{2,6},{3,7},{4,0},{5,1},{6,2},{7,3},{8,12},{9,13},{10,... | collective-permute-start | bytes 1536008 | tf_op jit(solution)/shard_map/ppermute | solution.py:404
  8.7 56.2 %collective-permute-start.9 = (bf16[8,1024]{1,0:T(8,128)(2,1)}, bf16[8,1024]{1,0:T(8,128)(2,1)S(1)}, u32[]{:S(2)}, u32[]{:S(2)}) collective-permute-start(bf16[8,1024]{1,0:T(8,128)(2,1)} %param.30), channel_id=1, source_target_pairs={{0,4},{1,5},{2,6},{3,7},{4,0},{5,1},{6,2},{7,3},{8,12},{9,13},{10,... | collective-permute-start | bytes 49160 | tf_op jit(solution)/shard_map/ppermute | solution.py:404
  32.7 24.4 %collective-permute-start.1 = (bf16[2,1000,256]{2,1,0:T(8,128)(2,1)S(1)}, bf16[2,1000,256]{2,1,0:T(8,128)(2,1)S(1)}, u32[]{:S(2)}, u32[]{:S(2)}) collective-permute-start(bf16[2,1000,256]{2,1,0:T(8,128)(2,1)S(1)} %maximum_select_fusion.4), channel_id=1, source_target_pairs={{0,2},{1,3},{2,0},{3,1},{4,6},{5,7},{6,4},{7,5},{8,10},{9,11},{10,... | collective-permute-start | bytes 3072008 | tf_op jit(solution)/shard_map/ppermute | solution.py:404
  58.7 46.4 %collective-permute-start.2 = (bf16[2,2,1000,256]{3,2,0,1:T(8,128)(2,1)}, bf16[2,2,1000,256]{3,2,0,1:T(8,128)(2,1)}, u32[]{:S(2)}, u32[]{:S(2)}) collective-permute-start(bf16[2,2,1000,256]{3,2,0,1:T(8,128)(2,1)} %maximum_select_fusion.2), channel_id=1, source_target_pairs={{0,1},{1,0},{2,3},{3,2},{4,5},{5,4},{6,7},{7,6},{8,9},{9,8},{10,11... | collective-permute-start | bytes 6144008 | tf_op jit(solution)/shard_map/ppermute | solution.py:404
  68.9 49.7 %collective-permute-start.11 = (bf16[2,2,8,1024]{3,2,1,0:T(8,128)(2,1)S(1)}, bf16[2,2,8,1024]{3,2,1,0:T(8,128)(2,1)S(1)}, u32[]{:S(2)}, u32[]{:S(2)}) collective-permute-start(bf16[2,2,8,1024]{3,2,1,0:T(8,128)(2,1)S(1)} %maximum_select_fusion.15), channel_id=1, source_target_pairs={{0,1},{1,0},{2,3},{3,2},{4,5},{5,4},{6,7},{7,6},{8,9},{9,8},{10,11... | collective-permute-start | bytes 196616 | tf_op jit(solution)/shard_map/ppermute | solution.py:404
  117.5 5.7 collective-permute-start.5
  123.4 9.2 %collective-permute-start.13 = (bf16[2,8,8,1024]{3,2,1,0:T(8,128)(2,1)S(1)}, bf16[2,8,8,1024]{3,2,1,0:T(8,128)(2,1)S(1)}, u32[]{:S(2)}, u32[]{:S(2)}) collective-permute-start(bf16[2,8,8,1024]{3,2,1,0:T(8,128)(2,1)S(1)} %maximum_select_fusion.9), channel_id=1, source_target_pairs={{0,16},{8,24},{16,0},{24,8},{1,17},{9,25},{17,1},{25,9},{2,18},{10... | collective-permute-start | bytes 786440 | tf_op jit(solution)/shard_map/ppermute | solution.py:404
  126.8 9.6 %collective-permute-start.8 = (bf16[2,4,48,256]{3,2,1,0:T(8,128)(2,1)S(1)}, bf16[2,4,48,256]{3,2,1,0:T(8,128)(2,1)S(1)}, u32[]{:S(2)}, u32[]{:S(2)}) collective-permute-start(bf16[2,4,48,256]{3,2,1,0:T(8,128)(2,1)S(1)} %maximum_select_fusion.11), channel_id=1, source_target_pairs={{0,16},{8,24},{16,0},{24,8},{1,17},{9,25},{17,1},{25,9},{2,18},{10... | collective-permute-start | bytes 589832 | tf_op jit(solution)/shard_map/ppermute | solution.py:404
  170.7 18.0 %collective-permute-start.17 = (bf16[192,1024]{1,0:T(8,128)(2,1)S(1)}, bf16[192,1024]{1,0:T(8,128)(2,1)S(1)}, u32[]{:S(2)}, u32[]{:S(2)}) collective-permute-start(bf16[192,1024]{1,0:T(8,128)(2,1)S(1)} %get-tuple-element.209), channel_id=1, source_target_pairs={{8,16},{9,17},{10,18},{11,19},{12,20},{13,21},{14,22},{15,23}} | collective-permute-start | bytes 1179656 | tf_op jit(solution)/shard_map/ppermute | solution.py:670
  188.1 17.1 %collective-permute-start.19 = (bf16[192,1024]{1,0:T(8,128)(2,1)S(1)}, bf16[192,1024]{1,0:T(8,128)(2,1)S(1)}, u32[]{:S(2)}, u32[]{:S(2)}) collective-permute-start(bf16[192,1024]{1,0:T(8,128)(2,1)S(1)} %get-tuple-element.219), channel_id=1, source_target_pairs={{8,16},{9,17},{10,18},{11,19},{12,20},{13,21},{14,22},{15,23}} | collective-permute-start | bytes 1179656 | tf_op jit(solution)/shard_map/ppermute | solution.py:670
  204.4 11.7 %collective-permute-start.21 = (bf16[192,1024]{1,0:T(8,128)(2,1)S(1)}, bf16[192,1024]{1,0:T(8,128)(2,1)S(1)}, u32[]{:S(2)}, u32[]{:S(2)}) collective-permute-start(bf16[192,1024]{1,0:T(8,128)(2,1)S(1)} %get-tuple-element.229), channel_id=1, source_target_pairs={{8,16},{9,17},{10,18},{11,19},{12,20},{13,21},{14,22},{15,23}} | collective-permute-start | bytes 1179656 | tf_op jit(solution)/shard_map/ppermute | solution.py:670
  249.5 30.2 %collective-permute-start.25 = (bf16[768,256]{1,0:T(8,128)(2,1)S(1)}, bf16[768,256]{1,0:T(8,128)(2,1)S(1)}, u32[]{:S(2)}, u32[]{:S(2)}) collective-permute-start(bf16[768,256]{1,0:T(8,128)(2,1)S(1)} %fusion.24), channel_id=1, source_target_pairs={{24,16},{25,17},{26,18},{27,19},{28,20},{29,21},{30,22},{31,23}} | collective-permute-start | bytes 1179656 | tf_op jit(solution)/shard_map/ppermute | solution.py:574
  250.2 7.9 collective-permute-start.29
  258.2 27.2 %collective-permute-start.30 = (bf16[2,4,48,256]{3,2,1,0:T(8,128)(2,1)S(1)}, bf16[2,4,48,256]{3,2,1,0:T(8,128)(2,1)S(1)}, u32[]{:S(2)}, u32[]{:S(2)}) collective-permute-start(bf16[2,4,48,256]{3,2,1,0:T(8,128)(2,1)S(1)} %maximum_select_fusion.13), channel_id=1, source_target_pairs={{0,16},{8,24},{16,0},{24,8},{1,17},{9,25},{17,1},{25,9},{2,18},{10... | collective-permute-start | bytes 589832 | tf_op jit(solution)/shard_map/ppermute | solution.py:404
  279.7 13.5 %collective-permute-start.26 = (bf16[768,256]{1,0:T(8,128)(2,1)S(1)}, bf16[768,256]{1,0:T(8,128)(2,1)S(1)}, u32[]{:S(2)}, u32[]{:S(2)}) collective-permute-start(bf16[768,256]{1,0:T(8,128)(2,1)S(1)} %broadcast_select_fusion.1), channel_id=1, source_target_pairs={{24,8},{16,0},{25,9},{17,1},{26,10},{18,2},{27,11},{19,3},{28,12},... | collective-permute-start | bytes 1179656 | tf_op jit(solution)/shard_map/ppermute | solution.py:574
  314.7 11.2 %collective-permute-start.33 = (bf16[256,768]{0,1:T(8,128)(2,1)S(1)}, bf16[256,768]{0,1:T(8,128)(2,1)S(1)}, u32[]{:S(2)}, u32[]{:S(2)}) collective-permute-start(bf16[256,768]{0,1:T(8,128)(2,1)S(1)} %add_convert_fusion.7), channel_id=1, source_target_pairs={{0,16},{8,24},{16,0},{24,8},{1,17},{9,25},{17,1},{25,9},{2,18},{10... | collective-permute-start | bytes 1179656 | tf_op jit(solution)/shard_map/ppermute | solution.py:404
  344.5 20.5 %collective-permute-start.39 = (bf16[192,1024]{1,0:T(8,128)(2,1)}, bf16[192,1024]{1,0:T(8,128)(2,1)S(1)}, u32[]{:S(2)}, u32[]{:S(2)}) collective-permute-start(bf16[192,1024]{1,0:T(8,128)(2,1)} %get-tuple-element.298), channel_id=1, source_target_pairs={{16,8},{17,9},{18,10},{19,11},{20,12},{21,13},{22,14},{23,15}} | collective-permute-start | bytes 1179656 | tf_op jit(solution)/shard_map/ppermute | solution.py:714
  365.9 38.3 %collective-permute-start.40 = (bf16[192,1024]{1,0:T(8,128)(2,1)S(1)}, bf16[192,1024]{1,0:T(8,128)(2,1)S(1)}, u32[]{:S(2)}, u32[]{:S(2)}) collective-permute-start(bf16[192,1024]{1,0:T(8,128)(2,1)S(1)} %get-tuple-element.311), channel_id=1, source_target_pairs={{8,0},{24,16},{9,1},{25,17},{10,2},{26,18},{11,3},{27,19},{12,4},{... | collective-permute-start | bytes 1179656 | tf_op jit(solution)/shard_map/ppermute | solution.py:712
  367.2 55.6 %collective-permute-start.43 = (bf16[192,1024]{1,0:T(8,128)(2,1)S(1)}, bf16[192,1024]{1,0:T(8,128)(2,1)S(1)}, u32[]{:S(2)}, u32[]{:S(2)}) collective-permute-start(bf16[192,1024]{1,0:T(8,128)(2,1)S(1)} %get-tuple-element.311), channel_id=1, source_target_pairs={{16,8},{17,9},{18,10},{19,11},{20,12},{21,13},{22,14},{23,15}} | collective-permute-start | bytes 1179656 | tf_op jit(solution)/shard_map/ppermute | solution.py:714
  420.8 12.4 %collective-permute-start.42 = (bf16[192,1024]{1,0:T(8,128)(2,1)S(1)}, bf16[192,1024]{1,0:T(8,128)(2,1)S(1)}, u32[]{:S(2)}, u32[]{:S(2)}) collective-permute-start(bf16[192,1024]{1,0:T(8,128)(2,1)S(1)} %get-tuple-element.317), channel_id=1, source_target_pairs={{8,0},{9,1},{10,2},{11,3},{12,4},{13,5},{14,6},{15,7}} | collective-permute-start | bytes 1179656 | tf_op jit(solution)/shard_map/ppermute | solution.py:712
  422.1 35.2 %collective-permute-start.45 = (bf16[192,1024]{1,0:T(8,128)(2,1)S(1)}, bf16[192,1024]{1,0:T(8,128)(2,1)S(1)}, u32[]{:S(2)}, u32[]{:S(2)}) collective-permute-start(bf16[192,1024]{1,0:T(8,128)(2,1)S(1)} %get-tuple-element.317), channel_id=1, source_target_pairs={{16,8},{17,9},{18,10},{19,11},{20,12},{21,13},{22,14},{23,15}} | collective-permute-start | bytes 1179656 | tf_op jit(solution)/shard_map/ppermute | solution.py:714
  449.2 8.1 collective-permute-start.44
  454.3 21.0 %collective-permute-start.34 = (f32[3]{0:T(128)S(1)}, f32[3]{0:T(128)S(1)}, u32[]{:S(2)}, u32[]{:S(2)}) collective-permute-start(f32[3]{0:T(128)S(1)} %add_add_fusion.6), channel_id=1, source_target_pairs={{0,2},{1,3},{2,0},{3,1},{4,6},{5,7},{6,4},{7,5},{8,10},{9,11},{10,... | collective-permute-start | bytes 44 | tf_op jit(solution)/shard_map/ppermute | solution.py:404
  474.0 6.8 collective-permute-start.46
  505.6 87.7 %collective-permute-start.47 = (bf16[2,2,512,1024]{3,2,1,0:T(8,128)(2,1)}, bf16[2,2,512,1024]{3,2,1,0:T(8,128)(2,1)}, u32[]{:S(2)}, u32[]{:S(2)}) collective-permute-start(bf16[2,2,512,1024]{3,2,1,0:T(8,128)(2,1)} %bitcast.88), channel_id=1, source_target_pairs={{0,1},{1,0},{2,3},{3,2},{4,5},{5,4},{6,7},{7,6},{8,9},{9,8},{10,11... | collective-permute-start | bytes 12582920 | tf_op jit(solution)/shard_map/ppermute | solution.py:545
  521.2 20.7 %collective-permute-start.48 = (bf16[2,2,128,1024]{3,2,1,0:T(8,128)(2,1)}, bf16[2,2,128,1024]{3,2,1,0:T(8,128)(2,1)}, u32[]{:S(2)}, u32[]{:S(2)}) collective-permute-start(bf16[2,2,128,1024]{3,2,1,0:T(8,128)(2,1)} %bitcast.90), channel_id=1, source_target_pairs={{0,2},{1,3},{2,0},{3,1},{4,6},{5,7},{6,4},{7,5},{8,10},{9,11},{10,... | collective-permute-start | bytes 3145736 | tf_op jit(solution)/shard_map/ppermute | solution.py:545
  543.2 35.1 %collective-permute-start.49 = (bf16[2,128,1024]{2,1,0:T(8,128)(2,1)S(1)}, bf16[2,128,1024]{2,1,0:T(8,128)(2,1)S(1)}, u32[]{:S(2)}, u32[]{:S(2)}) collective-permute-start(bf16[2,128,1024]{2,1,0:T(8,128)(2,1)S(1)} %fusion.50), channel_id=1, source_target_pairs={{0,4},{1,5},{2,6},{3,7},{4,0},{5,1},{6,2},{7,3},{8,12},{9,13},{10,... | collective-permute-start | bytes 1572872 | tf_op jit(solution)/shard_map/ppermute | solution.py:463
  596.2 31.2 %collective-permute-start.54 = (bf16[2,512,1024]{2,1,0:T(8,128)(2,1)S(1)}, bf16[2,512,1024]{2,1,0:T(8,128)(2,1)S(1)}, u32[]{:S(2)}, u32[]{:S(2)}) collective-permute-start(bf16[2,512,1024]{2,1,0:T(8,128)(2,1)S(1)} %fusion.6.token), channel_id=1, source_target_pairs={{0,2},{1,3},{2,0},{3,1},{4,6},{5,7},{6,4},{7,5},{8,10},{9,11},{10,... | collective-permute-start | bytes 6291464 | tf_op jit(solution)/shard_map/ppermute | solution.py:463
  596.3 87.1 %collective-permute-start.59 = (bf16[2,2,128,4096]{3,2,1,0:T(8,128)(2,1)}, bf16[2,2,128,4096]{3,2,1,0:T(8,128)(2,1)}, u32[]{:S(2)}, u32[]{:S(2)}) collective-permute-start(bf16[2,2,128,4096]{3,2,1,0:T(8,128)(2,1)} %bitcast.138), channel_id=1, source_target_pairs={{0,1},{1,0},{2,3},{3,2},{4,5},{5,4},{6,7},{7,6},{8,9},{9,8},{10,11... | collective-permute-start | bytes 12582920 | tf_op jit(solution)/shard_map/ppermute | solution.py:545
  602.2 10.5 %collective-permute-start.51 = (bf16[768,256]{1,0:T(8,128)(2,1)S(1)}, bf16[768,256]{1,0:T(8,128)(2,1)S(1)}, u32[]{:S(2)}, u32[]{:S(2)}) collective-permute-start(bf16[768,256]{1,0:T(8,128)(2,1)S(1)} %broadcast_select_fusion), channel_id=1, source_target_pairs={{0,16},{8,24},{1,17},{9,25},{2,18},{10,26},{3,19},{11,27},{4,20},{... | collective-permute-start | bytes 1179656 | tf_op jit(solution)/shard_map/ppermute | solution.py:574
  633.8 8.9 %collective-permute-start.55 = (bf16[2,64,1024]{2,1,0:T(8,128)(2,1)S(1)}, bf16[2,64,1024]{2,1,0:T(8,128)(2,1)S(1)}, u32[]{:S(2)}, u32[]{:S(2)}) collective-permute-start(bf16[2,64,1024]{2,1,0:T(8,128)(2,1)S(1)} %dynamic-slice_bitcast_fusion), channel_id=1, source_target_pairs={{0,16},{8,24},{16,0},{24,8},{1,17},{9,25},{17,1},{25,9},{2,18},{10... | collective-permute-start | bytes 786440 | tf_op jit(solution)/shard_map/ppermute | solution.py:404
  687.3 79.5 %collective-permute-start.63 = (bf16[2,128,4096]{2,1,0:T(8,128)(2,1)}, bf16[2,128,4096]{2,1,0:T(8,128)(2,1)}, u32[]{:S(2)}, u32[]{:S(2)}) collective-permute-start(bf16[2,128,4096]{2,1,0:T(8,128)(2,1)} %fusion.7), channel_id=1, source_target_pairs={{0,2},{1,3},{2,0},{3,1},{4,6},{5,7},{6,4},{7,5},{8,10},{9,11},{10,... | collective-permute-start | bytes 6291464 | tf_op jit(solution)/shard_map/ppermute | solution.py:463
  687.3 74.5 %collective-permute-start.53 = (bf16[2,2,128,1536]{3,2,1,0:T(8,128)(2,1)S(1)}, bf16[2,2,128,1536]{3,2,1,0:T(8,128)(2,1)}, u32[]{:S(2)}, u32[]{:S(2)}) collective-permute-start(bf16[2,2,128,1536]{3,2,1,0:T(8,128)(2,1)S(1)} %bitcast.502), channel_id=1, source_target_pairs={{0,1},{1,0},{2,3},{3,2},{4,5},{5,4},{6,7},{7,6},{8,9},{9,8},{10,11... | collective-permute-start | bytes 4718600 | tf_op jit(solution)/shard_map/ppermute | solution.py:545
  688.5 49.1 %collective-permute-start.58 = (bf16[512,1024]{1,0:T(8,128)(2,1)}, bf16[512,1024]{1,0:T(8,128)(2,1)}, u32[]{:S(2)}, u32[]{:S(2)}) collective-permute-start(bf16[512,1024]{1,0:T(8,128)(2,1)} %fusion.15), channel_id=1, source_target_pairs={{0,4},{1,5},{2,6},{3,7},{4,0},{5,1},{6,2},{7,3},{8,12},{9,13},{10,... | collective-permute-start | bytes 3145736 | tf_op jit(solution)/shard_map/ppermute | solution.py:463
  691.2 86.8 %collective-permute-start.61 = (bf16[2,2,128,1536]{3,2,1,0:T(8,128)(2,1)S(1)}, bf16[2,2,128,1536]{3,2,1,0:T(8,128)(2,1)}, u32[]{:S(2)}, u32[]{:S(2)}) collective-permute-start(bf16[2,2,128,1536]{3,2,1,0:T(8,128)(2,1)S(1)} %bitcast.501), channel_id=1, source_target_pairs={{0,1},{1,0},{2,3},{3,2},{4,5},{5,4},{6,7},{7,6},{8,9},{9,8},{10,11... | collective-permute-start | bytes 4718600 | tf_op jit(solution)/shard_map/ppermute | solution.py:545
  699.0 46.1 %collective-permute-start.57 = (bf16[2,2,48,1024]{3,2,1,0:T(8,128)(2,1)S(1)}, bf16[2,2,48,1024]{3,2,1,0:T(8,128)(2,1)S(1)}, u32[]{:S(2)}, u32[]{:S(2)}) collective-permute-start(bf16[2,2,48,1024]{3,2,1,0:T(8,128)(2,1)S(1)} %fusion.57), channel_id=1, source_target_pairs={{0,2},{1,3},{2,0},{3,1},{4,6},{5,7},{6,4},{7,5},{8,10},{9,11},{10,... | collective-permute-start | bytes 1179656 | tf_op jit(solution)/shard_map/ppermute | solution.py:463
  737.6 65.5 %collective-permute-start.52 = (bf16[2,2,1000,256]{3,2,1,0:T(8,128)(2,1)}, bf16[2,2,1000,256]{3,2,1,0:T(8,128)(2,1)S(1)}, u32[]{:S(2)}, u32[]{:S(2)}) collective-permute-start(bf16[2,2,1000,256]{3,2,1,0:T(8,128)(2,1)} %copy-done.105), channel_id=1, source_target_pairs={{0,1},{1,0},{2,3},{3,2},{4,5},{5,4},{6,7},{7,6},{8,9},{9,8},{10,11... | collective-permute-start | bytes 6144008 | tf_op jit(solution)/shard_map/ppermute | solution.py:463
  746.7 29.1 %collective-permute-start.62 = (bf16[2,48,1024]{2,1,0:T(8,128)(2,1)S(1)}, bf16[2,48,1024]{2,1,0:T(8,128)(2,1)S(1)}, u32[]{:S(2)}, u32[]{:S(2)}) collective-permute-start(bf16[2,48,1024]{2,1,0:T(8,128)(2,1)S(1)} %fusion.59), channel_id=1, source_target_pairs={{0,4},{1,5},{2,6},{3,7},{4,0},{5,1},{6,2},{7,3},{8,12},{9,13},{10,... | collective-permute-start | bytes 589832 | tf_op jit(solution)/shard_map/ppermute | solution.py:463
  763.7 35.0 %collective-permute-start.60 = (bf16[2,128,1536]{2,1,0:T(8,128)(2,1)S(1)}, bf16[2,128,1536]{2,1,0:T(8,128)(2,1)S(1)}, u32[]{:S(2)}, u32[]{:S(2)}) collective-permute-start(bf16[2,128,1536]{2,1,0:T(8,128)(2,1)S(1)} %fusion.36), channel_id=1, source_target_pairs={{0,2},{1,3},{2,0},{3,1},{4,6},{5,7},{6,4},{7,5},{8,10},{9,11},{10,... | collective-permute-start | bytes 2359304 | tf_op jit(solution)/shard_map/ppermute | solution.py:463
  769.6 59.5 %collective-permute-start.68 = (bf16[128,4096]{1,0:T(8,128)(2,1)S(1)}, bf16[128,4096]{1,0:T(8,128)(2,1)S(1)}, u32[]{:S(2)}, u32[]{:S(2)}) collective-permute-start(bf16[128,4096]{1,0:T(8,128)(2,1)S(1)} %fusion.11), channel_id=1, source_target_pairs={{0,4},{1,5},{2,6},{3,7},{4,0},{5,1},{6,2},{7,3},{8,12},{9,13},{10,... | collective-permute-start | bytes 3145736 | tf_op jit(solution)/shard_map/ppermute | solution.py:463
  779.5 47.2 %collective-permute-start.69 = (bf16[2,128,1536]{2,1,0:T(8,128)(2,1)S(1)}, bf16[2,128,1536]{2,1,0:T(8,128)(2,1)S(1)}, u32[]{:S(2)}, u32[]{:S(2)}) collective-permute-start(bf16[2,128,1536]{2,1,0:T(8,128)(2,1)S(1)} %fusion.37), channel_id=1, source_target_pairs={{0,2},{1,3},{2,0},{3,1},{4,6},{5,7},{6,4},{7,5},{8,10},{9,11},{10,... | collective-permute-start | bytes 2359304 | tf_op jit(solution)/shard_map/ppermute | solution.py:463
  780.1 56.5 %collective-permute-start.67 = (bf16[128,1024]{1,0:T(8,128)(2,1)S(1)}, bf16[128,1024]{1,0:T(8,128)(2,1)S(1)}, u32[]{:S(2)}, u32[]{:S(2)}) collective-permute-start(bf16[128,1024]{1,0:T(8,128)(2,1)S(1)} %copy-done.114), channel_id=1, source_target_pairs={{0,1},{1,0},{2,3},{3,2},{4,5},{5,4},{6,7},{7,6},{8,9},{9,8},{10,11... | collective-permute-start | bytes 786440 | tf_op jit(solution)/shard_map/ppermute | solution.py:463
  800.4 40.8 %collective-permute-start.65 = (bf16[128,1536]{1,0:T(8,128)(2,1)S(1)}, bf16[128,1536]{1,0:T(8,128)(2,1)S(1)}, u32[]{:S(2)}, u32[]{:S(2)}) collective-permute-start(bf16[128,1536]{1,0:T(8,128)(2,1)S(1)} %fusion.45), channel_id=1, source_target_pairs={{0,4},{1,5},{2,6},{3,7},{4,0},{5,1},{6,2},{7,3},{8,12},{9,13},{10,... | collective-permute-start | bytes 1179656 | tf_op jit(solution)/shard_map/ppermute | solution.py:463
  803.0 36.0 %collective-permute-start.66 = (bf16[48,1024]{1,0:T(8,128)(2,1)S(1)}, bf16[48,1024]{1,0:T(8,128)(2,1)S(1)}, u32[]{:S(2)}, u32[]{:S(2)}) collective-permute-start(bf16[48,1024]{1,0:T(8,128)(2,1)S(1)} %fusion.65), channel_id=1, source_target_pairs={{0,1},{1,0},{2,3},{3,2},{4,5},{5,4},{6,7},{7,6},{8,9},{9,8},{10,11... | collective-permute-start | bytes 294920 | tf_op jit(solution)/shard_map/ppermute | solution.py:463
  826.7 24.2 %collective-permute-start.64 = (bf16[2,1000,256]{2,1,0:T(8,128)(2,1)S(1)}, bf16[2,1000,256]{2,1,0:T(8,128)(2,1)S(1)}, u32[]{:S(2)}, u32[]{:S(2)}) collective-permute-start(bf16[2,1000,256]{2,1,0:T(8,128)(2,1)S(1)} %fusion.18), channel_id=1, source_target_pairs={{0,2},{1,3},{2,0},{3,1},{4,6},{5,7},{6,4},{7,5},{8,10},{9,11},{10,... | collective-permute-start | bytes 3072008 | tf_op jit(solution)/shard_map/ppermute | solution.py:463
  829.1 25.1 %collective-permute-start.71 = (bf16[128,1536]{1,0:T(8,128)(2,1)S(1)}, bf16[128,1536]{1,0:T(8,128)(2,1)S(1)}, u32[]{:S(2)}, u32[]{:S(2)}) collective-permute-start(bf16[128,1536]{1,0:T(8,128)(2,1)S(1)} %fusion.41), channel_id=1, source_target_pairs={{0,4},{1,5},{2,6},{3,7},{4,0},{5,1},{6,2},{7,3},{8,12},{9,13},{10,... | collective-permute-start | bytes 1179656 | tf_op jit(solution)/shard_map/ppermute | solution.py:463
  851.7 14.4 %collective-permute-start.70 = (bf16[1000,256]{1,0:T(8,128)(2,1)S(1)}, bf16[1000,256]{1,0:T(8,128)(2,1)S(1)}, u32[]{:S(2)}, u32[]{:S(2)}) collective-permute-start(bf16[1000,256]{1,0:T(8,128)(2,1)S(1)} %fusion.30), channel_id=1, source_target_pairs={{0,4},{1,5},{2,6},{3,7},{4,0},{5,1},{6,2},{7,3},{8,12},{9,13},{10,... | collective-permute-start | bytes 1536008 | tf_op jit(solution)/shard_map/ppermute | solution.py:463
  (185 other events, 2309.1 us)

commit v3 on v2

--- a/solution.py
+++ b/solution.py
@@ -16,7 +16,8 @@
 SCORE_SCALE=0.125
 DEPTH=3
 F32=jnp.float32; BF=jnp.bfloat16
-VMEM_LIMIT=34*1024*1024
+VMEM_LIMIT=26*1024*1024
+HEAD_LIMIT=16*1024*1024
 GELU_A=math.sqrt(2.0/math.pi); GELU_B=0.044715
 
 def dot(a,b): return jnp.dot(a,b,preferred_element_type=F32)
@@ -61,9 +62,9 @@
         @pl.when(source==1)
         def _(): b_hid[...]=hid_in[...]
         @pl.when(source==2)
-        def _(): b_hid[...]=far_in[...]
+        def _(): pltpu.make_async_copy(far_in,b_hid,hsem).start()
         outs=Puts(osem)
-        @pl.when(source==0)
+        @pl.when(source!=1)
         def _(): src_copy.wait()
         outs.add(b_hid,o_hid.at[slot])
         first=b_hid[...].astype(F32)+time_rows[pl.ds(slot,1),:]
@@ -145,7 +146,7 @@
              V(T,width),V(nw,T,width),V(nw,T,width),
              pltpu.SemaphoreType.DMA,pltpu.SemaphoreType.DMA((7+2*nw,))]
     out=pl.pallas_call(functools.partial(fwd_kernel,tick),
-        in_specs=[SM,VM,VM,HB,VM,VM,VM,VM,VM,VM,VM,VM,VM]+[HB]*9,
+        in_specs=[SM,VM,HB,HB,VM,VM,VM,VM,VM,VM,VM,VM,VM]+[HB]*9,
         out_specs=[VM,VM]+[HB]*9,
         out_shape=[jax.ShapeDtypeStruct((T,width),BF),jax.ShapeDtypeStruct((3,width),F32)]+[pltpu.HBM(s.shape,s.dtype) for s in store_shapes(micro,T,width,hidden)],
         input_output_aliases={13+i:2+i for i in range(9)},
@@ -153,7 +154,7 @@
         compiler_params=pltpu.CompilerParams(vmem_limit_bytes=LAYER_LIMIT),
         cost_estimate=pl.CostEstimate(flops=2*T*width*(4*width+2*hidden),bytes_accessed=2*width*(4*width+2*hidden)+8*1024*1024,transcendentals=0),
         name="layer_fwd",
-    )(info,hid,far,in_hbm(entry),time_rows,ga,gm,cos,sin,w_qkv,w_out,w_up,w_down,*map(in_hbm,stores))
+    )(info,hid,in_hbm(far),in_hbm(entry),time_rows,ga,gm,cos,sin,w_qkv,w_out,w_up,w_down,*map(in_hbm,stores))
     return out[0],out[1],out[2:]
 
 def bwd_kernel(tick,info,g_in,far_in,exits,time_rows,gain_attn,gain_mlp,cos,sin,w_qkv,w_out,w_up,w_down,
@@ -173,7 +174,7 @@
         @pl.when(source==1)
         def _(): b_g[...]=g_in[...]
         @pl.when(source==2)
-        def _(): b_g[...]=far_in[...]
+        def _(): pltpu.make_async_copy(far_in,b_g,hsem).start()
         ld=Loads(wsem,DEPTH)
         kg=[]
         for i in range(nw):
@@ -185,7 +186,7 @@
         kh=ld.add(hid.at[slot],b_hid)
         ld.fill(DEPTH)
         outs=Puts(osem)
-        @pl.when(source==0)
+        @pl.when(source!=1)
         def _(): src_copy.wait()
         outs.add(b_g,o_g.at[slot])
         g=b_g[...]
@@ -259,7 +260,7 @@
              V(T,width),V(T,3*width),V(npair,2*T,T),V(T,width),V(nw,T,width),V(nw,T,width),V(T,width),V(T,width),pltpu.VMEM((T,width),F32),V(T,3*width),
              pltpu.SemaphoreType.DMA((4+nw,)),pltpu.SemaphoreType.DMA,pltpu.SemaphoreType.DMA((4+nw,))]
     out=pl.pallas_call(functools.partial(bwd_kernel,tick),
-        in_specs=[SM,VM,VM,HB,VM,VM,VM,VM,VM]+[VM]*4+[HB]*5+[HB]*5,
+        in_specs=[SM,VM,HB,HB,VM,VM,VM,VM,VM]+[VM]*4+[HB]*5+[HB]*5,
         out_specs=[VM,VM]+[HB]*5,
         out_shape=[jax.ShapeDtypeStruct((T,width),BF),jax.ShapeDtypeStruct((3,width),F32)]+[pltpu.HBM(s.shape,s.dtype) for s in grad_shapes(micro,T,width,hidden)],
         input_output_aliases={18+i:2+i for i in range(5)},
@@ -267,7 +268,7 @@
         compiler_params=pltpu.CompilerParams(vmem_limit_bytes=LAYER_LIMIT),
         cost_estimate=pl.CostEstimate(flops=2*T*width*(4*width+2*hidden),bytes_accessed=2*width*(4*width+2*hidden)+8*1024*1024,transcendentals=0),
         name="layer_bwd",
-    )(info,g,far,in_hbm(exits),time_rows,ga,gm,cos,sin,w_qkv,w_out,w_up,w_down,*map(in_hbm,saved),*map(in_hbm,stores))
+    )(info,g,in_hbm(far),in_hbm(exits),time_rows,ga,gm,cos,sin,w_qkv,w_out,w_up,w_down,*map(in_hbm,saved),*map(in_hbm,stores))
     return out[0],out[1],out[2:]
 
 def rope_tables(T,head):
@@ -336,7 +337,7 @@
         out_specs=[pl.BlockSpec((emb, tokens), lambda i: (0, 0)), pl.BlockSpec((2, tokens), lambda i: (0, 0))],
         out_shape=[jax.ShapeDtypeStruct((emb, tokens), BF), jax.ShapeDtypeStruct((2, tokens), F32)],
         scratch_shapes=[pltpu.VMEM((1, tokens), F32), pltpu.VMEM((1, tokens), F32), pltpu.VMEM((emb, tokens), F32)],
-        compiler_params=pltpu.CompilerParams(vmem_limit_bytes=VMEM_LIMIT),
+        compiler_params=pltpu.CompilerParams(vmem_limit_bytes=HEAD_LIMIT),
         cost_estimate=pl.CostEstimate(flops=4 * rows * emb * tokens, bytes_accessed=2 * rows * emb, transcendentals=rows * tokens),
         name="head_fwd",
     )(table, latent)
@@ -368,7 +369,7 @@
         ],
         out_specs=pl.BlockSpec((tile, emb), lambda i: (i, 0)),
         out_shape=jax.ShapeDtypeStruct((rows, emb), BF),
-        compiler_params=pltpu.CompilerParams(vmem_limit_bytes=VMEM_LIMIT),
+        compiler_params=pltpu.CompilerParams(vmem_limit_bytes=HEAD_LIMIT),
         cost_estimate=pl.CostEstimate(flops=1, bytes_accessed=1, transcendentals=0),
         name="head_bwd",
     )(table, latent, log_total, weight, ids, terms, token)
@@ -415,6 +416,26 @@
         held.append(bit)
     size = lax.axis_size(axis)
     return x.reshape((size,) + x.shape[len(order):])
+
+
+def gather_rows(x, axis, order):
+    rows = x.shape[0]
+    piece = -(-rows // 4) // 16 * 16 + 16 if rows >= 512 else rows
+    pieces = [x[i : min(i + piece, rows)] for i in range(0, rows, piece)]
+    index = lax.axis_index(axis)
+    held = []
+    token = None
+    for bit in order:
+        at = sum(1 for b in held if b > bit)
+        mine = (index >> bit) & 1
+        for n, part in enumerate(pieces):
+            other = swap(part, axis, bit)
+            if token is not None:
+                other = after(other, token)
+            token = pieces[n] = jnp.where(mine == 0, jnp.stack([part, other], at), jnp.stack([other, part], at))
+        held.append(bit)
+    pieces = [p.reshape((-1,) + p.shape[len(order) :]) for p in pieces]
+    return jnp.concatenate(pieces, axis=1)
 
 
 def scatter_sum(x, axis, order):
@@ -612,7 +633,6 @@
     emb = table.shape[1]
     last = sections - 1
     count = seq_counts[lax.axis_index("dp")]
-    count_all = jnp.sum(seq_counts).astype(F32)
     valid = (jnp.arange(micro) < count).astype(F32)
     low_first, high_first, mid_first = dp_orders(groups)
     gather_order = low_first[::-1]
@@ -621,30 +641,27 @@
     own_rows, table_back = jax.vjp(rms_scale, table.astype(F32))
     own_low = own_rows.astype(BF)
     own_count = own_low.shape[0]
-    rows_sec = gather(own_low, "dp", gather_order).reshape(groups * own_count, emb)
+    bundle = gather_rows(jnp.concatenate([own_low, proj.reshape(-1, emb)]), "dp", gather_order)
+    rows_sec = bundle[:, :own_count].reshape(groups * own_count, emb)
+    proj_sec = bundle[:, own_count:].reshape(groups * proj.shape[0], width)
     vocab_sec = groups * own_count
-    proj_sec = gather(proj, "dp", gather_order)
     proj_full = gather(proj_sec, "section", section_order).reshape(emb, width)
     both = gather(jnp.stack([token_ids, loss_mask]), "section", section_order)
-    ids_blocks = both[:, 0].reshape(-1) - section * vocab_sec
     both_rows = jnp.transpose(both, (1, 2, 0, 3)).reshape(2, tokens)
+    noise_all = gather(noise, "section", section_order)
+    noise_all = jnp.transpose(noise_all, (1, 0, 2, 3)).reshape(micro, seq_len, emb)
     ids_rows = both_rows[0] - section * vocab_sec
     weight = both_rows[1].astype(F32) * jnp.repeat(valid, seq_len)
-    onehot = (ids_blocks[:, None] == jnp.arange(vocab_sec)[None, :]).astype(BF)
-    partial = dot(onehot, rows_sec).astype(BF).reshape(sections, micro * shard, emb)
-    picked = scatter_sum(partial, "section", section_order[::-1])
+    onehot = (ids_rows[:, None] == jnp.arange(vocab_sec)[None, :]).astype(BF)
+    picked_all = sum_all(dot(onehot, rows_sec).astype(BF), "section")
     sigma = noise_level(time_index)
     shrink = lax.rsqrt(1.0 + sigma * sigma)
-    inputs = (
-        (picked.reshape(micro, shard, emb) + sigma[:, None, None] * noise) * shrink[:, None, None]
-    ).astype(BF)
-    inputs_all = gather(inputs, "section", section_order)
-    inputs_all = jnp.transpose(inputs_all, (1, 0, 2, 3)).reshape(tokens, emb)
+    inputs_all = (
+        (picked_all.astype(F32).reshape(micro, seq_len, emb) + sigma[:, None, None] * noise_all) * shrink[:, None, None]
+    ).astype(BF).reshape(tokens, emb)
     entry = dot(inputs_all, proj_full).astype(BF).reshape(micro, seq_len, width)
-    picked_all = gather(picked.astype(BF).reshape(micro, shard, emb), "section", section_order)
-    picked_all = jnp.transpose(picked_all, (1, 0, 2, 3)).reshape(tokens, emb)
     time_low = time_features(sigma, emb).astype(BF)
-    time_rows = dot(time_low, w_time[0])
+    time_rows = dot(time_low, w_time[0]) + zero_of(weight)
     cosines, sines = rope_tables(seq_len, width // HEADS)
     weights = tuple(pltpu.with_memory_space_constraint(w[0], pltpu.VMEM) for w in (w_qkv, w_out, w_up, w_down))
 
@@ -786,6 +803,7 @@
     target_logit = jnp.sum(latent.astype(F32) * picked_all.astype(F32), axis=1)
     token_loss = (log_total - target_logit) * weight
     seq_loss = jnp.sum(token_loss.reshape(micro, seq_len), axis=1) / seq_len
+    count_all = jnp.sum(after(seq_counts.astype(F32), token))
     layer_rms = jnp.sqrt(square_sums / (count_all * seq_len * width))[None, :]
     packed = pack.total
     w_out_grad = out.total

time: 879 us -> 871 us (level)
  starting transfers between devices: 117 us -> 94.2 us
  waiting for transfers between devices: 343 us -> 359 us
    ppermute x25 -> x29, waiting for transfers between devices: 117 us -> 76.3 us  [swap(): return lax.ppermute(x, axis, pairs)]
    ppermute x4, waiting for transfers between devices: 17.9 us -> 48.9 us  [spread(): got = lax.ppermute(x, axis, pairs)]
    ppermute x21, waiting for transfers between devices: 159 us -> 182 us  [send(): lax.ppermute(sent, 'dp', [(i, i ^ 1 << bit) for i in range(lax.axis_size(...]
    ppermute x25 -> x29, starting transfers between devices: 52.5 us -> 32.6 us  [swap(): return lax.ppermute(x, axis, pairs)]
    unnamed x338 -> x302, local copies, waits for them, and re-layouts: 48.2 us -> 41.7 us
    slice x24 -> x37, local copies, waits for them, and re-layouts: 15.8 us -> 20.9 us  [zero_of(): return jnp.minimum(jnp.abs(token[(0,) * token.ndim].astype(F32)), 0.0)]
  transfers between devices with their start and end apart: 72 -> 76, of which waited for: 36 -> 38; matrix products, arithmetic and copies ran while one was open for 11% -> 10% of each run, Pallas kernels for 17% -> 17%
where the time goes in v3:
time: 871 us; the launch traced here: 864 us
  waiting for transfers between devices  359 us (41%)
  Pallas kernels  227 us (26%)
  starting transfers between devices  94.2 us (11%)
  local copies, waits for them, and re-layouts  71.5 us (8%)
  other arithmetic  70.5 us (8%)
  between operations  28.8 us (3%)
  matrix products  13.1 us (2%)
    ppermute x21, waiting for transfers between devices, send(): lax.ppermute(sent, 'dp', [(i, i ^ 1 << bit) for i in range(lax.axis_size(...  182 us
    pallas_call x8, Pallas kernels, layer_backward(): pl.pallas_call(functools.partial(bwd_kernel, tick), in_specs=[SM, VM, HB,...  79.1 us
    ppermute x29, waiting for transfers between devices, swap(): return lax.ppermute(x, axis, pairs)  76.3 us
    pallas_call x8, Pallas kernels, layer_forward(): pl.pallas_call(functools.partial(fwd_kernel, tick), in_specs=[SM, VM, HB,...  75.8 us
    ppermute x14, waiting for transfers between devices, body(): core_in = lax.ppermute(sent, 'section', core_pairs) if core_pairs else sent  51.9 us
    ppermute x4, waiting for transfers between devices, spread(): got = lax.ppermute(x, axis, pairs)  48.9 us
    pallas_call x10, Pallas kernels, product(): pl.pallas_call(product_kernel, grid_spec=pltpu.PrefetchScalarGridSpec(num...  43.3 us
    unnamed x302, local copies, waits for them, and re-layouts  41.7 us
  transfers between devices with their start and end apart: 76, of which 38 were waited for; matrix products, arithmetic and copies ran while one was open for 10% of the time, Pallas kernels for 17%

profile of v3, /device:TPU:0, one launch (start us, length us, event | category | flops | bytes accessed | tf_op | source)
XLA Modules:
  0.0 863.9 jit_solution(4138307993547084556)
XLA Ops:
  4.0 4.1 collective-permute-start
  20.3 3.6 collective-permute-done
  58.8 6.7 collective-permute-done.9
  67.1 10.4 %collective-permute-done.10 = bf16[2,2,272,256]{3,2,0,1:T(8,128)(2,1)S(1)} collective-permute-done((bf16[2,2,272,256]{3,2,0,1:T(8,128)(2,1)S(1)}, bf16[2,2,272,256]{3,2,0,1:T(8,128)(2,1)S(1)}, u32[]{:S(2)}, u32[]{:S(2)}) %collective-permute-start.10) | collective-permute-done | bytes 557088 | tf_op jit(solution)/shard_map/ppermute | solution.py:405
  79.1 6.8 collective-permute-done.11
  86.9 4.2 fusion.34
  99.8 4.6 collective-permute-done.17
  104.7 5.5 collective-permute-done.19
  111.3 6.8 collective-permute-done.15
  130.0 14.2 %layer_fwd.8 = (bf16[192,1024]{1,0:T(8,128)(2,1)S(1)}, f32[3,1024]{1,0:T(4,128)S(1)}, bf16[4,192,1024]{2,1,0:T(8,128)(2,1)}, bf16[4,192,1024]{2,1,0:T(8,128)(2,1...) custom-call(s32[8,3]{1,0:T(8,128)S(1)} %add_add_fusion.2.info, ...), custom_call_target="tpu_custom_call", output_to_operand_aliasing={{2}: (13, {}), {3}: (14, {}), {4}: (15, {}), {5}: (16, {}),... | custom-call | flops 4831838208 | bytes 33554432 | tf_op jit(solution)/shard_map/layer_fwd/pallas_call | solution.py:148
  146.9 13.7 %layer_fwd.9 = (bf16[192,1024]{1,0:T(8,128)(2,1)S(1)}, f32[3,1024]{1,0:T(4,128)S(1)}, bf16[4,192,1024]{2,1,0:T(8,128)(2,1)}, bf16[4,192,1024]{2,1,0:T(8,128)(2,1...) custom-call(s32[8,3]{1,0:T(8,128)S(1)} %add_add_fusion.2.info, ...), custom_call_target="tpu_custom_call", output_to_operand_aliasing={{2}: (13, {}), {3}: (14, {}), {4}: (15, {}), {5}: (16, {}),... | custom-call | flops 4831838208 | bytes 33554432 | tf_op jit(solution)/shard_map/layer_fwd/pallas_call | solution.py:148
  163.2 14.0 %layer_fwd.10 = (bf16[192,1024]{1,0:T(8,128)(2,1)S(1)}, f32[3,1024]{1,0:T(4,128)S(1)}, bf16[4,192,1024]{2,1,0:T(8,128)(2,1)}, bf16[4,192,1024]{2,1,0:T(8,128)(2,...) custom-call(s32[8,3]{1,0:T(8,128)S(1)} %add_add_fusion.2.info, ...), custom_call_target="tpu_custom_call", output_to_operand_aliasing={{2}: (13, {}), {3}: (14, {}), {4}: (15, {}), {5}: (16, {}),... | custom-call | flops 4831838208 | bytes 33554432 | tf_op jit(solution)/shard_map/layer_fwd/pallas_call | solution.py:148
  180.3 13.7 %layer_fwd.11 = (bf16[192,1024]{1,0:T(8,128)(2,1)S(1)}, f32[3,1024]{1,0:T(4,128)S(1)}, bf16[4,192,1024]{2,1,0:T(8,128)(2,1)}, bf16[4,192,1024]{2,1,0:T(8,128)(2,...) custom-call(s32[8,3]{1,0:T(8,128)S(1)} %add_add_fusion.2.info, ...), custom_call_target="tpu_custom_call", output_to_operand_aliasing={{2}: (13, {}), {3}: (14, {}), {4}: (15, {}), {5}: (16, {}),... | custom-call | flops 4831838208 | bytes 33554432 | tf_op jit(solution)/shard_map/layer_fwd/pallas_call | solution.py:148
  196.8 8.2 layer_fwd.12
  209.4 10.6 %layer_fwd.14 = (bf16[192,1024]{1,0:T(8,128)(2,1)S(1)}, f32[3,1024]{1,0:T(4,128)S(1)}, bf16[4,192,1024]{2,1,0:T(8,128)(2,1)}, bf16[4,192,1024]{2,1,0:T(8,128)(2,...) custom-call(s32[8,3]{1,0:T(8,128)S(1)} %add_add_fusion.2.info, ...), custom_call_target="tpu_custom_call", output_to_operand_aliasing={{2}: (13, {}), {3}: (14, {}), {4}: (15, {}), {5}: (16, {}),... | custom-call | flops 4831838208 | bytes 33554432 | tf_op jit(solution)/shard_map/layer_fwd/pallas_call | solution.py:148
  226.8 3.7 collective-permute-start.32
  230.5 38.5 %collective-permute-done.32 = bf16[768,256]{1,0:T(8,128)(2,1)} collective-permute-done((bf16[768,256]{1,0:T(8,128)(2,1)}, bf16[768,256]{1,0:T(8,128)(2,1)}, u32[]{:S(2)}, u32[]{:S(2)}) %collective-permute-start.32) | collective-permute-done | bytes 393248 | tf_op jit(solution)/shard_map/ppermute | solution.py:595
  273.4 17.3 %head_fwd.1 = (bf16[256,768]{1,0:T(8,128)(2,1)S(1)}, f32[2,768]{1,0:T(2,128)}) custom-call(bf16[8000,256]{1,0:T(8,128)(2,1)S(1)} %bitcast.529, bf16[768,256]{1,0:T(8,128)(2,1)S(1)} %get-tuple-element.393.latent), custom_call_target="tpu_custom_call" | custom-call | flops 6291456000 | bytes 4096000 | tf_op jit(solution)/shard_map/head_fwd/pallas_call | solution.py:333
  304.8 7.1 collective-permute-done.37
  318.9 3.4 copy-done.5
  339.7 8.9 %layer_bwd.10 = (bf16[192,1024]{1,0:T(8,128)(2,1)S(1)}, f32[3,1024]{1,0:T(4,128)S(1)}, bf16[4,192,1024]{2,1,0:T(8,128)(2,1)}, bf16[4,192,4096]{2,1,0:T(8,128)(2,...) custom-call(s32[8,3]{1,0:T(8,128)S(1)} %add_add_fusion.3.info, ...), custom_call_target="tpu_custom_call", output_to_operand_aliasing={{2}: (18, {}), {3}: (19, {}), {4}: (20, {}), {5}: (21, {}),... | custom-call | flops 4831838208 | bytes 33554432 | tf_op jit(solution)/shard_map/layer_bwd/pallas_call | solution.py:262
  353.7 37.1 %collective-permute-done.44.g_in = bf16[192,1024]{1,0:T(8,128)(2,1)S(1)} collective-permute-done((bf16[192,1024]{1,0:T(8,128)(2,1)S(1)}, bf16[192,1024]{1,0:T(8,128)(2,1)S(1)}, u32[]{:S(2)}, u32[]{:S(2)}) %collective-permute-start.44) | collective-permute-done | bytes 393248 | tf_op jit(solution)/shard_map/ppermute | solution.py:729
  390.8 16.4 %layer_bwd.12 = (bf16[192,1024]{1,0:T(8,128)(2,1)S(1)}, f32[3,1024]{1,0:T(4,128)S(1)}, bf16[4,192,1024]{2,1,0:T(8,128)(2,1)}, bf16[4,192,4096]{2,1,0:T(8,128)(2,...) custom-call(s32[8,3]{1,0:T(8,128)S(1)} %add_add_fusion.3.info, ...), custom_call_target="tpu_custom_call", output_to_operand_aliasing={{2}: (18, {}), {3}: (19, {}), {4}: (20, {}), {5}: (21, {}),... | custom-call | flops 4831838208 | bytes 33554432 | tf_op jit(solution)/shard_map/layer_bwd/pallas_call | solution.py:262
  409.3 11.6 %collective-permute-done.46.g_in = bf16[192,1024]{1,0:T(8,128)(2,1)S(1)} collective-permute-done((bf16[192,1024]{1,0:T(8,128)(2,1)S(1)}, bf16[192,1024]{1,0:T(8,128)(2,1)S(1)}, u32[]{:S(2)}, u32[]{:S(2)}) %collective-permute-start.46) | collective-permute-done | bytes 393248 | tf_op jit(solution)/shard_map/ppermute | solution.py:729
  420.9 16.0 %layer_bwd.13 = (bf16[192,1024]{1,0:T(8,128)(2,1)S(1)}, f32[3,1024]{1,0:T(4,128)S(1)}, bf16[4,192,1024]{2,1,0:T(8,128)(2,1)}, bf16[4,192,4096]{2,1,0:T(8,128)(2,...) custom-call(s32[8,3]{1,0:T(8,128)S(1)} %add_add_fusion.3.info, ...), custom_call_target="tpu_custom_call", output_to_operand_aliasing={{2}: (18, {}), {3}: (19, {}), {4}: (20, {}), {5}: (21, {}),... | custom-call | flops 4831838208 | bytes 33554432 | tf_op jit(solution)/shard_map/layer_bwd/pallas_call | solution.py:262
  443.9 16.6 %layer_bwd.14 = (bf16[192,1024]{1,0:T(8,128)(2,1)S(1)}, f32[3,1024]{1,0:T(4,128)S(1)}, bf16[4,192,1024]{2,1,0:T(8,128)(2,1)}, bf16[4,192,4096]{2,1,0:T(8,128)(2,...) custom-call(s32[8,3]{1,0:T(8,128)S(1)} %add_add_fusion.3.info, ...), custom_call_target="tpu_custom_call", output_to_operand_aliasing={{2}: (18, {}), {3}: (19, {}), {4}: (20, {}), {5}: (21, {}),... | custom-call | flops 4831838208 | bytes 33554432 | tf_op jit(solution)/shard_map/layer_bwd/pallas_call | solution.py:262
  461.9 4.2 collective-permute-start.40
  467.6 17.5 %layer_bwd.15 = (bf16[192,1024]{1,0:T(8,128)(2,1)}, f32[3,1024]{1,0:T(4,128)S(1)}, bf16[4,192,1024]{2,1,0:T(8,128)(2,1)}, bf16[4,192,4096]{2,1,0:T(8,128)(2,1)},...) custom-call(s32[8,3]{1,0:T(8,128)S(1)} %add_add_fusion.3.info, ...), custom_call_target="tpu_custom_call", output_to_operand_aliasing={{2}: (18, {}), {3}: (19, {}), {4}: (20, {}), {5}: (21, {}),... | custom-call | flops 4831838208 | bytes 33554432 | tf_op jit(solution)/shard_map/layer_bwd/pallas_call | solution.py:262
  486.6 6.1 product.10
  497.0 7.5 product.11
  512.3 15.9 %collective-permute-done.52 = bf16[2,2,128,1024]{3,2,1,0:T(8,128)(2,1)} collective-permute-done((bf16[2,2,128,1024]{3,2,1,0:T(8,128)(2,1)}, bf16[2,2,128,1024]{3,2,1,0:T(8,128)(2,1)}, u32[]{:S(2)}, u32[]{:S(2)}) %collective-permute-start.52) | collective-permute-done | bytes 1048608 | tf_op jit(solution)/shard_map/ppermute | solution.py:566
  534.3 3.7 product.14
  546.8 6.5 product.18
  555.3 5.5 product.19
  563.8 22.6 %collective-permute-done.51 = bf16[2,2,512,1024]{3,2,1,0:T(8,128)(2,1)} collective-permute-done((bf16[2,2,512,1024]{3,2,1,0:T(8,128)(2,1)}, bf16[2,2,512,1024]{3,2,1,0:T(8,128)(2,1)}, u32[]{:S(2)}, u32[]{:S(2)}) %collective-permute-start.51) | collective-permute-done | bytes 4194336 | tf_op jit(solution)/shard_map/ppermute | solution.py:566
  596.2 9.1 %collective-permute-done.55 = bf16[768,256]{1,0:T(8,128)(2,1)S(1)} collective-permute-done((bf16[768,256]{1,0:T(8,128)(2,1)S(1)}, bf16[768,256]{1,0:T(8,128)(2,1)S(1)}, u32[]{:S(2)}, u32[]{:S(2)}) %collective-permute-start.55) | collective-permute-done | bytes 393248 | tf_op jit(solution)/shard_map/ppermute | solution.py:595
  606.4 11.6 %head_bwd.1 = bf16[8000,256]{1,0:T(8,128)(2,1)S(1)} custom-call(bf16[8000,256]{1,0:T(8,128)(2,1)S(1)} %bitcast.530, bf16[768,256]{1,0:T(8,128)(2,1)S(1)} %copy-done.32, f32[1,768]{1,0:T(1,128)S(1)} %get-tuple-element.384.log_total, f32[1,768]{1,0:T(1,128)S(1)} %mul.437.weight, s32[1,768]{1,0:T(1,128)S(1)} %sub.168.ids, ...), custom_call_target="tpu_custom_call" | custom-call | flops 1 | bytes 1 | tf_op jit(solution)/shard_map/head_bwd/pallas_call | solution.py:358
  620.0 3.6 fusion.15
  630.2 6.2 collective-permute-done.59
  639.4 27.6 %collective-permute-done.63 = bf16[2,2,128,4096]{3,2,1,0:T(8,128)(2,1)} collective-permute-done((bf16[2,2,128,4096]{3,2,1,0:T(8,128)(2,1)}, bf16[2,2,128,4096]{3,2,1,0:T(8,128)(2,1)}, u32[]{:S(2)}, u32[]{:S(2)}) %collective-permute-start.63) | collective-permute-done | bytes 4194336 | tf_op jit(solution)/shard_map/ppermute | solution.py:566
  667.1 3.8 fusion.7
  682.6 47.1 %collective-permute-done.62 = bf16[512,1024]{1,0:T(8,128)(2,1)} collective-permute-done((bf16[512,1024]{1,0:T(8,128)(2,1)}, bf16[512,1024]{1,0:T(8,128)(2,1)}, u32[]{:S(2)}, u32[]{:S(2)}) %collective-permute-start.62) | collective-permute-done | bytes 1048608 | tf_op jit(solution)/shard_map/ppermute | solution.py:484
  738.2 3.8 collective-permute-start.66
  759.3 17.2 %collective-permute-done.64 = bf16[2,128,1536]{2,1,0:T(8,128)(2,1)S(1)} collective-permute-done((bf16[2,128,1536]{2,1,0:T(8,128)(2,1)S(1)}, bf16[2,128,1536]{2,1,0:T(8,128)(2,1)S(1)}, u32[]{:S(2)}, u32[]{:S(2)}) %collective-permute-start.64) | collective-permute-done | bytes 786464 | tf_op jit(solution)/shard_map/ppermute | solution.py:484
  784.1 27.3 %collective-permute-done.73 = bf16[2,128,1536]{2,1,0:T(8,128)(2,1)S(1)} collective-permute-done((bf16[2,128,1536]{2,1,0:T(8,128)(2,1)S(1)}, bf16[2,128,1536]{2,1,0:T(8,128)(2,1)S(1)}, u32[]{:S(2)}, u32[]{:S(2)}) %collective-permute-start.73) | collective-permute-done | bytes 786464 | tf_op jit(solution)/shard_map/ppermute | solution.py:484
  813.7 4.2 collective-permute-start.75
  828.5 7.1 collective-permute-done.68
  843.5 15.5 %collective-permute-done.74 = bf16[1000,256]{1,0:T(8,128)(2,1)S(1)} collective-permute-done((bf16[1000,256]{1,0:T(8,128)(2,1)S(1)}, bf16[1000,256]{1,0:T(8,128)(2,1)S(1)}, u32[]{:S(2)}, u32[]{:S(2)}) %collective-permute-start.74) | collective-permute-done | bytes 512032 | tf_op jit(solution)/shard_map/ppermute | solution.py:484
  (662 shorter events, 257.7 us)
Async XLA Ops:
  4.0 19.9 %collective-permute-start = (bf16[272,256]{1,0:T(8,128)(2,1)S(1)}, bf16[272,256]{1,0:T(8,128)(2,1)S(1)}, u32[]{:S(2)}, u32[]{:S(2)}) collective-permute-start(bf16[272,256]{1,0:T(8,128)(2,1)S(1)} %get-tuple-element.404), channel_id=1, source_target_pairs={{0,4},{1,5},{2,6},{3,7},{4,0},{5,1},{6,2},{7,3},{8,12},{9,13},{10,... | collective-permute-start | bytes 417800 | tf_op jit(solution)/shard_map/ppermute | solution.py:405
  8.1 18.9 %collective-permute-start.4 = (bf16[272,256]{1,0:T(8,128)(2,1)S(1)}, bf16[272,256]{1,0:T(8,128)(2,1)S(1)}, u32[]{:S(2)}, u32[]{:S(2)}) collective-permute-start(bf16[272,256]{1,0:T(8,128)(2,1)S(1)} %get-tuple-element.402), channel_id=1, source_target_pairs={{0,4},{1,5},{2,6},{3,7},{4,0},{5,1},{6,2},{7,3},{8,12},{9,13},{10,... | collective-permute-start | bytes 417800 | tf_op jit(solution)/shard_map/ppermute | solution.py:405
  8.1 21.8 %collective-permute-start.3 = (bf16[272,256]{1,0:T(8,128)(2,1)S(1)}, bf16[272,256]{1,0:T(8,128)(2,1)S(1)}, u32[]{:S(2)}, u32[]{:S(2)}) collective-permute-start(bf16[272,256]{1,0:T(8,128)(2,1)S(1)} %get-tuple-element.403), channel_id=1, source_target_pairs={{0,4},{1,5},{2,6},{3,7},{4,0},{5,1},{6,2},{7,3},{8,12},{9,13},{10,... | collective-permute-start | bytes 417800 | tf_op jit(solution)/shard_map/ppermute | solution.py:405
  11.0 20.5 %collective-permute-start.2 = (bf16[216,256]{1,0:T(8,128)(2,1)S(1)}, bf16[216,256]{1,0:T(8,128)(2,1)S(1)}, u32[]{:S(2)}, u32[]{:S(2)}) collective-permute-start(bf16[216,256]{1,0:T(8,128)(2,1)S(1)} %pad_maximum_fusion.6), channel_id=1, source_target_pairs={{0,4},{1,5},{2,6},{3,7},{4,0},{5,1},{6,2},{7,3},{8,12},{9,13},{10,... | collective-permute-start | bytes 331784 | tf_op jit(solution)/shard_map/ppermute | solution.py:405
  18.3 72.9 %collective-permute-start.16 = (f32[4,48,256]{2,1,0:T(8,128)}, f32[4,48,256]{2,1,0:T(8,128)}, u32[]{:S(2)}, u32[]{:S(2)}) collective-permute-start(f32[4,48,256]{2,1,0:T(8,128)} %param.25), channel_id=1, source_target_pairs={{0,8},{8,0},{16,24},{24,16},{1,9},{9,1},{17,25},{25,17},{2,10},{10... | collective-permute-start | bytes 589832 | tf_op jit(solution)/shard_map/ppermute | solution.py:405
  24.4 13.0 %collective-permute-start.1 = (bf16[2,272,256]{2,1,0:T(8,128)(2,1)S(1)}, bf16[2,272,256]{2,1,0:T(8,128)(2,1)S(1)}, u32[]{:S(2)}, u32[]{:S(2)}) collective-permute-start(bf16[2,272,256]{2,1,0:T(8,128)(2,1)S(1)} %maximum_select_fusion.14), channel_id=1, source_target_pairs={{0,2},{1,3},{2,0},{3,1},{4,6},{5,7},{6,4},{7,5},{8,10},{9,11},{10,... | collective-permute-start | bytes 835592 | tf_op jit(solution)/shard_map/ppermute | solution.py:405
  27.5 15.9 %collective-permute-start.8 = (bf16[2,272,256]{2,1,0:T(8,128)(2,1)S(1)}, bf16[2,272,256]{2,1,0:T(8,128)(2,1)S(1)}, u32[]{:S(2)}, u32[]{:S(2)}) collective-permute-start(bf16[2,272,256]{2,1,0:T(8,128)(2,1)S(1)} %maximum_select_fusion.15), channel_id=1, source_target_pairs={{0,2},{1,3},{2,0},{3,1},{4,6},{5,7},{6,4},{7,5},{8,10},{9,11},{10,... | collective-permute-start | bytes 835592 | tf_op jit(solution)/shard_map/ppermute | solution.py:405
  30.5 18.9 %collective-permute-start.7 = (bf16[2,272,256]{2,1,0:T(8,128)(2,1)S(1)}, bf16[2,272,256]{2,1,0:T(8,128)(2,1)S(1)}, u32[]{:S(2)}, u32[]{:S(2)}) collective-permute-start(bf16[2,272,256]{2,1,0:T(8,128)(2,1)S(1)} %maximum_select_fusion.16), channel_id=1, source_target_pairs={{0,2},{1,3},{2,0},{3,1},{4,6},{5,7},{6,4},{7,5},{8,10},{9,11},{10,... | collective-permute-start | bytes 835592 | tf_op jit(solution)/shard_map/ppermute | solution.py:405
  31.7 22.3 %collective-permute-start.6 = (bf16[2,216,256]{2,1,0:T(8,128)(2,1)S(1)}, bf16[2,216,256]{2,1,0:T(8,128)(2,1)S(1)}, u32[]{:S(2)}, u32[]{:S(2)}) collective-permute-start(bf16[2,216,256]{2,1,0:T(8,128)(2,1)S(1)} %maximum_select_fusion.20), channel_id=1, source_target_pairs={{0,2},{1,3},{2,0},{3,1},{4,6},{5,7},{6,4},{7,5},{8,10},{9,11},{10,... | collective-permute-start | bytes 663560 | tf_op jit(solution)/shard_map/ppermute | solution.py:405
  38.1 19.3 %collective-permute-start.5 = (bf16[2,2,272,256]{3,2,0,1:T(8,128)(2,1)S(1)}, bf16[2,2,272,256]{3,2,0,1:T(8,128)(2,1)S(1)}, u32[]{:S(2)}, u32[]{:S(2)}) collective-permute-start(bf16[2,2,272,256]{3,2,0,1:T(8,128)(2,1)S(1)} %maximum_select_fusion.6), channel_id=1, source_target_pairs={{0,1},{1,0},{2,3},{3,2},{4,5},{5,4},{6,7},{7,6},{8,9},{9,8},{10,11... | collective-permute-start | bytes 1671176 | tf_op jit(solution)/shard_map/ppermute | solution.py:405
  44.1 21.5 %collective-permute-start.9 = (bf16[2,2,272,256]{3,2,0,1:T(8,128)(2,1)S(1)}, bf16[2,2,272,256]{3,2,0,1:T(8,128)(2,1)S(1)}, u32[]{:S(2)}, u32[]{:S(2)}) collective-permute-start(bf16[2,2,272,256]{3,2,0,1:T(8,128)(2,1)S(1)} %maximum_select_fusion.7), channel_id=1, source_target_pairs={{0,1},{1,0},{2,3},{3,2},{4,5},{5,4},{6,7},{7,6},{8,9},{9,8},{10,11... | collective-permute-start | bytes 1671176 | tf_op jit(solution)/shard_map/ppermute | solution.py:405
  50.0 27.4 %collective-permute-start.10 = (bf16[2,2,272,256]{3,2,0,1:T(8,128)(2,1)S(1)}, bf16[2,2,272,256]{3,2,0,1:T(8,128)(2,1)S(1)}, u32[]{:S(2)}, u32[]{:S(2)}) collective-permute-start(bf16[2,2,272,256]{3,2,0,1:T(8,128)(2,1)S(1)} %maximum_select_fusion.8), channel_id=1, source_target_pairs={{0,1},{1,0},{2,3},{3,2},{4,5},{5,4},{6,7},{7,6},{8,9},{9,8},{10,11... | collective-permute-start | bytes 1671176 | tf_op jit(solution)/shard_map/ppermute | solution.py:405
  54.1 31.8 %collective-permute-start.11 = (bf16[2,2,216,256]{3,2,0,1:T(8,128)(2,1)S(1)}, bf16[2,2,216,256]{3,2,0,1:T(8,128)(2,1)S(1)}, u32[]{:S(2)}, u32[]{:S(2)}) collective-permute-start(bf16[2,2,216,256]{3,2,0,1:T(8,128)(2,1)S(1)} %maximum_select_fusion.10), channel_id=1, source_target_pairs={{0,1},{1,0},{2,3},{3,2},{4,5},{5,4},{6,7},{7,6},{8,9},{9,8},{10,11... | collective-permute-start | bytes 1327112 | tf_op jit(solution)/shard_map/ppermute | solution.py:405
  92.5 12.0 %collective-permute-start.17 = (f32[2,4,48,256]{3,2,1,0:T(8,128)S(1)}, f32[2,4,48,256]{3,2,1,0:T(8,128)S(1)}, u32[]{:S(2)}, u32[]{:S(2)}) collective-permute-start(f32[2,4,48,256]{3,2,1,0:T(8,128)S(1)} %maximum_select_fusion.13), channel_id=1, source_target_pairs={{0,16},{8,24},{16,0},{24,8},{1,17},{9,25},{17,1},{25,9},{2,18},{10... | collective-permute-start | bytes 1179656 | tf_op jit(solution)/shard_map/ppermute | solution.py:405
  96.3 13.8 %collective-permute-start.19 = (bf16[2,64,1024]{2,1,0:T(8,128)(2,1)}, bf16[2,64,1024]{2,1,0:T(8,128)(2,1)}, u32[]{:S(2)}, u32[]{:S(2)}) collective-permute-start(bf16[2,64,1024]{2,1,0:T(8,128)(2,1)} %maximum_select_fusion.19), channel_id=1, source_target_pairs={{0,16},{8,24},{16,0},{24,8},{1,17},{9,25},{17,1},{25,9},{2,18},{10... | collective-permute-start | bytes 786440 | tf_op jit(solution)/shard_map/ppermute | solution.py:405
  96.9 21.2 %collective-permute-start.15 = (bf16[768,256]{1,0:T(8,128)(2,1)S(1)}, bf16[768,256]{1,0:T(8,128)(2,1)S(1)}, u32[]{:S(2)}, u32[]{:S(2)}) collective-permute-start(bf16[768,256]{1,0:T(8,128)(2,1)S(1)} %add.854), channel_id=1, source_target_pairs={{0,16},{8,24},{16,0},{24,8},{1,17},{9,25},{17,1},{25,9},{2,18},{10... | collective-permute-start | bytes 1179656 | tf_op jit(solution)/shard_map/ppermute | solution.py:405
  161.9 17.6 %collective-permute-start.23 = (bf16[192,1024]{1,0:T(8,128)(2,1)S(1)}, bf16[192,1024]{1,0:T(8,128)(2,1)S(1)}, u32[]{:S(2)}, u32[]{:S(2)}) collective-permute-start(bf16[192,1024]{1,0:T(8,128)(2,1)S(1)} %get-tuple-element.209), channel_id=1, source_target_pairs={{8,16},{9,17},{10,18},{11,19},{12,20},{13,21},{14,22},{15,23}} | collective-permute-start | bytes 1179656 | tf_op jit(solution)/shard_map/ppermute | solution.py:687
  178.8 17.2 %collective-permute-start.25 = (bf16[192,1024]{1,0:T(8,128)(2,1)S(1)}, bf16[192,1024]{1,0:T(8,128)(2,1)S(1)}, u32[]{:S(2)}, u32[]{:S(2)}) collective-permute-start(bf16[192,1024]{1,0:T(8,128)(2,1)S(1)} %get-tuple-element.219), channel_id=1, source_target_pairs={{8,16},{9,17},{10,18},{11,19},{12,20},{13,21},{14,22},{15,23}} | collective-permute-start | bytes 1179656 | tf_op jit(solution)/shard_map/ppermute | solution.py:687
  195.3 11.1 %collective-permute-start.27 = (bf16[192,1024]{1,0:T(8,128)(2,1)S(1)}, bf16[192,1024]{1,0:T(8,128)(2,1)S(1)}, u32[]{:S(2)}, u32[]{:S(2)}) collective-permute-start(bf16[192,1024]{1,0:T(8,128)(2,1)S(1)} %get-tuple-element.229), channel_id=1, source_target_pairs={{8,16},{9,17},{10,18},{11,19},{12,20},{13,21},{14,22},{15,23}} | collective-permute-start | bytes 1179656 | tf_op jit(solution)/shard_map/ppermute | solution.py:687
  226.8 42.2 %collective-permute-start.32 = (bf16[768,256]{1,0:T(8,128)(2,1)}, bf16[768,256]{1,0:T(8,128)(2,1)}, u32[]{:S(2)}, u32[]{:S(2)}) collective-permute-start(bf16[768,256]{1,0:T(8,128)(2,1)} %broadcast_select_fusion.1), channel_id=1, source_target_pairs={{24,8},{16,0},{25,9},{17,1},{26,10},{18,2},{27,11},{19,3},{28,12},... | collective-permute-start | bytes 1179656 | tf_op jit(solution)/shard_map/ppermute | solution.py:595
  300.6 11.3 %collective-permute-start.37 = (bf16[256,768]{0,1:T(8,128)(2,1)}, bf16[256,768]{0,1:T(8,128)(2,1)}, u32[]{:S(2)}, u32[]{:S(2)}) collective-permute-start(bf16[256,768]{0,1:T(8,128)(2,1)} %add_convert_fusion.7), channel_id=1, source_target_pairs={{0,16},{8,24},{16,0},{24,8},{1,17},{9,25},{17,1},{25,9},{2,18},{10... | collective-permute-start | bytes 1179656 | tf_op jit(solution)/shard_map/ppermute | solution.py:405
  329.4 20.6 %collective-permute-start.43 = (bf16[192,1024]{1,0:T(8,128)(2,1)}, bf16[192,1024]{1,0:T(8,128)(2,1)S(1)}, u32[]{:S(2)}, u32[]{:S(2)}) collective-permute-start(bf16[192,1024]{1,0:T(8,128)(2,1)} %get-tuple-element.298), channel_id=1, source_target_pairs={{16,8},{17,9},{18,10},{19,11},{20,12},{21,13},{22,14},{23,15}} | collective-permute-start | bytes 1179656 | tf_op jit(solution)/shard_map/ppermute | solution.py:731
  351.6 39.2 %collective-permute-start.44 = (bf16[192,1024]{1,0:T(8,128)(2,1)S(1)}, bf16[192,1024]{1,0:T(8,128)(2,1)S(1)}, u32[]{:S(2)}, u32[]{:S(2)}) collective-permute-start(bf16[192,1024]{1,0:T(8,128)(2,1)S(1)} %get-tuple-element.311), channel_id=1, source_target_pairs={{8,0},{24,16},{9,1},{25,17},{10,2},{26,18},{11,3},{27,19},{12,4},{... | collective-permute-start | bytes 1179656 | tf_op jit(solution)/shard_map/ppermute | solution.py:729
  353.0 56.3 %collective-permute-start.47 = (bf16[192,1024]{1,0:T(8,128)(2,1)S(1)}, bf16[192,1024]{1,0:T(8,128)(2,1)S(1)}, u32[]{:S(2)}, u32[]{:S(2)}) collective-permute-start(bf16[192,1024]{1,0:T(8,128)(2,1)S(1)} %get-tuple-element.311), channel_id=1, source_target_pairs={{16,8},{17,9},{18,10},{19,11},{20,12},{21,13},{22,14},{23,15}} | collective-permute-start | bytes 1179656 | tf_op jit(solution)/shard_map/ppermute | solution.py:731
  407.2 13.7 %collective-permute-start.46 = (bf16[192,1024]{1,0:T(8,128)(2,1)S(1)}, bf16[192,1024]{1,0:T(8,128)(2,1)S(1)}, u32[]{:S(2)}, u32[]{:S(2)}) collective-permute-start(bf16[192,1024]{1,0:T(8,128)(2,1)S(1)} %get-tuple-element.317), channel_id=1, source_target_pairs={{8,0},{9,1},{10,2},{11,3},{12,4},{13,5},{14,6},{15,7}} | collective-permute-start | bytes 1179656 | tf_op jit(solution)/shard_map/ppermute | solution.py:729
  408.5 34.6 %collective-permute-start.49 = (bf16[192,1024]{1,0:T(8,128)(2,1)S(1)}, bf16[192,1024]{1,0:T(8,128)(2,1)S(1)}, u32[]{:S(2)}, u32[]{:S(2)}) collective-permute-start(bf16[192,1024]{1,0:T(8,128)(2,1)S(1)} %get-tuple-element.317), channel_id=1, source_target_pairs={{16,8},{17,9},{18,10},{19,11},{20,12},{21,13},{22,14},{23,15}} | collective-permute-start | bytes 1179656 | tf_op jit(solution)/shard_map/ppermute | solution.py:731
  442.0 19.8 %collective-permute-start.38 = (f32[3]{0:T(128)S(1)}, f32[3]{0:T(128)S(1)}, u32[]{:S(2)}, u32[]{:S(2)}) collective-permute-start(f32[3]{0:T(128)S(1)} %add_add_fusion.6), channel_id=1, source_target_pairs={{0,2},{1,3},{2,0},{3,1},{4,6},{5,7},{6,4},{7,5},{8,10},{9,11},{10,... | collective-permute-start | bytes 44 | tf_op jit(solution)/shard_map/ppermute | solution.py:405
  492.6 93.8 %collective-permute-start.51 = (bf16[2,2,512,1024]{3,2,1,0:T(8,128)(2,1)}, bf16[2,2,512,1024]{3,2,1,0:T(8,128)(2,1)}, u32[]{:S(2)}, u32[]{:S(2)}) collective-permute-start(bf16[2,2,512,1024]{3,2,1,0:T(8,128)(2,1)} %bitcast.110), channel_id=1, source_target_pairs={{0,1},{1,0},{2,3},{3,2},{4,5},{5,4},{6,7},{7,6},{8,9},{9,8},{10,11... | collective-permute-start | bytes 12582920 | tf_op jit(solution)/shard_map/ppermute | solution.py:566
  507.5 20.7 %collective-permute-start.52 = (bf16[2,2,128,1024]{3,2,1,0:T(8,128)(2,1)}, bf16[2,2,128,1024]{3,2,1,0:T(8,128)(2,1)}, u32[]{:S(2)}, u32[]{:S(2)}) collective-permute-start(bf16[2,2,128,1024]{3,2,1,0:T(8,128)(2,1)} %bitcast.112), channel_id=1, source_target_pairs={{0,2},{1,3},{2,0},{3,1},{4,6},{5,7},{6,4},{7,5},{8,10},{9,11},{10,... | collective-permute-start | bytes 3145736 | tf_op jit(solution)/shard_map/ppermute | solution.py:566
  529.5 31.8 %collective-permute-start.53 = (bf16[2,128,1024]{2,1,0:T(8,128)(2,1)S(1)}, bf16[2,128,1024]{2,1,0:T(8,128)(2,1)S(1)}, u32[]{:S(2)}, u32[]{:S(2)}) collective-permute-start(bf16[2,128,1024]{2,1,0:T(8,128)(2,1)S(1)} %fusion.62), channel_id=1, source_target_pairs={{0,4},{1,5},{2,6},{3,7},{4,0},{5,1},{6,2},{7,3},{8,12},{9,13},{10,... | collective-permute-start | bytes 1572872 | tf_op jit(solution)/shard_map/ppermute | solution.py:484
  560.9 106.2 %collective-permute-start.63 = (bf16[2,2,128,4096]{3,2,1,0:T(8,128)(2,1)}, bf16[2,2,128,4096]{3,2,1,0:T(8,128)(2,1)}, u32[]{:S(2)}, u32[]{:S(2)}) collective-permute-start(bf16[2,2,128,4096]{3,2,1,0:T(8,128)(2,1)} %bitcast.157), channel_id=1, source_target_pairs={{0,1},{1,0},{2,3},{3,2},{4,5},{5,4},{6,7},{7,6},{8,9},{9,8},{10,11... | collective-permute-start | bytes 12582920 | tf_op jit(solution)/shard_map/ppermute | solution.py:566
  589.2 30.7 %collective-permute-start.58 = (bf16[2,512,1024]{2,1,0:T(8,128)(2,1)S(1)}, bf16[2,512,1024]{2,1,0:T(8,128)(2,1)S(1)}, u32[]{:S(2)}, u32[]{:S(2)}) collective-permute-start(bf16[2,512,1024]{2,1,0:T(8,128)(2,1)S(1)} %fusion.6.token), channel_id=1, source_target_pairs={{0,2},{1,3},{2,0},{3,1},{4,6},{5,7},{6,4},{7,5},{8,10},{9,11},{10,... | collective-permute-start | bytes 6291464 | tf_op jit(solution)/shard_map/ppermute | solution.py:484
  670.9 74.4 %collective-permute-start.67 = (bf16[2,128,4096]{2,1,0:T(8,128)(2,1)}, bf16[2,128,4096]{2,1,0:T(8,128)(2,1)}, u32[]{:S(2)}, u32[]{:S(2)}) collective-permute-start(bf16[2,128,4096]{2,1,0:T(8,128)(2,1)} %fusion.7), channel_id=1, source_target_pairs={{0,2},{1,3},{2,0},{3,1},{4,6},{5,7},{6,4},{7,5},{8,10},{9,11},{10,... | collective-permute-start | bytes 6291464 | tf_op jit(solution)/shard_map/ppermute | solution.py:484
  674.1 68.6 %collective-permute-start.57 = (bf16[2,2,128,1536]{3,2,1,0:T(8,128)(2,1)}, bf16[2,2,128,1536]{3,2,1,0:T(8,128)(2,1)}, u32[]{:S(2)}, u32[]{:S(2)}) collective-permute-start(bf16[2,2,128,1536]{3,2,1,0:T(8,128)(2,1)} %bitcast.126), channel_id=1, source_target_pairs={{0,1},{1,0},{2,3},{3,2},{4,5},{5,4},{6,7},{7,6},{8,9},{9,8},{10,11... | collective-permute-start | bytes 4718600 | tf_op jit(solution)/shard_map/ppermute | solution.py:566
  675.7 54.1 %collective-permute-start.62 = (bf16[512,1024]{1,0:T(8,128)(2,1)}, bf16[512,1024]{1,0:T(8,128)(2,1)}, u32[]{:S(2)}, u32[]{:S(2)}) collective-permute-start(bf16[512,1024]{1,0:T(8,128)(2,1)} %fusion.15), channel_id=1, source_target_pairs={{0,4},{1,5},{2,6},{3,7},{4,0},{5,1},{6,2},{7,3},{8,12},{9,13},{10,... | collective-permute-start | bytes 3145736 | tf_op jit(solution)/shard_map/ppermute | solution.py:484
  677.4 75.7 %collective-permute-start.65 = (bf16[2,2,128,1536]{3,2,1,0:T(8,128)(2,1)S(1)}, bf16[2,2,128,1536]{3,2,1,0:T(8,128)(2,1)}, u32[]{:S(2)}, u32[]{:S(2)}) collective-permute-start(bf16[2,2,128,1536]{3,2,1,0:T(8,128)(2,1)S(1)} %bitcast.546), channel_id=1, source_target_pairs={{0,1},{1,0},{2,3},{3,2},{4,5},{5,4},{6,7},{7,6},{8,9},{9,8},{10,11... | collective-permute-start | bytes 4718600 | tf_op jit(solution)/shard_map/ppermute | solution.py:566
  678.6 58.1 %collective-permute-start.61 = (bf16[2,2,48,1024]{3,2,0,1:T(8,128)(2,1)}, bf16[2,2,48,1024]{3,2,0,1:T(8,128)(2,1)S(1)}, u32[]{:S(2)}, u32[]{:S(2)}) collective-permute-start(bf16[2,2,48,1024]{3,2,0,1:T(8,128)(2,1)} %copy-done.86), channel_id=1, source_target_pairs={{0,2},{1,3},{2,0},{3,1},{4,6},{5,7},{6,4},{7,5},{8,10},{9,11},{10,... | collective-permute-start | bytes 1179656 | tf_op jit(solution)/shard_map/ppermute | solution.py:484
  729.8 50.6 %collective-permute-start.56 = (bf16[2,2,1000,256]{3,2,1,0:T(8,128)(2,1)}, bf16[2,2,1000,256]{3,2,1,0:T(8,128)(2,1)S(1)}, u32[]{:S(2)}, u32[]{:S(2)}) collective-permute-start(bf16[2,2,1000,256]{3,2,1,0:T(8,128)(2,1)} %copy-done.73), channel_id=1, source_target_pairs={{0,1},{1,0},{2,3},{3,2},{4,5},{5,4},{6,7},{7,6},{8,9},{9,8},{10,11... | collective-permute-start | bytes 6144008 | tf_op jit(solution)/shard_map/ppermute | solution.py:484
  738.2 12.8 %collective-permute-start.66 = (bf16[2,48,1024]{2,1,0:T(8,128)(2,1)S(1)}, bf16[2,48,1024]{2,1,0:T(8,128)(2,1)S(1)}, u32[]{:S(2)}, u32[]{:S(2)}) collective-permute-start(bf16[2,48,1024]{2,1,0:T(8,128)(2,1)S(1)} %fusion.69), channel_id=1, source_target_pairs={{0,4},{1,5},{2,6},{3,7},{4,0},{5,1},{6,2},{7,3},{8,12},{9,13},{10,... | collective-permute-start | bytes 589832 | tf_op jit(solution)/shard_map/ppermute | solution.py:484
  744.7 31.8 %collective-permute-start.64 = (bf16[2,128,1536]{2,1,0:T(8,128)(2,1)S(1)}, bf16[2,128,1536]{2,1,0:T(8,128)(2,1)S(1)}, u32[]{:S(2)}, u32[]{:S(2)}) collective-permute-start(bf16[2,128,1536]{2,1,0:T(8,128)(2,1)S(1)} %fusion.49), channel_id=1, source_target_pairs={{0,2},{1,3},{2,0},{3,1},{4,6},{5,7},{6,4},{7,5},{8,10},{9,11},{10,... | collective-permute-start | bytes 2359304 | tf_op jit(solution)/shard_map/ppermute | solution.py:484
  747.9 65.8 %collective-permute-start.72 = (bf16[128,4096]{1,0:T(8,128)(2,1)S(1)}, bf16[128,4096]{1,0:T(8,128)(2,1)S(1)}, u32[]{:S(2)}, u32[]{:S(2)}) collective-permute-start(bf16[128,4096]{1,0:T(8,128)(2,1)S(1)} %fusion.11), channel_id=1, source_target_pairs={{0,4},{1,5},{2,6},{3,7},{4,0},{5,1},{6,2},{7,3},{8,12},{9,13},{10,... | collective-permute-start | bytes 3145736 | tf_op jit(solution)/shard_map/ppermute | solution.py:484
  754.7 56.7 %collective-permute-start.73 = (bf16[2,128,1536]{2,1,0:T(8,128)(2,1)S(1)}, bf16[2,128,1536]{2,1,0:T(8,128)(2,1)S(1)}, u32[]{:S(2)}, u32[]{:S(2)}) collective-permute-start(bf16[2,128,1536]{2,1,0:T(8,128)(2,1)S(1)} %fusion.50), channel_id=1, source_target_pairs={{0,2},{1,3},{2,0},{3,1},{4,6},{5,7},{6,4},{7,5},{8,10},{9,11},{10,... | collective-permute-start | bytes 2359304 | tf_op jit(solution)/shard_map/ppermute | solution.py:484
  755.3 66.1 %collective-permute-start.71 = (bf16[128,1024]{1,0:T(8,128)(2,1)S(1)}, bf16[128,1024]{1,0:T(8,128)(2,1)S(1)}, u32[]{:S(2)}, u32[]{:S(2)}) collective-permute-start(bf16[128,1024]{1,0:T(8,128)(2,1)S(1)} %copy-done.90), channel_id=1, source_target_pairs={{0,1},{1,0},{2,3},{3,2},{4,5},{5,4},{6,7},{7,6},{8,9},{9,8},{10,11... | collective-permute-start | bytes 786440 | tf_op jit(solution)/shard_map/ppermute | solution.py:484
  776.5 47.4 %collective-permute-start.70 = (bf16[48,1024]{1,0:T(8,128)(2,1)S(1)}, bf16[48,1024]{1,0:T(8,128)(2,1)S(1)}, u32[]{:S(2)}, u32[]{:S(2)}) collective-permute-start(bf16[48,1024]{1,0:T(8,128)(2,1)S(1)} %fusion.75), channel_id=1, source_target_pairs={{0,1},{1,0},{2,3},{3,2},{4,5},{5,4},{6,7},{7,6},{8,9},{9,8},{10,11... | collective-permute-start | bytes 294920 | tf_op jit(solution)/shard_map/ppermute | solution.py:484
  780.4 45.6 %collective-permute-start.69 = (bf16[128,1536]{1,0:T(8,128)(2,1)S(1)}, bf16[128,1536]{1,0:T(8,128)(2,1)S(1)}, u32[]{:S(2)}, u32[]{:S(2)}) collective-permute-start(bf16[128,1536]{1,0:T(8,128)(2,1)S(1)} %fusion.58), channel_id=1, source_target_pairs={{0,4},{1,5},{2,6},{3,7},{4,0},{5,1},{6,2},{7,3},{8,12},{9,13},{10,... | collective-permute-start | bytes 1179656 | tf_op jit(solution)/shard_map/ppermute | solution.py:484
  811.4 24.2 %collective-permute-start.68 = (bf16[2,1000,256]{2,1,0:T(8,128)(2,1)S(1)}, bf16[2,1000,256]{2,1,0:T(8,128)(2,1)S(1)}, u32[]{:S(2)}, u32[]{:S(2)}) collective-permute-start(bf16[2,1000,256]{2,1,0:T(8,128)(2,1)S(1)} %fusion.18), channel_id=1, source_target_pairs={{0,2},{1,3},{2,0},{3,1},{4,6},{5,7},{6,4},{7,5},{8,10},{9,11},{10,... | collective-permute-start | bytes 3072008 | tf_op jit(solution)/shard_map/ppermute | solution.py:484
  813.7 26.1 %collective-permute-start.75 = (bf16[128,1536]{1,0:T(8,128)(2,1)S(1)}, bf16[128,1536]{1,0:T(8,128)(2,1)S(1)}, u32[]{:S(2)}, u32[]{:S(2)}) collective-permute-start(bf16[128,1536]{1,0:T(8,128)(2,1)S(1)} %fusion.54), channel_id=1, source_target_pairs={{0,4},{1,5},{2,6},{3,7},{4,0},{5,1},{6,2},{7,3},{8,12},{9,13},{10,... | collective-permute-start | bytes 1179656 | tf_op jit(solution)/shard_map/ppermute | solution.py:484
  836.3 22.6 %collective-permute-start.74 = (bf16[1000,256]{1,0:T(8,128)(2,1)S(1)}, bf16[1000,256]{1,0:T(8,128)(2,1)S(1)}, u32[]{:S(2)}, u32[]{:S(2)}) collective-permute-start(bf16[1000,256]{1,0:T(8,128)(2,1)S(1)} %fusion.39), channel_id=1, source_target_pairs={{0,4},{1,5},{2,6},{3,7},{4,0},{5,1},{6,2},{7,3},{8,12},{9,13},{10,... | collective-permute-start | bytes 1536008 | tf_op jit(solution)/shard_map/ppermute | solution.py:484
  (171 other events, 2153.8 us)

commit v4 on v3

--- a/solution.py
+++ b/solution.py
@@ -465,10 +465,10 @@
 
 
 class Scatter:
-    def __init__(self, blocks, order):
+    def __init__(self, blocks, order, index):
         self.order = list(order)
         self.left = list(range(len(order) - 1, -1, -1))
-        self.index = lax.axis_index("dp")
+        self.index = index
         self.terms = [blocks.reshape((2,) * len(order) + blocks.shape[1:])]
 
     def _side(self, side, at):
@@ -504,14 +504,13 @@
     mark[...] = jnp.zeros_like(mark)
 
 
-def product(left, right, ids, block, part, parts, token):
+def product(left, right, ids, row, count, block, part, parts, token):
     rows, columns = left.shape[0], right.shape[1] // parts
-    count = ids.shape[0]
     tile = 512 if columns % 512 == 0 else columns
     first = part * columns // tile
 
     def pick(j):
-        return pl.BlockSpec((rows, block), lambda i, ids: (0, ids[j]))
+        return pl.BlockSpec((rows, block), lambda i, ids: (0, ids[row, j]))
 
     return pl.pallas_call(
         product_kernel,
@@ -535,22 +534,24 @@
 
 
 class Product(Scatter):
-    def __init__(self, left, right, order, part=0, parts=1):
+    def __init__(self, left, right, order, index, table, first_row, part=0, parts=1):
+        self.table, self.first_row = table, first_row
         self.order = list(order)
         self.bits = len(order)
         self.left = list(range(self.bits - 1, -1, -1))
-        self.index = lax.axis_index("dp")
+        self.index = index
         self.a, self.g = left, right
         self.part, self.parts = part, parts
 
-    def _half(self, side, token):
+    def _half(self, stays, token):
         rows = self.a.shape[1]
         block = rows >> self.bits
-        ids = jnp.array([i for i in range(1 << self.bits) if not (i >> self.bit) & 1], jnp.int32)
-        ids = ids + side.astype(jnp.int32) * (1 << self.bit)
+        count = 1 << (self.bits - 1)
+        row = self.first_row + 2 * self.bit + stays
         if block % 128 == 0:
-            x, mark = product(self.a, self.g, ids, block, self.part, self.parts, token)
+            x, mark = product(self.a, self.g, self.table, row, count, block, self.part, self.parts, token)
         else:
+            ids = self.table[row, :count]
             a = jnp.take(self.a.reshape(self.a.shape[0], -1, block), ids, axis=1).reshape(self.a.shape[0], -1)
             wide = self.g.shape[1] // self.parts
             x = dot_tn(after(a, token), self.g[:, self.part * wide : (self.part + 1) * wide]).astype(BF)
@@ -562,13 +563,13 @@
             self.bit = bit = self.order.pop(0)
             self.left.remove(bit)
             self.mine = (self.index >> bit) & 1
-            sent, mark = self._half(1 - self.mine, token)
+            sent, mark = self._half(0, token)
             self.got = lax.ppermute(sent, "dp", [(i, i ^ (1 << bit)) for i in range(lax.axis_size("dp"))])
             return mark
         return super().send(token)
 
     def keep(self, token):
-        kept, mark = self._half(self.mine, token)
+        kept, mark = self._half(1, token)
         self.terms = [kept]
         return mark
 
@@ -579,6 +580,21 @@
     return jnp.stack(
         [active.astype(jnp.int32), jnp.clip(slot, 0, micro - 1), jnp.full((ticks,), source, jnp.int32)], axis=1
     ).astype(jnp.int32)
+
+
+def with_halves(infos, groups):
+    bits = bits_of(groups)
+    index = lax.axis_index("dp")
+    rows = []
+    for bit in range(bits):
+        base = jnp.array([i for i in range(groups) if not (i >> bit) & 1], jnp.int32)
+        mine = ((index >> bit) & 1).astype(jnp.int32)
+        rows += [base + ((1 - mine) << bit), base + (mine << bit)]
+    rows = jnp.stack(rows)
+    wide = max(infos.shape[1], rows.shape[1])
+    infos = jnp.pad(infos, ((0, 0), (0, wide - infos.shape[1])))
+    rows = jnp.pad(rows, ((0, 0), (0, wide - rows.shape[1])))
+    return jnp.concatenate([infos, rows])
 
 
 def sum_all(x, axis):
@@ -652,6 +668,7 @@
     noise_all = jnp.transpose(noise_all, (1, 0, 2, 3)).reshape(micro, seq_len, emb)
     ids_rows = both_rows[0] - section * vocab_sec
     weight = both_rows[1].astype(F32) * jnp.repeat(valid, seq_len)
+    weight, ids_rows = lax.optimization_barrier((weight, ids_rows))
     onehot = (ids_rows[:, None] == jnp.arange(vocab_sec)[None, :]).astype(BF)
     picked_all = sum_all(dot(onehot, rows_sec).astype(BF), "section")
     sigma = noise_level(time_index)
@@ -665,11 +682,15 @@
     cosines, sines = rope_tables(seq_len, width // HEADS)
     weights = tuple(pltpu.with_memory_space_constraint(w[0], pltpu.VMEM) for w in (w_qkv, w_out, w_up, w_down))
 
-    stores = blanks(store_shapes(micro, seq_len, width, hidden))
+    stores = blanks(store_shapes(micro, seq_len, width, hidden) + [jax.ShapeDtypeStruct((seq_len, width), BF)])
+    stores, unused = stores[:-1], stores[-1]
     offset = delay(section)
     ticks = micro + delay(last)
-    infos = tick_infos(ticks, offset, micro, jnp.where(section == 0, 0, jnp.where(section % 2 == 1, 1, 2)))
-    core_in = x_next = x_in = entry[0]
+    back_offset = delay(last) - offset
+    ahead = tick_infos(ticks, offset, micro, jnp.where(section == 0, 0, jnp.where(section % 2 == 1, 1, 2)))
+    back = tick_infos(ticks, back_offset, micro, jnp.where(section == last, 0, jnp.where(section % 2 == 0, 1, 2)))
+    infos = lax.optimization_barrier(with_halves(jnp.concatenate([ahead, back]), groups))
+    core_in = x_next = x_in = unused
     tick_sums = []
     finals = []
     for tick in range(ticks):
@@ -710,19 +731,15 @@
 
     saved = [stores[0], stores[2], stores[3], stores[5], stores[7]]
     grads = blanks(grad_shapes(micro, seq_len, width, hidden))
-    back_offset = delay(last) - offset
-    infos = tick_infos(ticks, back_offset, micro, jnp.where(section == last, 0, jnp.where(section % 2 == 0, 1, 2)))
-    core_in = x_next = x_in = exit_grad[0]
+    core_in = x_next = x_in = unused
     tick_rows = []
     sums = jnp.sum(lax.dynamic_slice_in_dim(jnp.stack(tick_sums), offset, micro, 0), axis=2)
     square_sums = jnp.sum(sums * valid[:, None], axis=0)
     for tick in range(ticks):
         sent, rows, grads = layer_backward(
-            tick, infos, core_in, x_in, exit_grad, time_rows, gain_attn, gain_mlp, cosines, sines, *weights, saved, grads
+            ticks + tick, infos, core_in, x_in, exit_grad, time_rows, gain_attn, gain_mlp, cosines, sines, *weights, saved, grads
         )
         tick_rows.append(rows)
-        if tick < bits_of(groups):
-            square_sums = square_sums + after(swap(square_sums, "dp", tick), rows)
         going = [s for s in range(1, sections) if 0 <= tick - (delay(last) - delay(s)) < micro]
         core_pairs = [(s, s - 1) for s in going if s % 2 == 1]
         x_pairs = [(s, s - 1) for s in going if s % 2 == 0]
@@ -736,33 +753,48 @@
         stores[i].reshape(tokens, stores[i].shape[2]) for i in (1, 4, 6, 8)
     )
 
-    out = Product(context_all, grad_attn_all, high_first)
-    down = Product(activated_all, grad_out_all, low_first)
-    up = Product(mlp_in_all, grad_pre_all, low_first)
-    qkv = [Product(attn_in_all, grad_mixed_all, low_first, part, 2) for part in range(2)]
-    token = down.send(square_sums)
-    token = up.send(token)
+    dp_index = lax.axis_index("dp")
+    out = Product(context_all, grad_attn_all, high_first, dp_index, infos, 2 * ticks)
+    down = [Product(activated_all, grad_out_all, low_first, dp_index, infos, 2 * ticks, part, 2) for part in range(2)]
+    up = [Product(mlp_in_all, grad_pre_all, low_first, dp_index, infos, 2 * ticks, part, 2) for part in range(2)]
+    qkv = [Product(attn_in_all, grad_mixed_all, low_first, dp_index, infos, 2 * ticks, part, 2) for part in range(2)]
+    token = down[0].send(grad_first_all)
+    token = down[1].send(token)
     token = out.send(token)
+    token = up[0].send(token)
     token = out.keep(token)
-    token = qkv[0].send(token)
-    token = qkv[1].send(token)
-    token = qkv[0].keep(token)
-    token = qkv[1].keep(token)
-    token = up.keep(token)
-    token = down.keep(token)
-    token = out.step(None)
-    token = out.step(None)
-    token = down.step(token)
+    token = down[1].keep(token)
+    token = up[0].keep(token)
+    token = down[0].keep(token)
+    token = down[0].step(None)
 
     grad_inputs = (dot_nt(grad_first_all, proj_full) + zero_of(token)).astype(BF)
     grad_inputs = spread(grad_inputs, "section", 0).astype(F32)
     row_terms = grad_inputs * jnp.repeat(shrink, seq_len)[:, None] - latent.astype(F32) * weight[:, None]
+    zero = zero_of(token)
     grad_table = head_backward(
-        rows_sec, latent, log_total[None, :], weight[None, :], ids_rows[None, :], row_terms.astype(BF), token
+        rows_sec,
+        latent,
+        log_total[None, :] + zero,
+        (weight + zero)[None, :],
+        (ids_rows + zero.astype(jnp.int32))[None, :],
+        row_terms.astype(BF),
+        token,
     )
-    tab = Scatter(grad_table.reshape(groups, -1, emb), low_first)
+    tab = Scatter(grad_table.reshape(groups, -1, emb), low_first, dp_index)
     token = tab.send(token)
-    token = down.step(token)
+    token = up[1].send(token)
+    token = up[1].keep(token)
+    token = down[1].step(token)
+    token = down[0].step(token)
+    token = out.step(token)
+    for part in qkv:
+        token = part.send(token)
+        token = part.keep(token)
+    token = up[0].step(token)
+    token = down[1].step(token)
+    token = down[0].end(token)
+    token = out.step(token)
     grad_proj = grad_proj + jnp.where(section == 0, dot_tn(inputs_all, after(grad_first_all, token)), 0.0)
     proj_part = scatter_sum(grad_proj.astype(BF).reshape(sections, emb // sections, width), "section", section_order[::-1])
     rows = lax.dynamic_slice_in_dim(jnp.stack(tick_rows), back_offset, micro, 0)
@@ -781,25 +813,28 @@
         ],
         axis=1,
     )
-    pack = Scatter(packed, high_first)
+    pack = Scatter(packed, high_first, dp_index)
     token = pack.send(token)
-    token = up.step(token)
-    token = down.end(token)
+    token = tab.step(token)
+    token = up[0].step(token)
+    token = down[1].end(token)
+    token = pack.step(token)
+    token = up[1].step(token)
+    token = tab.step(token)
+    token = up[0].end(token)
     token = pack.step(token)
     token = qkv[0].step(token)
-    token = up.step(token)
-    token = pack.step(token)
+    token = up[1].step(token)
+    token = tab.end(token)
     token = qkv[1].step(token)
     token = qkv[0].step(token)
-    token = tab.step(token)
+    token = up[1].end(token)
+    square_sums = sum_all(after(square_sums, token), "dp")
+    token = qkv[0].end(token)
     token = qkv[1].step(token)
-    token = up.end(token)
     token = out.end(token)
     token = pack.end(token)
-    token = qkv[0].end(token)
-    token = tab.step(token)
     token = qkv[1].end(token)
-    token = tab.end(token)
     target_logit = jnp.sum(latent.astype(F32) * picked_all.astype(F32), axis=1)
     token_loss = (log_total - target_logit) * weight
     seq_loss = jnp.sum(token_loss.reshape(micro, seq_len), axis=1) / seq_len
@@ -807,8 +842,8 @@
     layer_rms = jnp.sqrt(square_sums / (count_all * seq_len * width))[None, :]
     packed = pack.total
     w_out_grad = out.total
-    w_down_grad = down.total
-    w_up_grad = up.total
+    w_down_grad = jnp.concatenate([part.total for part in down], axis=1)
+    w_up_grad = jnp.concatenate([part.total for part in up], axis=1)
     w_qkv_grad = jnp.concatenate([qkv[0].total, qkv[1].total], axis=1)
     w_time_grad = packed[: at[0]]
     proj_grad = packed[at[0] : sum(at)]

time: 871 us -> 857 us (0.984)
  waiting for transfers between devices: 359 us -> 328 us
  local copies, waits for them, and re-layouts: 71.5 us -> 83.2 us
    ppermute x21 -> x27, waiting for transfers between devices: 182 us -> 152 us  [send(): lax.ppermute(sent, 'dp', [(i, i ^ 1 << bit) for i in range(lax.axis_size(...]
    unnamed x302 -> x320, local copies, waits for them, and re-layouts: 41.7 us -> 53 us
    ppermute x21 -> x27, starting transfers between devices: 33.5 us -> 29 us  [send(): lax.ppermute(sent, 'dp', [(i, i ^ 1 << bit) for i in range(lax.axis_size(...]
    pallas_call x10 -> x14, Pallas kernels: 43.3 us -> 46.5 us  [product(): pl.pallas_call(product_kernel, grid_spec=pltpu.PrefetchScalarGridSpec(num...]
    convert_element_type x16 -> x20, other arithmetic: 23.1 us -> 19.9 us  [send(): (self._side(1 - mine, at) + (0.0 if token is None else zero_of(token))).a...]
    slice x37 -> x41, local copies, waits for them, and re-layouts: 20.9 us -> 22.7 us  [zero_of(): return jnp.minimum(jnp.abs(token[(0,) * token.ndim].astype(F32)), 0.0)]
  transfers between devices with their start and end apart: 76 -> 82, of which waited for: 38 -> 45; matrix products, arithmetic and copies ran while one was open for 10% -> 11% of each run, Pallas kernels for 17% -> 16%
where the time goes in v4:
time: 857 us; the launch traced here: 850 us
  waiting for transfers between devices  328 us (38%)
  Pallas kernels  234 us (27%)
  starting transfers between devices  90 us (11%)
  local copies, waits for them, and re-layouts  83.2 us (10%)
  other arithmetic  68.4 us (8%)
  between operations  31.8 us (4%)
  matrix products  14.1 us (2%)
    ppermute x27, waiting for transfers between devices, send(): lax.ppermute(sent, 'dp', [(i, i ^ 1 << bit) for i in range(lax.axis_size(...  152 us
    pallas_call x8, Pallas kernels, layer_backward(): pl.pallas_call(functools.partial(bwd_kernel, tick), in_specs=[SM, VM, HB,...  83 us
    ppermute x29, waiting for transfers between devices, swap(): return lax.ppermute(x, axis, pairs)  80.7 us
    pallas_call x8, Pallas kernels, layer_forward(): pl.pallas_call(functools.partial(fwd_kernel, tick), in_specs=[SM, VM, HB,...  76.7 us
    unnamed x320, local copies, waits for them, and re-layouts  53 us
    ppermute x14, waiting for transfers between devices, body(): core_in = lax.ppermute(sent, 'section', core_pairs) if core_pairs else sent  52.4 us
    pallas_call x14, Pallas kernels, product(): pl.pallas_call(product_kernel, grid_spec=pltpu.PrefetchScalarGridSpec(num...  46.5 us
    ppermute x4, waiting for transfers between devices, spread(): got = lax.ppermute(x, axis, pairs)  42.3 us
  transfers between devices with their start and end apart: 82, of which 45 were waited for; matrix products, arithmetic and copies ran while one was open for 11% of the time, Pallas kernels for 16%

profile of v4, /device:TPU:0, one launch (start us, length us, event | category | flops | bytes accessed | tf_op | source)
XLA Modules:
  0.0 849.7 jit_solution(6511020737528878873)
XLA Ops:
  4.0 4.1 collective-permute-start
  59.0 6.7 collective-permute-done.9
  67.2 10.4 %collective-permute-done.10 = bf16[2,2,272,256]{3,2,0,1:T(8,128)(2,1)S(1)} collective-permute-done((bf16[2,2,272,256]{3,2,0,1:T(8,128)(2,1)S(1)}, bf16[2,2,272,256]{3,2,0,1:T(8,128)(2,1)S(1)}, u32[]{:S(2)}, u32[]{:S(2)}) %collective-permute-start.10) | collective-permute-done | bytes 557088 | tf_op jit(solution)/shard_map/ppermute | solution.py:405
  79.2 6.8 collective-permute-done.11
  87.1 4.2 fusion.24
  98.5 5.8 collective-permute-done.17
  110.0 7.9 collective-permute-done.15
  129.6 14.2 %layer_fwd.8 = (bf16[192,1024]{1,0:T(8,128)(2,1)S(1)}, f32[3,1024]{1,0:T(4,128)S(1)}, bf16[4,192,1024]{2,1,0:T(8,128)(2,1)}, bf16[4,192,1024]{2,1,0:T(8,128)(2,1...) custom-call(s32[22,4]{1,0:T(8,128)S(1)} %copy.296.info.ids, ...), custom_call_target="tpu_custom_call", output_to_operand_aliasing={{2}: (13, {}), {3}: (14, {}), {4}: (15, {}), {5}: (16, {}),... | custom-call | flops 4831838208 | bytes 33554432 | tf_op jit(solution)/shard_map/layer_fwd/pallas_call | solution.py:148
  146.4 13.8 %layer_fwd.9 = (bf16[192,1024]{1,0:T(8,128)(2,1)S(1)}, f32[3,1024]{1,0:T(4,128)S(1)}, bf16[4,192,1024]{2,1,0:T(8,128)(2,1)}, bf16[4,192,1024]{2,1,0:T(8,128)(2,1...) custom-call(s32[22,4]{1,0:T(8,128)S(1)} %copy.296.info.ids, ...), custom_call_target="tpu_custom_call", output_to_operand_aliasing={{2}: (13, {}), {3}: (14, {}), {4}: (15, {}), {5}: (16, {}),... | custom-call | flops 4831838208 | bytes 33554432 | tf_op jit(solution)/shard_map/layer_fwd/pallas_call | solution.py:148
  162.9 14.2 %layer_fwd.10 = (bf16[192,1024]{1,0:T(8,128)(2,1)S(1)}, f32[3,1024]{1,0:T(4,128)S(1)}, bf16[4,192,1024]{2,1,0:T(8,128)(2,1)}, bf16[4,192,1024]{2,1,0:T(8,128)(2,...) custom-call(s32[22,4]{1,0:T(8,128)S(1)} %copy.296.info.ids, ...), custom_call_target="tpu_custom_call", output_to_operand_aliasing={{2}: (13, {}), {3}: (14, {}), {4}: (15, {}), {5}: (16, {}),... | custom-call | flops 4831838208 | bytes 33554432 | tf_op jit(solution)/shard_map/layer_fwd/pallas_call | solution.py:148
  180.1 13.8 %layer_fwd.11 = (bf16[192,1024]{1,0:T(8,128)(2,1)S(1)}, f32[3,1024]{1,0:T(4,128)S(1)}, bf16[4,192,1024]{2,1,0:T(8,128)(2,1)}, bf16[4,192,1024]{2,1,0:T(8,128)(2,...) custom-call(s32[22,4]{1,0:T(8,128)S(1)} %copy.296.info.ids, ...), custom_call_target="tpu_custom_call", output_to_operand_aliasing={{2}: (13, {}), {3}: (14, {}), {4}: (15, {}), {5}: (16, {}),... | custom-call | flops 4831838208 | bytes 33554432 | tf_op jit(solution)/shard_map/layer_fwd/pallas_call | solution.py:148
  196.8 8.3 layer_fwd.12
  209.6 10.5 %layer_fwd.14 = (bf16[192,1024]{1,0:T(8,128)(2,1)S(1)}, f32[3,1024]{1,0:T(4,128)S(1)}, bf16[4,192,1024]{2,1,0:T(8,128)(2,1)}, bf16[4,192,1024]{2,1,0:T(8,128)(2,...) custom-call(s32[22,4]{1,0:T(8,128)S(1)} %copy.296.info.ids, ...), custom_call_target="tpu_custom_call", output_to_operand_aliasing={{2}: (13, {}), {3}: (14, {}), {4}: (15, {}), {5}: (16, {}),... | custom-call | flops 4831838208 | bytes 33554432 | tf_op jit(solution)/shard_map/layer_fwd/pallas_call | solution.py:148
  227.0 3.6 collective-permute-start.32
  230.6 38.6 %collective-permute-done.32 = bf16[768,256]{1,0:T(8,128)(2,1)} collective-permute-done((bf16[768,256]{1,0:T(8,128)(2,1)}, bf16[768,256]{1,0:T(8,128)(2,1)}, u32[]{:S(2)}, u32[]{:S(2)}) %collective-permute-start.32) | collective-permute-done | bytes 393248 | tf_op jit(solution)/shard_map/ppermute | solution.py:611
  273.6 16.8 %head_fwd.1 = (bf16[256,768]{1,0:T(8,128)(2,1)S(1)}, f32[2,768]{1,0:T(2,128)S(1)}) custom-call(bf16[8000,256]{1,0:T(8,128)(2,1)S(1)} %bitcast.592, bf16[768,256]{1,0:T(8,128)(2,1)S(1)} %get-tuple-element.412.latent), custom_call_target="tpu_custom_call" | custom-call | flops 6291456000 | bytes 4096000 | tf_op jit(solution)/shard_map/head_fwd/pallas_call | solution.py:333
  299.9 8.2 collective-permute-done.36
  313.5 3.4 copy-done.5
  324.1 12.4 %layer_bwd.10 = (bf16[192,1024]{1,0:T(8,128)(2,1)S(1)}, f32[3,1024]{1,0:T(4,128)S(1)}, bf16[4,192,1024]{2,1,0:T(8,128)(2,1)}, bf16[4,192,4096]{2,1,0:T(8,128)(2,...) custom-call(s32[22,4]{1,0:T(8,128)S(1)} %copy.296.info.ids, ...), custom_call_target="tpu_custom_call", output_to_operand_aliasing={{2}: (18, {}), {3}: (19, {}), {4}: (20, {}), {5}: (21, {}),... | custom-call | flops 4831838208 | bytes 33554432 | tf_op jit(solution)/shard_map/layer_bwd/pallas_call | solution.py:262
  342.3 42.3 %collective-permute-done.41.g_in = bf16[192,1024]{1,0:T(8,128)(2,1)S(1)} collective-permute-done((bf16[192,1024]{1,0:T(8,128)(2,1)S(1)}, bf16[192,1024]{1,0:T(8,128)(2,1)S(1)}, u32[]{:S(2)}, u32[]{:S(2)}) %collective-permute-start.41) | collective-permute-done | bytes 393248 | tf_op jit(solution)/shard_map/ppermute | solution.py:746
  384.6 17.2 %layer_bwd.12 = (bf16[192,1024]{1,0:T(8,128)(2,1)}, f32[3,1024]{1,0:T(4,128)S(1)}, bf16[4,192,1024]{2,1,0:T(8,128)(2,1)}, bf16[4,192,4096]{2,1,0:T(8,128)(2,1)},...) custom-call(s32[22,4]{1,0:T(8,128)S(1)} %copy.296.info.ids, ...), custom_call_target="tpu_custom_call", output_to_operand_aliasing={{2}: (18, {}), {3}: (19, {}), {4}: (20, {}), {5}: (21, {}),... | custom-call | flops 4831838208 | bytes 33554432 | tf_op jit(solution)/shard_map/layer_bwd/pallas_call | solution.py:262
  406.9 3.4 copy-done.3
  416.5 16.1 %layer_bwd.13 = (bf16[192,1024]{1,0:T(8,128)(2,1)S(1)}, f32[3,1024]{1,0:T(4,128)S(1)}, bf16[4,192,1024]{2,1,0:T(8,128)(2,1)}, bf16[4,192,4096]{2,1,0:T(8,128)(2,...) custom-call(s32[22,4]{1,0:T(8,128)S(1)} %copy.296.info.ids, ...), custom_call_target="tpu_custom_call", output_to_operand_aliasing={{2}: (18, {}), {3}: (19, {}), {4}: (20, {}), {5}: (21, {}),... | custom-call | flops 4831838208 | bytes 33554432 | tf_op jit(solution)/shard_map/layer_bwd/pallas_call | solution.py:262
  436.2 16.7 %layer_bwd.14 = (bf16[192,1024]{1,0:T(8,128)(2,1)S(1)}, f32[3,1024]{1,0:T(4,128)S(1)}, bf16[4,192,1024]{2,1,0:T(8,128)(2,1)}, bf16[4,192,4096]{2,1,0:T(8,128)(2,...) custom-call(s32[22,4]{1,0:T(8,128)S(1)} %copy.296.info.ids, ...), custom_call_target="tpu_custom_call", output_to_operand_aliasing={{2}: (18, {}), {3}: (19, {}), {4}: (20, {}), {5}: (21, {}),... | custom-call | flops 4831838208 | bytes 33554432 | tf_op jit(solution)/shard_map/layer_bwd/pallas_call | solution.py:262
  456.6 17.4 %layer_bwd.15 = (bf16[192,1024]{1,0:T(8,128)(2,1)}, f32[3,1024]{1,0:T(4,128)S(1)}, bf16[4,192,1024]{2,1,0:T(8,128)(2,1)}, bf16[4,192,4096]{2,1,0:T(8,128)(2,1)},...) custom-call(s32[22,4]{1,0:T(8,128)S(1)} %copy.296.info.ids, ...), custom_call_target="tpu_custom_call", output_to_operand_aliasing={{2}: (18, {}), {3}: (19, {}), {4}: (20, {}), {5}: (21, {}),... | custom-call | flops 4831838208 | bytes 33554432 | tf_op jit(solution)/shard_map/layer_bwd/pallas_call | solution.py:262
  484.4 3.9 product.15
  491.5 4.6 product.17
  502.4 3.8 product.20
  511.1 17.7 %collective-permute-done.48 = bf16[2,2,512,512]{3,2,1,0:T(8,128)(2,1)S(1)} collective-permute-done((bf16[2,2,512,512]{3,2,1,0:T(8,128)(2,1)S(1)}, bf16[2,2,512,512]{3,2,1,0:T(8,128)(2,1)S(1)}, u32[]{:S(2)}, u32[]{:S(2)}) %collective-permute-start.48) | collective-permute-done | bytes 2097184 | tf_op jit(solution)/shard_map/ppermute | solution.py:567
  544.9 3.7 collective-permute-done.50
  552.7 11.5 %head_bwd.1 = bf16[8000,256]{1,0:T(8,128)(2,1)S(1)} custom-call(bf16[8000,256]{1,0:T(8,128)(2,1)S(1)} %bitcast.593, bf16[768,256]{1,0:T(8,128)(2,1)S(1)} %copy-done.29, f32[1,768]{1,0:T(1,128)S(1)} %get-tuple-element.446.log_total, f32[1,768]{1,0:T(1,128)S(1)} %broadcast_in_dim.29.weight, s32[1,768]{1,0:T(1,128)S(1)} %broadcast_in_dim.30.ids, ...), custom_call_target="tpu_custom_call" | custom-call | flops 1 | bytes 1 | tf_op jit(solution)/shard_map/head_bwd/pallas_call | solution.py:358
  566.7 3.9 product.22
  571.9 3.9 product.23
  584.7 4.0 collective-permute-start.56
  613.6 5.2 collective-permute-done.58
  629.0 8.4 collective-permute-done.55
  654.7 8.0 collective-permute-done.64
  665.5 18.8 %collective-permute-done.63 = bf16[2,128,2048]{2,1,0:T(8,128)(2,1)S(1)} collective-permute-done((bf16[2,128,2048]{2,1,0:T(8,128)(2,1)S(1)}, bf16[2,128,2048]{2,1,0:T(8,128)(2,1)S(1)}, u32[]{:S(2)}, u32[]{:S(2)}) %collective-permute-start.63) | collective-permute-done | bytes 1048608 | tf_op jit(solution)/shard_map/ppermute | solution.py:484
  694.5 13.1 %collective-permute-done.51 = bf16[2,2,128,2048]{3,2,1,0:T(8,128)(2,1)} collective-permute-done((bf16[2,2,128,2048]{3,2,1,0:T(8,128)(2,1)}, bf16[2,2,128,2048]{3,2,1,0:T(8,128)(2,1)}, u32[]{:S(2)}, u32[]{:S(2)}) %collective-permute-start.51) | collective-permute-done | bytes 2097184 | tf_op jit(solution)/shard_map/ppermute | solution.py:567
  711.9 13.9 %collective-permute-done.69 = bf16[2,1000,256]{2,1,0:T(8,128)(2,1)S(1)} collective-permute-done((bf16[2,1000,256]{2,1,0:T(8,128)(2,1)S(1)}, bf16[2,1000,256]{2,1,0:T(8,128)(2,1)S(1)}, u32[]{:S(2)}, u32[]{:S(2)}) %collective-permute-start.69) | collective-permute-done | bytes 1024032 | tf_op jit(solution)/shard_map/ppermute | solution.py:484
  733.4 15.6 %collective-permute-done.67 = bf16[2,48,1024]{2,1,0:T(8,128)(2,1)S(1)} collective-permute-done((bf16[2,48,1024]{2,1,0:T(8,128)(2,1)S(1)}, bf16[2,48,1024]{2,1,0:T(8,128)(2,1)S(1)}, u32[]{:S(2)}, u32[]{:S(2)}) %collective-permute-start.67) | collective-permute-done | bytes 196640 | tf_op jit(solution)/shard_map/ppermute | solution.py:484
  749.1 3.4 collective-permute-start.73
  760.2 14.3 %collective-permute-done.73 = bf16[1000,256]{1,0:T(8,128)(2,1)S(1)} collective-permute-done((bf16[1000,256]{1,0:T(8,128)(2,1)S(1)}, bf16[1000,256]{1,0:T(8,128)(2,1)S(1)}, u32[]{:S(2)}, u32[]{:S(2)}) %collective-permute-start.73) | collective-permute-done | bytes 512032 | tf_op jit(solution)/shard_map/ppermute | solution.py:484
  781.4 7.1 collective-permute-done.71
  789.8 10.6 %collective-permute-done.70 = bf16[128,2048]{1,0:T(8,128)(2,1)S(1)} collective-permute-done((bf16[128,2048]{1,0:T(8,128)(2,1)S(1)}, bf16[128,2048]{1,0:T(8,128)(2,1)S(1)}, u32[]{:S(2)}, u32[]{:S(2)}) %collective-permute-start.70) | collective-permute-done | bytes 524320 | tf_op jit(solution)/shard_map/ppermute | solution.py:484
  808.8 7.5 collective-permute-done.75
  817.6 14.2 %collective-permute-done.78 = bf16[128,1536]{1,0:T(8,128)(2,1)S(1)} collective-permute-done((bf16[128,1536]{1,0:T(8,128)(2,1)S(1)}, bf16[128,1536]{1,0:T(8,128)(2,1)S(1)}, u32[]{:S(2)}, u32[]{:S(2)}) %collective-permute-start.78) | collective-permute-done | bytes 393248 | tf_op jit(solution)/shard_map/ppermute | solution.py:484
  840.0 5.0 collective-permute-done.79
  (708 shorter events, 299.2 us)
Async XLA Ops:
  4.0 19.9 %collective-permute-start = (bf16[272,256]{1,0:T(8,128)(2,1)S(1)}, bf16[272,256]{1,0:T(8,128)(2,1)S(1)}, u32[]{:S(2)}, u32[]{:S(2)}) collective-permute-start(bf16[272,256]{1,0:T(8,128)(2,1)S(1)} %get-tuple-element.423), channel_id=1, source_target_pairs={{0,4},{1,5},{2,6},{3,7},{4,0},{5,1},{6,2},{7,3},{8,12},{9,13},{10,... | collective-permute-start | bytes 417800 | tf_op jit(solution)/shard_map/ppermute | solution.py:405
  8.1 18.9 %collective-permute-start.4 = (bf16[272,256]{1,0:T(8,128)(2,1)S(1)}, bf16[272,256]{1,0:T(8,128)(2,1)S(1)}, u32[]{:S(2)}, u32[]{:S(2)}) collective-permute-start(bf16[272,256]{1,0:T(8,128)(2,1)S(1)} %get-tuple-element.421), channel_id=1, source_target_pairs={{0,4},{1,5},{2,6},{3,7},{4,0},{5,1},{6,2},{7,3},{8,12},{9,13},{10,... | collective-permute-start | bytes 417800 | tf_op jit(solution)/shard_map/ppermute | solution.py:405
  8.2 21.8 %collective-permute-start.3 = (bf16[272,256]{1,0:T(8,128)(2,1)S(1)}, bf16[272,256]{1,0:T(8,128)(2,1)S(1)}, u32[]{:S(2)}, u32[]{:S(2)}) collective-permute-start(bf16[272,256]{1,0:T(8,128)(2,1)S(1)} %get-tuple-element.422), channel_id=1, source_target_pairs={{0,4},{1,5},{2,6},{3,7},{4,0},{5,1},{6,2},{7,3},{8,12},{9,13},{10,... | collective-permute-start | bytes 417800 | tf_op jit(solution)/shard_map/ppermute | solution.py:405
  11.1 20.5 %collective-permute-start.2 = (bf16[216,256]{1,0:T(8,128)(2,1)S(1)}, bf16[216,256]{1,0:T(8,128)(2,1)S(1)}, u32[]{:S(2)}, u32[]{:S(2)}) collective-permute-start(bf16[216,256]{1,0:T(8,128)(2,1)S(1)} %pad_maximum_fusion.8), channel_id=1, source_target_pairs={{0,4},{1,5},{2,6},{3,7},{4,0},{5,1},{6,2},{7,3},{8,12},{9,13},{10,... | collective-permute-start | bytes 331784 | tf_op jit(solution)/shard_map/ppermute | solution.py:405
  19.7 71.7 %collective-permute-start.16 = (f32[4,48,256]{2,1,0:T(8,128)S(1)}, f32[4,48,256]{2,1,0:T(8,128)S(1)}, u32[]{:S(2)}, u32[]{:S(2)}) collective-permute-start(f32[4,48,256]{2,1,0:T(8,128)S(1)} %copy-done.96), channel_id=1, source_target_pairs={{0,8},{8,0},{16,24},{24,16},{1,9},{9,1},{17,25},{25,17},{2,10},{10... | collective-permute-start | bytes 589832 | tf_op jit(solution)/shard_map/ppermute | solution.py:405
  27.6 15.9 %collective-permute-start.8 = (bf16[2,272,256]{2,1,0:T(8,128)(2,1)S(1)}, bf16[2,272,256]{2,1,0:T(8,128)(2,1)S(1)}, u32[]{:S(2)}, u32[]{:S(2)}) collective-permute-start(bf16[2,272,256]{2,1,0:T(8,128)(2,1)S(1)} %maximum_select_fusion.15), channel_id=1, source_target_pairs={{0,2},{1,3},{2,0},{3,1},{4,6},{5,7},{6,4},{7,5},{8,10},{9,11},{10,... | collective-permute-start | bytes 835592 | tf_op jit(solution)/shard_map/ppermute | solution.py:405
  30.6 18.9 %collective-permute-start.7 = (bf16[2,272,256]{2,1,0:T(8,128)(2,1)S(1)}, bf16[2,272,256]{2,1,0:T(8,128)(2,1)S(1)}, u32[]{:S(2)}, u32[]{:S(2)}) collective-permute-start(bf16[2,272,256]{2,1,0:T(8,128)(2,1)S(1)} %maximum_select_fusion.16), channel_id=1, source_target_pairs={{0,2},{1,3},{2,0},{3,1},{4,6},{5,7},{6,4},{7,5},{8,10},{9,11},{10,... | collective-permute-start | bytes 835592 | tf_op jit(solution)/shard_map/ppermute | solution.py:405
  31.8 22.3 %collective-permute-start.6 = (bf16[2,216,256]{2,1,0:T(8,128)(2,1)S(1)}, bf16[2,216,256]{2,1,0:T(8,128)(2,1)S(1)}, u32[]{:S(2)}, u32[]{:S(2)}) collective-permute-start(bf16[2,216,256]{2,1,0:T(8,128)(2,1)S(1)} %maximum_select_fusion.19), channel_id=1, source_target_pairs={{0,2},{1,3},{2,0},{3,1},{4,6},{5,7},{6,4},{7,5},{8,10},{9,11},{10,... | collective-permute-start | bytes 663560 | tf_op jit(solution)/shard_map/ppermute | solution.py:405
  38.2 19.3 %collective-permute-start.5 = (bf16[2,2,272,256]{3,2,0,1:T(8,128)(2,1)S(1)}, bf16[2,2,272,256]{3,2,0,1:T(8,128)(2,1)S(1)}, u32[]{:S(2)}, u32[]{:S(2)}) collective-permute-start(bf16[2,2,272,256]{3,2,0,1:T(8,128)(2,1)S(1)} %maximum_select_fusion.6), channel_id=1, source_target_pairs={{0,1},{1,0},{2,3},{3,2},{4,5},{5,4},{6,7},{7,6},{8,9},{9,8},{10,11... | collective-permute-start | bytes 1671176 | tf_op jit(solution)/shard_map/ppermute | solution.py:405
  44.2 21.5 %collective-permute-start.9 = (bf16[2,2,272,256]{3,2,0,1:T(8,128)(2,1)S(1)}, bf16[2,2,272,256]{3,2,0,1:T(8,128)(2,1)S(1)}, u32[]{:S(2)}, u32[]{:S(2)}) collective-permute-start(bf16[2,2,272,256]{3,2,0,1:T(8,128)(2,1)S(1)} %maximum_select_fusion.7), channel_id=1, source_target_pairs={{0,1},{1,0},{2,3},{3,2},{4,5},{5,4},{6,7},{7,6},{8,9},{9,8},{10,11... | collective-permute-start | bytes 1671176 | tf_op jit(solution)/shard_map/ppermute | solution.py:405
  50.1 27.4 %collective-permute-start.10 = (bf16[2,2,272,256]{3,2,0,1:T(8,128)(2,1)S(1)}, bf16[2,2,272,256]{3,2,0,1:T(8,128)(2,1)S(1)}, u32[]{:S(2)}, u32[]{:S(2)}) collective-permute-start(bf16[2,2,272,256]{3,2,0,1:T(8,128)(2,1)S(1)} %maximum_select_fusion.8), channel_id=1, source_target_pairs={{0,1},{1,0},{2,3},{3,2},{4,5},{5,4},{6,7},{7,6},{8,9},{9,8},{10,11... | collective-permute-start | bytes 1671176 | tf_op jit(solution)/shard_map/ppermute | solution.py:405
  54.3 31.7 %collective-permute-start.11 = (bf16[2,2,216,256]{3,2,1,0:T(8,128)(2,1)S(1)}, bf16[2,2,216,256]{3,2,1,0:T(8,128)(2,1)S(1)}, u32[]{:S(2)}, u32[]{:S(2)}) collective-permute-start(bf16[2,2,216,256]{3,2,1,0:T(8,128)(2,1)S(1)} %copy_select_fusion), channel_id=1, source_target_pairs={{0,1},{1,0},{2,3},{3,2},{4,5},{5,4},{6,7},{7,6},{8,9},{9,8},{10,11... | collective-permute-start | bytes 1327112 | tf_op jit(solution)/shard_map/ppermute | solution.py:405
  95.2 14.6 %collective-permute-start.19 = (bf16[2,64,1024]{2,1,0:T(8,128)(2,1)S(1)}, bf16[2,64,1024]{2,1,0:T(8,128)(2,1)S(1)}, u32[]{:S(2)}, u32[]{:S(2)}) collective-permute-start(bf16[2,64,1024]{2,1,0:T(8,128)(2,1)S(1)} %maximum_select_fusion.18), channel_id=1, source_target_pairs={{0,16},{8,24},{16,0},{24,8},{1,17},{9,25},{17,1},{25,9},{2,18},{10... | collective-permute-start | bytes 786440 | tf_op jit(solution)/shard_map/ppermute | solution.py:405
  96.9 21.0 %collective-permute-start.15 = (bf16[768,256]{1,0:T(8,128)(2,1)S(1)}, bf16[768,256]{1,0:T(8,128)(2,1)S(1)}, u32[]{:S(2)}, u32[]{:S(2)}) collective-permute-start(bf16[768,256]{1,0:T(8,128)(2,1)S(1)} %add.1006), channel_id=1, source_target_pairs={{0,16},{8,24},{16,0},{24,8},{1,17},{9,25},{17,1},{25,9},{2,18},{10... | collective-permute-start | bytes 1179656 | tf_op jit(solution)/shard_map/ppermute | solution.py:405
  161.6 17.8 %collective-permute-start.23 = (bf16[192,1024]{1,0:T(8,128)(2,1)S(1)}, bf16[192,1024]{1,0:T(8,128)(2,1)S(1)}, u32[]{:S(2)}, u32[]{:S(2)}) collective-permute-start(bf16[192,1024]{1,0:T(8,128)(2,1)S(1)} %get-tuple-element.223), channel_id=1, source_target_pairs={{8,16},{9,17},{10,18},{11,19},{12,20},{13,21},{14,22},{15,23}} | collective-permute-start | bytes 1179656 | tf_op jit(solution)/shard_map/ppermute | solution.py:708
  178.7 17.3 %collective-permute-start.25 = (bf16[192,1024]{1,0:T(8,128)(2,1)S(1)}, bf16[192,1024]{1,0:T(8,128)(2,1)S(1)}, u32[]{:S(2)}, u32[]{:S(2)}) collective-permute-start(bf16[192,1024]{1,0:T(8,128)(2,1)S(1)} %get-tuple-element.233), channel_id=1, source_target_pairs={{8,16},{9,17},{10,18},{11,19},{12,20},{13,21},{14,22},{15,23}} | collective-permute-start | bytes 1179656 | tf_op jit(solution)/shard_map/ppermute | solution.py:708
  227.0 42.2 %collective-permute-start.32 = (bf16[768,256]{1,0:T(8,128)(2,1)}, bf16[768,256]{1,0:T(8,128)(2,1)}, u32[]{:S(2)}, u32[]{:S(2)}) collective-permute-start(bf16[768,256]{1,0:T(8,128)(2,1)} %broadcast_select_fusion.1), channel_id=1, source_target_pairs={{24,8},{16,0},{25,9},{17,1},{26,10},{18,2},{27,11},{19,3},{28,12},... | collective-permute-start | bytes 1179656 | tf_op jit(solution)/shard_map/ppermute | solution.py:611
  323.4 14.5 %collective-permute-start.40 = (bf16[192,1024]{1,0:T(8,128)(2,1)S(1)}, bf16[192,1024]{1,0:T(8,128)(2,1)S(1)}, u32[]{:S(2)}, u32[]{:S(2)}) collective-permute-start(bf16[192,1024]{1,0:T(8,128)(2,1)S(1)} %get-tuple-element.311), channel_id=1, source_target_pairs={{16,8},{17,9},{18,10},{19,11},{20,12},{21,13},{22,14},{23,15}} | collective-permute-start | bytes 1179656 | tf_op jit(solution)/shard_map/ppermute | solution.py:748
  339.5 45.0 %collective-permute-start.41 = (bf16[192,1024]{1,0:T(8,128)(2,1)S(1)}, bf16[192,1024]{1,0:T(8,128)(2,1)S(1)}, u32[]{:S(2)}, u32[]{:S(2)}) collective-permute-start(bf16[192,1024]{1,0:T(8,128)(2,1)S(1)} %get-tuple-element.323), channel_id=1, source_target_pairs={{8,0},{24,16},{9,1},{25,17},{10,2},{26,18},{11,3},{27,19},{12,4},{... | collective-permute-start | bytes 1179656 | tf_op jit(solution)/shard_map/ppermute | solution.py:746
  340.8 63.6 %collective-permute-start.44 = (bf16[192,1024]{1,0:T(8,128)(2,1)S(1)}, bf16[192,1024]{1,0:T(8,128)(2,1)}, u32[]{:S(2)}, u32[]{:S(2)}) collective-permute-start(bf16[192,1024]{1,0:T(8,128)(2,1)S(1)} %get-tuple-element.323), channel_id=1, source_target_pairs={{16,8},{17,9},{18,10},{19,11},{20,12},{21,13},{22,14},{23,15}} | collective-permute-start | bytes 1179656 | tf_op jit(solution)/shard_map/ppermute | solution.py:748
  403.8 30.2 %collective-permute-start.46 = (bf16[192,1024]{1,0:T(8,128)(2,1)}, bf16[192,1024]{1,0:T(8,128)(2,1)S(1)}, u32[]{:S(2)}, u32[]{:S(2)}) collective-permute-start(bf16[192,1024]{1,0:T(8,128)(2,1)} %get-tuple-element.329), channel_id=1, source_target_pairs={{16,8},{17,9},{18,10},{19,11},{20,12},{21,13},{22,14},{23,15}} | collective-permute-start | bytes 1179656 | tf_op jit(solution)/shard_map/ppermute | solution.py:748
  480.2 48.6 %collective-permute-start.48 = (bf16[2,2,512,512]{3,2,1,0:T(8,128)(2,1)S(1)}, bf16[2,2,512,512]{3,2,1,0:T(8,128)(2,1)S(1)}, u32[]{:S(2)}, u32[]{:S(2)}) collective-permute-start(bf16[2,2,512,512]{3,2,1,0:T(8,128)(2,1)S(1)} %bitcast.616), channel_id=1, source_target_pairs={{0,1},{1,0},{2,3},{3,2},{4,5},{5,4},{6,7},{7,6},{8,9},{9,8},{10,11... | collective-permute-start | bytes 6291464 | tf_op jit(solution)/shard_map/ppermute | solution.py:567
  510.7 67.7 %collective-permute-start.54 = (bf16[2,2,512,512]{3,2,1,0:T(8,128)(2,1)}, bf16[2,2,512,512]{3,2,1,0:T(8,128)(2,1)}, u32[]{:S(2)}, u32[]{:S(2)}) collective-permute-start(bf16[2,2,512,512]{3,2,1,0:T(8,128)(2,1)} %bitcast.136), channel_id=1, source_target_pairs={{0,1},{1,0},{2,3},{3,2},{4,5},{5,4},{6,7},{7,6},{8,9},{9,8},{10,11... | collective-permute-start | bytes 6291464 | tf_op jit(solution)/shard_map/ppermute | solution.py:567
  536.3 55.6 %collective-permute-start.52 = (bf16[2,2,128,1024]{3,2,1,0:T(8,128)(2,1)}, bf16[2,2,128,1024]{3,2,1,0:T(8,128)(2,1)}, u32[]{:S(2)}, u32[]{:S(2)}) collective-permute-start(bf16[2,2,128,1024]{3,2,1,0:T(8,128)(2,1)} %bitcast.131), channel_id=1, source_target_pairs={{0,2},{1,3},{2,0},{3,1},{4,6},{5,7},{6,4},{7,5},{8,10},{9,11},{10,... | collective-permute-start | bytes 3145736 | tf_op jit(solution)/shard_map/ppermute | solution.py:567
  536.3 82.5 %collective-permute-start.58 = (bf16[2,2,128,2048]{3,2,1,0:T(8,128)(2,1)}, bf16[2,2,128,2048]{3,2,1,0:T(8,128)(2,1)}, u32[]{:S(2)}, u32[]{:S(2)}) collective-permute-start(bf16[2,2,128,2048]{3,2,1,0:T(8,128)(2,1)} %bitcast.148), channel_id=1, source_target_pairs={{0,1},{1,0},{2,3},{3,2},{4,5},{5,4},{6,7},{7,6},{8,9},{9,8},{10,11... | collective-permute-start | bytes 6291464 | tf_op jit(solution)/shard_map/ppermute | solution.py:567
  537.9 45.2 %collective-permute-start.53 = (bf16[2,512,512]{2,1,0:T(8,128)(2,1)}, bf16[2,512,512]{2,1,0:T(8,128)(2,1)}, u32[]{:S(2)}, u32[]{:S(2)}) collective-permute-start(bf16[2,512,512]{2,1,0:T(8,128)(2,1)} %fusion.25.token), channel_id=1, source_target_pairs={{0,2},{1,3},{2,0},{3,1},{4,6},{5,7},{6,4},{7,5},{8,10},{9,11},{10,... | collective-permute-start | bytes 3145736 | tf_op jit(solution)/shard_map/ppermute | solution.py:484
  580.9 42.4 %collective-permute-start.57 = (bf16[2,512,512]{2,1,0:T(8,128)(2,1)}, bf16[2,512,512]{2,1,0:T(8,128)(2,1)}, u32[]{:S(2)}, u32[]{:S(2)}) collective-permute-start(bf16[2,512,512]{2,1,0:T(8,128)(2,1)} %fusion.26), channel_id=1, source_target_pairs={{0,2},{1,3},{2,0},{3,1},{4,6},{5,7},{6,4},{7,5},{8,10},{9,11},{10,... | collective-permute-start | bytes 3145736 | tf_op jit(solution)/shard_map/ppermute | solution.py:484
  584.7 41.3 %collective-permute-start.56 = (bf16[512,512]{1,0:T(8,128)(2,1)S(1)}, bf16[512,512]{1,0:T(8,128)(2,1)S(1)}, u32[]{:S(2)}, u32[]{:S(2)}) collective-permute-start(bf16[512,512]{1,0:T(8,128)(2,1)S(1)} %fusion.44), channel_id=1, source_target_pairs={{0,4},{1,5},{2,6},{3,7},{4,0},{5,1},{6,2},{7,3},{8,12},{9,13},{10,... | collective-permute-start | bytes 1572872 | tf_op jit(solution)/shard_map/ppermute | solution.py:484
  589.2 73.5 %collective-permute-start.64 = (bf16[2,2,1000,256]{3,2,1,0:T(8,128)(2,1)}, bf16[2,2,1000,256]{3,2,1,0:T(8,128)(2,1)}, u32[]{:S(2)}, u32[]{:S(2)}) collective-permute-start(bf16[2,2,1000,256]{3,2,1,0:T(8,128)(2,1)} %copy-done.24), channel_id=1, source_target_pairs={{0,1},{1,0},{2,3},{3,2},{4,5},{5,4},{6,7},{7,6},{8,9},{9,8},{10,11... | collective-permute-start | bytes 6144008 | tf_op jit(solution)/shard_map/ppermute | solution.py:484
  591.9 115.7 %collective-permute-start.51 = (bf16[2,2,128,2048]{3,2,1,0:T(8,128)(2,1)}, bf16[2,2,128,2048]{3,2,1,0:T(8,128)(2,1)}, u32[]{:S(2)}, u32[]{:S(2)}) collective-permute-start(bf16[2,2,128,2048]{3,2,1,0:T(8,128)(2,1)} %bitcast.615), channel_id=1, source_target_pairs={{0,1},{1,0},{2,3},{3,2},{4,5},{5,4},{6,7},{7,6},{8,9},{9,8},{10,11... | collective-permute-start | bytes 6291464 | tf_op jit(solution)/shard_map/ppermute | solution.py:567
  618.8 18.6 %collective-permute-start.55 = (bf16[2,128,1024]{2,1,0:T(8,128)(2,1)S(1)}, bf16[2,128,1024]{2,1,0:T(8,128)(2,1)S(1)}, u32[]{:S(2)}, u32[]{:S(2)}) collective-permute-start(bf16[2,128,1024]{2,1,0:T(8,128)(2,1)S(1)} %fusion.72.refs_5_), channel_id=1, source_target_pairs={{0,4},{1,5},{2,6},{3,7},{4,0},{5,1},{6,2},{7,3},{8,12},{9,13},{10,... | collective-permute-start | bytes 1572872 | tf_op jit(solution)/shard_map/ppermute | solution.py:484
  647.0 37.3 %collective-permute-start.63 = (bf16[2,128,2048]{2,1,0:T(8,128)(2,1)S(1)}, bf16[2,128,2048]{2,1,0:T(8,128)(2,1)S(1)}, u32[]{:S(2)}, u32[]{:S(2)}) collective-permute-start(bf16[2,128,2048]{2,1,0:T(8,128)(2,1)S(1)} %copy-done.95), channel_id=1, source_target_pairs={{0,2},{1,3},{2,0},{3,1},{4,6},{5,7},{6,4},{7,5},{8,10},{9,11},{10,... | collective-permute-start | bytes 3145736 | tf_op jit(solution)/shard_map/ppermute | solution.py:484
  647.0 106.8 %collective-permute-start.66 = (bf16[2,2,128,1536]{3,2,1,0:T(8,128)(2,1)S(1)}, bf16[2,2,128,1536]{3,2,1,0:T(8,128)(2,1)S(1)}, u32[]{:S(2)}, u32[]{:S(2)}) collective-permute-start(bf16[2,2,128,1536]{3,2,1,0:T(8,128)(2,1)S(1)} %bitcast.618), channel_id=1, source_target_pairs={{0,1},{1,0},{2,3},{3,2},{4,5},{5,4},{6,7},{7,6},{8,9},{9,8},{10,11... | collective-permute-start | bytes 4718600 | tf_op jit(solution)/shard_map/ppermute | solution.py:567
  653.3 33.6 %collective-permute-start.62 = (bf16[512,512]{1,0:T(8,128)(2,1)S(1)}, bf16[512,512]{1,0:T(8,128)(2,1)S(1)}, u32[]{:S(2)}, u32[]{:S(2)}) collective-permute-start(bf16[512,512]{1,0:T(8,128)(2,1)S(1)} %copy-done.98), channel_id=1, source_target_pairs={{0,4},{1,5},{2,6},{3,7},{4,0},{5,1},{6,2},{7,3},{8,12},{9,13},{10,... | collective-permute-start | bytes 1572872 | tf_op jit(solution)/shard_map/ppermute | solution.py:484
  662.7 30.0 %collective-permute-start.61 = (bf16[2,2,48,1024]{3,2,1,0:T(8,128)(2,1)S(1)}, bf16[2,2,48,1024]{3,2,1,0:T(8,128)(2,1)S(1)}, u32[]{:S(2)}, u32[]{:S(2)}) collective-permute-start(bf16[2,2,48,1024]{3,2,1,0:T(8,128)(2,1)S(1)} %fusion.79), channel_id=1, source_target_pairs={{0,2},{1,3},{2,0},{3,1},{4,6},{5,7},{6,4},{7,5},{8,10},{9,11},{10,... | collective-permute-start | bytes 1179656 | tf_op jit(solution)/shard_map/ppermute | solution.py:484
  684.2 41.6 %collective-permute-start.69 = (bf16[2,1000,256]{2,1,0:T(8,128)(2,1)S(1)}, bf16[2,1000,256]{2,1,0:T(8,128)(2,1)S(1)}, u32[]{:S(2)}, u32[]{:S(2)}) collective-permute-start(bf16[2,1000,256]{2,1,0:T(8,128)(2,1)S(1)} %fusion.8), channel_id=1, source_target_pairs={{0,2},{1,3},{2,0},{3,1},{4,6},{5,7},{6,4},{7,5},{8,10},{9,11},{10,... | collective-permute-start | bytes 3072008 | tf_op jit(solution)/shard_map/ppermute | solution.py:484
  686.9 90.3 %collective-permute-start.72 = (bf16[2,2,128,1536]{3,2,1,0:T(8,128)(2,1)S(1)}, bf16[2,2,128,1536]{3,2,1,0:T(8,128)(2,1)S(1)}, u32[]{:S(2)}, u32[]{:S(2)}) collective-permute-start(bf16[2,2,128,1536]{3,2,1,0:T(8,128)(2,1)S(1)} %bitcast.617), channel_id=1, source_target_pairs={{0,1},{1,0},{2,3},{3,2},{4,5},{5,4},{6,7},{7,6},{8,9},{9,8},{10,11... | collective-permute-start | bytes 4718600 | tf_op jit(solution)/shard_map/ppermute | solution.py:567
  692.7 38.1 %collective-permute-start.68 = (bf16[128,2048]{1,0:T(8,128)(2,1)S(1)}, bf16[128,2048]{1,0:T(8,128)(2,1)S(1)}, u32[]{:S(2)}, u32[]{:S(2)}) collective-permute-start(bf16[128,2048]{1,0:T(8,128)(2,1)S(1)} %fusion.36), channel_id=1, source_target_pairs={{0,4},{1,5},{2,6},{3,7},{4,0},{5,1},{6,2},{7,3},{8,12},{9,13},{10,... | collective-permute-start | bytes 1572872 | tf_op jit(solution)/shard_map/ppermute | solution.py:484
  709.2 46.0 %collective-permute-start.65 = (bf16[2,128,2048]{2,1,0:T(8,128)(2,1)S(1)}, bf16[2,128,2048]{2,1,0:T(8,128)(2,1)S(1)}, u32[]{:S(2)}, u32[]{:S(2)}) collective-permute-start(bf16[2,128,2048]{2,1,0:T(8,128)(2,1)S(1)} %fusion.28), channel_id=1, source_target_pairs={{0,2},{1,3},{2,0},{3,1},{4,6},{5,7},{6,4},{7,5},{8,10},{9,11},{10,... | collective-permute-start | bytes 3145736 | tf_op jit(solution)/shard_map/ppermute | solution.py:484
  725.9 108.7 %collective-permute-start.81 = (bf16[128,1024]{1,0:T(8,128)(2,1)S(1)}, bf16[128,1024]{1,0:T(8,128)(2,1)S(1)}, u32[]{:S(2)}, u32[]{:S(2)}) collective-permute-start(bf16[128,1024]{1,0:T(8,128)(2,1)S(1)} %fusion.77), channel_id=1, source_target_pairs={{0,1},{1,0},{2,3},{3,2},{4,5},{5,4},{6,7},{7,6},{8,9},{9,8},{10,11... | collective-permute-start | bytes 786440 | tf_op jit(solution)/shard_map/ppermute | solution.py:484
  730.8 18.3 %collective-permute-start.67 = (bf16[2,48,1024]{2,1,0:T(8,128)(2,1)S(1)}, bf16[2,48,1024]{2,1,0:T(8,128)(2,1)S(1)}, u32[]{:S(2)}, u32[]{:S(2)}) collective-permute-start(bf16[2,48,1024]{2,1,0:T(8,128)(2,1)S(1)} %fusion.81), channel_id=1, source_target_pairs={{0,4},{1,5},{2,6},{3,7},{4,0},{5,1},{6,2},{7,3},{8,12},{9,13},{10,... | collective-permute-start | bytes 589832 | tf_op jit(solution)/shard_map/ppermute | solution.py:484
  749.1 25.5 %collective-permute-start.73 = (bf16[1000,256]{1,0:T(8,128)(2,1)S(1)}, bf16[1000,256]{1,0:T(8,128)(2,1)S(1)}, u32[]{:S(2)}, u32[]{:S(2)}) collective-permute-start(bf16[1000,256]{1,0:T(8,128)(2,1)S(1)} %fusion.51), channel_id=1, source_target_pairs={{0,4},{1,5},{2,6},{3,7},{4,0},{5,1},{6,2},{7,3},{8,12},{9,13},{10,... | collective-permute-start | bytes 1536008 | tf_op jit(solution)/shard_map/ppermute | solution.py:484
  754.5 33.9 %collective-permute-start.71 = (bf16[2,128,1536]{2,1,0:T(8,128)(2,1)S(1)}, bf16[2,128,1536]{2,1,0:T(8,128)(2,1)S(1)}, u32[]{:S(2)}, u32[]{:S(2)}) collective-permute-start(bf16[2,128,1536]{2,1,0:T(8,128)(2,1)S(1)} %fusion.59), channel_id=1, source_target_pairs={{0,2},{1,3},{2,0},{3,1},{4,6},{5,7},{6,4},{7,5},{8,10},{9,11},{10,... | collective-permute-start | bytes 2359304 | tf_op jit(solution)/shard_map/ppermute | solution.py:484
  755.2 81.8 %collective-permute-start.80 = (bf16[48,1024]{1,0:T(8,128)(2,1)S(1)}, bf16[48,1024]{1,0:T(8,128)(2,1)S(1)}, u32[]{:S(2)}, u32[]{:S(2)}) collective-permute-start(bf16[48,1024]{1,0:T(8,128)(2,1)S(1)} %fusion.87), channel_id=1, source_target_pairs={{0,1},{1,0},{2,3},{3,2},{4,5},{5,4},{6,7},{7,6},{8,9},{9,8},{10,11... | collective-permute-start | bytes 294920 | tf_op jit(solution)/shard_map/ppermute | solution.py:484
  774.5 25.9 %collective-permute-start.70 = (bf16[128,2048]{1,0:T(8,128)(2,1)S(1)}, bf16[128,2048]{1,0:T(8,128)(2,1)S(1)}, u32[]{:S(2)}, u32[]{:S(2)}) collective-permute-start(bf16[128,2048]{1,0:T(8,128)(2,1)S(1)} %fusion.32), channel_id=1, source_target_pairs={{0,4},{1,5},{2,6},{3,7},{4,0},{5,1},{6,2},{7,3},{8,12},{9,13},{10,... | collective-permute-start | bytes 1572872 | tf_op jit(solution)/shard_map/ppermute | solution.py:484
  778.0 55.2 %collective-permute-start.77 = (bf16[2,128,1536]{2,1,0:T(8,128)(2,1)S(1)}, bf16[2,128,1536]{2,1,0:T(8,128)(2,1)S(1)}, u32[]{:S(2)}, u32[]{:S(2)}) collective-permute-start(bf16[2,128,1536]{2,1,0:T(8,128)(2,1)S(1)} %fusion.60), channel_id=1, source_target_pairs={{0,2},{1,3},{2,0},{3,1},{4,6},{5,7},{6,4},{7,5},{8,10},{9,11},{10,... | collective-permute-start | bytes 2359304 | tf_op jit(solution)/shard_map/ppermute | solution.py:484
  803.8 28.0 %collective-permute-start.78 = (bf16[128,1536]{1,0:T(8,128)(2,1)S(1)}, bf16[128,1536]{1,0:T(8,128)(2,1)S(1)}, u32[]{:S(2)}, u32[]{:S(2)}) collective-permute-start(bf16[128,1536]{1,0:T(8,128)(2,1)S(1)} %fusion.68), channel_id=1, source_target_pairs={{0,4},{1,5},{2,6},{3,7},{4,0},{5,1},{6,2},{7,3},{8,12},{9,13},{10,... | collective-permute-start | bytes 1179656 | tf_op jit(solution)/shard_map/ppermute | solution.py:484
  816.3 32.7 %collective-permute-start.76 = (f32[3]{0:T(128)S(1)}, f32[3]{0:T(128)S(1)}, u32[]{:S(2)}, u32[]{:S(2)}) collective-permute-start(f32[3]{0:T(128)S(1)} %add.1149), channel_id=1, source_target_pairs={{0,4},{1,5},{2,6},{3,7},{4,0},{5,1},{6,2},{7,3},{8,12},{9,13},{10,... | collective-permute-start | bytes 44 | tf_op jit(solution)/shard_map/ppermute | solution.py:405
  (186 other events, 2022.2 us)

commit v5 on v4

--- a/solution.py
+++ b/solution.py
@@ -17,7 +17,7 @@
 DEPTH=3
 F32=jnp.float32; BF=jnp.bfloat16
 VMEM_LIMIT=26*1024*1024
-HEAD_LIMIT=16*1024*1024
+HEAD_LIMIT=20*1024*1024
 GELU_A=math.sqrt(2.0/math.pi); GELU_B=0.044715
 
 def dot(a,b): return jnp.dot(a,b,preferred_element_type=F32)
@@ -320,7 +320,7 @@
 
 
 def vocab_tile(rows):
-    for tile in (800, 500, 400):
+    for tile in (1600, 800, 400):
         if rows % tile == 0 and tile % 16 == 0:
             return tile
     return rows
@@ -826,14 +826,14 @@
     token = qkv[0].step(token)
     token = up[1].step(token)
     token = tab.end(token)
+    token = qkv[0].step(token)
     token = qkv[1].step(token)
-    token = qkv[0].step(token)
     token = up[1].end(token)
-    square_sums = sum_all(after(square_sums, token), "dp")
+    token = qkv[1].step(token)
     token = qkv[0].end(token)
-    token = qkv[1].step(token)
     token = out.end(token)
     token = pack.end(token)
+    square_sums = sum_all(after(square_sums, token), "dp")
     token = qkv[1].end(token)
     target_logit = jnp.sum(latent.astype(F32) * picked_all.astype(F32), axis=1)
     token_loss = (log_total - target_logit) * weight

time: 857 us -> 851 us (level)
  transfers between devices with their start and end apart: 82 -> 82, of which waited for: 45 -> 44; matrix products, arithmetic and copies ran while one was open for 11% -> 11% of each run, Pallas kernels for 16% -> 16%
where the time goes in v5:
time: 851 us; the launch traced here: 844 us
  waiting for transfers between devices  322 us (38%)
  Pallas kernels  232 us (27%)
  starting transfers between devices  92.4 us (11%)
  local copies, waits for them, and re-layouts  83.2 us (10%)
  other arithmetic  68.2 us (8%)
  between operations  32 us (4%)
  matrix products  14.1 us (2%)
    ppermute x27, waiting for transfers between devices, send(): lax.ppermute(sent, 'dp', [(i, i ^ 1 << bit) for i in range(lax.axis_size(...  151 us
    pallas_call x8, Pallas kernels, layer_backward(): pl.pallas_call(functools.partial(bwd_kernel, tick), in_specs=[SM, VM, HB,...  83.2 us
    pallas_call x8, Pallas kernels, layer_forward(): pl.pallas_call(functools.partial(fwd_kernel, tick), in_specs=[SM, VM, HB,...  76.9 us
    ppermute x29, waiting for transfers between devices, swap(): return lax.ppermute(x, axis, pairs)  76.2 us
    unnamed x320, local copies, waits for them, and re-layouts  53 us
    ppermute x14, waiting for transfers between devices, body(): core_in = lax.ppermute(sent, 'section', core_pairs) if core_pairs else sent  52.6 us
    pallas_call x14, Pallas kernels, product(): pl.pallas_call(product_kernel, grid_spec=pltpu.PrefetchScalarGridSpec(num...  46.6 us
    ppermute x4, waiting for transfers between devices, spread(): got = lax.ppermute(x, axis, pairs)  42.1 us
  transfers between devices with their start and end apart: 82, of which 44 were waited for; matrix products, arithmetic and copies ran while one was open for 11% of the time, Pallas kernels for 16%

profile of v5, /device:TPU:0, one launch (start us, length us, event | category | flops | bytes accessed | tf_op | source)
XLA Modules:
  0.0 843.7 jit_solution(4295592536068385888)
XLA Ops:
  4.0 4.1 collective-permute-start
  59.0 6.7 collective-permute-done.9
  67.2 10.4 %collective-permute-done.10 = bf16[2,2,272,256]{3,2,0,1:T(8,128)(2,1)S(1)} collective-permute-done((bf16[2,2,272,256]{3,2,0,1:T(8,128)(2,1)S(1)}, bf16[2,2,272,256]{3,2,0,1:T(8,128)(2,1)S(1)}, u32[]{:S(2)}, u32[]{:S(2)}) %collective-permute-start.10) | collective-permute-done | bytes 557088 | tf_op jit(solution)/shard_map/ppermute | solution.py:405
  79.2 6.8 collective-permute-done.11
  86.8 4.2 fusion.24
  98.3 5.8 collective-permute-done.17
  109.7 7.9 collective-permute-done.15
  129.3 14.4 %layer_fwd.8 = (bf16[192,1024]{1,0:T(8,128)(2,1)S(1)}, f32[3,1024]{1,0:T(4,128)S(1)}, bf16[4,192,1024]{2,1,0:T(8,128)(2,1)}, bf16[4,192,1024]{2,1,0:T(8,128)(2,1...) custom-call(s32[22,4]{1,0:T(8,128)S(1)} %copy.296.info.ids, ...), custom_call_target="tpu_custom_call", output_to_operand_aliasing={{2}: (13, {}), {3}: (14, {}), {4}: (15, {}), {5}: (16, {}),... | custom-call | flops 4831838208 | bytes 33554432 | tf_op jit(solution)/shard_map/layer_fwd/pallas_call | solution.py:148
  146.4 13.8 %layer_fwd.9 = (bf16[192,1024]{1,0:T(8,128)(2,1)S(1)}, f32[3,1024]{1,0:T(4,128)S(1)}, bf16[4,192,1024]{2,1,0:T(8,128)(2,1)}, bf16[4,192,1024]{2,1,0:T(8,128)(2,1...) custom-call(s32[22,4]{1,0:T(8,128)S(1)} %copy.296.info.ids, ...), custom_call_target="tpu_custom_call", output_to_operand_aliasing={{2}: (13, {}), {3}: (14, {}), {4}: (15, {}), {5}: (16, {}),... | custom-call | flops 4831838208 | bytes 33554432 | tf_op jit(solution)/shard_map/layer_fwd/pallas_call | solution.py:148
  162.9 14.0 %layer_fwd.10 = (bf16[192,1024]{1,0:T(8,128)(2,1)S(1)}, f32[3,1024]{1,0:T(4,128)S(1)}, bf16[4,192,1024]{2,1,0:T(8,128)(2,1)}, bf16[4,192,1024]{2,1,0:T(8,128)(2,...) custom-call(s32[22,4]{1,0:T(8,128)S(1)} %copy.296.info.ids, ...), custom_call_target="tpu_custom_call", output_to_operand_aliasing={{2}: (13, {}), {3}: (14, {}), {4}: (15, {}), {5}: (16, {}),... | custom-call | flops 4831838208 | bytes 33554432 | tf_op jit(solution)/shard_map/layer_fwd/pallas_call | solution.py:148
  179.9 13.8 %layer_fwd.11 = (bf16[192,1024]{1,0:T(8,128)(2,1)S(1)}, f32[3,1024]{1,0:T(4,128)S(1)}, bf16[4,192,1024]{2,1,0:T(8,128)(2,1)}, bf16[4,192,1024]{2,1,0:T(8,128)(2,...) custom-call(s32[22,4]{1,0:T(8,128)S(1)} %copy.296.info.ids, ...), custom_call_target="tpu_custom_call", output_to_operand_aliasing={{2}: (13, {}), {3}: (14, {}), {4}: (15, {}), {5}: (16, {}),... | custom-call | flops 4831838208 | bytes 33554432 | tf_op jit(solution)/shard_map/layer_fwd/pallas_call | solution.py:148
  196.5 8.5 %layer_fwd.12 = (bf16[192,1024]{1,0:T(8,128)(2,1)S(1)}, f32[3,1024]{1,0:T(4,128)S(1)}, bf16[4,192,1024]{2,1,0:T(8,128)(2,1)}, bf16[4,192,1024]{2,1,0:T(8,128)(2,...) custom-call(s32[22,4]{1,0:T(8,128)S(1)} %copy.296.info.ids, ...), custom_call_target="tpu_custom_call", output_to_operand_aliasing={{2}: (13, {}), {3}: (14, {}), {4}: (15, {}), {5}: (16, {}),... | custom-call | flops 4831838208 | bytes 33554432 | tf_op jit(solution)/shard_map/layer_fwd/pallas_call | solution.py:148
  209.6 10.6 %layer_fwd.14 = (bf16[192,1024]{1,0:T(8,128)(2,1)S(1)}, f32[3,1024]{1,0:T(4,128)S(1)}, bf16[4,192,1024]{2,1,0:T(8,128)(2,1)}, bf16[4,192,1024]{2,1,0:T(8,128)(2,...) custom-call(s32[22,4]{1,0:T(8,128)S(1)} %copy.296.info.ids, ...), custom_call_target="tpu_custom_call", output_to_operand_aliasing={{2}: (13, {}), {3}: (14, {}), {4}: (15, {}), {5}: (16, {}),... | custom-call | flops 4831838208 | bytes 33554432 | tf_op jit(solution)/shard_map/layer_fwd/pallas_call | solution.py:148
  226.9 4.1 collective-permute-start.32
  231.1 38.4 %collective-permute-done.32 = bf16[768,256]{1,0:T(8,128)(2,1)} collective-permute-done((bf16[768,256]{1,0:T(8,128)(2,1)}, bf16[768,256]{1,0:T(8,128)(2,1)}, u32[]{:S(2)}, u32[]{:S(2)}) %collective-permute-start.32) | collective-permute-done | bytes 393248 | tf_op jit(solution)/shard_map/ppermute | solution.py:611
  273.9 14.9 %head_fwd.1 = (bf16[256,768]{1,0:T(8,128)(2,1)S(1)}, f32[2,768]{1,0:T(2,128)S(1)}) custom-call(bf16[8000,256]{1,0:T(8,128)(2,1)S(1)} %bitcast.592, bf16[768,256]{1,0:T(8,128)(2,1)S(1)} %get-tuple-element.412.latent), custom_call_target="tpu_custom_call" | custom-call | flops 6291456000 | bytes 4096000 | tf_op jit(solution)/shard_map/head_fwd/pallas_call | solution.py:333
  298.3 8.2 collective-permute-done.36
  311.9 3.4 copy-done.5
  322.7 12.2 %layer_bwd.10 = (bf16[192,1024]{1,0:T(8,128)(2,1)S(1)}, f32[3,1024]{1,0:T(4,128)S(1)}, bf16[4,192,1024]{2,1,0:T(8,128)(2,1)}, bf16[4,192,4096]{2,1,0:T(8,128)(2,...) custom-call(s32[22,4]{1,0:T(8,128)S(1)} %copy.296.info.ids, ...), custom_call_target="tpu_custom_call", output_to_operand_aliasing={{2}: (18, {}), {3}: (19, {}), {4}: (20, {}), {5}: (21, {}),... | custom-call | flops 4831838208 | bytes 33554432 | tf_op jit(solution)/shard_map/layer_bwd/pallas_call | solution.py:262
  340.7 42.5 %collective-permute-done.41.g_in = bf16[192,1024]{1,0:T(8,128)(2,1)S(1)} collective-permute-done((bf16[192,1024]{1,0:T(8,128)(2,1)S(1)}, bf16[192,1024]{1,0:T(8,128)(2,1)S(1)}, u32[]{:S(2)}, u32[]{:S(2)}) %collective-permute-start.41) | collective-permute-done | bytes 393248 | tf_op jit(solution)/shard_map/ppermute | solution.py:746
  383.2 17.4 %layer_bwd.12 = (bf16[192,1024]{1,0:T(8,128)(2,1)}, f32[3,1024]{1,0:T(4,128)S(1)}, bf16[4,192,1024]{2,1,0:T(8,128)(2,1)}, bf16[4,192,4096]{2,1,0:T(8,128)(2,1)},...) custom-call(s32[22,4]{1,0:T(8,128)S(1)} %copy.296.info.ids, ...), custom_call_target="tpu_custom_call", output_to_operand_aliasing={{2}: (18, {}), {3}: (19, {}), {4}: (20, {}), {5}: (21, {}),... | custom-call | flops 4831838208 | bytes 33554432 | tf_op jit(solution)/shard_map/layer_bwd/pallas_call | solution.py:262
  405.7 3.4 copy-done.3
  409.1 3.4 copy-done.6
  415.3 16.1 %layer_bwd.13 = (bf16[192,1024]{1,0:T(8,128)(2,1)S(1)}, f32[3,1024]{1,0:T(4,128)S(1)}, bf16[4,192,1024]{2,1,0:T(8,128)(2,1)}, bf16[4,192,4096]{2,1,0:T(8,128)(2,...) custom-call(s32[22,4]{1,0:T(8,128)S(1)} %copy.296.info.ids, ...), custom_call_target="tpu_custom_call", output_to_operand_aliasing={{2}: (18, {}), {3}: (19, {}), {4}: (20, {}), {5}: (21, {}),... | custom-call | flops 4831838208 | bytes 33554432 | tf_op jit(solution)/shard_map/layer_bwd/pallas_call | solution.py:262
  435.1 16.7 %layer_bwd.14 = (bf16[192,1024]{1,0:T(8,128)(2,1)S(1)}, f32[3,1024]{1,0:T(4,128)S(1)}, bf16[4,192,1024]{2,1,0:T(8,128)(2,1)}, bf16[4,192,4096]{2,1,0:T(8,128)(2,...) custom-call(s32[22,4]{1,0:T(8,128)S(1)} %copy.296.info.ids, ...), custom_call_target="tpu_custom_call", output_to_operand_aliasing={{2}: (18, {}), {3}: (19, {}), {4}: (20, {}), {5}: (21, {}),... | custom-call | flops 4831838208 | bytes 33554432 | tf_op jit(solution)/shard_map/layer_bwd/pallas_call | solution.py:262
  455.4 17.4 %layer_bwd.15 = (bf16[192,1024]{1,0:T(8,128)(2,1)}, f32[3,1024]{1,0:T(4,128)S(1)}, bf16[4,192,1024]{2,1,0:T(8,128)(2,1)}, bf16[4,192,4096]{2,1,0:T(8,128)(2,1)},...) custom-call(s32[22,4]{1,0:T(8,128)S(1)} %copy.296.info.ids, ...), custom_call_target="tpu_custom_call", output_to_operand_aliasing={{2}: (18, {}), {3}: (19, {}), {4}: (20, {}), {5}: (21, {}),... | custom-call | flops 4831838208 | bytes 33554432 | tf_op jit(solution)/shard_map/layer_bwd/pallas_call | solution.py:262
  483.2 3.9 product.15
  490.3 4.6 product.17
  501.2 3.8 product.20
  509.9 17.7 %collective-permute-done.49 = bf16[2,2,512,512]{3,2,1,0:T(8,128)(2,1)S(1)} collective-permute-done((bf16[2,2,512,512]{3,2,1,0:T(8,128)(2,1)S(1)}, bf16[2,2,512,512]{3,2,1,0:T(8,128)(2,1)S(1)}, u32[]{:S(2)}, u32[]{:S(2)}) %collective-permute-start.49) | collective-permute-done | bytes 2097184 | tf_op jit(solution)/shard_map/ppermute | solution.py:567
  543.5 3.7 collective-permute-done.53
  551.3 10.6 %head_bwd.1 = bf16[8000,256]{1,0:T(8,128)(2,1)S(1)} custom-call(bf16[8000,256]{1,0:T(8,128)(2,1)S(1)} %bitcast.593, bf16[768,256]{1,0:T(8,128)(2,1)S(1)} %copy-done.29, f32[1,768]{1,0:T(1,128)S(1)} %get-tuple-element.446.log_total, f32[1,768]{1,0:T(1,128)S(1)} %broadcast_in_dim.29.weight, s32[1,768]{1,0:T(1,128)S(1)} %broadcast_in_dim.30.ids, ...), custom_call_target="tpu_custom_call" | custom-call | flops 1 | bytes 1 | tf_op jit(solution)/shard_map/head_bwd/pallas_call | solution.py:358
  564.4 3.9 product.22
  569.6 3.9 product.23
  582.4 4.0 collective-permute-start.55
  611.4 6.2 collective-permute-done.57
  627.8 7.3 collective-permute-done.54
  652.4 9.1 %collective-permute-done.63 = bf16[2,2,1000,256]{3,2,1,0:T(8,128)(2,1)} collective-permute-done((bf16[2,2,1000,256]{3,2,1,0:T(8,128)(2,1)}, bf16[2,2,1000,256]{3,2,1,0:T(8,128)(2,1)}, u32[]{:S(2)}, u32[]{:S(2)}) %collective-permute-start.63) | collective-permute-done | bytes 2048032 | tf_op jit(solution)/shard_map/ppermute | solution.py:484
  664.3 17.7 %collective-permute-done.62 = bf16[2,128,2048]{2,1,0:T(8,128)(2,1)S(1)} collective-permute-done((bf16[2,128,2048]{2,1,0:T(8,128)(2,1)S(1)}, bf16[2,128,2048]{2,1,0:T(8,128)(2,1)S(1)}, u32[]{:S(2)}, u32[]{:S(2)}) %collective-permute-start.62) | collective-permute-done | bytes 1048608 | tf_op jit(solution)/shard_map/ppermute | solution.py:484
  692.2 14.2 %collective-permute-done.67 = bf16[2,2,128,2048]{3,2,1,0:T(8,128)(2,1)} collective-permute-done((bf16[2,2,128,2048]{3,2,1,0:T(8,128)(2,1)}, bf16[2,2,128,2048]{3,2,1,0:T(8,128)(2,1)}, u32[]{:S(2)}, u32[]{:S(2)}) %collective-permute-start.67) | collective-permute-done | bytes 2097184 | tf_op jit(solution)/shard_map/ppermute | solution.py:567
  710.7 12.8 %collective-permute-done.66 = bf16[2,1000,256]{2,1,0:T(8,128)(2,1)S(1)} collective-permute-done((bf16[2,1000,256]{2,1,0:T(8,128)(2,1)S(1)}, bf16[2,1000,256]{2,1,0:T(8,128)(2,1)S(1)}, u32[]{:S(2)}, u32[]{:S(2)}) %collective-permute-start.66) | collective-permute-done | bytes 1024032 | tf_op jit(solution)/shard_map/ppermute | solution.py:484
  731.2 15.6 %collective-permute-done.64 = bf16[2,48,1024]{2,1,0:T(8,128)(2,1)S(1)} collective-permute-done((bf16[2,48,1024]{2,1,0:T(8,128)(2,1)S(1)}, bf16[2,48,1024]{2,1,0:T(8,128)(2,1)S(1)}, u32[]{:S(2)}, u32[]{:S(2)}) %collective-permute-start.64) | collective-permute-done | bytes 196640 | tf_op jit(solution)/shard_map/ppermute | solution.py:484
  746.8 3.4 collective-permute-start.72
  757.9 14.3 %collective-permute-done.72 = bf16[1000,256]{1,0:T(8,128)(2,1)S(1)} collective-permute-done((bf16[1000,256]{1,0:T(8,128)(2,1)S(1)}, bf16[1000,256]{1,0:T(8,128)(2,1)S(1)}, u32[]{:S(2)}, u32[]{:S(2)}) %collective-permute-start.72) | collective-permute-done | bytes 512032 | tf_op jit(solution)/shard_map/ppermute | solution.py:484
  776.2 7.8 collective-permute-done.71
  788.9 10.0 %collective-permute-done.77 = bf16[128,2048]{1,0:T(8,128)(2,1)S(1)} collective-permute-done((bf16[128,2048]{1,0:T(8,128)(2,1)S(1)}, bf16[128,2048]{1,0:T(8,128)(2,1)S(1)}, u32[]{:S(2)}, u32[]{:S(2)}) %collective-permute-start.77) | collective-permute-done | bytes 524320 | tf_op jit(solution)/shard_map/ppermute | solution.py:484
  803.0 17.5 %collective-permute-done.76 = bf16[2,128,1536]{2,1,0:T(8,128)(2,1)S(1)} collective-permute-done((bf16[2,128,1536]{2,1,0:T(8,128)(2,1)S(1)}, bf16[2,128,1536]{2,1,0:T(8,128)(2,1)S(1)}, u32[]{:S(2)}, u32[]{:S(2)}) %collective-permute-start.76) | collective-permute-done | bytes 786464 | tf_op jit(solution)/shard_map/ppermute | solution.py:484
  832.3 3.5 collective-permute-done.79
  (708 shorter events, 297.2 us)
Async XLA Ops:
  4.0 19.9 %collective-permute-start = (bf16[272,256]{1,0:T(8,128)(2,1)S(1)}, bf16[272,256]{1,0:T(8,128)(2,1)S(1)}, u32[]{:S(2)}, u32[]{:S(2)}) collective-permute-start(bf16[272,256]{1,0:T(8,128)(2,1)S(1)} %get-tuple-element.423), channel_id=1, source_target_pairs={{0,4},{1,5},{2,6},{3,7},{4,0},{5,1},{6,2},{7,3},{8,12},{9,13},{10,... | collective-permute-start | bytes 417800 | tf_op jit(solution)/shard_map/ppermute | solution.py:405
  8.1 18.9 %collective-permute-start.4 = (bf16[272,256]{1,0:T(8,128)(2,1)S(1)}, bf16[272,256]{1,0:T(8,128)(2,1)S(1)}, u32[]{:S(2)}, u32[]{:S(2)}) collective-permute-start(bf16[272,256]{1,0:T(8,128)(2,1)S(1)} %get-tuple-element.421), channel_id=1, source_target_pairs={{0,4},{1,5},{2,6},{3,7},{4,0},{5,1},{6,2},{7,3},{8,12},{9,13},{10,... | collective-permute-start | bytes 417800 | tf_op jit(solution)/shard_map/ppermute | solution.py:405
  8.2 21.8 %collective-permute-start.3 = (bf16[272,256]{1,0:T(8,128)(2,1)S(1)}, bf16[272,256]{1,0:T(8,128)(2,1)S(1)}, u32[]{:S(2)}, u32[]{:S(2)}) collective-permute-start(bf16[272,256]{1,0:T(8,128)(2,1)S(1)} %get-tuple-element.422), channel_id=1, source_target_pairs={{0,4},{1,5},{2,6},{3,7},{4,0},{5,1},{6,2},{7,3},{8,12},{9,13},{10,... | collective-permute-start | bytes 417800 | tf_op jit(solution)/shard_map/ppermute | solution.py:405
  11.1 20.5 %collective-permute-start.2 = (bf16[216,256]{1,0:T(8,128)(2,1)S(1)}, bf16[216,256]{1,0:T(8,128)(2,1)S(1)}, u32[]{:S(2)}, u32[]{:S(2)}) collective-permute-start(bf16[216,256]{1,0:T(8,128)(2,1)S(1)} %pad_maximum_fusion.8), channel_id=1, source_target_pairs={{0,4},{1,5},{2,6},{3,7},{4,0},{5,1},{6,2},{7,3},{8,12},{9,13},{10,... | collective-permute-start | bytes 331784 | tf_op jit(solution)/shard_map/ppermute | solution.py:405
  19.7 71.4 %collective-permute-start.16 = (f32[4,48,256]{2,1,0:T(8,128)S(1)}, f32[4,48,256]{2,1,0:T(8,128)S(1)}, u32[]{:S(2)}, u32[]{:S(2)}) collective-permute-start(f32[4,48,256]{2,1,0:T(8,128)S(1)} %copy-done.96), channel_id=1, source_target_pairs={{0,8},{8,0},{16,24},{24,16},{1,9},{9,1},{17,25},{25,17},{2,10},{10... | collective-permute-start | bytes 589832 | tf_op jit(solution)/shard_map/ppermute | solution.py:405
  27.6 15.9 %collective-permute-start.8 = (bf16[2,272,256]{2,1,0:T(8,128)(2,1)S(1)}, bf16[2,272,256]{2,1,0:T(8,128)(2,1)S(1)}, u32[]{:S(2)}, u32[]{:S(2)}) collective-permute-start(bf16[2,272,256]{2,1,0:T(8,128)(2,1)S(1)} %maximum_select_fusion.15), channel_id=1, source_target_pairs={{0,2},{1,3},{2,0},{3,1},{4,6},{5,7},{6,4},{7,5},{8,10},{9,11},{10,... | collective-permute-start | bytes 835592 | tf_op jit(solution)/shard_map/ppermute | solution.py:405
  30.6 18.9 %collective-permute-start.7 = (bf16[2,272,256]{2,1,0:T(8,128)(2,1)S(1)}, bf16[2,272,256]{2,1,0:T(8,128)(2,1)S(1)}, u32[]{:S(2)}, u32[]{:S(2)}) collective-permute-start(bf16[2,272,256]{2,1,0:T(8,128)(2,1)S(1)} %maximum_select_fusion.16), channel_id=1, source_target_pairs={{0,2},{1,3},{2,0},{3,1},{4,6},{5,7},{6,4},{7,5},{8,10},{9,11},{10,... | collective-permute-start | bytes 835592 | tf_op jit(solution)/shard_map/ppermute | solution.py:405
  31.8 22.3 %collective-permute-start.6 = (bf16[2,216,256]{2,1,0:T(8,128)(2,1)S(1)}, bf16[2,216,256]{2,1,0:T(8,128)(2,1)S(1)}, u32[]{:S(2)}, u32[]{:S(2)}) collective-permute-start(bf16[2,216,256]{2,1,0:T(8,128)(2,1)S(1)} %maximum_select_fusion.19), channel_id=1, source_target_pairs={{0,2},{1,3},{2,0},{3,1},{4,6},{5,7},{6,4},{7,5},{8,10},{9,11},{10,... | collective-permute-start | bytes 663560 | tf_op jit(solution)/shard_map/ppermute | solution.py:405
  38.2 19.3 %collective-permute-start.5 = (bf16[2,2,272,256]{3,2,0,1:T(8,128)(2,1)S(1)}, bf16[2,2,272,256]{3,2,0,1:T(8,128)(2,1)S(1)}, u32[]{:S(2)}, u32[]{:S(2)}) collective-permute-start(bf16[2,2,272,256]{3,2,0,1:T(8,128)(2,1)S(1)} %maximum_select_fusion.6), channel_id=1, source_target_pairs={{0,1},{1,0},{2,3},{3,2},{4,5},{5,4},{6,7},{7,6},{8,9},{9,8},{10,11... | collective-permute-start | bytes 1671176 | tf_op jit(solution)/shard_map/ppermute | solution.py:405
  44.2 21.5 %collective-permute-start.9 = (bf16[2,2,272,256]{3,2,0,1:T(8,128)(2,1)S(1)}, bf16[2,2,272,256]{3,2,0,1:T(8,128)(2,1)S(1)}, u32[]{:S(2)}, u32[]{:S(2)}) collective-permute-start(bf16[2,2,272,256]{3,2,0,1:T(8,128)(2,1)S(1)} %maximum_select_fusion.7), channel_id=1, source_target_pairs={{0,1},{1,0},{2,3},{3,2},{4,5},{5,4},{6,7},{7,6},{8,9},{9,8},{10,11... | collective-permute-start | bytes 1671176 | tf_op jit(solution)/shard_map/ppermute | solution.py:405
  50.1 27.4 %collective-permute-start.10 = (bf16[2,2,272,256]{3,2,0,1:T(8,128)(2,1)S(1)}, bf16[2,2,272,256]{3,2,0,1:T(8,128)(2,1)S(1)}, u32[]{:S(2)}, u32[]{:S(2)}) collective-permute-start(bf16[2,2,272,256]{3,2,0,1:T(8,128)(2,1)S(1)} %maximum_select_fusion.8), channel_id=1, source_target_pairs={{0,1},{1,0},{2,3},{3,2},{4,5},{5,4},{6,7},{7,6},{8,9},{9,8},{10,11... | collective-permute-start | bytes 1671176 | tf_op jit(solution)/shard_map/ppermute | solution.py:405
  54.3 31.7 %collective-permute-start.11 = (bf16[2,2,216,256]{3,2,1,0:T(8,128)(2,1)S(1)}, bf16[2,2,216,256]{3,2,1,0:T(8,128)(2,1)S(1)}, u32[]{:S(2)}, u32[]{:S(2)}) collective-permute-start(bf16[2,2,216,256]{3,2,1,0:T(8,128)(2,1)S(1)} %copy_select_fusion), channel_id=1, source_target_pairs={{0,1},{1,0},{2,3},{3,2},{4,5},{5,4},{6,7},{7,6},{8,9},{9,8},{10,11... | collective-permute-start | bytes 1327112 | tf_op jit(solution)/shard_map/ppermute | solution.py:405
  95.0 14.6 %collective-permute-start.19 = (bf16[2,64,1024]{2,1,0:T(8,128)(2,1)S(1)}, bf16[2,64,1024]{2,1,0:T(8,128)(2,1)S(1)}, u32[]{:S(2)}, u32[]{:S(2)}) collective-permute-start(bf16[2,64,1024]{2,1,0:T(8,128)(2,1)S(1)} %maximum_select_fusion.18), channel_id=1, source_target_pairs={{0,16},{8,24},{16,0},{24,8},{1,17},{9,25},{17,1},{25,9},{2,18},{10... | collective-permute-start | bytes 786440 | tf_op jit(solution)/shard_map/ppermute | solution.py:405
  96.6 21.0 %collective-permute-start.15 = (bf16[768,256]{1,0:T(8,128)(2,1)S(1)}, bf16[768,256]{1,0:T(8,128)(2,1)S(1)}, u32[]{:S(2)}, u32[]{:S(2)}) collective-permute-start(bf16[768,256]{1,0:T(8,128)(2,1)S(1)} %add.1006), channel_id=1, source_target_pairs={{0,16},{8,24},{16,0},{24,8},{1,17},{9,25},{17,1},{25,9},{2,18},{10... | collective-permute-start | bytes 1179656 | tf_op jit(solution)/shard_map/ppermute | solution.py:405
  161.6 17.6 %collective-permute-start.23 = (bf16[192,1024]{1,0:T(8,128)(2,1)S(1)}, bf16[192,1024]{1,0:T(8,128)(2,1)S(1)}, u32[]{:S(2)}, u32[]{:S(2)}) collective-permute-start(bf16[192,1024]{1,0:T(8,128)(2,1)S(1)} %get-tuple-element.223), channel_id=1, source_target_pairs={{8,16},{9,17},{10,18},{11,19},{12,20},{13,21},{14,22},{15,23}} | collective-permute-start | bytes 1179656 | tf_op jit(solution)/shard_map/ppermute | solution.py:708
  178.5 17.3 %collective-permute-start.25 = (bf16[192,1024]{1,0:T(8,128)(2,1)S(1)}, bf16[192,1024]{1,0:T(8,128)(2,1)S(1)}, u32[]{:S(2)}, u32[]{:S(2)}) collective-permute-start(bf16[192,1024]{1,0:T(8,128)(2,1)S(1)} %get-tuple-element.233), channel_id=1, source_target_pairs={{8,16},{9,17},{10,18},{11,19},{12,20},{13,21},{14,22},{15,23}} | collective-permute-start | bytes 1179656 | tf_op jit(solution)/shard_map/ppermute | solution.py:708
  226.9 42.5 %collective-permute-start.32 = (bf16[768,256]{1,0:T(8,128)(2,1)}, bf16[768,256]{1,0:T(8,128)(2,1)}, u32[]{:S(2)}, u32[]{:S(2)}) collective-permute-start(bf16[768,256]{1,0:T(8,128)(2,1)} %broadcast_select_fusion.1), channel_id=1, source_target_pairs={{24,8},{16,0},{25,9},{17,1},{26,10},{18,2},{27,11},{19,3},{28,12},... | collective-permute-start | bytes 1179656 | tf_op jit(solution)/shard_map/ppermute | solution.py:611
  322.0 14.3 %collective-permute-start.40 = (bf16[192,1024]{1,0:T(8,128)(2,1)S(1)}, bf16[192,1024]{1,0:T(8,128)(2,1)S(1)}, u32[]{:S(2)}, u32[]{:S(2)}) collective-permute-start(bf16[192,1024]{1,0:T(8,128)(2,1)S(1)} %get-tuple-element.312), channel_id=1, source_target_pairs={{16,8},{17,9},{18,10},{19,11},{20,12},{21,13},{22,14},{23,15}} | collective-permute-start | bytes 1179656 | tf_op jit(solution)/shard_map/ppermute | solution.py:748
  337.9 45.2 %collective-permute-start.41 = (bf16[192,1024]{1,0:T(8,128)(2,1)S(1)}, bf16[192,1024]{1,0:T(8,128)(2,1)S(1)}, u32[]{:S(2)}, u32[]{:S(2)}) collective-permute-start(bf16[192,1024]{1,0:T(8,128)(2,1)S(1)} %get-tuple-element.326), channel_id=1, source_target_pairs={{8,0},{24,16},{9,1},{25,17},{10,2},{26,18},{11,3},{27,19},{12,4},{... | collective-permute-start | bytes 1179656 | tf_op jit(solution)/shard_map/ppermute | solution.py:746
  339.2 64.0 %collective-permute-start.44 = (bf16[192,1024]{1,0:T(8,128)(2,1)S(1)}, bf16[192,1024]{1,0:T(8,128)(2,1)}, u32[]{:S(2)}, u32[]{:S(2)}) collective-permute-start(bf16[192,1024]{1,0:T(8,128)(2,1)S(1)} %get-tuple-element.326), channel_id=1, source_target_pairs={{16,8},{17,9},{18,10},{19,11},{20,12},{21,13},{22,14},{23,15}} | collective-permute-start | bytes 1179656 | tf_op jit(solution)/shard_map/ppermute | solution.py:748
  402.6 30.2 %collective-permute-start.46 = (bf16[192,1024]{1,0:T(8,128)(2,1)}, bf16[192,1024]{1,0:T(8,128)(2,1)S(1)}, u32[]{:S(2)}, u32[]{:S(2)}) collective-permute-start(bf16[192,1024]{1,0:T(8,128)(2,1)} %get-tuple-element.333), channel_id=1, source_target_pairs={{16,8},{17,9},{18,10},{19,11},{20,12},{21,13},{22,14},{23,15}} | collective-permute-start | bytes 1179656 | tf_op jit(solution)/shard_map/ppermute | solution.py:748
  479.0 48.6 %collective-permute-start.49 = (bf16[2,2,512,512]{3,2,1,0:T(8,128)(2,1)S(1)}, bf16[2,2,512,512]{3,2,1,0:T(8,128)(2,1)S(1)}, u32[]{:S(2)}, u32[]{:S(2)}) collective-permute-start(bf16[2,2,512,512]{3,2,1,0:T(8,128)(2,1)S(1)} %bitcast.616), channel_id=1, source_target_pairs={{0,1},{1,0},{2,3},{3,2},{4,5},{5,4},{6,7},{7,6},{8,9},{9,8},{10,11... | collective-permute-start | bytes 6291464 | tf_op jit(solution)/shard_map/ppermute | solution.py:567
  509.5 66.6 %collective-permute-start.51 = (bf16[2,2,512,512]{3,2,1,0:T(8,128)(2,1)}, bf16[2,2,512,512]{3,2,1,0:T(8,128)(2,1)}, u32[]{:S(2)}, u32[]{:S(2)}) collective-permute-start(bf16[2,2,512,512]{3,2,1,0:T(8,128)(2,1)} %bitcast.130), channel_id=1, source_target_pairs={{0,1},{1,0},{2,3},{3,2},{4,5},{5,4},{6,7},{7,6},{8,9},{9,8},{10,11... | collective-permute-start | bytes 6291464 | tf_op jit(solution)/shard_map/ppermute | solution.py:567
  535.1 54.5 %collective-permute-start.48 = (bf16[2,2,128,1024]{3,2,1,0:T(8,128)(2,1)}, bf16[2,2,128,1024]{3,2,1,0:T(8,128)(2,1)}, u32[]{:S(2)}, u32[]{:S(2)}) collective-permute-start(bf16[2,2,128,1024]{3,2,1,0:T(8,128)(2,1)} %bitcast.122), channel_id=1, source_target_pairs={{0,2},{1,3},{2,0},{3,1},{4,6},{5,7},{6,4},{7,5},{8,10},{9,11},{10,... | collective-permute-start | bytes 3145736 | tf_op jit(solution)/shard_map/ppermute | solution.py:567
  535.1 82.5 %collective-permute-start.57 = (bf16[2,2,128,2048]{3,2,1,0:T(8,128)(2,1)}, bf16[2,2,128,2048]{3,2,1,0:T(8,128)(2,1)}, u32[]{:S(2)}, u32[]{:S(2)}) collective-permute-start(bf16[2,2,128,2048]{3,2,1,0:T(8,128)(2,1)} %bitcast.145), channel_id=1, source_target_pairs={{0,1},{1,0},{2,3},{3,2},{4,5},{5,4},{6,7},{7,6},{8,9},{9,8},{10,11... | collective-permute-start | bytes 6291464 | tf_op jit(solution)/shard_map/ppermute | solution.py:567
  536.7 44.2 %collective-permute-start.50 = (bf16[2,512,512]{2,1,0:T(8,128)(2,1)}, bf16[2,512,512]{2,1,0:T(8,128)(2,1)}, u32[]{:S(2)}, u32[]{:S(2)}) collective-permute-start(bf16[2,512,512]{2,1,0:T(8,128)(2,1)} %fusion.25.token), channel_id=1, source_target_pairs={{0,2},{1,3},{2,0},{3,1},{4,6},{5,7},{6,4},{7,5},{8,10},{9,11},{10,... | collective-permute-start | bytes 3145736 | tf_op jit(solution)/shard_map/ppermute | solution.py:484
  578.6 43.4 %collective-permute-start.56 = (bf16[2,512,512]{2,1,0:T(8,128)(2,1)}, bf16[2,512,512]{2,1,0:T(8,128)(2,1)}, u32[]{:S(2)}, u32[]{:S(2)}) collective-permute-start(bf16[2,512,512]{2,1,0:T(8,128)(2,1)} %fusion.26), channel_id=1, source_target_pairs={{0,2},{1,3},{2,0},{3,1},{4,6},{5,7},{6,4},{7,5},{8,10},{9,11},{10,... | collective-permute-start | bytes 3145736 | tf_op jit(solution)/shard_map/ppermute | solution.py:484
  582.4 42.4 %collective-permute-start.55 = (bf16[512,512]{1,0:T(8,128)(2,1)S(1)}, bf16[512,512]{1,0:T(8,128)(2,1)S(1)}, u32[]{:S(2)}, u32[]{:S(2)}) collective-permute-start(bf16[512,512]{1,0:T(8,128)(2,1)S(1)} %fusion.44), channel_id=1, source_target_pairs={{0,4},{1,5},{2,6},{3,7},{4,0},{5,1},{6,2},{7,3},{8,12},{9,13},{10,... | collective-permute-start | bytes 1572872 | tf_op jit(solution)/shard_map/ppermute | solution.py:484
  586.9 74.5 %collective-permute-start.63 = (bf16[2,2,1000,256]{3,2,1,0:T(8,128)(2,1)}, bf16[2,2,1000,256]{3,2,1,0:T(8,128)(2,1)}, u32[]{:S(2)}, u32[]{:S(2)}) collective-permute-start(bf16[2,2,1000,256]{3,2,1,0:T(8,128)(2,1)} %copy-done.24), channel_id=1, source_target_pairs={{0,1},{1,0},{2,3},{3,2},{4,5},{5,4},{6,7},{7,6},{8,9},{9,8},{10,11... | collective-permute-start | bytes 6144008 | tf_op jit(solution)/shard_map/ppermute | solution.py:484
  589.6 116.8 %collective-permute-start.67 = (bf16[2,2,128,2048]{3,2,1,0:T(8,128)(2,1)}, bf16[2,2,128,2048]{3,2,1,0:T(8,128)(2,1)}, u32[]{:S(2)}, u32[]{:S(2)}) collective-permute-start(bf16[2,2,128,2048]{3,2,1,0:T(8,128)(2,1)} %bitcast.615), channel_id=1, source_target_pairs={{0,1},{1,0},{2,3},{3,2},{4,5},{5,4},{6,7},{7,6},{8,9},{9,8},{10,11... | collective-permute-start | bytes 6291464 | tf_op jit(solution)/shard_map/ppermute | solution.py:567
  617.6 17.6 %collective-permute-start.54 = (bf16[2,128,1024]{2,1,0:T(8,128)(2,1)S(1)}, bf16[2,128,1024]{2,1,0:T(8,128)(2,1)S(1)}, u32[]{:S(2)}, u32[]{:S(2)}) collective-permute-start(bf16[2,128,1024]{2,1,0:T(8,128)(2,1)S(1)} %fusion.72.refs_5_), channel_id=1, source_target_pairs={{0,4},{1,5},{2,6},{3,7},{4,0},{5,1},{6,2},{7,3},{8,12},{9,13},{10,... | collective-permute-start | bytes 1572872 | tf_op jit(solution)/shard_map/ppermute | solution.py:484
  644.7 37.3 %collective-permute-start.62 = (bf16[2,128,2048]{2,1,0:T(8,128)(2,1)S(1)}, bf16[2,128,2048]{2,1,0:T(8,128)(2,1)S(1)}, u32[]{:S(2)}, u32[]{:S(2)}) collective-permute-start(bf16[2,128,2048]{2,1,0:T(8,128)(2,1)S(1)} %copy-done.95), channel_id=1, source_target_pairs={{0,2},{1,3},{2,0},{3,1},{4,6},{5,7},{6,4},{7,5},{8,10},{9,11},{10,... | collective-permute-start | bytes 3145736 | tf_op jit(solution)/shard_map/ppermute | solution.py:484
  644.7 106.8 %collective-permute-start.70 = (bf16[2,2,128,1536]{3,2,1,0:T(8,128)(2,1)S(1)}, bf16[2,2,128,1536]{3,2,1,0:T(8,128)(2,1)S(1)}, u32[]{:S(2)}, u32[]{:S(2)}) collective-permute-start(bf16[2,2,128,1536]{3,2,1,0:T(8,128)(2,1)S(1)} %bitcast.618), channel_id=1, source_target_pairs={{0,1},{1,0},{2,3},{3,2},{4,5},{5,4},{6,7},{7,6},{8,9},{9,8},{10,11... | collective-permute-start | bytes 4718600 | tf_op jit(solution)/shard_map/ppermute | solution.py:567
  651.0 33.6 %collective-permute-start.61 = (bf16[512,512]{1,0:T(8,128)(2,1)S(1)}, bf16[512,512]{1,0:T(8,128)(2,1)S(1)}, u32[]{:S(2)}, u32[]{:S(2)}) collective-permute-start(bf16[512,512]{1,0:T(8,128)(2,1)S(1)} %copy-done.98), channel_id=1, source_target_pairs={{0,4},{1,5},{2,6},{3,7},{4,0},{5,1},{6,2},{7,3},{8,12},{9,13},{10,... | collective-permute-start | bytes 1572872 | tf_op jit(solution)/shard_map/ppermute | solution.py:484
  661.5 28.9 %collective-permute-start.60 = (bf16[2,2,48,1024]{3,2,1,0:T(8,128)(2,1)S(1)}, bf16[2,2,48,1024]{3,2,1,0:T(8,128)(2,1)S(1)}, u32[]{:S(2)}, u32[]{:S(2)}) collective-permute-start(bf16[2,2,48,1024]{3,2,1,0:T(8,128)(2,1)S(1)} %fusion.79), channel_id=1, source_target_pairs={{0,2},{1,3},{2,0},{3,1},{4,6},{5,7},{6,4},{7,5},{8,10},{9,11},{10,... | collective-permute-start | bytes 1179656 | tf_op jit(solution)/shard_map/ppermute | solution.py:484
  682.0 41.6 %collective-permute-start.66 = (bf16[2,1000,256]{2,1,0:T(8,128)(2,1)S(1)}, bf16[2,1000,256]{2,1,0:T(8,128)(2,1)S(1)}, u32[]{:S(2)}, u32[]{:S(2)}) collective-permute-start(bf16[2,1000,256]{2,1,0:T(8,128)(2,1)S(1)} %fusion.8), channel_id=1, source_target_pairs={{0,2},{1,3},{2,0},{3,1},{4,6},{5,7},{6,4},{7,5},{8,10},{9,11},{10,... | collective-permute-start | bytes 3072008 | tf_op jit(solution)/shard_map/ppermute | solution.py:484
  684.6 100.8 %collective-permute-start.75 = (bf16[2,2,128,1536]{3,2,1,0:T(8,128)(2,1)S(1)}, bf16[2,2,128,1536]{3,2,1,0:T(8,128)(2,1)S(1)}, u32[]{:S(2)}, u32[]{:S(2)}) collective-permute-start(bf16[2,2,128,1536]{3,2,1,0:T(8,128)(2,1)S(1)} %bitcast.617), channel_id=1, source_target_pairs={{0,1},{1,0},{2,3},{3,2},{4,5},{5,4},{6,7},{7,6},{8,9},{9,8},{10,11... | collective-permute-start | bytes 4718600 | tf_op jit(solution)/shard_map/ppermute | solution.py:567
  690.4 38.1 %collective-permute-start.65 = (bf16[128,2048]{1,0:T(8,128)(2,1)S(1)}, bf16[128,2048]{1,0:T(8,128)(2,1)S(1)}, u32[]{:S(2)}, u32[]{:S(2)}) collective-permute-start(bf16[128,2048]{1,0:T(8,128)(2,1)S(1)} %fusion.36), channel_id=1, source_target_pairs={{0,4},{1,5},{2,6},{3,7},{4,0},{5,1},{6,2},{7,3},{8,12},{9,13},{10,... | collective-permute-start | bytes 1572872 | tf_op jit(solution)/shard_map/ppermute | solution.py:484
  708.0 44.9 %collective-permute-start.73 = (bf16[2,128,2048]{2,1,0:T(8,128)(2,1)S(1)}, bf16[2,128,2048]{2,1,0:T(8,128)(2,1)S(1)}, u32[]{:S(2)}, u32[]{:S(2)}) collective-permute-start(bf16[2,128,2048]{2,1,0:T(8,128)(2,1)S(1)} %fusion.28), channel_id=1, source_target_pairs={{0,2},{1,3},{2,0},{3,1},{4,6},{5,7},{6,4},{7,5},{8,10},{9,11},{10,... | collective-permute-start | bytes 3145736 | tf_op jit(solution)/shard_map/ppermute | solution.py:484
  723.6 99.7 %collective-permute-start.69 = (bf16[128,1024]{1,0:T(8,128)(2,1)S(1)}, bf16[128,1024]{1,0:T(8,128)(2,1)S(1)}, u32[]{:S(2)}, u32[]{:S(2)}) collective-permute-start(bf16[128,1024]{1,0:T(8,128)(2,1)S(1)} %fusion.77), channel_id=1, source_target_pairs={{0,1},{1,0},{2,3},{3,2},{4,5},{5,4},{6,7},{7,6},{8,9},{9,8},{10,11... | collective-permute-start | bytes 786440 | tf_op jit(solution)/shard_map/ppermute | solution.py:484
  728.5 18.3 %collective-permute-start.64 = (bf16[2,48,1024]{2,1,0:T(8,128)(2,1)S(1)}, bf16[2,48,1024]{2,1,0:T(8,128)(2,1)S(1)}, u32[]{:S(2)}, u32[]{:S(2)}) collective-permute-start(bf16[2,48,1024]{2,1,0:T(8,128)(2,1)S(1)} %fusion.81), channel_id=1, source_target_pairs={{0,4},{1,5},{2,6},{3,7},{4,0},{5,1},{6,2},{7,3},{8,12},{9,13},{10,... | collective-permute-start | bytes 589832 | tf_op jit(solution)/shard_map/ppermute | solution.py:484
  746.8 25.5 %collective-permute-start.72 = (bf16[1000,256]{1,0:T(8,128)(2,1)S(1)}, bf16[1000,256]{1,0:T(8,128)(2,1)S(1)}, u32[]{:S(2)}, u32[]{:S(2)}) collective-permute-start(bf16[1000,256]{1,0:T(8,128)(2,1)S(1)} %fusion.51), channel_id=1, source_target_pairs={{0,4},{1,5},{2,6},{3,7},{4,0},{5,1},{6,2},{7,3},{8,12},{9,13},{10,... | collective-permute-start | bytes 1536008 | tf_op jit(solution)/shard_map/ppermute | solution.py:484
  752.2 31.8 %collective-permute-start.71 = (bf16[2,128,1536]{2,1,0:T(8,128)(2,1)S(1)}, bf16[2,128,1536]{2,1,0:T(8,128)(2,1)S(1)}, u32[]{:S(2)}, u32[]{:S(2)}) collective-permute-start(bf16[2,128,1536]{2,1,0:T(8,128)(2,1)S(1)} %fusion.59), channel_id=1, source_target_pairs={{0,2},{1,3},{2,0},{3,1},{4,6},{5,7},{6,4},{7,5},{8,10},{9,11},{10,... | collective-permute-start | bytes 2359304 | tf_op jit(solution)/shard_map/ppermute | solution.py:484
  752.9 72.7 %collective-permute-start.68 = (bf16[48,1024]{1,0:T(8,128)(2,1)S(1)}, bf16[48,1024]{1,0:T(8,128)(2,1)S(1)}, u32[]{:S(2)}, u32[]{:S(2)}) collective-permute-start(bf16[48,1024]{1,0:T(8,128)(2,1)S(1)} %fusion.85), channel_id=1, source_target_pairs={{0,1},{1,0},{2,3},{3,2},{4,5},{5,4},{6,7},{7,6},{8,9},{9,8},{10,11... | collective-permute-start | bytes 294920 | tf_op jit(solution)/shard_map/ppermute | solution.py:484
  772.2 26.7 %collective-permute-start.77 = (bf16[128,2048]{1,0:T(8,128)(2,1)S(1)}, bf16[128,2048]{1,0:T(8,128)(2,1)S(1)}, u32[]{:S(2)}, u32[]{:S(2)}) collective-permute-start(bf16[128,2048]{1,0:T(8,128)(2,1)S(1)} %fusion.32), channel_id=1, source_target_pairs={{0,4},{1,5},{2,6},{3,7},{4,0},{5,1},{6,2},{7,3},{8,12},{9,13},{10,... | collective-permute-start | bytes 1572872 | tf_op jit(solution)/shard_map/ppermute | solution.py:484
  786.1 34.3 %collective-permute-start.76 = (bf16[2,128,1536]{2,1,0:T(8,128)(2,1)S(1)}, bf16[2,128,1536]{2,1,0:T(8,128)(2,1)S(1)}, u32[]{:S(2)}, u32[]{:S(2)}) collective-permute-start(bf16[2,128,1536]{2,1,0:T(8,128)(2,1)S(1)} %fusion.60), channel_id=1, source_target_pairs={{0,2},{1,3},{2,0},{3,1},{4,6},{5,7},{6,4},{7,5},{8,10},{9,11},{10,... | collective-permute-start | bytes 2359304 | tf_op jit(solution)/shard_map/ppermute | solution.py:484
  786.1 35.7 %collective-permute-start.74 = (bf16[128,1536]{1,0:T(8,128)(2,1)S(1)}, bf16[128,1536]{1,0:T(8,128)(2,1)S(1)}, u32[]{:S(2)}, u32[]{:S(2)}) collective-permute-start(bf16[128,1536]{1,0:T(8,128)(2,1)S(1)} %fusion.66), channel_id=1, source_target_pairs={{0,4},{1,5},{2,6},{3,7},{4,0},{5,1},{6,2},{7,3},{8,12},{9,13},{10,... | collective-permute-start | bytes 1179656 | tf_op jit(solution)/shard_map/ppermute | solution.py:484
  821.1 17.6 %collective-permute-start.81 = (bf16[128,1536]{1,0:T(8,128)(2,1)S(1)}, bf16[128,1536]{1,0:T(8,128)(2,1)S(1)}, u32[]{:S(2)}, u32[]{:S(2)}) collective-permute-start(bf16[128,1536]{1,0:T(8,128)(2,1)S(1)} %fusion.64), channel_id=1, source_target_pairs={{0,4},{1,5},{2,6},{3,7},{4,0},{5,1},{6,2},{7,3},{8,12},{9,13},{10,... | collective-permute-start | bytes 1179656 | tf_op jit(solution)/shard_map/ppermute | solution.py:484
  (186 other events, 2020.5 us)

commit v6 on v5

--- a/solution.py
+++ b/solution.py
@@ -828,13 +828,17 @@
     token = tab.end(token)
     token = qkv[0].step(token)
     token = qkv[1].step(token)
+    square_sums = after(square_sums, token)
+    square_got = swap(square_sums, "dp", low_first[0])
     token = up[1].end(token)
-    token = qkv[1].step(token)
+    square_sums = square_sums + after(square_got, token)
+    token = qkv[1].step(square_sums)
     token = qkv[0].end(token)
     token = out.end(token)
     token = pack.end(token)
-    square_sums = sum_all(after(square_sums, token), "dp")
-    token = qkv[1].end(token)
+    for bit in low_first[1:]:
+        square_sums = square_sums + swap(square_sums, "dp", bit)
+    token = qkv[1].end(after(square_sums, token))
     target_logit = jnp.sum(latent.astype(F32) * picked_all.astype(F32), axis=1)
     token_loss = (log_total - target_logit) * weight
     seq_loss = jnp.sum(token_loss.reshape(micro, seq_len), axis=1) / seq_len

time: 851 us -> 852 us (level)
    ppermute x29, waiting for transfers between devices: 76.2 us -> 86.6 us  [swap(): return lax.ppermute(x, axis, pairs)]
    ppermute x27, waiting for transfers between devices: 151 us -> 140 us  [send(): lax.ppermute(sent, 'dp', [(i, i ^ 1 << bit) for i in range(lax.axis_size(...]
  transfers between devices with their start and end apart: 82 -> 82, of which waited for: 44 -> 43; matrix products, arithmetic and copies ran while one was open for 11% -> 11% of each run, Pallas kernels for 16% -> 16%
where the time goes in v6:
time: 852 us; the launch traced here: 844 us
  waiting for transfers between devices  322 us (38%)
  Pallas kernels  232 us (27%)
  starting transfers between devices  92.2 us (11%)
  local copies, waits for them, and re-layouts  83.2 us (10%)
  other arithmetic  68.2 us (8%)
  between operations  32.1 us (4%)
  matrix products  14.1 us (2%)
    ppermute x27, waiting for transfers between devices, send(): lax.ppermute(sent, 'dp', [(i, i ^ 1 << bit) for i in range(lax.axis_size(...  140 us
    ppermute x29, waiting for transfers between devices, swap(): return lax.ppermute(x, axis, pairs)  86.6 us
    pallas_call x8, Pallas kernels, layer_backward(): pl.pallas_call(functools.partial(bwd_kernel, tick), in_specs=[SM, VM, HB,...  83.3 us
    pallas_call x8, Pallas kernels, layer_forward(): pl.pallas_call(functools.partial(fwd_kernel, tick), in_specs=[SM, VM, HB,...  77 us
    unnamed x320, local copies, waits for them, and re-layouts  53.1 us
    ppermute x14, waiting for transfers between devices, body(): core_in = lax.ppermute(sent, 'section', core_pairs) if core_pairs else sent  52.6 us
    pallas_call x14, Pallas kernels, product(): pl.pallas_call(product_kernel, grid_spec=pltpu.PrefetchScalarGridSpec(num...  46.6 us
    ppermute x4, waiting for transfers between devices, spread(): got = lax.ppermute(x, axis, pairs)  42.1 us
  transfers between devices with their start and end apart: 82, of which 43 were waited for; matrix products, arithmetic and copies ran while one was open for 11% of the time, Pallas kernels for 16%

profile of v6, /device:TPU:0, one launch (start us, length us, event | category | flops | bytes accessed | tf_op | source)
XLA Modules:
  0.0 843.7 jit_solution(12797832413930758296)
XLA Ops:
  4.0 4.1 collective-permute-start
  59.0 6.7 collective-permute-done.9
  67.2 10.4 %collective-permute-done.10 = bf16[2,2,272,256]{3,2,0,1:T(8,128)(2,1)S(1)} collective-permute-done((bf16[2,2,272,256]{3,2,0,1:T(8,128)(2,1)S(1)}, bf16[2,2,272,256]{3,2,0,1:T(8,128)(2,1)S(1)}, u32[]{:S(2)}, u32[]{:S(2)}) %collective-permute-start.10) | collective-permute-done | bytes 557088 | tf_op jit(solution)/shard_map/ppermute | solution.py:405
  79.2 6.8 collective-permute-done.11
  86.8 4.2 fusion.24
  98.3 5.8 collective-permute-done.17
  109.7 7.9 collective-permute-done.15
  123.2 3.4 copy-done.4
  129.3 14.5 %layer_fwd.8 = (bf16[192,1024]{1,0:T(8,128)(2,1)S(1)}, f32[3,1024]{1,0:T(4,128)S(1)}, bf16[4,192,1024]{2,1,0:T(8,128)(2,1)}, bf16[4,192,1024]{2,1,0:T(8,128)(2,1...) custom-call(s32[22,4]{1,0:T(8,128)S(1)} %copy.296.info.ids, ...), custom_call_target="tpu_custom_call", output_to_operand_aliasing={{2}: (13, {}), {3}: (14, {}), {4}: (15, {}), {5}: (16, {}),... | custom-call | flops 4831838208 | bytes 33554432 | tf_op jit(solution)/shard_map/layer_fwd/pallas_call | solution.py:148
  146.5 13.8 %layer_fwd.9 = (bf16[192,1024]{1,0:T(8,128)(2,1)S(1)}, f32[3,1024]{1,0:T(4,128)S(1)}, bf16[4,192,1024]{2,1,0:T(8,128)(2,1)}, bf16[4,192,1024]{2,1,0:T(8,128)(2,1...) custom-call(s32[22,4]{1,0:T(8,128)S(1)} %copy.296.info.ids, ...), custom_call_target="tpu_custom_call", output_to_operand_aliasing={{2}: (13, {}), {3}: (14, {}), {4}: (15, {}), {5}: (16, {}),... | custom-call | flops 4831838208 | bytes 33554432 | tf_op jit(solution)/shard_map/layer_fwd/pallas_call | solution.py:148
  163.0 14.0 %layer_fwd.10 = (bf16[192,1024]{1,0:T(8,128)(2,1)S(1)}, f32[3,1024]{1,0:T(4,128)S(1)}, bf16[4,192,1024]{2,1,0:T(8,128)(2,1)}, bf16[4,192,1024]{2,1,0:T(8,128)(2,...) custom-call(s32[22,4]{1,0:T(8,128)S(1)} %copy.296.info.ids, ...), custom_call_target="tpu_custom_call", output_to_operand_aliasing={{2}: (13, {}), {3}: (14, {}), {4}: (15, {}), {5}: (16, {}),... | custom-call | flops 4831838208 | bytes 33554432 | tf_op jit(solution)/shard_map/layer_fwd/pallas_call | solution.py:148
  180.0 13.8 %layer_fwd.11 = (bf16[192,1024]{1,0:T(8,128)(2,1)S(1)}, f32[3,1024]{1,0:T(4,128)S(1)}, bf16[4,192,1024]{2,1,0:T(8,128)(2,1)}, bf16[4,192,1024]{2,1,0:T(8,128)(2,...) custom-call(s32[22,4]{1,0:T(8,128)S(1)} %copy.296.info.ids, ...), custom_call_target="tpu_custom_call", output_to_operand_aliasing={{2}: (13, {}), {3}: (14, {}), {4}: (15, {}), {5}: (16, {}),... | custom-call | flops 4831838208 | bytes 33554432 | tf_op jit(solution)/shard_map/layer_fwd/pallas_call | solution.py:148
  196.6 8.5 %layer_fwd.12 = (bf16[192,1024]{1,0:T(8,128)(2,1)S(1)}, f32[3,1024]{1,0:T(4,128)S(1)}, bf16[4,192,1024]{2,1,0:T(8,128)(2,1)}, bf16[4,192,1024]{2,1,0:T(8,128)(2,...) custom-call(s32[22,4]{1,0:T(8,128)S(1)} %copy.296.info.ids, ...), custom_call_target="tpu_custom_call", output_to_operand_aliasing={{2}: (13, {}), {3}: (14, {}), {4}: (15, {}), {5}: (16, {}),... | custom-call | flops 4831838208 | bytes 33554432 | tf_op jit(solution)/shard_map/layer_fwd/pallas_call | solution.py:148
  209.6 10.6 %layer_fwd.14 = (bf16[192,1024]{1,0:T(8,128)(2,1)S(1)}, f32[3,1024]{1,0:T(4,128)S(1)}, bf16[4,192,1024]{2,1,0:T(8,128)(2,1)}, bf16[4,192,1024]{2,1,0:T(8,128)(2,...) custom-call(s32[22,4]{1,0:T(8,128)S(1)} %copy.296.info.ids, ...), custom_call_target="tpu_custom_call", output_to_operand_aliasing={{2}: (13, {}), {3}: (14, {}), {4}: (15, {}), {5}: (16, {}),... | custom-call | flops 4831838208 | bytes 33554432 | tf_op jit(solution)/shard_map/layer_fwd/pallas_call | solution.py:148
  227.0 4.1 collective-permute-start.32
  231.1 38.4 %collective-permute-done.32 = bf16[768,256]{1,0:T(8,128)(2,1)} collective-permute-done((bf16[768,256]{1,0:T(8,128)(2,1)}, bf16[768,256]{1,0:T(8,128)(2,1)}, u32[]{:S(2)}, u32[]{:S(2)}) %collective-permute-start.32) | collective-permute-done | bytes 393248 | tf_op jit(solution)/shard_map/ppermute | solution.py:611
  273.9 14.9 %head_fwd.1 = (bf16[256,768]{1,0:T(8,128)(2,1)S(1)}, f32[2,768]{1,0:T(2,128)S(1)}) custom-call(bf16[8000,256]{1,0:T(8,128)(2,1)S(1)} %bitcast.596, bf16[768,256]{1,0:T(8,128)(2,1)S(1)} %get-tuple-element.414.latent), custom_call_target="tpu_custom_call" | custom-call | flops 6291456000 | bytes 4096000 | tf_op jit(solution)/shard_map/head_fwd/pallas_call | solution.py:333
  298.4 8.2 collective-permute-done.36
  312.0 3.4 copy-done.5
  322.8 12.2 %layer_bwd.10 = (bf16[192,1024]{1,0:T(8,128)(2,1)S(1)}, f32[3,1024]{1,0:T(4,128)S(1)}, bf16[4,192,1024]{2,1,0:T(8,128)(2,1)}, bf16[4,192,4096]{2,1,0:T(8,128)(2,...) custom-call(s32[22,4]{1,0:T(8,128)S(1)} %copy.296.info.ids, ...), custom_call_target="tpu_custom_call", output_to_operand_aliasing={{2}: (18, {}), {3}: (19, {}), {4}: (20, {}), {5}: (21, {}),... | custom-call | flops 4831838208 | bytes 33554432 | tf_op jit(solution)/shard_map/layer_bwd/pallas_call | solution.py:262
  340.7 42.5 %collective-permute-done.41.g_in = bf16[192,1024]{1,0:T(8,128)(2,1)S(1)} collective-permute-done((bf16[192,1024]{1,0:T(8,128)(2,1)S(1)}, bf16[192,1024]{1,0:T(8,128)(2,1)S(1)}, u32[]{:S(2)}, u32[]{:S(2)}) %collective-permute-start.41) | collective-permute-done | bytes 393248 | tf_op jit(solution)/shard_map/ppermute | solution.py:746
  383.3 17.4 %layer_bwd.12 = (bf16[192,1024]{1,0:T(8,128)(2,1)}, f32[3,1024]{1,0:T(4,128)S(1)}, bf16[4,192,1024]{2,1,0:T(8,128)(2,1)}, bf16[4,192,4096]{2,1,0:T(8,128)(2,1)},...) custom-call(s32[22,4]{1,0:T(8,128)S(1)} %copy.296.info.ids, ...), custom_call_target="tpu_custom_call", output_to_operand_aliasing={{2}: (18, {}), {3}: (19, {}), {4}: (20, {}), {5}: (21, {}),... | custom-call | flops 4831838208 | bytes 33554432 | tf_op jit(solution)/shard_map/layer_bwd/pallas_call | solution.py:262
  405.8 3.4 copy-done.3
  415.4 16.1 %layer_bwd.13 = (bf16[192,1024]{1,0:T(8,128)(2,1)S(1)}, f32[3,1024]{1,0:T(4,128)S(1)}, bf16[4,192,1024]{2,1,0:T(8,128)(2,1)}, bf16[4,192,4096]{2,1,0:T(8,128)(2,...) custom-call(s32[22,4]{1,0:T(8,128)S(1)} %copy.296.info.ids, ...), custom_call_target="tpu_custom_call", output_to_operand_aliasing={{2}: (18, {}), {3}: (19, {}), {4}: (20, {}), {5}: (21, {}),... | custom-call | flops 4831838208 | bytes 33554432 | tf_op jit(solution)/shard_map/layer_bwd/pallas_call | solution.py:262
  435.2 16.7 %layer_bwd.14 = (bf16[192,1024]{1,0:T(8,128)(2,1)S(1)}, f32[3,1024]{1,0:T(4,128)S(1)}, bf16[4,192,1024]{2,1,0:T(8,128)(2,1)}, bf16[4,192,4096]{2,1,0:T(8,128)(2,...) custom-call(s32[22,4]{1,0:T(8,128)S(1)} %copy.296.info.ids, ...), custom_call_target="tpu_custom_call", output_to_operand_aliasing={{2}: (18, {}), {3}: (19, {}), {4}: (20, {}), {5}: (21, {}),... | custom-call | flops 4831838208 | bytes 33554432 | tf_op jit(solution)/shard_map/layer_bwd/pallas_call | solution.py:262
  455.5 17.4 %layer_bwd.15 = (bf16[192,1024]{1,0:T(8,128)(2,1)}, f32[3,1024]{1,0:T(4,128)S(1)}, bf16[4,192,1024]{2,1,0:T(8,128)(2,1)}, bf16[4,192,4096]{2,1,0:T(8,128)(2,1)},...) custom-call(s32[22,4]{1,0:T(8,128)S(1)} %copy.296.info.ids, ...), custom_call_target="tpu_custom_call", output_to_operand_aliasing={{2}: (18, {}), {3}: (19, {}), {4}: (20, {}), {5}: (21, {}),... | custom-call | flops 4831838208 | bytes 33554432 | tf_op jit(solution)/shard_map/layer_bwd/pallas_call | solution.py:262
  483.3 3.9 product.15
  490.4 4.6 product.17
  501.3 3.8 product.20
  510.0 17.6 %collective-permute-done.49 = bf16[2,2,512,512]{3,2,1,0:T(8,128)(2,1)S(1)} collective-permute-done((bf16[2,2,512,512]{3,2,1,0:T(8,128)(2,1)S(1)}, bf16[2,2,512,512]{3,2,1,0:T(8,128)(2,1)S(1)}, u32[]{:S(2)}, u32[]{:S(2)}) %collective-permute-start.49) | collective-permute-done | bytes 2097184 | tf_op jit(solution)/shard_map/ppermute | solution.py:567
  543.6 3.7 collective-permute-done.53
  551.4 10.6 %head_bwd.1 = bf16[8000,256]{1,0:T(8,128)(2,1)S(1)} custom-call(bf16[8000,256]{1,0:T(8,128)(2,1)S(1)} %bitcast.597, bf16[768,256]{1,0:T(8,128)(2,1)S(1)} %copy-done.29, f32[1,768]{1,0:T(1,128)S(1)} %get-tuple-element.448.log_total, f32[1,768]{1,0:T(1,128)S(1)} %broadcast_in_dim.29.weight, s32[1,768]{1,0:T(1,128)S(1)} %broadcast_in_dim.30.ids, ...), custom_call_target="tpu_custom_call" | custom-call | flops 1 | bytes 1 | tf_op jit(solution)/shard_map/head_bwd/pallas_call | solution.py:358
  564.5 3.9 product.22
  569.7 3.9 product.23
  582.5 4.0 collective-permute-start.57
  611.4 6.2 collective-permute-done.59
  627.9 7.3 collective-permute-done.56
  652.5 9.1 %collective-permute-done.65 = bf16[2,2,1000,256]{3,2,1,0:T(8,128)(2,1)} collective-permute-done((bf16[2,2,1000,256]{3,2,1,0:T(8,128)(2,1)}, bf16[2,2,1000,256]{3,2,1,0:T(8,128)(2,1)}, u32[]{:S(2)}, u32[]{:S(2)}) %collective-permute-start.65) | collective-permute-done | bytes 2048032 | tf_op jit(solution)/shard_map/ppermute | solution.py:484
  664.4 17.7 %collective-permute-done.64 = bf16[2,128,2048]{2,1,0:T(8,128)(2,1)S(1)} collective-permute-done((bf16[2,128,2048]{2,1,0:T(8,128)(2,1)S(1)}, bf16[2,128,2048]{2,1,0:T(8,128)(2,1)S(1)}, u32[]{:S(2)}, u32[]{:S(2)}) %collective-permute-start.64) | collective-permute-done | bytes 1048608 | tf_op jit(solution)/shard_map/ppermute | solution.py:484
  692.3 14.2 %collective-permute-done.69 = bf16[2,2,128,2048]{3,2,1,0:T(8,128)(2,1)} collective-permute-done((bf16[2,2,128,2048]{3,2,1,0:T(8,128)(2,1)}, bf16[2,2,128,2048]{3,2,1,0:T(8,128)(2,1)}, u32[]{:S(2)}, u32[]{:S(2)}) %collective-permute-start.69) | collective-permute-done | bytes 2097184 | tf_op jit(solution)/shard_map/ppermute | solution.py:567
  710.8 12.8 %collective-permute-done.68 = bf16[2,1000,256]{2,1,0:T(8,128)(2,1)S(1)} collective-permute-done((bf16[2,1000,256]{2,1,0:T(8,128)(2,1)S(1)}, bf16[2,1000,256]{2,1,0:T(8,128)(2,1)S(1)}, u32[]{:S(2)}, u32[]{:S(2)}) %collective-permute-start.68) | collective-permute-done | bytes 1024032 | tf_op jit(solution)/shard_map/ppermute | solution.py:484
  731.2 15.7 %collective-permute-done.66 = bf16[2,48,1024]{2,1,0:T(8,128)(2,1)S(1)} collective-permute-done((bf16[2,48,1024]{2,1,0:T(8,128)(2,1)S(1)}, bf16[2,48,1024]{2,1,0:T(8,128)(2,1)S(1)}, u32[]{:S(2)}, u32[]{:S(2)}) %collective-permute-start.66) | collective-permute-done | bytes 196640 | tf_op jit(solution)/shard_map/ppermute | solution.py:484
  746.9 3.4 collective-permute-start.71
  758.0 14.3 %collective-permute-done.71 = bf16[1000,256]{1,0:T(8,128)(2,1)S(1)} collective-permute-done((bf16[1000,256]{1,0:T(8,128)(2,1)S(1)}, bf16[1000,256]{1,0:T(8,128)(2,1)S(1)}, u32[]{:S(2)}, u32[]{:S(2)}) %collective-permute-start.71) | collective-permute-done | bytes 512032 | tf_op jit(solution)/shard_map/ppermute | solution.py:484
  776.3 7.8 collective-permute-done.70
  789.1 10.0 %collective-permute-done.74 = bf16[128,2048]{1,0:T(8,128)(2,1)S(1)} collective-permute-done((bf16[128,2048]{1,0:T(8,128)(2,1)S(1)}, bf16[128,2048]{1,0:T(8,128)(2,1)S(1)}, u32[]{:S(2)}, u32[]{:S(2)}) %collective-permute-start.74) | collective-permute-done | bytes 524320 | tf_op jit(solution)/shard_map/ppermute | solution.py:484
  805.7 14.9 %collective-permute-done.75 = f32[3]{0:T(128)S(1)} collective-permute-done((f32[3]{0:T(128)S(1)}, f32[3]{0:T(128)S(1)}, u32[]{:S(2)}, u32[]{:S(2)}) %collective-permute-start.75) | collective-permute-done | bytes 44 | tf_op jit(solution)/shard_map/ppermute | solution.py:405
  831.8 7.0 collective-permute-done.78
  (709 shorter events, 296.2 us)
Async XLA Ops:
  4.0 19.9 %collective-permute-start = (bf16[272,256]{1,0:T(8,128)(2,1)S(1)}, bf16[272,256]{1,0:T(8,128)(2,1)S(1)}, u32[]{:S(2)}, u32[]{:S(2)}) collective-permute-start(bf16[272,256]{1,0:T(8,128)(2,1)S(1)} %get-tuple-element.425), channel_id=1, source_target_pairs={{0,4},{1,5},{2,6},{3,7},{4,0},{5,1},{6,2},{7,3},{8,12},{9,13},{10,... | collective-permute-start | bytes 417800 | tf_op jit(solution)/shard_map/ppermute | solution.py:405
  8.1 18.9 %collective-permute-start.4 = (bf16[272,256]{1,0:T(8,128)(2,1)S(1)}, bf16[272,256]{1,0:T(8,128)(2,1)S(1)}, u32[]{:S(2)}, u32[]{:S(2)}) collective-permute-start(bf16[272,256]{1,0:T(8,128)(2,1)S(1)} %get-tuple-element.423), channel_id=1, source_target_pairs={{0,4},{1,5},{2,6},{3,7},{4,0},{5,1},{6,2},{7,3},{8,12},{9,13},{10,... | collective-permute-start | bytes 417800 | tf_op jit(solution)/shard_map/ppermute | solution.py:405
  8.2 21.8 %collective-permute-start.3 = (bf16[272,256]{1,0:T(8,128)(2,1)S(1)}, bf16[272,256]{1,0:T(8,128)(2,1)S(1)}, u32[]{:S(2)}, u32[]{:S(2)}) collective-permute-start(bf16[272,256]{1,0:T(8,128)(2,1)S(1)} %get-tuple-element.424), channel_id=1, source_target_pairs={{0,4},{1,5},{2,6},{3,7},{4,0},{5,1},{6,2},{7,3},{8,12},{9,13},{10,... | collective-permute-start | bytes 417800 | tf_op jit(solution)/shard_map/ppermute | solution.py:405
  11.1 20.5 %collective-permute-start.2 = (bf16[216,256]{1,0:T(8,128)(2,1)S(1)}, bf16[216,256]{1,0:T(8,128)(2,1)S(1)}, u32[]{:S(2)}, u32[]{:S(2)}) collective-permute-start(bf16[216,256]{1,0:T(8,128)(2,1)S(1)} %pad_maximum_fusion.8), channel_id=1, source_target_pairs={{0,4},{1,5},{2,6},{3,7},{4,0},{5,1},{6,2},{7,3},{8,12},{9,13},{10,... | collective-permute-start | bytes 331784 | tf_op jit(solution)/shard_map/ppermute | solution.py:405
  19.7 71.4 %collective-permute-start.16 = (f32[4,48,256]{2,1,0:T(8,128)S(1)}, f32[4,48,256]{2,1,0:T(8,128)S(1)}, u32[]{:S(2)}, u32[]{:S(2)}) collective-permute-start(f32[4,48,256]{2,1,0:T(8,128)S(1)} %copy-done.96), channel_id=1, source_target_pairs={{0,8},{8,0},{16,24},{24,16},{1,9},{9,1},{17,25},{25,17},{2,10},{10... | collective-permute-start | bytes 589832 | tf_op jit(solution)/shard_map/ppermute | solution.py:405
  27.6 15.9 %collective-permute-start.8 = (bf16[2,272,256]{2,1,0:T(8,128)(2,1)S(1)}, bf16[2,272,256]{2,1,0:T(8,128)(2,1)S(1)}, u32[]{:S(2)}, u32[]{:S(2)}) collective-permute-start(bf16[2,272,256]{2,1,0:T(8,128)(2,1)S(1)} %maximum_select_fusion.15), channel_id=1, source_target_pairs={{0,2},{1,3},{2,0},{3,1},{4,6},{5,7},{6,4},{7,5},{8,10},{9,11},{10,... | collective-permute-start | bytes 835592 | tf_op jit(solution)/shard_map/ppermute | solution.py:405
  30.6 18.9 %collective-permute-start.7 = (bf16[2,272,256]{2,1,0:T(8,128)(2,1)S(1)}, bf16[2,272,256]{2,1,0:T(8,128)(2,1)S(1)}, u32[]{:S(2)}, u32[]{:S(2)}) collective-permute-start(bf16[2,272,256]{2,1,0:T(8,128)(2,1)S(1)} %maximum_select_fusion.16), channel_id=1, source_target_pairs={{0,2},{1,3},{2,0},{3,1},{4,6},{5,7},{6,4},{7,5},{8,10},{9,11},{10,... | collective-permute-start | bytes 835592 | tf_op jit(solution)/shard_map/ppermute | solution.py:405
  31.8 22.3 %collective-permute-start.6 = (bf16[2,216,256]{2,1,0:T(8,128)(2,1)S(1)}, bf16[2,216,256]{2,1,0:T(8,128)(2,1)S(1)}, u32[]{:S(2)}, u32[]{:S(2)}) collective-permute-start(bf16[2,216,256]{2,1,0:T(8,128)(2,1)S(1)} %maximum_select_fusion.19), channel_id=1, source_target_pairs={{0,2},{1,3},{2,0},{3,1},{4,6},{5,7},{6,4},{7,5},{8,10},{9,11},{10,... | collective-permute-start | bytes 663560 | tf_op jit(solution)/shard_map/ppermute | solution.py:405
  38.2 19.3 %collective-permute-start.5 = (bf16[2,2,272,256]{3,2,0,1:T(8,128)(2,1)S(1)}, bf16[2,2,272,256]{3,2,0,1:T(8,128)(2,1)S(1)}, u32[]{:S(2)}, u32[]{:S(2)}) collective-permute-start(bf16[2,2,272,256]{3,2,0,1:T(8,128)(2,1)S(1)} %maximum_select_fusion.6), channel_id=1, source_target_pairs={{0,1},{1,0},{2,3},{3,2},{4,5},{5,4},{6,7},{7,6},{8,9},{9,8},{10,11... | collective-permute-start | bytes 1671176 | tf_op jit(solution)/shard_map/ppermute | solution.py:405
  44.2 21.5 %collective-permute-start.9 = (bf16[2,2,272,256]{3,2,0,1:T(8,128)(2,1)S(1)}, bf16[2,2,272,256]{3,2,0,1:T(8,128)(2,1)S(1)}, u32[]{:S(2)}, u32[]{:S(2)}) collective-permute-start(bf16[2,2,272,256]{3,2,0,1:T(8,128)(2,1)S(1)} %maximum_select_fusion.7), channel_id=1, source_target_pairs={{0,1},{1,0},{2,3},{3,2},{4,5},{5,4},{6,7},{7,6},{8,9},{9,8},{10,11... | collective-permute-start | bytes 1671176 | tf_op jit(solution)/shard_map/ppermute | solution.py:405
  50.1 27.4 %collective-permute-start.10 = (bf16[2,2,272,256]{3,2,0,1:T(8,128)(2,1)S(1)}, bf16[2,2,272,256]{3,2,0,1:T(8,128)(2,1)S(1)}, u32[]{:S(2)}, u32[]{:S(2)}) collective-permute-start(bf16[2,2,272,256]{3,2,0,1:T(8,128)(2,1)S(1)} %maximum_select_fusion.8), channel_id=1, source_target_pairs={{0,1},{1,0},{2,3},{3,2},{4,5},{5,4},{6,7},{7,6},{8,9},{9,8},{10,11... | collective-permute-start | bytes 1671176 | tf_op jit(solution)/shard_map/ppermute | solution.py:405
  54.3 31.7 %collective-permute-start.11 = (bf16[2,2,216,256]{3,2,1,0:T(8,128)(2,1)S(1)}, bf16[2,2,216,256]{3,2,1,0:T(8,128)(2,1)S(1)}, u32[]{:S(2)}, u32[]{:S(2)}) collective-permute-start(bf16[2,2,216,256]{3,2,1,0:T(8,128)(2,1)S(1)} %copy_select_fusion), channel_id=1, source_target_pairs={{0,1},{1,0},{2,3},{3,2},{4,5},{5,4},{6,7},{7,6},{8,9},{9,8},{10,11... | collective-permute-start | bytes 1327112 | tf_op jit(solution)/shard_map/ppermute | solution.py:405
  95.0 14.6 %collective-permute-start.19 = (bf16[2,64,1024]{2,1,0:T(8,128)(2,1)S(1)}, bf16[2,64,1024]{2,1,0:T(8,128)(2,1)S(1)}, u32[]{:S(2)}, u32[]{:S(2)}) collective-permute-start(bf16[2,64,1024]{2,1,0:T(8,128)(2,1)S(1)} %maximum_select_fusion.18), channel_id=1, source_target_pairs={{0,16},{8,24},{16,0},{24,8},{1,17},{9,25},{17,1},{25,9},{2,18},{10... | collective-permute-start | bytes 786440 | tf_op jit(solution)/shard_map/ppermute | solution.py:405
  96.6 21.0 %collective-permute-start.15 = (bf16[768,256]{1,0:T(8,128)(2,1)S(1)}, bf16[768,256]{1,0:T(8,128)(2,1)S(1)}, u32[]{:S(2)}, u32[]{:S(2)}) collective-permute-start(bf16[768,256]{1,0:T(8,128)(2,1)S(1)} %add.1018), channel_id=1, source_target_pairs={{0,16},{8,24},{16,0},{24,8},{1,17},{9,25},{17,1},{25,9},{2,18},{10... | collective-permute-start | bytes 1179656 | tf_op jit(solution)/shard_map/ppermute | solution.py:405
  161.7 17.6 %collective-permute-start.23 = (bf16[192,1024]{1,0:T(8,128)(2,1)S(1)}, bf16[192,1024]{1,0:T(8,128)(2,1)S(1)}, u32[]{:S(2)}, u32[]{:S(2)}) collective-permute-start(bf16[192,1024]{1,0:T(8,128)(2,1)S(1)} %get-tuple-element.223), channel_id=1, source_target_pairs={{8,16},{9,17},{10,18},{11,19},{12,20},{13,21},{14,22},{15,23}} | collective-permute-start | bytes 1179656 | tf_op jit(solution)/shard_map/ppermute | solution.py:708
  178.5 17.3 %collective-permute-start.25 = (bf16[192,1024]{1,0:T(8,128)(2,1)S(1)}, bf16[192,1024]{1,0:T(8,128)(2,1)S(1)}, u32[]{:S(2)}, u32[]{:S(2)}) collective-permute-start(bf16[192,1024]{1,0:T(8,128)(2,1)S(1)} %get-tuple-element.233), channel_id=1, source_target_pairs={{8,16},{9,17},{10,18},{11,19},{12,20},{13,21},{14,22},{15,23}} | collective-permute-start | bytes 1179656 | tf_op jit(solution)/shard_map/ppermute | solution.py:708
  227.0 42.5 %collective-permute-start.32 = (bf16[768,256]{1,0:T(8,128)(2,1)}, bf16[768,256]{1,0:T(8,128)(2,1)}, u32[]{:S(2)}, u32[]{:S(2)}) collective-permute-start(bf16[768,256]{1,0:T(8,128)(2,1)} %broadcast_select_fusion.1), channel_id=1, source_target_pairs={{24,8},{16,0},{25,9},{17,1},{26,10},{18,2},{27,11},{19,3},{28,12},... | collective-permute-start | bytes 1179656 | tf_op jit(solution)/shard_map/ppermute | solution.py:611
  338.0 45.3 %collective-permute-start.41 = (bf16[192,1024]{1,0:T(8,128)(2,1)S(1)}, bf16[192,1024]{1,0:T(8,128)(2,1)S(1)}, u32[]{:S(2)}, u32[]{:S(2)}) collective-permute-start(bf16[192,1024]{1,0:T(8,128)(2,1)S(1)} %get-tuple-element.323), channel_id=1, source_target_pairs={{8,0},{24,16},{9,1},{25,17},{10,2},{26,18},{11,3},{27,19},{12,4},{... | collective-permute-start | bytes 1179656 | tf_op jit(solution)/shard_map/ppermute | solution.py:746
  339.3 64.1 %collective-permute-start.44 = (bf16[192,1024]{1,0:T(8,128)(2,1)S(1)}, bf16[192,1024]{1,0:T(8,128)(2,1)}, u32[]{:S(2)}, u32[]{:S(2)}) collective-permute-start(bf16[192,1024]{1,0:T(8,128)(2,1)S(1)} %get-tuple-element.323), channel_id=1, source_target_pairs={{16,8},{17,9},{18,10},{19,11},{20,12},{21,13},{22,14},{23,15}} | collective-permute-start | bytes 1179656 | tf_op jit(solution)/shard_map/ppermute | solution.py:748
  402.7 30.2 %collective-permute-start.46 = (bf16[192,1024]{1,0:T(8,128)(2,1)}, bf16[192,1024]{1,0:T(8,128)(2,1)S(1)}, u32[]{:S(2)}, u32[]{:S(2)}) collective-permute-start(bf16[192,1024]{1,0:T(8,128)(2,1)} %get-tuple-element.329), channel_id=1, source_target_pairs={{16,8},{17,9},{18,10},{19,11},{20,12},{21,13},{22,14},{23,15}} | collective-permute-start | bytes 1179656 | tf_op jit(solution)/shard_map/ppermute | solution.py:748
  479.1 48.6 %collective-permute-start.49 = (bf16[2,2,512,512]{3,2,1,0:T(8,128)(2,1)S(1)}, bf16[2,2,512,512]{3,2,1,0:T(8,128)(2,1)S(1)}, u32[]{:S(2)}, u32[]{:S(2)}) collective-permute-start(bf16[2,2,512,512]{3,2,1,0:T(8,128)(2,1)S(1)} %bitcast.620), channel_id=1, source_target_pairs={{0,1},{1,0},{2,3},{3,2},{4,5},{5,4},{6,7},{7,6},{8,9},{9,8},{10,11... | collective-permute-start | bytes 6291464 | tf_op jit(solution)/shard_map/ppermute | solution.py:567
  509.6 66.6 %collective-permute-start.51 = (bf16[2,2,512,512]{3,2,1,0:T(8,128)(2,1)}, bf16[2,2,512,512]{3,2,1,0:T(8,128)(2,1)}, u32[]{:S(2)}, u32[]{:S(2)}) collective-permute-start(bf16[2,2,512,512]{3,2,1,0:T(8,128)(2,1)} %bitcast.123), channel_id=1, source_target_pairs={{0,1},{1,0},{2,3},{3,2},{4,5},{5,4},{6,7},{7,6},{8,9},{9,8},{10,11... | collective-permute-start | bytes 6291464 | tf_op jit(solution)/shard_map/ppermute | solution.py:567
  535.2 54.5 %collective-permute-start.48 = (bf16[2,2,128,1024]{3,2,1,0:T(8,128)(2,1)}, bf16[2,2,128,1024]{3,2,1,0:T(8,128)(2,1)}, u32[]{:S(2)}, u32[]{:S(2)}) collective-permute-start(bf16[2,2,128,1024]{3,2,1,0:T(8,128)(2,1)} %bitcast.116), channel_id=1, source_target_pairs={{0,2},{1,3},{2,0},{3,1},{4,6},{5,7},{6,4},{7,5},{8,10},{9,11},{10,... | collective-permute-start | bytes 3145736 | tf_op jit(solution)/shard_map/ppermute | solution.py:567
  535.2 82.5 %collective-permute-start.59 = (bf16[2,2,128,2048]{3,2,1,0:T(8,128)(2,1)}, bf16[2,2,128,2048]{3,2,1,0:T(8,128)(2,1)}, u32[]{:S(2)}, u32[]{:S(2)}) collective-permute-start(bf16[2,2,128,2048]{3,2,1,0:T(8,128)(2,1)} %bitcast.152), channel_id=1, source_target_pairs={{0,1},{1,0},{2,3},{3,2},{4,5},{5,4},{6,7},{7,6},{8,9},{9,8},{10,11... | collective-permute-start | bytes 6291464 | tf_op jit(solution)/shard_map/ppermute | solution.py:567
  536.8 44.1 %collective-permute-start.50 = (bf16[2,512,512]{2,1,0:T(8,128)(2,1)}, bf16[2,512,512]{2,1,0:T(8,128)(2,1)}, u32[]{:S(2)}, u32[]{:S(2)}) collective-permute-start(bf16[2,512,512]{2,1,0:T(8,128)(2,1)} %fusion.25.token), channel_id=1, source_target_pairs={{0,2},{1,3},{2,0},{3,1},{4,6},{5,7},{6,4},{7,5},{8,10},{9,11},{10,... | collective-permute-start | bytes 3145736 | tf_op jit(solution)/shard_map/ppermute | solution.py:484
  578.7 43.4 %collective-permute-start.58 = (bf16[2,512,512]{2,1,0:T(8,128)(2,1)}, bf16[2,512,512]{2,1,0:T(8,128)(2,1)}, u32[]{:S(2)}, u32[]{:S(2)}) collective-permute-start(bf16[2,512,512]{2,1,0:T(8,128)(2,1)} %fusion.26), channel_id=1, source_target_pairs={{0,2},{1,3},{2,0},{3,1},{4,6},{5,7},{6,4},{7,5},{8,10},{9,11},{10,... | collective-permute-start | bytes 3145736 | tf_op jit(solution)/shard_map/ppermute | solution.py:484
  582.5 42.4 %collective-permute-start.57 = (bf16[512,512]{1,0:T(8,128)(2,1)S(1)}, bf16[512,512]{1,0:T(8,128)(2,1)S(1)}, u32[]{:S(2)}, u32[]{:S(2)}) collective-permute-start(bf16[512,512]{1,0:T(8,128)(2,1)S(1)} %fusion.44), channel_id=1, source_target_pairs={{0,4},{1,5},{2,6},{3,7},{4,0},{5,1},{6,2},{7,3},{8,12},{9,13},{10,... | collective-permute-start | bytes 1572872 | tf_op jit(solution)/shard_map/ppermute | solution.py:484
  587.0 74.6 %collective-permute-start.65 = (bf16[2,2,1000,256]{3,2,1,0:T(8,128)(2,1)}, bf16[2,2,1000,256]{3,2,1,0:T(8,128)(2,1)}, u32[]{:S(2)}, u32[]{:S(2)}) collective-permute-start(bf16[2,2,1000,256]{3,2,1,0:T(8,128)(2,1)} %copy-done.24), channel_id=1, source_target_pairs={{0,1},{1,0},{2,3},{3,2},{4,5},{5,4},{6,7},{7,6},{8,9},{9,8},{10,11... | collective-permute-start | bytes 6144008 | tf_op jit(solution)/shard_map/ppermute | solution.py:484
  589.7 116.8 %collective-permute-start.69 = (bf16[2,2,128,2048]{3,2,1,0:T(8,128)(2,1)}, bf16[2,2,128,2048]{3,2,1,0:T(8,128)(2,1)}, u32[]{:S(2)}, u32[]{:S(2)}) collective-permute-start(bf16[2,2,128,2048]{3,2,1,0:T(8,128)(2,1)} %bitcast.619), channel_id=1, source_target_pairs={{0,1},{1,0},{2,3},{3,2},{4,5},{5,4},{6,7},{7,6},{8,9},{9,8},{10,11... | collective-permute-start | bytes 6291464 | tf_op jit(solution)/shard_map/ppermute | solution.py:567
  617.7 17.6 %collective-permute-start.56 = (bf16[2,128,1024]{2,1,0:T(8,128)(2,1)S(1)}, bf16[2,128,1024]{2,1,0:T(8,128)(2,1)S(1)}, u32[]{:S(2)}, u32[]{:S(2)}) collective-permute-start(bf16[2,128,1024]{2,1,0:T(8,128)(2,1)S(1)} %fusion.72.refs_5_), channel_id=1, source_target_pairs={{0,4},{1,5},{2,6},{3,7},{4,0},{5,1},{6,2},{7,3},{8,12},{9,13},{10,... | collective-permute-start | bytes 1572872 | tf_op jit(solution)/shard_map/ppermute | solution.py:484
  644.8 37.3 %collective-permute-start.64 = (bf16[2,128,2048]{2,1,0:T(8,128)(2,1)S(1)}, bf16[2,128,2048]{2,1,0:T(8,128)(2,1)S(1)}, u32[]{:S(2)}, u32[]{:S(2)}) collective-permute-start(bf16[2,128,2048]{2,1,0:T(8,128)(2,1)S(1)} %copy-done.95), channel_id=1, source_target_pairs={{0,2},{1,3},{2,0},{3,1},{4,6},{5,7},{6,4},{7,5},{8,10},{9,11},{10,... | collective-permute-start | bytes 3145736 | tf_op jit(solution)/shard_map/ppermute | solution.py:484
  644.8 106.8 %collective-permute-start.55 = (bf16[2,2,128,1536]{3,2,1,0:T(8,128)(2,1)S(1)}, bf16[2,2,128,1536]{3,2,1,0:T(8,128)(2,1)S(1)}, u32[]{:S(2)}, u32[]{:S(2)}) collective-permute-start(bf16[2,2,128,1536]{3,2,1,0:T(8,128)(2,1)S(1)} %bitcast.622), channel_id=1, source_target_pairs={{0,1},{1,0},{2,3},{3,2},{4,5},{5,4},{6,7},{7,6},{8,9},{9,8},{10,11... | collective-permute-start | bytes 4718600 | tf_op jit(solution)/shard_map/ppermute | solution.py:567
  651.1 33.6 %collective-permute-start.63 = (bf16[512,512]{1,0:T(8,128)(2,1)S(1)}, bf16[512,512]{1,0:T(8,128)(2,1)S(1)}, u32[]{:S(2)}, u32[]{:S(2)}) collective-permute-start(bf16[512,512]{1,0:T(8,128)(2,1)S(1)} %copy-done.98), channel_id=1, source_target_pairs={{0,4},{1,5},{2,6},{3,7},{4,0},{5,1},{6,2},{7,3},{8,12},{9,13},{10,... | collective-permute-start | bytes 1572872 | tf_op jit(solution)/shard_map/ppermute | solution.py:484
  661.6 28.9 %collective-permute-start.62 = (bf16[2,2,48,1024]{3,2,1,0:T(8,128)(2,1)S(1)}, bf16[2,2,48,1024]{3,2,1,0:T(8,128)(2,1)S(1)}, u32[]{:S(2)}, u32[]{:S(2)}) collective-permute-start(bf16[2,2,48,1024]{3,2,1,0:T(8,128)(2,1)S(1)} %fusion.79), channel_id=1, source_target_pairs={{0,2},{1,3},{2,0},{3,1},{4,6},{5,7},{6,4},{7,5},{8,10},{9,11},{10,... | collective-permute-start | bytes 1179656 | tf_op jit(solution)/shard_map/ppermute | solution.py:484
  682.1 41.6 %collective-permute-start.68 = (bf16[2,1000,256]{2,1,0:T(8,128)(2,1)S(1)}, bf16[2,1000,256]{2,1,0:T(8,128)(2,1)S(1)}, u32[]{:S(2)}, u32[]{:S(2)}) collective-permute-start(bf16[2,1000,256]{2,1,0:T(8,128)(2,1)S(1)} %fusion.8), channel_id=1, source_target_pairs={{0,2},{1,3},{2,0},{3,1},{4,6},{5,7},{6,4},{7,5},{8,10},{9,11},{10,... | collective-permute-start | bytes 3072008 | tf_op jit(solution)/shard_map/ppermute | solution.py:484
  684.7 100.8 %collective-permute-start.54 = (bf16[2,2,128,1536]{3,2,1,0:T(8,128)(2,1)S(1)}, bf16[2,2,128,1536]{3,2,1,0:T(8,128)(2,1)S(1)}, u32[]{:S(2)}, u32[]{:S(2)}) collective-permute-start(bf16[2,2,128,1536]{3,2,1,0:T(8,128)(2,1)S(1)} %bitcast.621), channel_id=1, source_target_pairs={{0,1},{1,0},{2,3},{3,2},{4,5},{5,4},{6,7},{7,6},{8,9},{9,8},{10,11... | collective-permute-start | bytes 4718600 | tf_op jit(solution)/shard_map/ppermute | solution.py:567
  690.5 38.1 %collective-permute-start.67 = (bf16[128,2048]{1,0:T(8,128)(2,1)S(1)}, bf16[128,2048]{1,0:T(8,128)(2,1)S(1)}, u32[]{:S(2)}, u32[]{:S(2)}) collective-permute-start(bf16[128,2048]{1,0:T(8,128)(2,1)S(1)} %fusion.36), channel_id=1, source_target_pairs={{0,4},{1,5},{2,6},{3,7},{4,0},{5,1},{6,2},{7,3},{8,12},{9,13},{10,... | collective-permute-start | bytes 1572872 | tf_op jit(solution)/shard_map/ppermute | solution.py:484
  708.1 44.9 %collective-permute-start.72 = (bf16[2,128,2048]{2,1,0:T(8,128)(2,1)S(1)}, bf16[2,128,2048]{2,1,0:T(8,128)(2,1)S(1)}, u32[]{:S(2)}, u32[]{:S(2)}) collective-permute-start(bf16[2,128,2048]{2,1,0:T(8,128)(2,1)S(1)} %fusion.28), channel_id=1, source_target_pairs={{0,2},{1,3},{2,0},{3,1},{4,6},{5,7},{6,4},{7,5},{8,10},{9,11},{10,... | collective-permute-start | bytes 3145736 | tf_op jit(solution)/shard_map/ppermute | solution.py:484
  723.7 102.7 %collective-permute-start.80 = (bf16[128,1024]{1,0:T(8,128)(2,1)S(1)}, bf16[128,1024]{1,0:T(8,128)(2,1)S(1)}, u32[]{:S(2)}, u32[]{:S(2)}) collective-permute-start(bf16[128,1024]{1,0:T(8,128)(2,1)S(1)} %fusion.77), channel_id=1, source_target_pairs={{0,1},{1,0},{2,3},{3,2},{4,5},{5,4},{6,7},{7,6},{8,9},{9,8},{10,11... | collective-permute-start | bytes 786440 | tf_op jit(solution)/shard_map/ppermute | solution.py:484
  728.6 18.3 %collective-permute-start.66 = (bf16[2,48,1024]{2,1,0:T(8,128)(2,1)S(1)}, bf16[2,48,1024]{2,1,0:T(8,128)(2,1)S(1)}, u32[]{:S(2)}, u32[]{:S(2)}) collective-permute-start(bf16[2,48,1024]{2,1,0:T(8,128)(2,1)S(1)} %fusion.81), channel_id=1, source_target_pairs={{0,4},{1,5},{2,6},{3,7},{4,0},{5,1},{6,2},{7,3},{8,12},{9,13},{10,... | collective-permute-start | bytes 589832 | tf_op jit(solution)/shard_map/ppermute | solution.py:484
  746.9 25.5 %collective-permute-start.71 = (bf16[1000,256]{1,0:T(8,128)(2,1)S(1)}, bf16[1000,256]{1,0:T(8,128)(2,1)S(1)}, u32[]{:S(2)}, u32[]{:S(2)}) collective-permute-start(bf16[1000,256]{1,0:T(8,128)(2,1)S(1)} %fusion.51), channel_id=1, source_target_pairs={{0,4},{1,5},{2,6},{3,7},{4,0},{5,1},{6,2},{7,3},{8,12},{9,13},{10,... | collective-permute-start | bytes 1536008 | tf_op jit(solution)/shard_map/ppermute | solution.py:484
  752.3 31.8 %collective-permute-start.70 = (bf16[2,128,1536]{2,1,0:T(8,128)(2,1)S(1)}, bf16[2,128,1536]{2,1,0:T(8,128)(2,1)S(1)}, u32[]{:S(2)}, u32[]{:S(2)}) collective-permute-start(bf16[2,128,1536]{2,1,0:T(8,128)(2,1)S(1)} %fusion.59), channel_id=1, source_target_pairs={{0,2},{1,3},{2,0},{3,1},{4,6},{5,7},{6,4},{7,5},{8,10},{9,11},{10,... | collective-permute-start | bytes 2359304 | tf_op jit(solution)/shard_map/ppermute | solution.py:484
  753.0 75.7 %collective-permute-start.79 = (bf16[48,1024]{1,0:T(8,128)(2,1)S(1)}, bf16[48,1024]{1,0:T(8,128)(2,1)S(1)}, u32[]{:S(2)}, u32[]{:S(2)}) collective-permute-start(bf16[48,1024]{1,0:T(8,128)(2,1)S(1)} %fusion.87), channel_id=1, source_target_pairs={{0,1},{1,0},{2,3},{3,2},{4,5},{5,4},{6,7},{7,6},{8,9},{9,8},{10,11... | collective-permute-start | bytes 294920 | tf_op jit(solution)/shard_map/ppermute | solution.py:484
  772.4 26.7 %collective-permute-start.74 = (bf16[128,2048]{1,0:T(8,128)(2,1)S(1)}, bf16[128,2048]{1,0:T(8,128)(2,1)S(1)}, u32[]{:S(2)}, u32[]{:S(2)}) collective-permute-start(bf16[128,2048]{1,0:T(8,128)(2,1)S(1)} %fusion.32), channel_id=1, source_target_pairs={{0,4},{1,5},{2,6},{3,7},{4,0},{5,1},{6,2},{7,3},{8,12},{9,13},{10,... | collective-permute-start | bytes 1572872 | tf_op jit(solution)/shard_map/ppermute | solution.py:484
  786.3 34.4 %collective-permute-start.77 = (bf16[2,128,1536]{2,1,0:T(8,128)(2,1)S(1)}, bf16[2,128,1536]{2,1,0:T(8,128)(2,1)S(1)}, u32[]{:S(2)}, u32[]{:S(2)}) collective-permute-start(bf16[2,128,1536]{2,1,0:T(8,128)(2,1)S(1)} %fusion.60), channel_id=1, source_target_pairs={{0,2},{1,3},{2,0},{3,1},{4,6},{5,7},{6,4},{7,5},{8,10},{9,11},{10,... | collective-permute-start | bytes 2359304 | tf_op jit(solution)/shard_map/ppermute | solution.py:484
  786.3 38.7 %collective-permute-start.81 = (bf16[128,1536]{1,0:T(8,128)(2,1)S(1)}, bf16[128,1536]{1,0:T(8,128)(2,1)S(1)}, u32[]{:S(2)}, u32[]{:S(2)}) collective-permute-start(bf16[128,1536]{1,0:T(8,128)(2,1)S(1)} %fusion.68), channel_id=1, source_target_pairs={{0,4},{1,5},{2,6},{3,7},{4,0},{5,1},{6,2},{7,3},{8,12},{9,13},{10,... | collective-permute-start | bytes 1179656 | tf_op jit(solution)/shard_map/ppermute | solution.py:484
  805.7 15.0 %collective-permute-start.75 = (f32[3]{0:T(128)S(1)}, f32[3]{0:T(128)S(1)}, u32[]{:S(2)}, u32[]{:S(2)}) collective-permute-start(f32[3]{0:T(128)S(1)} %add_add_fusion.4), channel_id=1, source_target_pairs={{0,2},{1,3},{2,0},{3,1},{4,6},{5,7},{6,4},{7,5},{8,10},{9,11},{10,... | collective-permute-start | bytes 44 | tf_op jit(solution)/shard_map/ppermute | solution.py:405
  821.4 17.5 %collective-permute-start.78 = (bf16[128,1536]{1,0:T(8,128)(2,1)S(1)}, bf16[128,1536]{1,0:T(8,128)(2,1)S(1)}, u32[]{:S(2)}, u32[]{:S(2)}) collective-permute-start(bf16[128,1536]{1,0:T(8,128)(2,1)S(1)} %fusion.64), channel_id=1, source_target_pairs={{0,4},{1,5},{2,6},{3,7},{4,0},{5,1},{6,2},{7,3},{8,12},{9,13},{10,... | collective-permute-start | bytes 1179656 | tf_op jit(solution)/shard_map/ppermute | solution.py:484
  (186 other events, 2039.3 us)
